TPU v7x, 32 devices: a whole 2x2x4 slice. The times are simulated.
32 devices in a mesh: row: 8 (over z, x), col: 4 (over y, core).
Axes of the slice: x: 2, y: 2, z: 4, core: 2. Of those that a mesh axis runs over, the one named last changes fastest.
Arguments:
- populations: float32 [256, 27, 4096], P(('row', 'col')), may hold values from 0 to 3, as said below
- destination: int32 [256], P(('row', 'col')), may hold values from 0 to 255, as said below
- refinement: int32 [256], P(('row', 'col')), may hold values from 0 to 4
Outputs:
- final_populations: float32 [256, 27, 4096], P(('row', 'col'))
Inputs may be any that keep to these rules, and one draw needn't show every extreme that they name: `destination`: A permutation of all slots. A slot's device is slot // 8, with row index device // 4 and column index device % 4. Of one device's blocks, 0 or 2 are bound for each row index, one row possibly taking a smaller remainder; the blocks of one column bound for one row number exactly 8, and of those, 0 or 4 are bound for each column index, one possibly taking a smaller remainder. Both bounds are reached. `populations`: Positive.
All inputs are finite; a program needn't handle non-finite values.
Results may differ from a plain program's by a relative error of at most 0.0001.
Values sent between devices are 32-bit elements; how exact they have to be, the bound alone decides.
No kernel may reach another device: no remote copies, remote signals or barrier semaphores. Data moves between devices by JAX's collectives and lax.ppermute only.
A program may use at most 192 MiB of HBM per device.

v0:
```python
import jax
import jax.numpy as jnp
from jax import lax
from jax.sharding import PartitionSpec as P

EDGE = 16


VISCOSITY = 0.01


def with_halo(cells, sides, width):
    for axis, dim in sides:
        count = lax.axis_size(axis)
        head = lax.slice_in_dim(cells, 0, width, axis=dim)
        tail = lax.slice_in_dim(cells, cells.shape[dim] - width, cells.shape[dim], axis=dim)
        cells = jnp.concatenate(
            [
                lax.ppermute(tail, axis, [(i, (i + 1) % count) for i in range(count)]),
                cells,
                lax.ppermute(head, axis, [((i + 1) % count, i) for i in range(count)]),
            ],
            axis=dim,
        )
    return cells


def relax_rate(levels):
    return 1.0 / (3.0 * VISCOSITY * jnp.exp2(levels.astype(jnp.float32)) + 0.5)


def axis_forward(values, velocity, axis):
    moved = jnp.moveaxis(values, axis, 0)
    minus_part, rest_part, plus_part = (moved[0], moved[1], moved[2])
    offset_minus = -1.0 - velocity
    offset_rest = -velocity
    offset_plus = 1.0 - velocity
    zeroth = minus_part + rest_part + plus_part
    first = offset_minus * minus_part + offset_rest * rest_part + offset_plus * plus_part
    second = (
        offset_minus * offset_minus * minus_part
        + offset_rest * offset_rest * rest_part
        + offset_plus * offset_plus * plus_part
    )
    return jnp.moveaxis(jnp.stack([zeroth, first, second]), 0, axis)


def axis_backward(moments, velocity, axis):
    moved = jnp.moveaxis(moments, axis, 0)
    zeroth, first, second = (moved[0], moved[1], moved[2])
    raw_one = first + velocity * zeroth
    raw_two = second + 2.0 * velocity * first + velocity * velocity * zeroth
    minus_part = 0.5 * (raw_two - raw_one)
    rest_part = zeroth - raw_two
    plus_part = 0.5 * (raw_one + raw_two)
    return jnp.moveaxis(jnp.stack([minus_part, rest_part, plus_part]), 0, axis)


def collide(flat, rate):
    grid = flat.reshape((3, 3, 3) + flat.shape[1:])
    density = jnp.sum(flat, axis=0)
    velocity_x = (jnp.sum(grid[2], axis=(0, 1)) - jnp.sum(grid[0], axis=(0, 1))) / density
    velocity_y = (jnp.sum(grid[:, 2], axis=(0, 1)) - jnp.sum(grid[:, 0], axis=(0, 1))) / density
    velocity_z = (
        jnp.sum(grid[:, :, 2], axis=(0, 1)) - jnp.sum(grid[:, :, 0], axis=(0, 1))
    ) / density
    central = axis_forward(grid, velocity_x, 0)
    central = axis_forward(central, velocity_y, 1)
    central = axis_forward(central, velocity_z, 2)
    keep = 1.0 - rate
    post_xy = keep * central[1, 1, 0]
    post_xz = keep * central[1, 0, 1]
    post_yz = keep * central[0, 1, 1]
    dev_one = keep * (central[2, 0, 0] - central[0, 2, 0])
    dev_two = keep * (central[2, 0, 0] - central[0, 0, 2])
    post_xx = (density + dev_one + dev_two) / 3.0
    post_yy = post_xx - dev_one
    post_zz = post_xx - dev_two
    inverse = 1.0 / density
    entries = {
        (0, 0, 0): density,
        (2, 0, 0): post_xx,
        (0, 2, 0): post_yy,
        (0, 0, 2): post_zz,
        (1, 1, 0): post_xy,
        (1, 0, 1): post_xz,
        (0, 1, 1): post_yz,
        (2, 2, 0): (post_xx * post_yy + 2.0 * post_xy * post_xy) * inverse,
        (2, 0, 2): (post_xx * post_zz + 2.0 * post_xz * post_xz) * inverse,
        (0, 2, 2): (post_yy * post_zz + 2.0 * post_yz * post_yz) * inverse,
        (2, 1, 1): (post_xx * post_yz + 2.0 * post_xy * post_xz) * inverse,
        (1, 2, 1): (post_yy * post_xz + 2.0 * post_xy * post_yz) * inverse,
        (1, 1, 2): (post_zz * post_xy + 2.0 * post_xz * post_yz) * inverse,
        (2, 2, 2): (
            post_xx * post_yy * post_zz
            + 2.0
            * (
                post_xx * post_yz * post_yz
                + post_yy * post_xz * post_xz
                + post_zz * post_xy * post_xy
            )
            + 8.0 * post_xy * post_xz * post_yz
        )
        * inverse
        * inverse,
    }
    zeros_field = jnp.zeros_like(density)
    stacked = jnp.stack(
        [
            entries.get((power_x, power_y, power_z), zeros_field)
            for power_x in range(3)
            for power_y in range(3)
            for power_z in range(3)
        ]
    )
    moments = stacked.reshape(grid.shape)
    back = axis_backward(moments, velocity_z, 2)
    back = axis_backward(back, velocity_y, 1)
    back = axis_backward(back, velocity_x, 0)
    return back.reshape(flat.shape)


def collide_brick(lattice, rates_field):
    return lax.map(lambda operands: collide(operands[0], operands[1]), (lattice, rates_field))


def bucket(targets, present, capacity, groups):
    count = targets.shape[0]
    positions = jnp.arange(count)
    alike = (targets[:, None] == targets[None, :]) & present[None, :]
    earlier = positions[None, :] < positions[:, None]
    rank_in = jnp.sum(alike & earlier, axis=1)
    placing = jnp.where(present, targets * capacity + rank_in, -1)
    hits = placing[None, :] == jnp.arange(groups * capacity)[:, None]
    source = jnp.sum(jnp.where(hits, positions[None, :], 0), axis=1)
    filled = jnp.any(hits, axis=1)
    return (source, filled)


def pack(source, filled, data, targets, levels):
    return (
        jnp.where(filled[:, None, None], jnp.take(data, source, axis=0), 0.0),
        jnp.where(filled, jnp.take(targets, source), -1),
        jnp.take(levels, source),
    )


def to_brick(arrived, blocks):
    shaped = arrived.reshape(blocks, 27, EDGE, EDGE, EDGE)
    ordered = jnp.transpose(shaped, (2, 1, 3, 0, 4))
    return ordered.reshape(EDGE, 27, EDGE, blocks * EDGE)


def from_brick(lattice, blocks):
    shaped = lattice.reshape(EDGE, 27, EDGE, blocks, EDGE)
    ordered = jnp.transpose(shaped, (3, 1, 0, 2, 4))
    return ordered.reshape(blocks, 27, EDGE * EDGE * EDGE)


def stream_brick(lattice):
    width_x = lattice.shape[0]
    width_y = lattice.shape[2]
    padded = with_halo(lattice, (("row", 0), ("col", 2)), 1)
    read = []
    for component in range(27):
        shift_x = component // 9 - 1
        shift_y = component // 3 % 3 - 1
        shift_z = component % 3 - 1
        mirror = lattice[:, 26 - component]
        shifted = padded[
            1 - shift_x : 1 - shift_x + width_x, component, 1 - shift_y : 1 - shift_y + width_y, :
        ]
        if shift_z == 1:
            shifted = jnp.concatenate([mirror[..., :1], shifted[..., :-1]], axis=-1)
        elif shift_z == -1:
            shifted = jnp.concatenate([shifted[..., 1:], mirror[..., -1:]], axis=-1)
        read.append(shifted)
    return jnp.stack(read, axis=1)


def on_device(populations, destination, refinement):
    blocks = populations.shape[0]
    row_count = lax.axis_size("row")
    col_count = lax.axis_size("col")
    cap_row = 2 * ((blocks + row_count - 1) // row_count)
    cap_col = 2 * ((blocks + col_count - 1) // col_count)
    all_present = jnp.ones((blocks,), dtype=bool)
    target_row = destination // blocks // col_count
    source_one, filled_one = bucket(target_row, all_present, cap_row, row_count)
    outgoing_one = pack(source_one, filled_one, populations, destination, refinement)
    sectioned, sectioned_target, sectioned_level = (
        lax.all_to_all(outgoing_one[0], "row", split_axis=0, concat_axis=0, tiled=True),
        lax.all_to_all(outgoing_one[1], "row", split_axis=0, concat_axis=0, tiled=True),
        lax.all_to_all(outgoing_one[2], "row", split_axis=0, concat_axis=0, tiled=True),
    )
    present_two = sectioned_target >= 0
    target_col = sectioned_target // blocks % col_count
    source_two, filled_two = bucket(target_col, present_two, cap_col, col_count)
    outgoing_two = pack(source_two, filled_two, sectioned, sectioned_target, sectioned_level)
    landed, landed_target, landed_level = (
        lax.all_to_all(outgoing_two[0], "col", split_axis=0, concat_axis=0, tiled=True),
        lax.all_to_all(outgoing_two[1], "col", split_axis=0, concat_axis=0, tiled=True),
        lax.all_to_all(outgoing_two[2], "col", split_axis=0, concat_axis=0, tiled=True),
    )
    slot_ids = jnp.arange(blocks)
    matches = (landed_target[None, :] % blocks == slot_ids[:, None]) & (landed_target[None, :] >= 0)
    picked = jnp.sum(jnp.where(matches, jnp.arange(landed_target.shape[0])[None, :], 0), axis=1)
    arrived = jnp.take(landed, picked, axis=0)
    levels = jnp.take(landed_level, picked)
    lattice = to_brick(arrived, blocks)
    rates = relax_rate(levels)
    rates_field = jnp.broadcast_to(rates[None, None, :, None], (EDGE, EDGE, blocks, EDGE))
    rates_field = rates_field.reshape(EDGE, EDGE, blocks * EDGE)
    lattice = collide_brick(lattice, rates_field)
    lattice = stream_brick(lattice)
    return from_brick(lattice, blocks)


def solution(mesh):
    return jax.shard_map(
        on_device,
        mesh=mesh,
        in_specs=(P(("row", "col"), None, None), P(("row", "col")), P(("row", "col"))),
        out_specs=P(("row", "col"), None, None),
        check_vma=False,
    )
```

profile of v0, /device:TPU:0, one launch (start us, length us, event | category | flops | bytes accessed | tf_op | source)
XLA Modules:
  0.0 692.7 jit_solution(11146136977860952474)
XLA Ops:
  7.5 7.3 %all-to-all-start = ((s32[8,2,1]{1,2,0:T(1,128)}), s32[8,2,1]{1,2,0:T(1,128)S(1)}, u32[]{:S(2)}, u32[]{:S(2)}) async-start(s32[8,2,1]{1,2,0:T(1,128)} %bitcast.21), calls=%async_computation | async-start | bytes 8192 | tf_op jit(solution)/shard_map/all_to_all | solution.py:193
  16.7 4.5 all-to-all-done
  21.2 3.2 all-to-all-start.4
  27.1 13.2 %gather_fusion = f32[16,27,4096]{2,0,1:T(8,128)} fusion(f32[8,27,4096]{2,0,1:T(8,128)S(1)} %copy-done, s32[1024]{0:T(1024)S(1)} %get-tuple-element.175), kind=kCustom, calls=%fused_computation.4 | custom fusion | bytes 14155840 | tf_op jit(solution)/shard_map/jit(_take)/gather | solution.py:142
  40.3 3.9 select_select_fusion
  44.2 7.7 %copy.137 = f32[16,27,4096]{2,1,0:T(8,128)} copy(f32[16,27,4096]{2,0,1:T(8,128)S(1)} %select_select_fusion) | data formatting | bytes 14155776 | tf_op jit(solution)/shard_map/jit(_where)/select_n | solution.py:142
  51.9 5.9 all-to-all-start.2
  60.8 178.6 %all-to-all-done.2 = f32[16,27,4096]{2,1,0:T(8,128)} async-done(((f32[16,27,4096]{2,1,0:T(8,128)}), f32[16,27,4096]{2,1,0:T(8,128)}, u32[]{:S(2)}, u32[]{:S(2)}) %all-to-all-start.2) | async-done | bytes 7077920 | tf_op jit(solution)/shard_map/all_to_all | solution.py:192
  239.3 3.2 all-to-all-start.1
  242.6 7.7 %gather_fusion.1 = f32[16,27,4096]{2,1,0:T(8,128)} fusion(f32[16,27,4096]{2,1,0:T(8,128)} %all-to-all-done.2, s32[1024]{0:T(1024)S(1)} %pad_clamp_fusion.1), kind=kCustom, calls=%fused_computation.5 | custom fusion | bytes 14155840 | tf_op jit(solution)/shard_map/jit(_take)/gather | solution.py:142
  250.3 8.4 %fusion.34 = f32[16,27,4096]{2,0,1:T(8,128)S(1)} fusion(f32[16,27,4096]{2,1,0:T(8,128)} %gather_fusion.1, pred[16]{0:T(512)(128)(4,1)S(1)} %get-tuple-element.73, pred[16]{0:T(512)(128)(4,1)S(1)} %fusion.37), kind=kLoop, calls=%fused_computation.138 | loop fusion | flops 3538944 | bytes 14155808 | tf_op jit(solution)/shard_map/jit(_where)/select_n | solution.py:142
  258.7 7.4 %copy.139 = f32[16,27,4096]{2,1,0:T(8,128)} copy(f32[16,27,4096]{2,0,1:T(8,128)S(1)} %fusion.34) | data formatting | bytes 14155776 | tf_op jit(solution)/shard_map/jit(_where)/select_n | solution.py:142
  266.1 6.8 all_to_all.58
  272.9 5.8 all-to-all-start.3
  281.0 90.8 %all-to-all-done.3 = f32[16,27,4096]{2,1,0:T(8,128)} async-done(((f32[16,27,4096]{2,1,0:T(8,128)}), f32[16,27,4096]{2,1,0:T(8,128)}, u32[]{:S(2)}, u32[]{:S(2)}) %all-to-all-start.3) | async-done | bytes 7077920 | tf_op jit(solution)/shard_map/all_to_all | solution.py:201
  371.8 6.2 gather_fusion.2
  378.0 4.2 copy.140
  382.2 13.7 %gather.27 = f32[8,27,16,16,16]{4,3,2,0,1:T(8,128)} reshape(f32[8,27,4096]{2,0,1:T(8,128)S(1)} %copy.140) | data formatting | bytes 7077888 | tf_op jit(solution)/shard_map/jit(_take)/gather | solution.py:208
  396.0 11.1 %select_bitcast_fusion = f32[16,27,16,8,16]{4,2,0,3,1:T(8,128)S(1)} fusion(f32[8,27,16,16,16]{4,3,2,0,1:T(8,128)} %gather.27, pred[8]{0:T(512)(128)(4,1)S(1)} %get-tuple-element.71), kind=kLoop, calls=%fused_computation.136 | loop fusion | flops 884736 | bytes 7077896 | tf_op jit(solution)/shard_map/transpose | solution.py:150
  407.1 18.9 %copy.141 = f32[16,27,16,8,16]{4,3,2,1,0:T(8,128)} copy(f32[16,27,16,8,16]{4,2,0,3,1:T(8,128)S(1)} %select_bitcast_fusion) | data formatting | bytes 7077888 | tf_op jit(solution)/shard_map/transpose | solution.py:150
  426.0 18.2 %reshape.672 = f32[16,27,16,128]{3,2,1,0:T(8,128)} reshape(f32[16,27,16,8,16]{4,3,2,1,0:T(8,128)} %copy.141) | data formatting | bytes 7077888 | tf_op jit(solution)/shard_map/reshape | solution.py:151
  444.2 58.3 %while.10 = (s32[]{:T(128)}, f32[16,27,16,128]{3,2,1,0:T(8,128)}, f32[16,27,16,128]{3,2,1,0:T(8,128)}, f32[16,16,128]{2,1,0:T(8,128)S(1)}, s32[]{:T(128)}, /*index=5*/s32[]{:T(128)}, s32[]{}, s32[]{}) while((s32[]{:T(128)}, f32[16,27,16,128]{3,2,1,0:T(8,128)}, f32[16,27,16,128]{3,2,1,0:T(8,128)}, f32[16,16,128]{2,1,0:T(8,128)S(1)}, ...), condition=%wide.region_15.18_spmd, body=%wide.region_7.17_spmd.sunk | while | flops 2406404 | bytes 9527949 | solution.py:124
  504.3 2.7 slice_bitcast_fusion.9
  509.5 3.3 collective-permute-start.1
  523.3 2.8 constant_dynamic-update-slice_fusion.33
  562.9 2.5 fusion.36
  618.7 2.6 copy_dynamic-update-slice_fusion.25
  621.3 3.2 copy_dynamic-update-slice_fusion.24
  635.3 2.5 copy_dynamic-update-slice_fusion.18
  647.5 2.6 copy_dynamic-update-slice_fusion.12
  662.0 2.7 copy_dynamic-update-slice_fusion.3
  668.3 24.0 %reshape.673 = f32[8,27,4096]{2,0,1:T(8,128)} reshape(f32[8,27,16,16,16]{4,3,2,0,1:T(8,128)} %bitcast.277) | data formatting | bytes 7077888 | tf_op jit(solution)/shard_map/reshape | solution.py:157
  (1006 shorter events, 211.0 us)
Async XLA Ops:
  0.0 27.1 %copy-start = (f32[8,27,4096]{2,0,1:T(8,128)S(1)}, f32[8,27,4096]{2,0,1:T(8,128)}, u32[]{:S(2)}) copy-start(f32[8,27,4096]{2,0,1:T(8,128)} %param.9) | copy-start | bytes 10616836
  1.8 0.6 copy-start.16
  1.9 19.2 %copy-start.13 = (pred[16]{0:T(512)(128)(4,1)}, pred[16]{0:T(512)(128)(4,1)S(1)}, u32[]{:S(2)}) copy-start(pred[16]{0:T(512)(128)(4,1)S(1)} %fusion.39) | copy-start | bytes 52
  6.3 0.6 copy-start.12
  7.5 13.6 %all-to-all-start = ((s32[8,2,1]{1,2,0:T(1,128)}), s32[8,2,1]{1,2,0:T(1,128)S(1)}, u32[]{:S(2)}, u32[]{:S(2)}) async-start(s32[8,2,1]{1,2,0:T(1,128)} %bitcast.21), calls=%async_computation | async-start | bytes 8192 | tf_op jit(solution)/shard_map/all_to_all | solution.py:193
  21.2 30.8 %all-to-all-start.4 = ((s32[8,2,1]{1,2,0:T(1,128)}), s32[8,2,1]{1,2,0:T(1,128)S(1)}, u32[]{:S(2)}, u32[]{:S(2)}) async-start(s32[8,2,1]{1,2,0:T(1,128)} %bitcast.30), calls=%async_computation.4 | async-start | bytes 8192 | tf_op jit(solution)/shard_map/all_to_all | solution.py:194
  25.8 0.5 copy-start.17
  26.5 0.7 copy-start.14
  40.3 19.6 %copy-start.18 = (s32[16]{0:T(128)S(1)}, s32[16]{0:T(128)}, u32[]{:S(2)}) copy-start(s32[16]{0:T(128)} %copy-done.17) | copy-start | bytes 196
  40.3 19.7 %copy-start.15 = (s32[16]{0:T(128)S(1)}, s32[16]{0:T(128)}, u32[]{:S(2)}) copy-start(s32[16]{0:T(128)} %copy-done.14) | copy-start | bytes 196
  51.9 187.4 %all-to-all-start.2 = ((f32[16,27,4096]{2,1,0:T(8,128)}), f32[16,27,4096]{2,1,0:T(8,128)}, u32[]{:S(2)}, u32[]{:S(2)}) async-start(f32[16,27,4096]{2,1,0:T(8,128)} %copy.137), calls=%async_computation.2 | async-start | bytes 16777216 | tf_op jit(solution)/shard_map/all_to_all | solution.py:192
  239.3 26.7 %all-to-all-start.1 = ((s32[4,4,1]{1,2,0:T(1,128)}), s32[4,4,1]{1,2,0:T(1,128)S(1)}, u32[]{:S(2)}, u32[]{:S(2)}) async-start(s32[4,4,1]{1,2,0:T(1,128)} %bitcast.22), calls=%async_computation.1 | async-start | bytes 4096 | tf_op jit(solution)/shard_map/all_to_all | solution.py:202
  272.9 99.0 %all-to-all-start.3 = ((f32[16,27,4096]{2,1,0:T(8,128)}), f32[16,27,4096]{2,1,0:T(8,128)}, u32[]{:S(2)}, u32[]{:S(2)}) async-start(f32[16,27,4096]{2,1,0:T(8,128)} %copy.139), calls=%async_computation.3 | async-start | bytes 16777216 | tf_op jit(solution)/shard_map/all_to_all | solution.py:201
  508.0 14.4 %collective-permute-start = (f32[1,27,16,128]{3,2,1,0:T(8,128)}, f32[1,27,16,128]{3,2,1,0:T(8,128)}, u32[]{:S(2)}, u32[]{:S(2)}) collective-permute-start(f32[1,27,16,128]{3,2,1,0:T(8,128)} %get-tuple-element.170), channel_id=1, source_target_pairs={{0,4},{4,8},{8,12},{12,16},{16,20},{20,24},{24,28},{28,0},{1,5},{5... | collective-permute-start | bytes 663560 | tf_op jit(solution)/shard_map/ppermute | solution.py:19
  509.5 16.7 %collective-permute-start.1 = (f32[1,27,16,128]{3,2,1,0:T(8,128)}, f32[1,27,16,128]{3,2,1,0:T(8,128)}, u32[]{:S(2)}, u32[]{:S(2)}) collective-permute-start(f32[1,27,16,128]{3,2,1,0:T(8,128)} %get-tuple-element.169), channel_id=1, source_target_pairs={{4,0},{8,4},{12,8},{16,12},{20,16},{24,20},{28,24},{0,28},{5,1},{9... | collective-permute-start | bytes 663560 | tf_op jit(solution)/shard_map/ppermute | solution.py:21
  527.1 1.9 copy-start.2
  530.1 21.7 %collective-permute-start.3 = (f32[18,27,1,128]{3,2,1,0:T(1,128)}, f32[18,27,1,128]{3,2,1,0:T(1,128)}, u32[]{:S(2)}, u32[]{:S(2)}) collective-permute-start(f32[18,27,1,128]{3,2,1,0:T(1,128)} %get-tuple-element.140), channel_id=1, source_target_pairs={{0,1},{1,2},{2,3},{3,0},{4,5},{5,6},{6,7},{7,4},{8,9},{9,10},{10,1... | collective-permute-start | bytes 746504 | tf_op jit(solution)/shard_map/ppermute | solution.py:19
  536.6 26.3 %collective-permute-start.2 = (f32[18,27,1,128]{3,2,1,0:T(1,128)}, f32[18,27,1,128]{3,2,1,0:T(1,128)}, u32[]{:S(2)}, u32[]{:S(2)}) collective-permute-start(f32[18,27,1,128]{3,2,1,0:T(1,128)} %get-tuple-element.141), channel_id=1, source_target_pairs={{1,0},{2,1},{3,2},{0,3},{5,4},{6,5},{7,6},{4,7},{9,8},{10,9},{11,1... | collective-permute-start | bytes 746504 | tf_op jit(solution)/shard_map/ppermute | solution.py:21
  618.6 31.4 %copy-start.4 = (f32[16,1,16,8,16]{4,3,2,0,1:T(8,128)S(1)}, f32[16,1,16,8,16]{4,3,2,0,1:T(8,128)}, u32[]{:S(2)}) copy-start(f32[16,1,16,8,16]{4,3,2,0,1:T(8,128)} %stack.145) | copy-start | bytes 393220
  618.6 32.6 %copy-start.3 = (f32[16,1,16,8,16]{4,3,2,0,1:T(8,128)S(1)}, f32[16,1,16,8,16]{4,3,2,0,1:T(8,128)}, u32[]{:S(2)}) copy-start(f32[16,1,16,8,16]{4,3,2,0,1:T(8,128)} %stack.146) | copy-start | bytes 393220
  618.6 33.7 %copy-start.5 = (f32[16,1,16,8,16]{4,3,2,0,1:T(8,128)S(1)}, f32[16,1,16,8,16]{4,3,2,0,1:T(8,128)}, u32[]{:S(2)}) copy-start(f32[16,1,16,8,16]{4,3,2,0,1:T(8,128)} %stack.147) | copy-start | bytes 393220
  618.7 34.9 %copy-start.9 = (f32[16,1,16,8,16]{4,3,2,0,1:T(8,128)S(1)}, f32[16,1,16,8,16]{4,3,2,0,1:T(8,128)}, u32[]{:S(2)}) copy-start(f32[16,1,16,8,16]{4,3,2,0,1:T(8,128)} %stack.148) | copy-start | bytes 393220
  618.7 36.1 %copy-start.8 = (f32[16,1,16,8,16]{4,3,2,0,1:T(8,128)S(1)}, f32[16,1,16,8,16]{4,3,2,0,1:T(8,128)}, u32[]{:S(2)}) copy-start(f32[16,1,16,8,16]{4,3,2,0,1:T(8,128)} %stack.149) | copy-start | bytes 393220
  618.7 37.3 %copy-start.11 = (f32[16,1,16,8,16]{4,3,2,0,1:T(8,128)S(1)}, f32[16,1,16,8,16]{4,3,2,0,1:T(8,128)}, u32[]{:S(2)}) copy-start(f32[16,1,16,8,16]{4,3,2,0,1:T(8,128)} %stack.150) | copy-start | bytes 393220
  618.7 46.0 %copy-start.7 = (f32[16,1,16,8,16]{4,3,2,0,1:T(8,128)S(1)}, f32[16,1,16,8,16]{4,3,2,0,1:T(8,128)}, u32[]{:S(2)}) copy-start(f32[16,1,16,8,16]{4,3,2,0,1:T(8,128)} %stack.154) | copy-start | bytes 393220
  618.7 47.2 %copy-start.6 = (f32[16,1,16,8,16]{4,3,2,0,1:T(8,128)S(1)}, f32[16,1,16,8,16]{4,3,2,0,1:T(8,128)}, u32[]{:S(2)}) copy-start(f32[16,1,16,8,16]{4,3,2,0,1:T(8,128)} %stack.155) | copy-start | bytes 393220
  618.7 48.4 %copy-start.10 = (f32[16,1,16,8,16]{4,3,2,0,1:T(8,128)S(1)}, f32[16,1,16,8,16]{4,3,2,0,1:T(8,128)}, u32[]{:S(2)}) copy-start(f32[16,1,16,8,16]{4,3,2,0,1:T(8,128)} %stack.156) | copy-start | bytes 393220
  647.5 44.8 %copy-start.1 = (f32[8,27,4096]{2,0,1:T(8,128)S(1)}, f32[8,27,4096]{2,0,1:T(8,128)}, u32[]{:S(2)}) copy-start(f32[8,27,4096]{2,0,1:T(8,128)} %param.9) | copy-start | bytes 10616836
where the time goes:
time: 706 us; the launch traced here: 693 us
  local copies, waits for them, and re-layouts  275 us (39%)
  waiting for transfers between devices  274 us (39%)
  other arithmetic  99 us (14%)
  starting transfers between devices  32.2 us (5%)
    all_to_all x1, waiting for transfers between devices, on_device(): lax.all_to_all(outgoing_one[0], 'row', split_axis=0, concat_axis=0, tiled...  179 us
    all_to_all x1, waiting for transfers between devices, on_device(): lax.all_to_all(outgoing_two[0], 'col', split_axis=0, concat_axis=0, tiled...  90.8 us
    unnamed x65, local copies, waits for them, and re-layouts  55.2 us
    another operation x28, local copies, waits for them, and re-layouts, stream_brick(): return jnp.stack(read, axis=1)  51.5 us
    gather x3, local copies, waits for them, and re-layouts, on_device(): arrived = jnp.take(landed, picked, axis=0)  24.1 us
    reshape x1, local copies, waits for them, and re-layouts, from_brick(): return ordered.reshape(blocks, 27, EDGE * EDGE * EDGE)  24 us
    gather x2, local copies, waits for them, and re-layouts, pack(): jnp.take(data, source, axis=0)  20.9 us
    transpose x1, local copies, waits for them, and re-layouts, to_brick(): ordered = jnp.transpose(shaped, (2, 1, 3, 0, 4))  18.9 us
  transfers between devices with their start and end apart: 9, of which 3 were waited for; matrix products, arithmetic and copies ran while one was open for 14% of the time, Pallas kernels for 0%

commit v1 on v0

v1 whole, which is shorter than its diff:
```python
import functools

import jax
import jax.numpy as jnp
import numpy as np
from jax import lax
from jax.experimental import pallas as pl
from jax.experimental.pallas import tpu as pltpu
from jax.sharding import PartitionSpec as P

EDGE = 16
VISCOSITY = 0.01
LANES = 128
SUB = 8
NQ = 27
QPAD = 32
NFIELD = 9
GROUPS = 4
VMEM_LIMIT = 50 * 1024 * 1024


def velocity(q):
    return (q // 9 - 1, (q // 3) % 3 - 1, q % 3 - 1)


def moment_matrix(blocks):
    powers = [
        (0, 0, 0), (1, 0, 0), (0, 1, 0), (0, 0, 1), (2, 0, 0),
        (0, 2, 0), (0, 0, 2), (1, 1, 0), (1, 0, 1), (0, 1, 1),
    ]
    out = np.zeros((len(powers), blocks, blocks, QPAD), np.float32)
    for m, (a, b, c) in enumerate(powers):
        for q in range(NQ):
            cx, cy, cz = velocity(q)
            for t in range(blocks):
                out[m, t, t, q] = float(cx**a * cy**b * cz**c)
    return out.reshape(len(powers) * blocks, blocks * QPAD)


def pre_kernel(cap, per_row, dest_ref, level_ref, w_ref, x_ref, out_ref, mom_ref, swap_ref):
    blocks = x_ref.shape[0]
    cells = x_ref.shape[2]
    chunks = cells // LANES
    x = x_ref[...]
    comp = lax.broadcasted_iota(jnp.int32, x.shape, 1)
    x = jnp.where(comp < NQ, x, 0.0).reshape(blocks * QPAD, cells)
    w = w_ref[...].astype(jnp.bfloat16)
    high = x.astype(jnp.bfloat16)
    rest = x - high.astype(jnp.float32)
    mid = rest.astype(jnp.bfloat16)
    low = (rest - mid.astype(jnp.float32)).astype(jnp.bfloat16)
    dot = functools.partial(jnp.dot, preferred_element_type=jnp.float32)
    mom_ref[...] = dot(w, low) + dot(w, mid) + dot(w, high)

    which = lax.broadcasted_iota(jnp.int32, (SUB, LANES), 0)
    scale = jnp.zeros((SUB, LANES), jnp.int32)
    for t in range(blocks):
        scale = jnp.where(which == t, jnp.left_shift(1, level_ref[t]), scale)
    rate = 1.0 / (3.0 * VISCOSITY * scale.astype(jnp.float32) + 0.5)
    keep = 1.0 - rate

    for c in range(chunks):
        rho, jx, jy, jz, mxx, myy, mzz, mxy, mxz, myz = [
            mom_ref[m * SUB : (m + 1) * SUB, c * LANES : (c + 1) * LANES] for m in range(10)
        ]
        inverse = 1.0 / rho
        ux, uy, uz = jx * inverse, jy * inverse, jz * inverse
        kxx = mxx - jx * ux
        fields = (
            rho, ux, uy, uz,
            keep * (mxy - jx * uy),
            keep * (mxz - jx * uz),
            keep * (myz - jy * uz),
            keep * (kxx - (myy - jy * uy)),
            keep * (kxx - (mzz - jz * uz)),
        )
        for n, field in enumerate(fields):
            base = (n * chunks + c) * SUB
            swap_ref[base : base + SUB, :] = field

    rows = [dest_ref[t] // per_row for t in range(blocks)]
    for t in range(blocks):
        slot = rows[t] * cap
        for other in range(t):
            slot = slot + jnp.where(rows[other] == rows[t], 1, 0)
        for n in range(NFIELD):
            out_ref[slot, 0, n] = swap_ref[pl.ds(n * chunks * SUB + t, SUB, stride=SUB), :]


def pre(populations, destination, refinement, row_count, cap, per_row):
    blocks = populations.shape[0]
    cells = populations.shape[2] // GROUPS
    weights = jnp.asarray(moment_matrix(blocks))
    slots = row_count * cap
    return pl.pallas_call(
        functools.partial(pre_kernel, cap, per_row),
        grid_spec=pltpu.PrefetchScalarGridSpec(
            num_scalar_prefetch=2,
            grid=(GROUPS,),
            in_specs=[
                pl.BlockSpec(weights.shape, lambda g, *_: (0, 0)),
                pl.BlockSpec((blocks, QPAD, cells), lambda g, *_: (0, 0, g)),
            ],
            out_specs=pl.BlockSpec((slots, 1, NFIELD, SUB, LANES), lambda g, *_: (0, g, 0, 0, 0)),
            scratch_shapes=[
                pltpu.VMEM((10 * SUB, cells), jnp.float32),
                pltpu.VMEM((NFIELD * cells // LANES * SUB, LANES), jnp.float32),
            ],
        ),
        out_shape=jax.ShapeDtypeStruct((slots, GROUPS, NFIELD, SUB, LANES), jnp.float32),
        compiler_params=pltpu.CompilerParams(vmem_limit_bytes=VMEM_LIMIT),
        cost_estimate=pl.CostEstimate(flops=10**8, bytes_accessed=6 * 10**6, transcendentals=0),
    )(destination, refinement, weights, populations)


def repack_kernel(source_ref, target_ref, in_ref, out_ref, sems):
    count = source_ref.shape[0]
    copies = [
        pltpu.make_async_copy(in_ref.at[source_ref[j]], out_ref.at[target_ref[j]], sems.at[j])
        for j in range(count)
    ]
    for copy in copies:
        copy.start()
    for copy in copies:
        copy.wait()


def repack(source, target, landed, slots):
    count = source.shape[0]
    return pl.pallas_call(
        repack_kernel,
        in_specs=[
            pl.BlockSpec(memory_space=pltpu.SMEM),
            pl.BlockSpec(memory_space=pltpu.SMEM),
            pl.BlockSpec(memory_space=pl.ANY),
        ],
        out_specs=pl.BlockSpec(memory_space=pl.ANY),
        scratch_shapes=[pltpu.SemaphoreType.DMA((count,))],
        out_shape=jax.ShapeDtypeStruct((slots,) + landed.shape[1:], jnp.float32),
        cost_estimate=pl.CostEstimate(flops=0, bytes_accessed=3 * 10**6, transcendentals=0),
    )(source, target, landed)


def backward(zeroth, first, second, u):
    raw_one, raw_two = first, second
    if zeroth is not None:
        moved = u * zeroth
        raw_one = moved if raw_one is None else raw_one + moved
        square = u * moved
        raw_two = square if raw_two is None else raw_two + square
    if first is not None:
        cross = (u + u) * first
        raw_two = cross if raw_two is None else raw_two + cross
    rest = -raw_two if zeroth is None else zeroth - raw_two
    return 0.5 * (raw_two - raw_one), rest, 0.5 * (raw_one + raw_two)


def post_populations(rho, ux, uy, uz, pxy, pxz, pyz, dev_one, dev_two):
    inverse = 1.0 / rho
    pxx = (rho + dev_one + dev_two) * (1.0 / 3.0)
    pyy = pxx - dev_one
    pzz = pxx - dev_two
    sxy, sxz, syz = pxy * inverse, pxz * inverse, pyz * inverse
    sxx, syy = pxx * inverse, pyy * inverse
    szz = pzz * inverse
    central = {
        (0, 0, 0): rho, (2, 0, 0): pxx, (0, 2, 0): pyy, (0, 0, 2): pzz,
        (1, 1, 0): pxy, (1, 0, 1): pxz, (0, 1, 1): pyz,
        (2, 2, 0): pxx * syy + 2.0 * pxy * sxy,
        (2, 0, 2): pxx * szz + 2.0 * pxz * sxz,
        (0, 2, 2): pyy * szz + 2.0 * pyz * syz,
        (2, 1, 1): pxx * syz + 2.0 * pxy * sxz,
        (1, 2, 1): pyy * sxz + 2.0 * pxy * syz,
        (1, 1, 2): pzz * sxy + 2.0 * pxz * syz,
        (2, 2, 2): pxx * syy * szz
        + 2.0 * (pxx * syz * syz + pyy * sxz * sxz + pzz * sxy * sxy)
        + 8.0 * pxy * sxz * syz,
    }
    along_z = {}
    for a in range(3):
        for b in range(3):
            parts = backward(*(central.get((a, b, c)) for c in range(3)), uz)
            for k in range(3):
                along_z[a, b, k] = parts[k]
    along_y = {}
    for a in range(3):
        for k in range(3):
            parts = backward(*(along_z[a, b, k] for b in range(3)), uy)
            for j in range(3):
                along_y[a, j, k] = parts[j]
    result = [None] * NQ
    for j in range(3):
        for k in range(3):
            parts = backward(*(along_y[a, j, k] for a in range(3)), ux)
            for i in range(3):
                result[i * 9 + j * 3 + k] = parts[i]
    return result


def post_kernel(picked_ref, *refs):
    ins, (post_ref, xlo_ref, xhi_ref, ylo_ref, yhi_ref, mm_ref, mp_ref, pm_ref, pp_ref, swap_ref) = (
        refs[:SUB], refs[SUB:],
    )
    g = pl.program_id(0)
    for t in range(SUB):
        for n in range(NFIELD):
            swap_ref[pl.ds(n * SUB * SUB + t, SUB, stride=SUB), :] = ins[t][0, 0, n]
    lane = lax.broadcasted_iota(jnp.int32, (SUB, LANES), 1)
    for c in range(SUB):
        fields = [swap_ref[(n * SUB + c) * SUB : (n * SUB + c + 1) * SUB, :] for n in range(NFIELD)]
        result = post_populations(*fields)
        for q in range(NQ):
            post_ref[q, c] = result[q]
        x_in, half = c // 2, c % 2
        spot = (g % 2) * 4 + x_in
        inside = (lane // EDGE) == spot
        face_ref, first, shift = ((ylo_ref, 0, 0), (yhi_ref, 6, EDGE))[half]
        turn = spot * EDGE + shift
        for i in range(3):
            for k in range(3):
                value = pltpu.roll(result[i * 9 + first + k], turn % LANES, axis=1)
                face_ref[i * 3 + k, 0] = jnp.where(inside, value, face_ref[i * 3 + k, 0])

        if x_in == 0:

            @pl.when(g == 0)
            def _():
                for q in range(9):
                    xlo_ref[q, half] = result[q]
                for k in range(3):
                    if half == 0:
                        mm_ref[k] = result[k]
                    else:
                        mp_ref[k] = result[6 + k]

        if x_in == 3:

            @pl.when(g == GROUPS - 1)
            def _():
                for q in range(9):
                    xhi_ref[q, half] = result[18 + q]
                for k in range(3):
                    if half == 0:
                        pm_ref[k] = result[18 + k]
                    else:
                        pp_ref[k] = result[24 + k]


def post(picked, landed):
    shape = jax.ShapeDtypeStruct
    face = (9, 2, SUB, LANES)
    corner = (3, SUB, LANES)

    def pick(t):
        return pl.BlockSpec(
            (1, 1, NFIELD, SUB, LANES), lambda g, picked_ref: (picked_ref[t], g, 0, 0, 0)
        )

    whole_face = pl.BlockSpec(face, lambda g, *_: (0, 0, 0, 0))
    half_face = pl.BlockSpec((9, 1, SUB, LANES), lambda g, *_: (0, g // 2, 0, 0))
    whole_corner = pl.BlockSpec(corner, lambda g, *_: (0, 0, 0))
    return pl.pallas_call(
        post_kernel,
        grid_spec=pltpu.PrefetchScalarGridSpec(
            num_scalar_prefetch=1,
            grid=(GROUPS,),
            in_specs=[pick(t) for t in range(SUB)],
            out_specs=[
                pl.BlockSpec((NQ, SUB, SUB, LANES), lambda g, *_: (0, g, 0, 0)),
                whole_face, whole_face, half_face, half_face,
                whole_corner, whole_corner, whole_corner, whole_corner,
            ],
            scratch_shapes=[pltpu.VMEM((NFIELD * SUB * SUB, LANES), jnp.float32)],
        ),
        out_shape=[shape((NQ, GROUPS * SUB, SUB, LANES), jnp.float32)]
        + [shape(face, jnp.float32)] * 4
        + [shape(corner, jnp.float32)] * 4,
        compiler_params=pltpu.CompilerParams(vmem_limit_bytes=VMEM_LIMIT),
        cost_estimate=pl.CostEstimate(flops=10**7, bytes_accessed=5 * 10**6, transcendentals=0),
    )(picked, *([landed] * SUB))


def stream_kernel(
    main_ref, prev_ref, next_ref, xlo_ref, xhi_ref, ylo_ref, yhi_ref,
    mm_ref, mp_ref, pm_ref, pp_ref, out_ref, below_ref, above_ref, swap_ref,
):
    g = pl.program_id(0)
    width = EDGE // GROUPS

    @pl.when(g == 0)
    def _():
        for k in range(9):
            for x in range(EDGE):
                packed = ylo_ref[k, x // 8]
                below_ref[k, x + 1] = pltpu.roll(packed, (LANES - EDGE - EDGE * (x % 8)) % LANES, axis=1)
                packed = yhi_ref[k, x // 8]
                above_ref[k, x + 1] = pltpu.roll(packed, (LANES - EDGE * (x % 8)) % LANES, axis=1)
        for k in range(3):
            below_ref[6 + k, 0] = pp_ref[k]
            below_ref[k, EDGE + 1] = mp_ref[k]
            above_ref[6 + k, 0] = pm_ref[k]
            above_ref[k, EDGE + 1] = mm_ref[k]

    lane = lax.broadcasted_iota(jnp.int32, (SUB, LANES), 1)
    block = lax.broadcasted_iota(jnp.int32, (SUB, LANES), 0)
    along = lane % EDGE
    first_z, last_z = along == 0, along == EDGE - 1
    floor = first_z & (block == 0)
    ceiling = last_z & (block == SUB - 1)
    low_y, high_y = lane < EDGE, lane >= LANES - EDGE

    for x in range(width):

        def source(q, half):
            cx = velocity(q)[0]
            at = x - cx
            if at < 0:
                return jnp.where(g == 0, xlo_ref[q - 18, half], prev_ref[q - 18, half])
            if at >= width:
                return jnp.where(g == GROUPS - 1, xhi_ref[q, half], next_ref[q, half])
            return main_ref[q, at * 2 + half]

        for half in range(2):
            c = x * 2 + half
            for q in range(NQ):
                cx, cy, cz = velocity(q)
                a = source(q, half)
                side = g * width + x - cx + 1
                k = (cx + 1) * 3 + cz + 1
                if cy == 1:
                    a = jnp.where(high_y, below_ref[k, side] if half == 0 else source(q, 0), a)
                elif cy == -1:
                    a = jnp.where(low_y, above_ref[k, side] if half == 1 else source(q, 1), a)
                shift = EDGE * cy + cz
                value = a if shift == 0 else pltpu.roll(a, shift % LANES, axis=1)
                if cz == 1:
                    fill = pltpu.roll(pltpu.roll(a, 1, axis=0), (shift - EDGE) % LANES, axis=1)
                    value = jnp.where(first_z, fill, value)
                    value = jnp.where(floor, main_ref[26 - q, c], value)
                elif cz == -1:
                    fill = pltpu.roll(pltpu.roll(a, SUB - 1, axis=0), (shift + EDGE) % LANES, axis=1)
                    value = jnp.where(last_z, fill, value)
                    value = jnp.where(ceiling, main_ref[26 - q, c], value)
                base = (c * QPAD + q) * SUB
                swap_ref[base : base + SUB, :] = value
            for t in range(SUB):
                moved = swap_ref[pl.ds(c * QPAD * SUB + t, QPAD, stride=SUB), :]
                out_ref[t, :, c * LANES : (c + 1) * LANES] = moved[:NQ]


def stream(lattice, halos):
    cells = GROUPS * SUB * LANES
    face = (9, 2, SUB, LANES)
    whole_face = pl.BlockSpec(face, lambda g: (0, 0, 0, 0))
    whole_corner = pl.BlockSpec((3, SUB, LANES), lambda g: (0, 0, 0))
    width = EDGE // GROUPS
    return pl.pallas_call(
        stream_kernel,
        grid=(GROUPS,),
        in_specs=[
            pl.BlockSpec((NQ, SUB, SUB, LANES), lambda g: (0, g, 0, 0)),
            pl.BlockSpec(face, lambda g: (2, jnp.maximum(width * g - 1, 0), 0, 0)),
            pl.BlockSpec(face, lambda g: (0, jnp.minimum(width * g + width, EDGE - 1), 0, 0)),
        ]
        + [whole_face] * 4
        + [whole_corner] * 4,
        out_specs=pl.BlockSpec((SUB, NQ, SUB * LANES), lambda g: (0, 0, g)),
        out_shape=jax.ShapeDtypeStruct((SUB, NQ, cells), jnp.float32),
        scratch_shapes=[
            pltpu.VMEM((9, EDGE + 2, SUB, LANES), jnp.float32),
            pltpu.VMEM((9, EDGE + 2, SUB, LANES), jnp.float32),
            pltpu.VMEM((SUB * QPAD * SUB, LANES), jnp.float32),
        ],
        compiler_params=pltpu.CompilerParams(vmem_limit_bytes=VMEM_LIMIT),
        cost_estimate=pl.CostEstimate(flops=10**7, bytes_accessed=8 * 10**6, transcendentals=0),
    )(lattice, lattice, lattice, *halos)


def exchange(xlo, xhi, ylo, yhi, mm, mp, pm, pp, row_count, col_count):
    def send(value, dr, dc):
        pairs = []
        for r in range(row_count):
            for c in range(col_count):
                to = ((r + dr) % row_count) * col_count + (c + dc) % col_count
                pairs.append((r * col_count + c, to))
        return lax.ppermute(value, ("row", "col"), pairs)

    return (
        send(xhi, 1, 0), send(xlo, -1, 0), send(yhi, 0, 1), send(ylo, 0, -1),
        send(mm, -1, -1), send(mp, -1, 1), send(pm, 1, -1), send(pp, 1, 1),
    )


def routes(everywhere, blocks, row_count, col_count, cap_row, cap_col):
    row = lax.axis_index("row")
    col = lax.axis_index("col")
    per_row = blocks * col_count
    count = row_count * blocks
    table = everywhere.reshape(row_count, col_count, blocks)
    to_row = table // per_row
    earlier = jnp.asarray(np.tril(np.ones((blocks, blocks), np.bool_), -1))
    rank = jnp.sum((to_row[..., :, None] == to_row[..., None, :]) & earlier, axis=-1)
    landed_at = jnp.arange(row_count)[:, None, None] * cap_row + rank
    table = jnp.transpose(table, (1, 0, 2)).reshape(col_count, count)
    landed_at = jnp.transpose(landed_at, (1, 0, 2)).reshape(col_count, count)
    here = table // per_row == row
    to_col = table // blocks % col_count
    before = jnp.asarray(np.tril(np.ones((count, count), np.bool_), -1))

    mine = lax.dynamic_index_in_dim(here, col, 0, False)
    my_col = lax.dynamic_index_in_dim(to_col, col, 0, False)
    my_landed = lax.dynamic_index_in_dim(landed_at, col, 0, False)
    order = jnp.sum(before & mine[None, :], axis=1)
    place = jnp.sum(before & mine[None, :] & (my_col[:, None] == my_col[None, :]), axis=1)
    hit = mine[None, :] & (order[None, :] == jnp.arange(blocks)[:, None])
    source = jnp.sum(jnp.where(hit, my_landed[None, :], 0), axis=1)
    target = jnp.sum(jnp.where(hit, (my_col * cap_col + place)[None, :], 0), axis=1)

    final = here & (to_col == col)
    place = jnp.sum(before[None] & final[:, None, :], axis=2)
    place = place + jnp.arange(col_count)[:, None] * cap_col
    hit = final[None] & ((table % blocks)[None] == jnp.arange(blocks)[:, None, None])
    picked = jnp.sum(jnp.where(hit, place[None], 0), axis=(1, 2))
    return source.astype(jnp.int32), target.astype(jnp.int32), picked.astype(jnp.int32)


def on_device(populations, destination, refinement):
    blocks = populations.shape[0]
    row_count = lax.axis_size("row")
    col_count = lax.axis_size("col")
    cap_row = 2 * ((blocks + row_count - 1) // row_count)
    cap_col = 2 * ((blocks + col_count - 1) // col_count)
    everywhere = lax.all_gather(destination, ("row", "col"), tiled=True)
    outgoing = pre(populations, destination, refinement, row_count, cap_row, blocks * col_count)
    source, target, picked = routes(everywhere, blocks, row_count, col_count, cap_row, cap_col)
    landed = lax.all_to_all(outgoing, "row", split_axis=0, concat_axis=0, tiled=True)
    outgoing = repack(source, target, landed, col_count * cap_col)
    landed = lax.all_to_all(outgoing, "col", split_axis=0, concat_axis=0, tiled=True)
    lattice, *sides = post(picked, landed)
    halos = exchange(*sides, row_count, col_count)
    return stream(lattice, halos)


def solution(mesh):
    return jax.shard_map(
        on_device,
        mesh=mesh,
        in_specs=(P(("row", "col"), None, None), P(("row", "col")), P(("row", "col"))),
        out_specs=P(("row", "col"), None, None),
        check_vma=False,
    )
```

time: 706 us -> 211 us (0.30); the launches traced: 693 us -> 210 us
  local copies, waits for them, and re-layouts: 275 us -> 16 us
  waiting for transfers between devices: 274 us -> 44.3 us
  other arithmetic: 99 us -> 2.08 us
  blocking collectives: 6.8 us -> 73.9 us
  Pallas kernels: 0 us -> 52.2 us
  starting transfers between devices: 32.2 us -> 21.8 us
    all_to_all x5 -> x2, waiting for transfers between devices: 274 us -> 28.1 us  [the longest x1 28.1 us: on_device(): lax.all_to_all(outgoing, 'col', split_axis=0, concat_axis=0, tiled=True)]
    unnamed x0 -> x1, blocking collectives: none -> 73.9 us
    pallas_call x0 -> x4, Pallas kernels: none -> 52.2 us  [the longest x1 37.6 us: repack(): pl.pallas_call(repack_kernel, in_specs=[pl.BlockSpec(memory_space=pltpu.S...]
    another operation x28 -> x0, local copies, waits for them, and re-layouts: 51.5 us -> none  [stream_brick(): return jnp.stack(read, axis=1)]
    gather x10 -> x0, local copies, waits for them, and re-layouts: 50.1 us -> none  [the longest x3 24.1 us: on_device(): arrived = jnp.take(landed, picked, axis=0)]
    unnamed x65 -> x17, local copies, waits for them, and re-layouts: 55.2 us -> 9.7 us
    reshape x18 -> x3, local copies, waits for them, and re-layouts: 42.5 us -> 0.25 us  [the longest x1 0.09 us: routes(): table = everywhere.reshape(row_count, col_count, blocks)]
    reduce_sum x69 -> x5, other arithmetic: 32.4 us -> 1.86 us  [the longest x1 0.71 us: routes(): jnp.sum(jnp.where(hit, (my_col * cap_col + place)[None, :], 0), axis=1)]
  transfers between devices with their start and end apart: 9 -> 10, of which waited for: 3 -> 5; matrix products, arithmetic and copies ran while one was open for 14% -> 1% of each run, Pallas kernels for 0% -> 0%
where the time goes in v1:
time: 211 us; the launch traced here: 210 us
  blocking collectives  73.9 us (35%)
  Pallas kernels  52.2 us (25%)
  waiting for transfers between devices  44.3 us (21%)
  starting transfers between devices  21.8 us (10%)
  local copies, waits for them, and re-layouts  16 us (8%)
    unnamed x1, blocking collectives  73.9 us
    pallas_call x1, Pallas kernels, repack(): pl.pallas_call(repack_kernel, in_specs=[pl.BlockSpec(memory_space=pltpu.S...  37.6 us
    all_to_all x1, waiting for transfers between devices, on_device(): lax.all_to_all(outgoing, 'col', split_axis=0, concat_axis=0, tiled=True)  28.1 us
    ppermute x8, waiting for transfers between devices, send(): return lax.ppermute(value, ('row', 'col'), pairs)  16.2 us
    ppermute x8, starting transfers between devices, send(): return lax.ppermute(value, ('row', 'col'), pairs)  10.8 us
    unnamed x17, local copies, waits for them, and re-layouts  9.7 us
    all_to_all x1, starting transfers between devices, on_device(): lax.all_to_all(outgoing, 'row', split_axis=0, concat_axis=0, tiled=True)  7.39 us
    pallas_call x1, local copies, waits for them, and re-layouts, stream(): pl.pallas_call(stream_kernel, grid=(GROUPS,), in_specs=[pl.BlockSpec((NQ,...  6.03 us
  transfers between devices with their start and end apart: 10, of which 5 were waited for; matrix products, arithmetic and copies ran while one was open for 1% of the time, Pallas kernels for 0%

profile of v1, /device:TPU:0, one launch (start us, length us, event | category | flops | bytes accessed | tf_op | source)
XLA Modules:
  0.0 210.5 jit_solution(8420569366699933657)
XLA Ops:
  0.0 6.0 %copy.21.x_ref = f32[8,27,4096]{2,1,0:T(8,128)} copy(f32[8,27,4096]{2,0,1:T(8,128)} %param.6) | data formatting | bytes 7077888 | tf_op args[0]
  6.1 5.7 %shard_map.64 = f32[16,4,9,8,128]{4,3,2,1,0:T(8,128)} custom-call(s32[8]{0:T(128)S(1)} %copy-done.3, s32[8]{0:T(128)S(1)} %copy-done.2, f32[80,256]{1,0:T(8,128)S(1)} %copy-done.1, f32[8,27,4096]{2,1,0:T(8,128)} %copy.21.x_ref), custom_call_target="tpu_custom_call" | custom-call | flops 100000000 | bytes 6000000 | tf_op jit(solution)/shard_map/pallas_call | solution.py:95
  11.8 7.4 %all-to-all-start = ((f32[16,4,9,8,128]{4,3,2,1,0:T(8,128)}), f32[16,4,9,8,128]{4,3,2,1,0:T(8,128)S(1)}, u32[]{:S(2)}, u32[]{:S(2)}) async-start(f32[16,4,9,8,128]{4,3,2,1,0:T(8,128)} %shard_map.64), calls=%async_computation | async-start | bytes 4718592 | tf_op jit(solution)/shard_map/all_to_all | solution.py:436
  19.2 0.2 dynamic-update-slice
  19.4 73.9 %all-reduce = s32[256]{0:T(256)S(1)} all-reduce(s32[256]{0:T(256)S(1)} %dynamic-update-slice), channel_id=1, replica_groups=mesh['row'=8,'col'=4] {'row','col'}, use_global_device_ids=true, to_apply=%add | all-reduce | flops 256 | bytes 2048
  93.3 0.1 reshape.221
  93.4 0.1 reshape.222
  93.6 0.7 convert_reduce_fusion
  94.3 0.1 add_bitcast_fusion
  94.4 0.1 reshape.223
  94.5 0.2 convert_reduce_fusion.2
  94.7 0.7 select_reduce_fusion.1
  95.4 1.4 copy-done.4
  96.8 37.6 %shard_map.65 = f32[16,4,9,8,128]{4,3,2,1,0:T(8,128)} custom-call(s32[8]{0:T(128)} %get-tuple-element.26.source_ref, s32[8]{0:T(128)} %get-tuple-element.25.target_ref, f32[16,4,9,8,128]{4,3,2,1,0:T(8,128)} %copy-done.4), custom_call_target="tpu_custom_call" | custom-call | bytes 3000000 | tf_op jit(solution)/shard_map/pallas_call | solution.py:130
  134.4 3.6 %all-to-all-start.1 = ((f32[16,4,9,8,128]{4,3,2,1,0:T(8,128)}), f32[16,4,9,8,128]{4,3,2,1,0:T(8,128)S(1)}, u32[]{:S(2)}, u32[]{:S(2)}) async-start(f32[16,4,9,8,128]{4,3,2,1,0:T(8,128)} %shard_map.65), calls=%async_computation.1 | async-start | bytes 4718592 | tf_op jit(solution)/shard_map/all_to_all | solution.py:438
  138.1 0.1 convert_reduce_fusion.1
  138.3 0.1 select_reduce_fusion.picked_ref
  138.4 28.1 %all-to-all-done.1.refs_0_.refs_1_.refs_2_.refs_3_.refs_4_.refs_5_.refs_6_.refs_7_ = f32[16,4,9,8,128]{4,3,2,1,0:T(8,128)S(1)} async-done(((f32[16,4,9,8,128]{4,3,2,1,0:T(8,128)}), f32[16,4,9,8,128]{4,3,2,1,0:T(8,128)S(1)}, u32[]{:S(2)}, u32[]{:S(2)}) %all-to-all-start.1) | async-done | bytes 2359328 | tf_op jit(solution)/shard_map/all_to_all | solution.py:438
  166.5 4.7 %shard_map.66 = (f32[27,32,8,128]{3,2,1,0:T(8,128)}, f32[9,2,8,128]{3,2,1,0:T(8,128)S(1)}, f32[9,2,8,128]{3,2,1,0:T(8,128)S(1)}, f32[9,2,8,128]{3,2,1,0:T(8,128)...) custom-call(s32[8]{0:T(128)S(1)} %select_reduce_fusion.picked_ref, ...), custom_call_target="tpu_custom_call" | custom-call | flops 10000000 | bytes 5000000 | tf_op jit(solution)/shard_map/pallas_call | solution.py:262
  171.2 2.3 %collective-permute-start = (f32[9,2,8,128]{3,2,1,0:T(8,128)S(1)}, f32[9,2,8,128]{3,2,1,0:T(8,128)S(1)}, u32[]{:S(2)}, u32[]{:S(2)}) collective-permute-start(f32[9,2,8,128]{3,2,1,0:T(8,128)S(1)} %get-tuple-element.15), channel_id=1, source_target_pairs={{0,4},{1,5},{2,6},{3,7},{4,8},{5,9},{6,10},{7,11},{8,12},{9,13},{1... | collective-permute-start | bytes 221192 | tf_op jit(solution)/shard_map/ppermute | solution.py:386
  173.5 2.4 %collective-permute-start.1 = (f32[9,2,8,128]{3,2,1,0:T(8,128)S(1)}, f32[9,2,8,128]{3,2,1,0:T(8,128)S(1)}, u32[]{:S(2)}, u32[]{:S(2)}) collective-permute-start(f32[9,2,8,128]{3,2,1,0:T(8,128)S(1)} %get-tuple-element.16), channel_id=1, source_target_pairs={{0,28},{1,29},{2,30},{3,31},{4,0},{5,1},{6,2},{7,3},{8,4},{9,5},{1... | collective-permute-start | bytes 221192 | tf_op jit(solution)/shard_map/ppermute | solution.py:386
  175.9 1.7 collective-permute-start.3
  177.7 0.8 collective-permute-start.4
  178.5 2.5 %collective-permute-done.4.mm_ref = f32[3,8,128]{2,1,0:T(8,128)S(1)} collective-permute-done((f32[3,8,128]{2,1,0:T(8,128)S(1)}, f32[3,8,128]{2,1,0:T(8,128)S(1)}, u32[]{:S(2)}, u32[]{:S(2)}) %collective-permute-start.4) | collective-permute-done | bytes 12320 | tf_op jit(solution)/shard_map/ppermute | solution.py:386
  180.9 3.3 %collective-permute-start.5 = (f32[3,8,128]{2,1,0:T(8,128)S(1)}, f32[3,8,128]{2,1,0:T(8,128)S(1)}, u32[]{:S(2)}, u32[]{:S(2)}) collective-permute-start(f32[3,8,128]{2,1,0:T(8,128)S(1)} %get-tuple-element.20), channel_id=1, source_target_pairs={{0,29},{1,30},{2,31},{3,28},{4,1},{5,2},{6,3},{7,0},{8,5},{9,6},{1... | collective-permute-start | bytes 36872 | tf_op jit(solution)/shard_map/ppermute | solution.py:386
  184.2 1.4 collective-permute-done.5.mp_ref
  185.6 0.3 collective-permute-start.6
  185.9 5.6 %collective-permute-done.6.pm_ref = f32[3,8,128]{2,1,0:T(8,128)S(1)} collective-permute-done((f32[3,8,128]{2,1,0:T(8,128)S(1)}, f32[3,8,128]{2,1,0:T(8,128)S(1)}, u32[]{:S(2)}, u32[]{:S(2)}) %collective-permute-start.6) | collective-permute-done | bytes 12320 | tf_op jit(solution)/shard_map/ppermute | solution.py:386
  191.5 6.7 %collective-permute-done.7.pp_ref = f32[3,8,128]{2,1,0:T(8,128)S(1)} collective-permute-done((f32[3,8,128]{2,1,0:T(8,128)S(1)}, f32[3,8,128]{2,1,0:T(8,128)S(1)}, u32[]{:S(2)}, u32[]{:S(2)}) %collective-permute-start.7) | collective-permute-done | bytes 12320 | tf_op jit(solution)/shard_map/ppermute | solution.py:386
  198.2 2.0 copy-done
  200.2 4.2 %shard_map.67 = f32[8,27,4096]{2,1,0:T(8,128)} custom-call(f32[27,32,8,128]{3,2,1,0:T(8,128)S(1)} %copy-done, f32[27,32,8,128]{3,2,1,0:T(8,128)S(1)} %copy-done, f32[27,32,8,128]{3,2,1,0:T(8,128)S(1)} %copy-done, f32[9,2,8,128]{3,2,1,0:T(8,128)S(1)} %collective-permute-done.xlo_ref, f32[9,2,8,128]{3,2,1,0:T(8,128)S(1)} %collective-permute-done.1.xhi_ref, ...), custom_call_target="tpu_custom_call" | custom-call | flops 10000000 | bytes 8000000 | tf_op jit(solution)/shard_map/pallas_call | solution.py:357
  204.4 6.0 %copy.22 = f32[8,27,4096]{2,0,1:T(8,128)} copy(f32[8,27,4096]{2,1,0:T(8,128)} %shard_map.67) | data formatting | bytes 7077888 | tf_op jit(solution)/shard_map/pallas_call | solution.py:357
  (30 shorter events, 0.2 us)
Async XLA Ops:
  0.0 6.0 %copy-start.1 = (f32[80,256]{1,0:T(8,128)S(1)}, f32[80,256]{1,0:T(8,128)}, u32[]{:S(2)}) copy-start(f32[80,256]{1,0:T(8,128)} %constant.92.clone.w_ref) | copy-start | bytes 245764
  0.0 6.0 %copy-start.3 = (s32[8]{0:T(128)S(1)}, s32[8]{0:T(128)}, u32[]{:S(2)}) copy-start(s32[8]{0:T(128)} %dest_ref.1) | copy-start | bytes 100
  0.0 6.0 %copy-start.2 = (s32[8]{0:T(128)S(1)}, s32[8]{0:T(128)}, u32[]{:S(2)}) copy-start(s32[8]{0:T(128)} %level_ref.1) | copy-start | bytes 100
  11.8 81.8 %copy-start.6 = (pred[8,8]{1,0:T(8,128)(4,1)S(1)}, pred[8,8]{1,0:T(8,128)(4,1)}, u32[]{:S(2)}) copy-start(pred[8,8]{1,0:T(8,128)(4,1)} %constant.93.clone) | copy-start | bytes 196
  11.8 82.7 %copy-start.5 = (pred[64,64]{1,0:T(32,128)(4,1)S(1)}, pred[64,64]{1,0:T(32,128)(4,1)}, u32[]{:S(2)}) copy-start(pred[64,64]{1,0:T(32,128)(4,1)} %constant.94.clone) | copy-start | bytes 12292
  11.8 83.6 %all-to-all-start = ((f32[16,4,9,8,128]{4,3,2,1,0:T(8,128)}), f32[16,4,9,8,128]{4,3,2,1,0:T(8,128)S(1)}, u32[]{:S(2)}, u32[]{:S(2)}) async-start(f32[16,4,9,8,128]{4,3,2,1,0:T(8,128)} %shard_map.64), calls=%async_computation | async-start | bytes 4718592 | tf_op jit(solution)/shard_map/all_to_all | solution.py:436
  95.4 1.4 copy-start.4
  134.4 32.1 %all-to-all-start.1 = ((f32[16,4,9,8,128]{4,3,2,1,0:T(8,128)}), f32[16,4,9,8,128]{4,3,2,1,0:T(8,128)S(1)}, u32[]{:S(2)}, u32[]{:S(2)}) async-start(f32[16,4,9,8,128]{4,3,2,1,0:T(8,128)} %shard_map.65), calls=%async_computation.1 | async-start | bytes 4718592 | tf_op jit(solution)/shard_map/all_to_all | solution.py:438
  171.2 27.0 %collective-permute-start = (f32[9,2,8,128]{3,2,1,0:T(8,128)S(1)}, f32[9,2,8,128]{3,2,1,0:T(8,128)S(1)}, u32[]{:S(2)}, u32[]{:S(2)}) collective-permute-start(f32[9,2,8,128]{3,2,1,0:T(8,128)S(1)} %get-tuple-element.15), channel_id=1, source_target_pairs={{0,4},{1,5},{2,6},{3,7},{4,8},{5,9},{6,10},{7,11},{8,12},{9,13},{1... | collective-permute-start | bytes 221192 | tf_op jit(solution)/shard_map/ppermute | solution.py:386
  173.5 24.7 %collective-permute-start.1 = (f32[9,2,8,128]{3,2,1,0:T(8,128)S(1)}, f32[9,2,8,128]{3,2,1,0:T(8,128)S(1)}, u32[]{:S(2)}, u32[]{:S(2)}) collective-permute-start(f32[9,2,8,128]{3,2,1,0:T(8,128)S(1)} %get-tuple-element.16), channel_id=1, source_target_pairs={{0,28},{1,29},{2,30},{3,31},{4,0},{5,1},{6,2},{7,3},{8,4},{9,5},{1... | collective-permute-start | bytes 221192 | tf_op jit(solution)/shard_map/ppermute | solution.py:386
  175.9 22.3 %collective-permute-start.2 = (f32[9,2,8,128]{3,2,1,0:T(8,128)S(1)}, f32[9,2,8,128]{3,2,1,0:T(8,128)S(1)}, u32[]{:S(2)}, u32[]{:S(2)}) collective-permute-start(f32[9,2,8,128]{3,2,1,0:T(8,128)S(1)} %get-tuple-element.17), channel_id=1, source_target_pairs={{0,1},{1,2},{2,3},{3,0},{4,5},{5,6},{6,7},{7,4},{8,9},{9,10},{10,1... | collective-permute-start | bytes 221192 | tf_op jit(solution)/shard_map/ppermute | solution.py:386
  175.9 22.3 %collective-permute-start.3 = (f32[9,2,8,128]{3,2,1,0:T(8,128)S(1)}, f32[9,2,8,128]{3,2,1,0:T(8,128)S(1)}, u32[]{:S(2)}, u32[]{:S(2)}) collective-permute-start(f32[9,2,8,128]{3,2,1,0:T(8,128)S(1)} %get-tuple-element.18), channel_id=1, source_target_pairs={{0,3},{1,0},{2,1},{3,2},{4,7},{5,4},{6,5},{7,6},{8,11},{9,8},{10,9... | collective-permute-start | bytes 221192 | tf_op jit(solution)/shard_map/ppermute | solution.py:386
  177.7 3.2 %collective-permute-start.4 = (f32[3,8,128]{2,1,0:T(8,128)S(1)}, f32[3,8,128]{2,1,0:T(8,128)S(1)}, u32[]{:S(2)}, u32[]{:S(2)}) collective-permute-start(f32[3,8,128]{2,1,0:T(8,128)S(1)} %get-tuple-element.19), channel_id=1, source_target_pairs={{0,31},{1,28},{2,29},{3,30},{4,3},{5,0},{6,1},{7,2},{8,7},{9,4},{1... | collective-permute-start | bytes 36872 | tf_op jit(solution)/shard_map/ppermute | solution.py:386
  180.9 4.7 %collective-permute-start.5 = (f32[3,8,128]{2,1,0:T(8,128)S(1)}, f32[3,8,128]{2,1,0:T(8,128)S(1)}, u32[]{:S(2)}, u32[]{:S(2)}) collective-permute-start(f32[3,8,128]{2,1,0:T(8,128)S(1)} %get-tuple-element.20), channel_id=1, source_target_pairs={{0,29},{1,30},{2,31},{3,28},{4,1},{5,2},{6,3},{7,0},{8,5},{9,6},{1... | collective-permute-start | bytes 36872 | tf_op jit(solution)/shard_map/ppermute | solution.py:386
  185.6 5.9 %collective-permute-start.6 = (f32[3,8,128]{2,1,0:T(8,128)S(1)}, f32[3,8,128]{2,1,0:T(8,128)S(1)}, u32[]{:S(2)}, u32[]{:S(2)}) collective-permute-start(f32[3,8,128]{2,1,0:T(8,128)S(1)} %get-tuple-element.21), channel_id=1, source_target_pairs={{0,7},{1,4},{2,5},{3,6},{4,11},{5,8},{6,9},{7,10},{8,15},{9,12},{1... | collective-permute-start | bytes 36872 | tf_op jit(solution)/shard_map/ppermute | solution.py:386
  191.5 6.7 %collective-permute-start.7 = (f32[3,8,128]{2,1,0:T(8,128)S(1)}, f32[3,8,128]{2,1,0:T(8,128)S(1)}, u32[]{:S(2)}, u32[]{:S(2)}) collective-permute-start(f32[3,8,128]{2,1,0:T(8,128)S(1)} %get-tuple-element.22), channel_id=1, source_target_pairs={{0,5},{1,6},{2,7},{3,4},{4,9},{5,10},{6,11},{7,8},{8,13},{9,14},{1... | collective-permute-start | bytes 36872 | tf_op jit(solution)/shard_map/ppermute | solution.py:386
  198.2 2.0 copy-start

commit v2 on v1

v2 whole, which is shorter than its diff:
```python
import functools

import jax
import jax.numpy as jnp
from jax import lax
from jax.experimental import pallas as pl
from jax.experimental.pallas import tpu as pltpu
from jax.sharding import PartitionSpec as P

EDGE = 16
VISCOSITY = 0.01
LANES = 128
SUB = 8
NQ = 27
NFIELD = 9
GROUPS = 4
WIDTH = EDGE // GROUPS
CHUNKS = ((0, 3), (1, 2))
VMEM_LIMIT = 50 * 1024 * 1024


def velocity(q):
    return (q // 9 - 1, (q // 3) % 3 - 1, q % 3 - 1)


def quarter(part, g):
    first, second = CHUNKS[part]
    return first + (second - first) * g


def raw_moments(f):
    whole, slope, outer = {}, {}, {}
    for i in range(3):
        for j in range(3):
            low, rest, high = (f[i * 9 + j * 3 + k] for k in range(3))
            outer[i, j] = low + high
            whole[i, j] = outer[i, j] + rest
            slope[i, j] = high - low
    column = [whole[i, 0] + whole[i, 1] + whole[i, 2] for i in range(3)]
    tilt = [slope[i, 0] + slope[i, 1] + slope[i, 2] for i in range(3)]
    low_y = whole[0, 0] + whole[1, 0] + whole[2, 0]
    high_y = whole[0, 2] + whole[1, 2] + whole[2, 2]
    ends = column[0] + column[2]
    mzz = sum(outer[i, j] for i in range(3) for j in range(3))
    mxy = (whole[2, 2] - whole[2, 0]) - (whole[0, 2] - whole[0, 0])
    myz = (slope[0, 2] + slope[1, 2] + slope[2, 2]) - (slope[0, 0] + slope[1, 0] + slope[2, 0])
    return (
        ends + column[1],
        column[2] - column[0],
        high_y - low_y,
        tilt[0] + tilt[1] + tilt[2],
        ends,
        low_y + high_y,
        mzz,
        mxy,
        tilt[2] - tilt[0],
        myz,
    )


def pre_kernel(cap, per_row, tagged, dest_ref, level_ref, x_ref, out_ref, swap_ref):
    g = pl.program_id(0)
    blocks = x_ref.shape[1]
    chunks = x_ref.shape[2] // LANES
    which = lax.broadcasted_iota(jnp.int32, (SUB, LANES), 0)
    scale = jnp.zeros((SUB, LANES), jnp.int32)
    for t in range(blocks):
        scale = jnp.where(which == t, jnp.left_shift(1, level_ref[t]), scale)
    rate = 1.0 / (3.0 * VISCOSITY * scale.astype(jnp.float32) + 0.5)
    keep = 1.0 - rate

    for c in range(chunks):
        rho, jx, jy, jz, mxx, myy, mzz, mxy, mxz, myz = raw_moments(
            [x_ref[q, :, c * LANES : (c + 1) * LANES] for q in range(NQ)]
        )
        inverse = 1.0 / rho
        ux, uy, uz = jx * inverse, jy * inverse, jz * inverse
        kxx = mxx - jx * ux
        fields = (
            rho, ux, uy, uz,
            keep * (mxy - jx * uy),
            keep * (mxz - jx * uz),
            keep * (myz - jy * uz),
            keep * (kxx - (myy - jy * uy)),
            keep * (kxx - (mzz - jz * uz)),
        )
        for n, field in enumerate(fields):
            base = (n * chunks + c) * SUB
            swap_ref[base : base + SUB, :] = field

    tag = out_ref.shape[1] - 1
    if tagged:

        @pl.when(g == 0)
        def _():
            for slot in range(out_ref.shape[0]):
                out_ref[slot, tag] = jnp.full((SUB, LANES), -1.0, jnp.float32)

    rows = [dest_ref[t] // per_row for t in range(blocks)]
    for t in range(blocks):
        slot = rows[t] * cap
        for other in range(t):
            slot = slot + jnp.where(rows[other] == rows[t], 1, 0)
        for n in range(NFIELD):
            moved = swap_ref[pl.ds(n * chunks * SUB + t, SUB, stride=SUB), :]
            out_ref[slot, g * NFIELD + n] = moved
        if tagged:

            @pl.when(g == 0)
            def _():
                out_ref[slot, tag] = jnp.full((SUB, LANES), dest_ref[t], jnp.int32).astype(jnp.float32)


def pre(populations, destination, refinement, part, row_count, cap, per_row):
    blocks = populations.shape[1]
    cells = populations.shape[2] // GROUPS
    steps = len(CHUNKS[part])
    tagged = part == 0
    shape = (row_count * cap, steps * NFIELD + tagged, SUB, LANES)
    return pl.pallas_call(
        functools.partial(pre_kernel, cap, per_row, tagged),
        grid_spec=pltpu.PrefetchScalarGridSpec(
            num_scalar_prefetch=2,
            grid=(steps,),
            in_specs=[pl.BlockSpec((NQ, blocks, cells), lambda g, *_: (0, 0, quarter(part, g)))],
            out_specs=pl.BlockSpec(shape, lambda g, *_: (0, 0, 0, 0)),
            scratch_shapes=[pltpu.VMEM((NFIELD * cells // LANES * SUB, LANES), jnp.float32)],
        ),
        out_shape=jax.ShapeDtypeStruct(shape, jnp.float32),
        compiler_params=pltpu.CompilerParams(vmem_limit_bytes=VMEM_LIMIT),
        cost_estimate=pl.CostEstimate(flops=10**7, bytes_accessed=4 * 10**6, transcendentals=0),
        name="pre_%d" % part,
    )(destination, refinement, populations)


def repack_kernel(cap, blocks, col_count, tagged, tags_ref, in_ref, out_ref, count_ref):
    tag = out_ref.shape[1] - 1
    if tagged:
        for slot in range(out_ref.shape[0]):
            out_ref[slot, tag] = jnp.full((SUB, LANES), -1.0, jnp.float32)
    for c in range(col_count):
        count_ref[c] = c * cap
    for slot in range(in_ref.shape[0]):

        @pl.when(tags_ref[slot] >= 0)
        def _():
            c = tags_ref[slot] // blocks % col_count
            target = count_ref[c]
            count_ref[c] = target + 1
            out_ref[target] = in_ref[slot]


def repack(tags, landed, part, blocks, col_count, cap):
    shape = (col_count * cap,) + landed.shape[1:]
    return pl.pallas_call(
        functools.partial(repack_kernel, cap, blocks, col_count, part == 0),
        in_specs=[pl.BlockSpec(memory_space=pltpu.SMEM), pl.BlockSpec(memory_space=pltpu.VMEM)],
        out_specs=pl.BlockSpec(memory_space=pltpu.VMEM),
        scratch_shapes=[pltpu.SMEM((col_count,), jnp.int32)],
        out_shape=jax.ShapeDtypeStruct(shape, jnp.float32),
        compiler_params=pltpu.CompilerParams(vmem_limit_bytes=VMEM_LIMIT),
        cost_estimate=pl.CostEstimate(flops=0, bytes_accessed=3 * 10**6, transcendentals=0),
        name="repack_%d" % part,
    )(tags, landed)


def backward(zeroth, first, second, u):
    raw_one, raw_two = first, second
    if zeroth is not None:
        moved = u * zeroth
        raw_one = moved if raw_one is None else raw_one + moved
        square = u * moved
        raw_two = square if raw_two is None else raw_two + square
    if first is not None:
        cross = (u + u) * first
        raw_two = cross if raw_two is None else raw_two + cross
    rest = -raw_two if zeroth is None else zeroth - raw_two
    return 0.5 * (raw_two - raw_one), rest, 0.5 * (raw_one + raw_two)


def post_populations(rho, ux, uy, uz, pxy, pxz, pyz, dev_one, dev_two):
    inverse = 1.0 / rho
    pxx = (rho + dev_one + dev_two) * (1.0 / 3.0)
    pyy = pxx - dev_one
    pzz = pxx - dev_two
    sxy, sxz, syz = pxy * inverse, pxz * inverse, pyz * inverse
    syy, szz = pyy * inverse, pzz * inverse
    central = {
        (0, 0, 0): rho, (2, 0, 0): pxx, (0, 2, 0): pyy, (0, 0, 2): pzz,
        (1, 1, 0): pxy, (1, 0, 1): pxz, (0, 1, 1): pyz,
        (2, 2, 0): pxx * syy + 2.0 * pxy * sxy,
        (2, 0, 2): pxx * szz + 2.0 * pxz * sxz,
        (0, 2, 2): pyy * szz + 2.0 * pyz * syz,
        (2, 1, 1): pxx * syz + 2.0 * pxy * sxz,
        (1, 2, 1): pyy * sxz + 2.0 * pxy * syz,
        (1, 1, 2): pzz * sxy + 2.0 * pxz * syz,
        (2, 2, 2): pxx * syy * szz
        + 2.0 * (pxx * syz * syz + pyy * sxz * sxz + pzz * sxy * sxy)
        + 8.0 * pxy * sxz * syz,
    }
    along_z = {}
    for a in range(3):
        for b in range(3):
            parts = backward(*(central.get((a, b, c)) for c in range(3)), uz)
            for k in range(3):
                along_z[a, b, k] = parts[k]
    along_y = {}
    for a in range(3):
        for k in range(3):
            parts = backward(*(along_z[a, b, k] for b in range(3)), uy)
            for j in range(3):
                along_y[a, j, k] = parts[j]
    result = [None] * NQ
    for j in range(3):
        for k in range(3):
            parts = backward(*(along_y[a, j, k] for a in range(3)), ux)
            for i in range(3):
                result[i * 9 + j * 3 + k] = parts[i]
    return result


def post_kernel(outer, tags_ref, *refs):
    if outer:
        in_ref, post_ref, ylo_ref, yhi_ref, xlo_ref, xhi_ref, swap_ref, picked_ref = refs
    else:
        in_ref, _, post_ref, ylo_ref, yhi_ref, swap_ref, picked_ref = refs
    g = pl.program_id(0)
    for t in range(SUB):
        picked_ref[t] = 0
    for slot in range(in_ref.shape[0]):

        @pl.when(tags_ref[slot] >= 0)
        def _():
            picked_ref[tags_ref[slot] % SUB] = slot

    for t in range(SUB):
        slot = picked_ref[t]
        for n in range(NFIELD):
            swap_ref[pl.ds(n * SUB * SUB + t, SUB, stride=SUB), :] = in_ref[slot, g * NFIELD + n]
    lane = lax.broadcasted_iota(jnp.int32, (SUB, LANES), 1)
    for c in range(SUB):
        fields = [swap_ref[(n * SUB + c) * SUB : (n * SUB + c + 1) * SUB, :] for n in range(NFIELD)]
        result = post_populations(*fields)
        for q in range(NQ):
            post_ref[q, c] = result[q]
        x, half = c // 2, c % 2
        spot = g * WIDTH + x
        inside = (lane // EDGE) == spot
        face_ref, first, shift = ((ylo_ref, 0, 0), (yhi_ref, 6, EDGE))[half]
        for i in range(3):
            for k in range(3):
                value = pltpu.roll(result[i * 9 + first + k], (spot * EDGE + shift) % LANES, axis=1)
                face_ref[i * 3 + k] = jnp.where(inside, value, face_ref[i * 3 + k])

        if outer and x == 0:

            @pl.when(g == 0)
            def _():
                for q in range(9):
                    xlo_ref[q, half] = result[q]

        if outer and x == WIDTH - 1:

            @pl.when(g == 1)
            def _():
                for q in range(9):
                    xhi_ref[q, half] = result[18 + q]


def post(tags, landed, part, before):
    shape = jax.ShapeDtypeStruct
    outer = part == 0
    side_y = (9, SUB, LANES)
    side_x = (9, 2, SUB, LANES)
    whole = (NQ, GROUPS * SUB, SUB, LANES)
    spec_y = pl.BlockSpec(side_y, lambda g, *_: (0, 0, 0))
    spec_x = pl.BlockSpec(side_x, lambda g, *_: (0, 0, 0, 0))
    in_specs = [pl.BlockSpec(landed.shape, lambda g, *_: (0, 0, 0, 0))]
    if not outer:
        in_specs.append(pl.BlockSpec(memory_space=pl.ANY))
    return pl.pallas_call(
        functools.partial(post_kernel, outer),
        grid_spec=pltpu.PrefetchScalarGridSpec(
            num_scalar_prefetch=1,
            grid=(len(CHUNKS[part]),),
            in_specs=in_specs,
            out_specs=[
                pl.BlockSpec((NQ, SUB, SUB, LANES), lambda g, *_: (0, quarter(part, g), 0, 0)),
                spec_y, spec_y,
            ]
            + ([spec_x, spec_x] if outer else []),
            scratch_shapes=[
                pltpu.VMEM((NFIELD * SUB * SUB, LANES), jnp.float32),
                pltpu.SMEM((SUB,), jnp.int32),
            ],
        ),
        out_shape=[shape(whole, jnp.float32)]
        + [shape(side_y, jnp.float32)] * 2
        + ([shape(side_x, jnp.float32)] * 2 if outer else []),
        input_output_aliases={} if outer else {2: 0},
        compiler_params=pltpu.CompilerParams(vmem_limit_bytes=VMEM_LIMIT),
        cost_estimate=pl.CostEstimate(flops=10**7, bytes_accessed=3 * 10**6, transcendentals=0),
        name="post_%d" % part,
    )(tags, landed, *(() if outer else (before,)))


def stream_kernel(
    main_ref, prev_ref, next_ref, xlo_ref, xhi_ref, below_0, above_0, below_1, above_1,
    out_ref, below_ref, above_ref,
):
    g = pl.program_id(0)

    @pl.when(g == 0)
    def _():
        for x in range(EDGE):
            inner = WIDTH <= x < EDGE - WIDTH
            spot = x - WIDTH if inner else (x if x < WIDTH else x - 2 * WIDTH)
            for k in range(9):
                packed = (below_1 if inner else below_0)[k]
                below_ref[k, x + 1] = pltpu.roll(packed, (LANES - EDGE - EDGE * spot) % LANES, axis=1)
                packed = (above_1 if inner else above_0)[k]
                above_ref[k, x + 1] = pltpu.roll(packed, (LANES - EDGE * spot) % LANES, axis=1)
        for k in range(3):
            below_ref[6 + k, 0] = xlo_ref[18 + k]
            above_ref[6 + k, 0] = pltpu.roll(xlo_ref[21 + k], EDGE, axis=1)
            below_ref[k, EDGE + 1] = pltpu.roll(xhi_ref[18 + k], LANES - EDGE, axis=1)
            above_ref[k, EDGE + 1] = xhi_ref[21 + k]

    lane = lax.broadcasted_iota(jnp.int32, (SUB, LANES), 1)
    block = lax.broadcasted_iota(jnp.int32, (SUB, LANES), 0)
    along = lane % EDGE
    first_z, last_z = along == 0, along == EDGE - 1
    floor = first_z & (block == 0)
    ceiling = last_z & (block == SUB - 1)
    low_y, high_y = lane < EDGE, lane >= LANES - EDGE

    for x in range(WIDTH):

        def source(q, half):
            at = x - velocity(q)[0]
            if at < 0:
                return jnp.where(g == 0, xlo_ref[(q - 18) * 2 + half], prev_ref[q - 18, half])
            if at >= WIDTH:
                return jnp.where(g == GROUPS - 1, xhi_ref[q * 2 + half], next_ref[q, half])
            return main_ref[q, at * 2 + half]

        for half in range(2):
            c = x * 2 + half
            for q in range(NQ):
                cx, cy, cz = velocity(q)
                a = source(q, half)
                side = g * WIDTH + x - cx + 1
                k = (cx + 1) * 3 + cz + 1
                if cy == 1:
                    a = jnp.where(high_y, below_ref[k, side] if half == 0 else source(q, 0), a)
                elif cy == -1:
                    a = jnp.where(low_y, above_ref[k, side] if half == 1 else source(q, 1), a)
                shift = EDGE * cy + cz
                value = a if shift == 0 else pltpu.roll(a, shift % LANES, axis=1)
                if cz == 1:
                    fill = pltpu.roll(pltpu.roll(a, 1, axis=0), (shift - EDGE) % LANES, axis=1)
                    value = jnp.where(first_z, fill, value)
                    value = jnp.where(floor, main_ref[26 - q, c], value)
                elif cz == -1:
                    fill = pltpu.roll(pltpu.roll(a, SUB - 1, axis=0), (shift + EDGE) % LANES, axis=1)
                    value = jnp.where(last_z, fill, value)
                    value = jnp.where(ceiling, main_ref[26 - q, c], value)
                out_ref[q, :, c * LANES : (c + 1) * LANES] = value


def stream(lattice, xlo, xhi, sides):
    cells = GROUPS * SUB * LANES
    face = (9, 2, SUB, LANES)
    spec_x = pl.BlockSpec(xlo.shape, lambda g: (0, 0, 0))
    spec_y = pl.BlockSpec((9, SUB, LANES), lambda g: (0, 0, 0))
    return pl.pallas_call(
        stream_kernel,
        grid=(GROUPS,),
        in_specs=[
            pl.BlockSpec((NQ, SUB, SUB, LANES), lambda g: (0, g, 0, 0)),
            pl.BlockSpec(face, lambda g: (2, jnp.maximum(WIDTH * g - 1, 0), 0, 0)),
            pl.BlockSpec(face, lambda g: (0, jnp.minimum(WIDTH * g + WIDTH, EDGE - 1), 0, 0)),
            spec_x, spec_x, spec_y, spec_y, spec_y, spec_y,
        ],
        out_specs=pl.BlockSpec((NQ, SUB, SUB * LANES), lambda g: (0, 0, g)),
        out_shape=jax.ShapeDtypeStruct((NQ, SUB, cells), jnp.float32),
        scratch_shapes=[
            pltpu.VMEM((9, EDGE + 2, SUB, LANES), jnp.float32),
            pltpu.VMEM((9, EDGE + 2, SUB, LANES), jnp.float32),
        ],
        compiler_params=pltpu.CompilerParams(vmem_limit_bytes=VMEM_LIMIT),
        cost_estimate=pl.CostEstimate(flops=10**7, bytes_accessed=8 * 10**6, transcendentals=0),
        name="stream",
    )(lattice, lattice, lattice, xlo, xhi, *sides)


def shifted(value, axis, step):
    count = lax.axis_size(axis)
    return lax.ppermute(value, axis, [(i, (i + step) % count) for i in range(count)])


def tags_of(landed):
    return landed[:, -1, 0, 0].astype(jnp.int32)


def on_device(populations, destination, refinement):
    blocks = populations.shape[0]
    row_count = lax.axis_size("row")
    col_count = lax.axis_size("col")
    cap_row = 2 * ((blocks + row_count - 1) // row_count)
    cap_col = 2 * ((blocks + col_count - 1) // col_count)
    swap = functools.partial(lax.all_to_all, split_axis=0, concat_axis=0, tiled=True)
    ordered = jnp.transpose(populations, (1, 0, 2))
    parts = range(len(CHUNKS))
    sent = [
        pre(ordered, destination, refinement, part, row_count, cap_row, blocks * col_count)
        for part in parts
    ]
    in_row = [swap(value, "row") for value in sent]
    tags = tags_of(in_row[0])
    packed = [repack(tags, in_row[part], part, blocks, col_count, cap_col) for part in parts]
    home = [swap(value, "col") for value in packed]
    tags = tags_of(home[0])
    lattice, ylo, yhi, xlo, xhi = post(tags, home[0], 0, None)
    below, above = shifted(yhi, "col", 1), shifted(ylo, "col", -1)
    up = jnp.concatenate([xhi.reshape(18, SUB, LANES), below[6:], above[6:]])
    down = jnp.concatenate([xlo.reshape(18, SUB, LANES), below[:3], above[:3]])
    xlo, xhi = shifted(up, "row", 1), shifted(down, "row", -1)
    lattice, ylo, yhi = post(tags, home[1], 1, lattice)
    sides = (below, above, shifted(yhi, "col", 1), shifted(ylo, "col", -1))
    return jnp.transpose(stream(lattice, xlo, xhi, sides), (1, 0, 2))


def solution(mesh):
    return jax.shard_map(
        on_device,
        mesh=mesh,
        in_specs=(P(("row", "col"), None, None), P(("row", "col")), P(("row", "col"))),
        out_specs=P(("row", "col"), None, None),
        check_vma=False,
    )
```

time: 211 us -> 133 us (0.63)
  blocking collectives: 73.9 us -> 0 us
  waiting for transfers between devices: 44.3 us -> 79.2 us
  Pallas kernels: 52.2 us -> 17.6 us
  local copies, waits for them, and re-layouts: 16 us -> 7.69 us
  starting transfers between devices: 21.8 us -> 26.4 us
    unnamed x1 -> x0, blocking collectives: 73.9 us -> none
    all_to_all x2 -> x4, waiting for transfers between devices: 28.1 us -> 66.6 us  [the longest x2 53.2 us: on_device(): in_row = [swap(value, 'row') for value in sent]]
    pallas_call x3 -> x6, Pallas kernels: 48 us -> 13.9 us  [the longest x2 5.74 us: post(): pl.pallas_call(functools.partial(post_kernel, outer), grid_spec=pltpu.Pre...]
    all_to_all x2 -> x4, starting transfers between devices: 11 us -> 18.1 us  [the longest x2 11 us: on_device(): in_row = [swap(value, 'row') for value in sent]]
    pallas_call x1 -> x0, local copies, waits for them, and re-layouts: 6.03 us -> none  [stream(): pl.pallas_call(stream_kernel, grid=(GROUPS,), in_specs=[pl.BlockSpec((NQ,...]
    ppermute x8 -> x6, waiting for transfers between devices: 16.2 us -> 12.6 us  [shifted(): lax.ppermute(value, axis, [(i, (i + step) % count) for i in range(count)])]
    ppermute x8 -> x6, starting transfers between devices: 10.8 us -> 8.31 us  [shifted(): lax.ppermute(value, axis, [(i, (i + step) % count) for i in range(count)])]
    unnamed x17 -> x18, local copies, waits for them, and re-layouts: 9.7 us -> 7.69 us
  transfers between devices with their start and end apart: 10 -> 10, of which waited for: 5 -> 5; matrix products, arithmetic and copies ran while one was open for 1% -> 1% of each run, Pallas kernels for 0% -> 8%
where the time goes in v2:
time: 133 us; the launch traced here: 132 us
  waiting for transfers between devices  79.2 us (60%)
  starting transfers between devices  26.4 us (20%)
  Pallas kernels  17.6 us (13%)
  local copies, waits for them, and re-layouts  7.69 us (6%)
    all_to_all x2, waiting for transfers between devices, on_device(): in_row = [swap(value, 'row') for value in sent]  53.2 us
    all_to_all x2, waiting for transfers between devices, on_device(): home = [swap(value, 'col') for value in packed]  13.4 us
    ppermute x6, waiting for transfers between devices, shifted(): lax.ppermute(value, axis, [(i, (i + step) % count) for i in range(count)])  12.6 us
    all_to_all x2, starting transfers between devices, on_device(): in_row = [swap(value, 'row') for value in sent]  11 us
    ppermute x6, starting transfers between devices, shifted(): lax.ppermute(value, axis, [(i, (i + step) % count) for i in range(count)])  8.31 us
    unnamed x18, local copies, waits for them, and re-layouts  7.69 us
    all_to_all x2, starting transfers between devices, on_device(): home = [swap(value, 'col') for value in packed]  7.06 us
    pallas_call x2, Pallas kernels, post(): pl.pallas_call(functools.partial(post_kernel, outer), grid_spec=pltpu.Pre...  5.74 us
  transfers between devices with their start and end apart: 10, of which 5 were waited for; matrix products, arithmetic and copies ran while one was open for 1% of the time, Pallas kernels for 8%

profile of v2, /device:TPU:0, one launch (start us, length us, event | category | flops | bytes accessed | tf_op | source)
XLA Modules:
  0.0 131.8 jit_solution(713117527980674443)
XLA Ops:
  0.0 0.7 copy-done.5
  0.7 0.7 copy-done.7
  1.3 3.3 %pre_0.1 = f32[16,19,8,128]{3,2,1,0:T(8,128)} custom-call(s32[8]{0:T(128)S(1)} %copy-done.5, s32[8]{0:T(128)S(1)} %copy-done.7, f32[27,8,4096]{2,1,0:T(8,128)} %bitcast.6), custom_call_target="tpu_custom_call" | custom-call | flops 10000000 | bytes 4000000 | tf_op jit(solution)/shard_map/pre_0/pallas_call | solution.py:120
  4.6 7.4 %all-to-all-start = ((f32[16,19,8,128]{3,2,1,0:T(8,128)}), f32[16,19,8,128]{3,2,1,0:T(8,128)S(1)}, u32[]{:S(2)}, u32[]{:S(2)}) async-start(f32[16,19,8,128]{3,2,1,0:T(8,128)} %pre_0.1), calls=%async_computation | async-start | bytes 2490368 | tf_op jit(solution)/shard_map/all_to_all | solution.py:419
  12.0 2.2 %pre_1.1 = f32[16,18,8,128]{3,2,1,0:T(8,128)S(1)} custom-call(s32[8]{0:T(128)S(1)} %copy-done.6, s32[8]{0:T(128)S(1)} %copy-done.8, f32[27,8,4096]{2,1,0:T(8,128)} %bitcast.7), custom_call_target="tpu_custom_call" | custom-call | flops 10000000 | bytes 4000000 | tf_op jit(solution)/shard_map/pre_1/pallas_call | solution.py:120
  14.2 1.0 copy-done.4
  15.2 26.7 %all-to-all-done.in_ref = f32[16,19,8,128]{3,2,1,0:T(8,128)S(1)} async-done(((f32[16,19,8,128]{3,2,1,0:T(8,128)}), f32[16,19,8,128]{3,2,1,0:T(8,128)S(1)}, u32[]{:S(2)}, u32[]{:S(2)}) %all-to-all-start) | async-done | bytes 1245216 | tf_op jit(solution)/shard_map/all_to_all | solution.py:419
  41.9 3.6 %all-to-all-start.2 = ((f32[16,18,8,128]{3,2,1,0:T(8,128)}), f32[16,18,8,128]{3,2,1,0:T(8,128)S(1)}, u32[]{:S(2)}, u32[]{:S(2)}) async-start(f32[16,18,8,128]{3,2,1,0:T(8,128)} %copy-done.4), calls=%async_computation.2 | async-start | bytes 2359296 | tf_op jit(solution)/shard_map/all_to_all | solution.py:419
  45.6 0.4 fusion.1.tags_ref
  46.0 1.9 %repack_0.1 = f32[16,19,8,128]{3,2,1,0:T(8,128)} custom-call(s32[16]{0:T(128)S(1)} %fusion.1.tags_ref, f32[16,19,8,128]{3,2,1,0:T(8,128)S(1)} %all-to-all-done.in_ref), custom_call_target="tpu_custom_call" | custom-call | bytes 3000000 | tf_op jit(solution)/shard_map/repack_0/pallas_call | solution.py:155
  47.8 26.5 %all-to-all-done.2.in_ref = f32[16,18,8,128]{3,2,1,0:T(8,128)S(1)} async-done(((f32[16,18,8,128]{3,2,1,0:T(8,128)}), f32[16,18,8,128]{3,2,1,0:T(8,128)S(1)}, u32[]{:S(2)}, u32[]{:S(2)}) %all-to-all-start.2) | async-done | bytes 1179680 | tf_op jit(solution)/shard_map/all_to_all | solution.py:419
  74.3 1.0 copy-done.2
  75.4 3.5 %all-to-all-start.1 = ((f32[16,19,8,128]{3,2,1,0:T(8,128)}), f32[16,19,8,128]{3,2,1,0:T(8,128)S(1)}, u32[]{:S(2)}, u32[]{:S(2)}) async-start(f32[16,19,8,128]{3,2,1,0:T(8,128)} %repack_0.1), calls=%async_computation.1 | async-start | bytes 2490368 | tf_op jit(solution)/shard_map/all_to_all | solution.py:422
  78.9 1.3 copy-done.3
  80.2 0.8 repack_1.1
  81.0 1.0 copy-done.1
  82.1 13.4 %all-to-all-done.1.refs_0_ = f32[16,19,8,128]{3,2,1,0:T(8,128)S(1)} async-done(((f32[16,19,8,128]{3,2,1,0:T(8,128)}), f32[16,19,8,128]{3,2,1,0:T(8,128)S(1)}, u32[]{:S(2)}, u32[]{:S(2)}) %all-to-all-start.1) | async-done | bytes 1245216 | tf_op jit(solution)/shard_map/all_to_all | solution.py:422
  95.5 3.5 %all-to-all-start.3 = ((f32[16,18,8,128]{3,2,1,0:T(8,128)}), f32[16,18,8,128]{3,2,1,0:T(8,128)S(1)}, u32[]{:S(2)}, u32[]{:S(2)}) async-start(f32[16,18,8,128]{3,2,1,0:T(8,128)} %copy-done.1), calls=%async_computation.3 | async-start | bytes 2359296 | tf_op jit(solution)/shard_map/all_to_all | solution.py:422
  99.0 0.4 fusion.tags_ref
  99.4 3.1 %post_0.1 = (f32[27,32,8,128]{3,2,1,0:T(8,128)}, f32[9,8,128]{2,1,0:T(8,128)S(1)}, f32[9,8,128]{2,1,0:T(8,128)S(1)}, f32[9,2,8,128]{3,2,1,0:T(8,128)S(1)}, f32[9,2,8,128]{3,2,1,0:T(8,128)S(1)}) custom-call(s32[16]{0:T(128)S(1)} %fusion.tags_ref, f32[16,19,8,128]{3,2,1,0:T(8,128)S(1)} %all-to-all-done.1.refs_0_), custom_call_target="tpu_custom_call" | custom-call | flops 10000000 | bytes 3000000 | tf_op jit(solution)/shard_map/post_0/pallas_call | solution.py:281
  102.5 0.5 collective-permute-start
  102.9 1.3 collective-permute-start.1
  104.2 10.9 %collective-permute-done.below_0 = f32[9,8,128]{2,1,0:T(8,128)S(1)} collective-permute-done((f32[9,8,128]{2,1,0:T(8,128)S(1)}, f32[9,8,128]{2,1,0:T(8,128)S(1)}, u32[]{:S(2)}, u32[]{:S(2)}) %collective-permute-start) | collective-permute-done | bytes 36896 | tf_op jit(solution)/shard_map/ppermute | solution.py:399
  115.2 1.5 %collective-permute-start.2 = (f32[24,8,128]{2,1,0:T(8,128)S(1)}, f32[24,8,128]{2,1,0:T(8,128)S(1)}, u32[]{:S(2)}, u32[]{:S(2)}) collective-permute-start(f32[24,8,128]{2,1,0:T(8,128)S(1)} %pad_maximum_fusion), channel_id=1, source_target_pairs={{0,4},{4,8},{8,12},{12,16},{16,20},{20,24},{24,28},{28,0},{1,5},{5... | collective-permute-start | bytes 294920 | tf_op jit(solution)/shard_map/ppermute | solution.py:399
  116.7 3.4 %collective-permute-start.3 = (f32[24,8,128]{2,1,0:T(8,128)S(1)}, f32[24,8,128]{2,1,0:T(8,128)S(1)}, u32[]{:S(2)}, u32[]{:S(2)}) collective-permute-start(f32[24,8,128]{2,1,0:T(8,128)S(1)} %pad_maximum_fusion.1), channel_id=1, source_target_pairs={{0,28},{4,0},{8,4},{12,8},{16,12},{20,16},{24,20},{28,24},{1,29},{... | collective-permute-start | bytes 294920 | tf_op jit(solution)/shard_map/ppermute | solution.py:399
  120.0 2.6 %post_1.1 = (f32[27,32,8,128]{3,2,1,0:T(8,128)}, f32[9,8,128]{2,1,0:T(8,128)S(1)}, f32[9,8,128]{2,1,0:T(8,128)S(1)}) custom-call(s32[16]{0:T(128)S(1)} %fusion.tags_ref, f32[16,18,8,128]{3,2,1,0:T(8,128)S(1)} %all-to-all-done.3.refs_0_, f32[27,32,8,128]{3,2,1,0:T(8,128)} %get-tuple-element.13.refs_1_), custom_call_target="tpu_custom_call", output_to_operand_aliasing={{0}: (2, {})} | custom-call | flops 10000000 | bytes 3000000 | tf_op jit(solution)/shard_map/post_1/pallas_call | solution.py:281
  122.6 1.7 %collective-permute-start.5 = (f32[9,8,128]{2,1,0:T(8,128)S(1)}, f32[9,8,128]{2,1,0:T(8,128)S(1)}, u32[]{:S(2)}, u32[]{:S(2)}) collective-permute-start(f32[9,8,128]{2,1,0:T(8,128)S(1)} %get-tuple-element.20), channel_id=1, source_target_pairs={{0,3},{1,0},{2,1},{3,2},{4,7},{5,4},{6,5},{7,6},{8,11},{9,8},{10,9... | collective-permute-start | bytes 110600 | tf_op jit(solution)/shard_map/ppermute | solution.py:399
  124.4 1.6 %collective-permute-done.4.below_1 = f32[9,8,128]{2,1,0:T(8,128)S(1)} collective-permute-done((f32[9,8,128]{2,1,0:T(8,128)S(1)}, f32[9,8,128]{2,1,0:T(8,128)S(1)}, u32[]{:S(2)}, u32[]{:S(2)}) %collective-permute-start.4) | collective-permute-done | bytes 36896 | tf_op jit(solution)/shard_map/ppermute | solution.py:399
  126.0 0.0 collective-permute-done.5.above_1
  126.0 0.0 copy-start
  126.1 2.0 %copy-done = f32[27,32,8,128]{3,2,1,0:T(8,128)S(1)} copy-done((f32[27,32,8,128]{3,2,1,0:T(8,128)S(1)}, f32[27,32,8,128]{3,2,1,0:T(8,128)}, u32[]{:S(2)}) %copy-start) | copy-done | bytes 3538968
  128.0 3.8 %stream.1 = f32[27,8,4096]{2,1,0:T(8,128)} custom-call(f32[27,32,8,128]{3,2,1,0:T(8,128)S(1)} %copy-done, f32[27,32,8,128]{3,2,1,0:T(8,128)S(1)} %copy-done, f32[27,32,8,128]{3,2,1,0:T(8,128)S(1)} %copy-done, f32[24,8,128]{2,1,0:T(8,128)S(1)} %collective-permute-done.2.xlo_ref, f32[24,8,128]{2,1,0:T(8,128)S(1)} %collective-permute-done.3.xhi_ref, ...), custom_call_target="tpu_custom_call" | custom-call | flops 10000000 | bytes 8000000 | tf_op jit(solution)/shard_map/stream/pallas_call | solution.py:376
  (19 shorter events, 0.1 us)
Async XLA Ops:
  0.0 0.7 copy-start.5
  0.7 0.7 copy-start.7
  4.6 7.4 %copy-start.6 = (s32[8]{0:T(128)S(1)}, s32[8]{0:T(128)}, u32[]{:S(2)}) copy-start(s32[8]{0:T(128)} %dest_ref.3) | copy-start | bytes 100
  4.6 7.4 %copy-start.8 = (s32[8]{0:T(128)S(1)}, s32[8]{0:T(128)}, u32[]{:S(2)}) copy-start(s32[8]{0:T(128)} %level_ref.3) | copy-start | bytes 100
  4.6 37.4 %all-to-all-start = ((f32[16,19,8,128]{3,2,1,0:T(8,128)}), f32[16,19,8,128]{3,2,1,0:T(8,128)S(1)}, u32[]{:S(2)}, u32[]{:S(2)}) async-start(f32[16,19,8,128]{3,2,1,0:T(8,128)} %pre_0.1), calls=%async_computation | async-start | bytes 2490368 | tf_op jit(solution)/shard_map/all_to_all | solution.py:419
  14.2 1.0 copy-start.4
  41.9 32.4 %all-to-all-start.2 = ((f32[16,18,8,128]{3,2,1,0:T(8,128)}), f32[16,18,8,128]{3,2,1,0:T(8,128)S(1)}, u32[]{:S(2)}, u32[]{:S(2)}) async-start(f32[16,18,8,128]{3,2,1,0:T(8,128)} %copy-done.4), calls=%async_computation.2 | async-start | bytes 2359296 | tf_op jit(solution)/shard_map/all_to_all | solution.py:419
  74.3 1.0 copy-start.2
  75.4 20.1 %all-to-all-start.1 = ((f32[16,19,8,128]{3,2,1,0:T(8,128)}), f32[16,19,8,128]{3,2,1,0:T(8,128)S(1)}, u32[]{:S(2)}, u32[]{:S(2)}) async-start(f32[16,19,8,128]{3,2,1,0:T(8,128)} %repack_0.1), calls=%async_computation.1 | async-start | bytes 2490368 | tf_op jit(solution)/shard_map/all_to_all | solution.py:422
  78.9 1.3 copy-start.3
  81.0 1.0 copy-start.1
  95.5 24.5 %all-to-all-start.3 = ((f32[16,18,8,128]{3,2,1,0:T(8,128)}), f32[16,18,8,128]{3,2,1,0:T(8,128)S(1)}, u32[]{:S(2)}, u32[]{:S(2)}) async-start(f32[16,18,8,128]{3,2,1,0:T(8,128)} %copy-done.1), calls=%async_computation.3 | async-start | bytes 2359296 | tf_op jit(solution)/shard_map/all_to_all | solution.py:422
  102.5 12.7 %collective-permute-start = (f32[9,8,128]{2,1,0:T(8,128)S(1)}, f32[9,8,128]{2,1,0:T(8,128)S(1)}, u32[]{:S(2)}, u32[]{:S(2)}) collective-permute-start(f32[9,8,128]{2,1,0:T(8,128)S(1)} %get-tuple-element.16), channel_id=1, source_target_pairs={{0,1},{1,2},{2,3},{3,0},{4,5},{5,6},{6,7},{7,4},{8,9},{9,10},{10,1... | collective-permute-start | bytes 110600 | tf_op jit(solution)/shard_map/ppermute | solution.py:399
  102.9 12.2 %collective-permute-start.1 = (f32[9,8,128]{2,1,0:T(8,128)S(1)}, f32[9,8,128]{2,1,0:T(8,128)S(1)}, u32[]{:S(2)}, u32[]{:S(2)}) collective-permute-start(f32[9,8,128]{2,1,0:T(8,128)S(1)} %get-tuple-element.17), channel_id=1, source_target_pairs={{0,3},{1,0},{2,1},{3,2},{4,7},{5,4},{6,5},{7,6},{8,11},{9,8},{10,9... | collective-permute-start | bytes 110600 | tf_op jit(solution)/shard_map/ppermute | solution.py:399
  115.2 10.9 %collective-permute-start.2 = (f32[24,8,128]{2,1,0:T(8,128)S(1)}, f32[24,8,128]{2,1,0:T(8,128)S(1)}, u32[]{:S(2)}, u32[]{:S(2)}) collective-permute-start(f32[24,8,128]{2,1,0:T(8,128)S(1)} %pad_maximum_fusion), channel_id=1, source_target_pairs={{0,4},{4,8},{8,12},{12,16},{16,20},{20,24},{24,28},{28,0},{1,5},{5... | collective-permute-start | bytes 294920 | tf_op jit(solution)/shard_map/ppermute | solution.py:399
  116.7 9.4 %collective-permute-start.3 = (f32[24,8,128]{2,1,0:T(8,128)S(1)}, f32[24,8,128]{2,1,0:T(8,128)S(1)}, u32[]{:S(2)}, u32[]{:S(2)}) collective-permute-start(f32[24,8,128]{2,1,0:T(8,128)S(1)} %pad_maximum_fusion.1), channel_id=1, source_target_pairs={{0,28},{4,0},{8,4},{12,8},{16,12},{20,16},{24,20},{28,24},{1,29},{... | collective-permute-start | bytes 294920 | tf_op jit(solution)/shard_map/ppermute | solution.py:399
  122.6 3.4 %collective-permute-start.4 = (f32[9,8,128]{2,1,0:T(8,128)S(1)}, f32[9,8,128]{2,1,0:T(8,128)S(1)}, u32[]{:S(2)}, u32[]{:S(2)}) collective-permute-start(f32[9,8,128]{2,1,0:T(8,128)S(1)} %get-tuple-element.19), channel_id=1, source_target_pairs={{0,1},{1,2},{2,3},{3,0},{4,5},{5,6},{6,7},{7,4},{8,9},{9,10},{10,1... | collective-permute-start | bytes 110600 | tf_op jit(solution)/shard_map/ppermute | solution.py:399
  122.6 3.4 %collective-permute-start.5 = (f32[9,8,128]{2,1,0:T(8,128)S(1)}, f32[9,8,128]{2,1,0:T(8,128)S(1)}, u32[]{:S(2)}, u32[]{:S(2)}) collective-permute-start(f32[9,8,128]{2,1,0:T(8,128)S(1)} %get-tuple-element.20), channel_id=1, source_target_pairs={{0,3},{1,0},{2,1},{3,2},{4,7},{5,4},{6,5},{7,6},{8,11},{9,8},{10,9... | collective-permute-start | bytes 110600 | tf_op jit(solution)/shard_map/ppermute | solution.py:399
  126.0 2.0 %copy-start = (f32[27,32,8,128]{3,2,1,0:T(8,128)S(1)}, f32[27,32,8,128]{3,2,1,0:T(8,128)}, u32[]{:S(2)}) copy-start(f32[27,32,8,128]{3,2,1,0:T(8,128)} %get-tuple-element.14.main_ref.prev_ref.next_ref) | copy-start | bytes 10616836

commit v3 on v2

v3 whole, which is shorter than its diff:
```python
import functools

import jax
import jax.numpy as jnp
from jax import lax
from jax.experimental import pallas as pl
from jax.experimental.pallas import tpu as pltpu
from jax.sharding import PartitionSpec as P

EDGE = 16
VISCOSITY = 0.01
LANES = 128
SUB = 8
NQ = 27
NFIELD = 9
GROUPS = 4
WIDTH = EDGE // GROUPS
CHUNKS = ((0, 3), (1, 2))
SIDE_TILES = 3
VMEM_LIMIT = 50 * 1024 * 1024


def velocity(q):
    return (q // 9 - 1, (q // 3) % 3 - 1, q % 3 - 1)


def tiles_of(part):
    return len(CHUNKS[part]) * NFIELD + (0 if part else SIDE_TILES)


def raw_moments(f):
    whole, slope, outer = {}, {}, {}
    for i in range(3):
        for j in range(3):
            low, rest, high = (f[i * 9 + j * 3 + k] for k in range(3))
            outer[i, j] = low + high
            whole[i, j] = outer[i, j] + rest
            slope[i, j] = high - low
    column = [whole[i, 0] + whole[i, 1] + whole[i, 2] for i in range(3)]
    tilt = [slope[i, 0] + slope[i, 1] + slope[i, 2] for i in range(3)]
    low_y = whole[0, 0] + whole[1, 0] + whole[2, 0]
    high_y = whole[0, 2] + whole[1, 2] + whole[2, 2]
    ends = column[0] + column[2]
    mzz = sum(outer[i, j] for i in range(3) for j in range(3))
    mxy = (whole[2, 2] - whole[2, 0]) - (whole[0, 2] - whole[0, 0])
    myz = (slope[0, 2] + slope[1, 2] + slope[2, 2]) - (slope[0, 0] + slope[1, 0] + slope[2, 0])
    return (
        ends + column[1],
        column[2] - column[0],
        high_y - low_y,
        tilt[0] + tilt[1] + tilt[2],
        ends,
        low_y + high_y,
        mzz,
        mxy,
        tilt[2] - tilt[0],
        myz,
    )


def collided(f, keep):
    rho, jx, jy, jz, mxx, myy, mzz, mxy, mxz, myz = raw_moments(f)
    inverse = 1.0 / rho
    ux, uy, uz = jx * inverse, jy * inverse, jz * inverse
    kxx = mxx - jx * ux
    return (
        rho, ux, uy, uz,
        keep * (mxy - jx * uy),
        keep * (mxz - jx * uz),
        keep * (myz - jy * uz),
        keep * (kxx - (myy - jy * uy)),
        keep * (kxx - (mzz - jz * uz)),
    )


def pre_kernel(cap, per_row, part, dest_ref, level_ref, x_ref, out_ref, swap_ref, *more):
    g = pl.program_id(0)
    steps = len(CHUNKS[part])
    blocks = x_ref.shape[1]
    chunks = x_ref.shape[2] // LANES
    which = lax.broadcasted_iota(jnp.int32, (SUB, LANES), 0)
    spot = lax.broadcasted_iota(jnp.int32, (SUB, LANES), 1) // EDGE
    scale = jnp.zeros((SUB, LANES), jnp.int32)
    for t in range(blocks):
        scale = jnp.where(which == t, jnp.left_shift(1, level_ref[t]), scale)
    rate = 1.0 / (3.0 * VISCOSITY * scale.astype(jnp.float32) + 0.5)
    keep = 1.0 - rate
    rows = [dest_ref[t] // per_row for t in range(blocks)]
    slots = []
    for t in range(blocks):
        slot = rows[t] * cap
        for other in range(t):
            slot = slot + jnp.where(rows[other] == rows[t], 1, 0)
        slots.append(slot)

    def full():
        for c in range(chunks):
            fields = collided([x_ref[q, :, c * LANES : (c + 1) * LANES] for q in range(NQ)], keep)
            for n, field in enumerate(fields):
                base = (n * chunks + c) * SUB
                swap_ref[base : base + SUB, :] = field
        for t in range(blocks):
            for n in range(NFIELD):
                moved = swap_ref[pl.ds(n * chunks * SUB + t, SUB, stride=SUB), :]
                out_ref[slots[t], g * NFIELD + n] = moved

    if part == 1:
        full()
        return
    pl.when(g < steps)(full)
    packed_ref, side_ref = more

    def pack(step):
        first_x = CHUNKS[1][step] * WIDTH
        for q in range(NQ):
            for half in range(2):
                value = packed_ref[half * NQ + q] if step else None
                for x in range(WIDTH):
                    c = x * 2 + half
                    at = (first_x + x) % SUB
                    moved = x_ref[q, :, c * LANES : (c + 1) * LANES]
                    turn = (at + half) * EDGE % LANES
                    if turn:
                        moved = pltpu.roll(moved, turn, axis=1)
                    value = moved if value is None else jnp.where(spot == at, moved, value)
                packed_ref[half * NQ + q] = value

    for step in range(len(CHUNKS[1])):
        pl.when(g == steps + step)(functools.partial(pack, step))

    @pl.when(g == pl.num_programs(0) - 1)
    def _():
        tag = jnp.zeros((SUB, LANES), jnp.int32)
        for t in range(blocks):
            tag = jnp.where(which == t, dest_ref[t], tag)
        tag = tag.astype(jnp.float32)
        for half in range(2):
            fields = collided([packed_ref[half * NQ + q] for q in range(NQ)], keep)
            for n, field in enumerate(fields):
                base = (half * NFIELD + n) * SUB
                side_ref[base : base + SUB, :] = field
        for row in range(2 * NFIELD, SIDE_TILES * SUB):
            side_ref[row * SUB : (row + 1) * SUB, :] = tag
        first = steps * NFIELD
        for slot in range(out_ref.shape[0]):
            out_ref[slot, first + SIDE_TILES - 1] = jnp.full((SUB, LANES), -1.0, jnp.float32)
        for t in range(blocks):
            for tile in range(SIDE_TILES):
                moved = side_ref[pl.ds(tile * SUB * SUB + t, SUB, stride=SUB), :]
                out_ref[slots[t], first + tile] = moved


def pre(populations, destination, refinement, part, row_count, cap, per_row):
    blocks = populations.shape[1]
    cells = populations.shape[2] // GROUPS
    order = CHUNKS[1] if part else CHUNKS[0] + CHUNKS[1]
    shape = (row_count * cap, tiles_of(part), SUB, LANES)

    def place(g, *_):
        index = order[-1]
        for step in range(len(order) - 1):
            index = jnp.where(g == step, order[step], index)
        return (0, 0, index)

    scratch = [pltpu.VMEM((NFIELD * cells // LANES * SUB, LANES), jnp.float32)]
    if part == 0:
        scratch += [
            pltpu.VMEM((2 * NQ, SUB, LANES), jnp.float32),
            pltpu.VMEM((SIDE_TILES * SUB * SUB, LANES), jnp.float32),
        ]
    return pl.pallas_call(
        functools.partial(pre_kernel, cap, per_row, part),
        grid_spec=pltpu.PrefetchScalarGridSpec(
            num_scalar_prefetch=2,
            grid=(len(order),),
            in_specs=[pl.BlockSpec((NQ, blocks, cells), place)],
            out_specs=pl.BlockSpec(shape, lambda g, *_: (0, 0, 0, 0)),
            scratch_shapes=scratch,
        ),
        out_shape=jax.ShapeDtypeStruct(shape, jnp.float32),
        compiler_params=pltpu.CompilerParams(vmem_limit_bytes=VMEM_LIMIT),
        cost_estimate=pl.CostEstimate(flops=10**7, bytes_accessed=4 * 10**6, transcendentals=0),
        name="pre_%d" % part,
    )(destination, refinement, populations)


def repack_kernel(cap, col_count, tagged, away_ref, in_ref, *refs):
    outs, (source_ref, count_ref) = refs[:col_count], refs[col_count:]
    for d in range(col_count):
        count_ref[d] = 0
        for k in range(cap):
            source_ref[d * cap + k] = -1
    for slot in range(in_ref.shape[0]):

        @pl.when(away_ref[slot] >= 0)
        def _():
            d = away_ref[slot]
            k = count_ref[d]
            count_ref[d] = k + 1
            source_ref[d * cap + k] = slot

    for d in range(col_count):
        for k in range(cap):
            slot = source_ref[d * cap + k]

            @pl.when(slot >= 0)
            def _():
                outs[d][k] = in_ref[slot]

            if tagged:

                @pl.when(slot < 0)
                def _():
                    outs[d][k, in_ref.shape[1] - 1] = jnp.full((SUB, LANES), -1.0, jnp.float32)


def repack(away, landed, part, col_count, cap):
    out = jax.ShapeDtypeStruct((cap,) + landed.shape[1:], jnp.float32)
    return pl.pallas_call(
        functools.partial(repack_kernel, cap, col_count, part == 0),
        in_specs=[pl.BlockSpec(memory_space=pltpu.SMEM), pl.BlockSpec(memory_space=pltpu.VMEM)],
        out_specs=[pl.BlockSpec(memory_space=pltpu.VMEM)] * col_count,
        scratch_shapes=[
            pltpu.SMEM((col_count * cap,), jnp.int32),
            pltpu.SMEM((col_count,), jnp.int32),
        ],
        out_shape=[out] * col_count,
        compiler_params=pltpu.CompilerParams(vmem_limit_bytes=VMEM_LIMIT),
        cost_estimate=pl.CostEstimate(flops=0, bytes_accessed=3 * 10**6, transcendentals=0),
        name="repack_%d" % part,
    )(away, landed)


def backward(zeroth, first, second, u):
    raw_one, raw_two = first, second
    if zeroth is not None:
        moved = u * zeroth
        raw_one = moved if raw_one is None else raw_one + moved
        square = u * moved
        raw_two = square if raw_two is None else raw_two + square
    if first is not None:
        cross = (u + u) * first
        raw_two = cross if raw_two is None else raw_two + cross
    rest = -raw_two if zeroth is None else zeroth - raw_two
    return 0.5 * (raw_two - raw_one), rest, 0.5 * (raw_one + raw_two)


def post_populations(rho, ux, uy, uz, pxy, pxz, pyz, dev_one, dev_two):
    inverse = 1.0 / rho
    pxx = (rho + dev_one + dev_two) * (1.0 / 3.0)
    pyy = pxx - dev_one
    pzz = pxx - dev_two
    sxy, sxz, syz = pxy * inverse, pxz * inverse, pyz * inverse
    syy, szz = pyy * inverse, pzz * inverse
    central = {
        (0, 0, 0): rho, (2, 0, 0): pxx, (0, 2, 0): pyy, (0, 0, 2): pzz,
        (1, 1, 0): pxy, (1, 0, 1): pxz, (0, 1, 1): pyz,
        (2, 2, 0): pxx * syy + 2.0 * pxy * sxy,
        (2, 0, 2): pxx * szz + 2.0 * pxz * sxz,
        (0, 2, 2): pyy * szz + 2.0 * pyz * syz,
        (2, 1, 1): pxx * syz + 2.0 * pxy * sxz,
        (1, 2, 1): pyy * sxz + 2.0 * pxy * syz,
        (1, 1, 2): pzz * sxy + 2.0 * pxz * syz,
        (2, 2, 2): pxx * syy * szz
        + 2.0 * (pxx * syz * syz + pyy * sxz * sxz + pzz * sxy * sxy)
        + 8.0 * pxy * sxz * syz,
    }
    along_z = {}
    for a in range(3):
        for b in range(3):
            parts = backward(*(central.get((a, b, c)) for c in range(3)), uz)
            for k in range(3):
                along_z[a, b, k] = parts[k]
    along_y = {}
    for a in range(3):
        for k in range(3):
            parts = backward(*(along_z[a, b, k] for b in range(3)), uy)
            for j in range(3):
                along_y[a, j, k] = parts[j]
    result = [None] * NQ
    for j in range(3):
        for k in range(3):
            parts = backward(*(along_y[a, j, k] for a in range(3)), ux)
            for i in range(3):
                result[i * 9 + j * 3 + k] = parts[i]
    return result


def unload(tags_ref, ins, block_ref):
    cap = ins[0].shape[0]
    for d, in_ref in enumerate(ins):
        for k in range(cap):
            tag = tags_ref[d * cap + k]

            @pl.when(tag >= 0)
            def _():
                block_ref[tag % SUB] = in_ref[k]


def side_spot(lane, x):
    return (lane // EDGE) == x % SUB


def post_kernel(count, tags_ref, *refs):
    ins = refs[:count]
    post_ref, ylo_ref, yhi_ref, xlo_ref, xhi_ref, block_ref, swap_ref, side_ref = refs[count:]
    g = pl.program_id(0)
    steps = len(CHUNKS[0])
    lane = lax.broadcasted_iota(jnp.int32, (SUB, LANES), 1)

    @pl.when(g == 0)
    def _():
        unload(tags_ref, ins, block_ref)
        for t in range(SUB):
            for tile in range(SIDE_TILES):
                side_ref[pl.ds(tile * SUB * SUB + t, SUB, stride=SUB), :] = block_ref[
                    t, steps * NFIELD + tile
                ]
        for half in range(2):
            fields = [
                side_ref[(half * NFIELD + n) * SUB : (half * NFIELD + n + 1) * SUB, :]
                for n in range(NFIELD)
            ]
            result = post_populations(*fields)
            for i in range(3):
                for k in range(3):
                    value = result[i * 9 + 6 * half + k]
                    for tile in range(2):
                        (yhi_ref if half else ylo_ref)[i * 3 + k, tile] = value

    for t in range(SUB):
        for n in range(NFIELD):
            swap_ref[pl.ds(n * SUB * SUB + t, SUB, stride=SUB), :] = block_ref[t, g * NFIELD + n]
    group = CHUNKS[0][0]
    for step in range(1, steps):
        group = jnp.where(g == step, CHUNKS[0][step], group)
    for c in range(SUB):
        fields = [swap_ref[(n * SUB + c) * SUB : (n * SUB + c + 1) * SUB, :] for n in range(NFIELD)]
        result = post_populations(*fields)
        for q in range(NQ):
            post_ref[q, c] = result[q]
        x_in, half = c // 2, c % 2
        x = group * WIDTH + x_in
        inside = side_spot(lane, x)
        face_ref, first, shift = ((ylo_ref, 0, 0), (yhi_ref, 6, EDGE))[half]
        turn = ((x % SUB) * EDGE + shift) % LANES
        for i in range(3):
            for k in range(3):
                value = pltpu.roll(result[i * 9 + first + k], turn, axis=1)
                at = (i * 3 + k, x // SUB)
                face_ref[at] = jnp.where(inside, value, face_ref[at])

        if x_in == 0:

            @pl.when(group == 0)
            def _():
                for q in range(9):
                    xlo_ref[q, half] = result[q]

        if x_in == WIDTH - 1:

            @pl.when(group == GROUPS - 1)
            def _():
                for q in range(9):
                    xhi_ref[q, half] = result[18 + q]


def post(tags, homes):
    shape = jax.ShapeDtypeStruct
    face = (9, 2, SUB, LANES)
    steps = len(CHUNKS[0])
    spec = pl.BlockSpec(face, lambda g, *_: (0, 0, 0, 0))
    return pl.pallas_call(
        functools.partial(post_kernel, len(homes)),
        grid_spec=pltpu.PrefetchScalarGridSpec(
            num_scalar_prefetch=1,
            grid=(steps,),
            in_specs=[pl.BlockSpec(homes[0].shape, lambda g, *_: (0, 0, 0, 0))] * len(homes),
            out_specs=[pl.BlockSpec((NQ, SUB, SUB, LANES), lambda g, *_: (0, g, 0, 0))] + [spec] * 4,
            scratch_shapes=[
                pltpu.VMEM((SUB, tiles_of(0), SUB, LANES), jnp.float32),
                pltpu.VMEM((NFIELD * SUB * SUB, LANES), jnp.float32),
                pltpu.VMEM((SIDE_TILES * SUB * SUB, LANES), jnp.float32),
            ],
        ),
        out_shape=[shape((NQ, steps * SUB, SUB, LANES), jnp.float32)]
        + [shape(face, jnp.float32)] * 4,
        compiler_params=pltpu.CompilerParams(vmem_limit_bytes=VMEM_LIMIT),
        cost_estimate=pl.CostEstimate(flops=10**7, bytes_accessed=3 * 10**6, transcendentals=0),
        name="post",
    )(tags, *homes)


def finish_kernel(count, tags_ref, *refs):
    ins = refs[:count]
    (
        early_ref, xlo_ref, xhi_ref, below_in, above_in,
        out_ref, main_ref, below_ref, above_ref, block_ref, swap_ref, sems,
    ) = refs[count:]
    g = pl.program_id(0)

    @pl.when(g == 0)
    def _():
        copies = [
            pltpu.make_async_copy(
                early_ref.at[:, pl.ds(step * SUB, SUB)],
                main_ref.at[:, pl.ds(group * SUB, SUB)],
                sems.at[step],
            )
            for step, group in enumerate(CHUNKS[0])
        ]
        for copy in copies:
            copy.start()
        unload(tags_ref, ins, block_ref)
        for step, group in enumerate(CHUNKS[1]):
            for t in range(SUB):
                for n in range(NFIELD):
                    swap_ref[pl.ds(n * SUB * SUB + t, SUB, stride=SUB), :] = block_ref[
                        t, step * NFIELD + n
                    ]
            for c in range(SUB):
                fields = [
                    swap_ref[(n * SUB + c) * SUB : (n * SUB + c + 1) * SUB, :] for n in range(NFIELD)
                ]
                for q, value in enumerate(post_populations(*fields)):
                    main_ref[q, group * SUB + c] = value
        for x in range(EDGE):
            at = x % SUB
            for k in range(9):
                packed = below_in[k, x // SUB]
                below_ref[k, x + 1] = pltpu.roll(packed, (LANES - EDGE - EDGE * at) % LANES, axis=1)
                packed = above_in[k, x // SUB]
                above_ref[k, x + 1] = pltpu.roll(packed, (LANES - EDGE * at) % LANES, axis=1)
        for k in range(3):
            below_ref[6 + k, 0] = xlo_ref[18 + k]
            above_ref[6 + k, 0] = pltpu.roll(xlo_ref[21 + k], EDGE, axis=1)
            below_ref[k, EDGE + 1] = pltpu.roll(xhi_ref[18 + k], LANES - EDGE, axis=1)
            above_ref[k, EDGE + 1] = xhi_ref[21 + k]
        for copy in copies:
            copy.wait()

    lane = lax.broadcasted_iota(jnp.int32, (SUB, LANES), 1)
    block = lax.broadcasted_iota(jnp.int32, (SUB, LANES), 0)
    along = lane % EDGE
    first_z, last_z = along == 0, along == EDGE - 1
    floor = first_z & (block == 0)
    ceiling = last_z & (block == SUB - 1)
    low_y, high_y = lane < EDGE, lane >= LANES - EDGE

    for x in range(WIDTH):

        def source(q, half):
            at = x - velocity(q)[0]
            row = (g * WIDTH + at) * 2 + half
            if at < 0:
                inside = main_ref[q, jnp.maximum(row, 0)]
                return jnp.where(g == 0, xlo_ref[(q - 18) * 2 + half], inside)
            if at >= WIDTH:
                inside = main_ref[q, jnp.minimum(row, GROUPS * SUB - 1)]
                return jnp.where(g == GROUPS - 1, xhi_ref[q * 2 + half], inside)
            return main_ref[q, row]

        for half in range(2):
            c = x * 2 + half
            for q in range(NQ):
                cx, cy, cz = velocity(q)
                a = source(q, half)
                side = g * WIDTH + x - cx + 1
                k = (cx + 1) * 3 + cz + 1
                if cy == 1:
                    a = jnp.where(high_y, below_ref[k, side] if half == 0 else source(q, 0), a)
                elif cy == -1:
                    a = jnp.where(low_y, above_ref[k, side] if half == 1 else source(q, 1), a)
                shift = EDGE * cy + cz
                value = a if shift == 0 else pltpu.roll(a, shift % LANES, axis=1)
                if cz == 1:
                    fill = pltpu.roll(pltpu.roll(a, 1, axis=0), (shift - EDGE) % LANES, axis=1)
                    value = jnp.where(first_z, fill, value)
                    value = jnp.where(floor, main_ref[26 - q, g * SUB + c], value)
                elif cz == -1:
                    fill = pltpu.roll(pltpu.roll(a, SUB - 1, axis=0), (shift + EDGE) % LANES, axis=1)
                    value = jnp.where(last_z, fill, value)
                    value = jnp.where(ceiling, main_ref[26 - q, g * SUB + c], value)
                out_ref[q, :, c * LANES : (c + 1) * LANES] = value


def finish(tags, homes, early, xlo, xhi, below, above):
    def whole(value):
        rank = len(value.shape)
        return pl.BlockSpec(value.shape, lambda g, *_: (0,) * rank)

    return pl.pallas_call(
        functools.partial(finish_kernel, len(homes)),
        grid_spec=pltpu.PrefetchScalarGridSpec(
            num_scalar_prefetch=1,
            grid=(GROUPS,),
            in_specs=[whole(value) for value in homes]
            + [pl.BlockSpec(memory_space=pl.ANY)]
            + [whole(value) for value in (xlo, xhi, below, above)],
            out_specs=pl.BlockSpec((NQ, SUB, SUB * LANES), lambda g, *_: (0, 0, g)),
            scratch_shapes=[
                pltpu.VMEM((NQ, GROUPS * SUB, SUB, LANES), jnp.float32),
                pltpu.VMEM((9, EDGE + 2, SUB, LANES), jnp.float32),
                pltpu.VMEM((9, EDGE + 2, SUB, LANES), jnp.float32),
                pltpu.VMEM((SUB, tiles_of(1), SUB, LANES), jnp.float32),
                pltpu.VMEM((NFIELD * SUB * SUB, LANES), jnp.float32),
                pltpu.SemaphoreType.DMA((len(CHUNKS[0]),)),
            ],
        ),
        out_shape=jax.ShapeDtypeStruct((NQ, SUB, GROUPS * SUB * LANES), jnp.float32),
        compiler_params=pltpu.CompilerParams(vmem_limit_bytes=VMEM_LIMIT),
        cost_estimate=pl.CostEstimate(flops=10**7, bytes_accessed=8 * 10**6, transcendentals=0),
        name="finish",
    )(tags, *homes, early, xlo, xhi, below, above)


def shifted(value, axis, step):
    count = lax.axis_size(axis)
    return lax.ppermute(value, axis, [(i, (i + step) % count) for i in range(count)])


def tags_of(landed):
    return landed[:, -1, 2 * NFIELD - (SIDE_TILES - 1) * SUB, 0].astype(jnp.int32)


def on_device(populations, destination, refinement):
    blocks = populations.shape[0]
    row_count = lax.axis_size("row")
    col_count = lax.axis_size("col")
    cap_row = 2 * ((blocks + row_count - 1) // row_count)
    cap_col = 2 * ((blocks + col_count - 1) // col_count)
    ordered = jnp.transpose(populations, (1, 0, 2))
    in_row = [
        lax.all_to_all(
            pre(ordered, destination, refinement, part, row_count, cap_row, blocks * col_count),
            "row", split_axis=0, concat_axis=0, tiled=True,
        )
        for part in range(2)
    ]
    tags = tags_of(in_row[0])
    away = jnp.where(tags >= 0, (tags // blocks - lax.axis_index("col")) % col_count, -1)

    def to_columns(part):
        packed = repack(away, in_row[part], part, col_count, cap_col)
        return [packed[d] if d == 0 else shifted(packed[d], "col", d) for d in range(col_count)]

    homes = to_columns(0)
    tags = jnp.concatenate([tags_of(value) for value in homes])
    early, ylo, yhi, xlo, xhi = post(tags, homes)
    below, above = shifted(yhi, "col", 1), shifted(ylo, "col", -1)
    up = jnp.concatenate([xhi.reshape(18, SUB, LANES), below[6:, 1], above[6:, 1]])
    down = jnp.concatenate([xlo.reshape(18, SUB, LANES), below[:3, 0], above[:3, 0]])
    xlo, xhi = shifted(up, "row", 1), shifted(down, "row", -1)
    homes = to_columns(1)
    return jnp.transpose(finish(tags, homes, early, xlo, xhi, below, above), (1, 0, 2))


def solution(mesh):
    return jax.shard_map(
        on_device,
        mesh=mesh,
        in_specs=(P(("row", "col"), None, None), P(("row", "col")), P(("row", "col"))),
        out_specs=P(("row", "col"), None, None),
        check_vma=False,
    )
```

time: 133 us -> 111 us (0.83)
  waiting for transfers between devices: 79.2 us -> 65.3 us
  starting transfers between devices: 26.4 us -> 22.7 us
  local copies, waits for them, and re-layouts: 7.69 us -> 4 us
    all_to_all x4 -> x2, waiting for transfers between devices: 66.6 us -> 35.5 us  [on_device(): lax.all_to_all(pre(ordered, destination, refinement, part, row_count, cap...]
    ppermute x6 -> x10, waiting for transfers between devices: 12.6 us -> 29.7 us  [shifted(): lax.ppermute(value, axis, [(i, (i + step) % count) for i in range(count)])]
    all_to_all x4 -> x2, starting transfers between devices: 18.1 us -> 11 us  [on_device(): lax.all_to_all(pre(ordered, destination, refinement, part, row_count, cap...]
    unnamed x18 -> x12, local copies, waits for them, and re-layouts: 7.69 us -> 3.99 us
    ppermute x6 -> x10, starting transfers between devices: 8.31 us -> 11.7 us  [shifted(): lax.ppermute(value, axis, [(i, (i + step) % count) for i in range(count)])]
    pallas_call x7 -> x6, Pallas kernels: 17.6 us -> 17.3 us  [the longest x2 8.14 us: pre(): pl.pallas_call(functools.partial(pre_kernel, cap, per_row, part), grid_sp...]
  transfers between devices with their start and end apart: 10 -> 12, of which waited for: 5 -> 8; matrix products, arithmetic and copies ran while one was open for 1% -> 1% of each run, Pallas kernels for 8% -> 7%
where the time goes in v3:
time: 111 us
  waiting for transfers between devices  65.3 us (59%)
  starting transfers between devices  22.7 us (20%)
  Pallas kernels  17.3 us (16%)
  local copies, waits for them, and re-layouts  4 us (4%)
  other arithmetic  1.14 us (1%)
    all_to_all x2, waiting for transfers between devices, on_device(): lax.all_to_all(pre(ordered, destination, refinement, part, row_count, cap...  35.5 us
    ppermute x10, waiting for transfers between devices, shifted(): lax.ppermute(value, axis, [(i, (i + step) % count) for i in range(count)])  29.7 us
    ppermute x10, starting transfers between devices, shifted(): lax.ppermute(value, axis, [(i, (i + step) % count) for i in range(count)])  11.7 us
    all_to_all x2, starting transfers between devices, on_device(): lax.all_to_all(pre(ordered, destination, refinement, part, row_count, cap...  11 us
    pallas_call x2, Pallas kernels, pre(): pl.pallas_call(functools.partial(pre_kernel, cap, per_row, part), grid_sp...  8.14 us
    pallas_call x1, Pallas kernels, finish(): pl.pallas_call(functools.partial(finish_kernel, len(homes)), grid_spec=pl...  5.06 us
    unnamed x12, local copies, waits for them, and re-layouts  3.99 us
    pallas_call x1, Pallas kernels, post(): pl.pallas_call(functools.partial(post_kernel, len(homes)), grid_spec=pltp...  2.48 us
  transfers between devices with their start and end apart: 12, of which 8 were waited for; matrix products, arithmetic and copies ran while one was open for 1% of the time, Pallas kernels for 7%

profile of v3, /device:TPU:0, one launch (start us, length us, event | category | flops | bytes accessed | tf_op | source)
XLA Modules:
  0.0 110.5 jit_solution(2458195678188718552)
XLA Ops:
  0.0 0.7 copy-done.2
  0.7 0.7 copy-done.4
  1.3 5.0 %pre_0.1 = f32[16,21,8,128]{3,2,1,0:T(8,128)} custom-call(s32[8]{0:T(128)S(1)} %copy-done.2, s32[8]{0:T(128)S(1)} %copy-done.4, f32[27,8,4096]{2,1,0:T(8,128)} %bitcast.14), custom_call_target="tpu_custom_call" | custom-call | flops 10000000 | bytes 4000000 | tf_op jit(solution)/shard_map/pre_0/pallas_call | solution.py:171
  6.3 7.4 %all-to-all-start = ((f32[16,21,8,128]{3,2,1,0:T(8,128)}), f32[16,21,8,128]{3,2,1,0:T(8,128)S(1)}, u32[]{:S(2)}, u32[]{:S(2)}) async-start(f32[16,21,8,128]{3,2,1,0:T(8,128)} %pre_0.1), calls=%async_computation | async-start | bytes 2752512 | tf_op jit(solution)/shard_map/all_to_all | solution.py:534
  13.7 3.2 %pre_1.1 = f32[16,18,8,128]{3,2,1,0:T(8,128)} custom-call(s32[8]{0:T(128)S(1)} %copy-done.3, s32[8]{0:T(128)S(1)} %copy-done.5, f32[27,8,4096]{2,1,0:T(8,128)} %bitcast.15), custom_call_target="tpu_custom_call" | custom-call | flops 10000000 | bytes 4000000 | tf_op jit(solution)/shard_map/pre_1/pallas_call | solution.py:171
  16.9 29.6 %all-to-all-done.in_ref = f32[16,21,8,128]{3,2,1,0:T(8,128)S(1)} async-done(((f32[16,21,8,128]{3,2,1,0:T(8,128)}), f32[16,21,8,128]{3,2,1,0:T(8,128)S(1)}, u32[]{:S(2)}, u32[]{:S(2)}) %all-to-all-start) | async-done | bytes 1376288 | tf_op jit(solution)/shard_map/all_to_all | solution.py:534
  46.5 3.6 %all-to-all-start.1 = ((f32[16,18,8,128]{3,2,1,0:T(8,128)}), f32[16,18,8,128]{3,2,1,0:T(8,128)S(1)}, u32[]{:S(2)}, u32[]{:S(2)}) async-start(f32[16,18,8,128]{3,2,1,0:T(8,128)} %pre_1.1), calls=%async_computation.1 | async-start | bytes 2359296 | tf_op jit(solution)/shard_map/all_to_all | solution.py:534
  50.1 0.4 fusion
  50.5 0.8 repack_0.1
  51.4 1.6 %collective-permute-start.1 = (f32[4,21,8,128]{3,2,1,0:T(8,128)S(1)}, f32[4,21,8,128]{3,2,1,0:T(8,128)S(1)}, u32[]{:S(2)}, u32[]{:S(2)}) collective-permute-start(f32[4,21,8,128]{3,2,1,0:T(8,128)S(1)} %get-tuple-element.20), channel_id=1, source_target_pairs={{0,2},{1,3},{2,0},{3,1},{4,6},{5,7},{6,4},{7,5},{8,10},{9,11},{10,... | collective-permute-start | bytes 1032200 | tf_op jit(solution)/shard_map/ppermute | solution.py:519
  53.0 1.4 %collective-permute-start.2 = (f32[4,21,8,128]{3,2,1,0:T(8,128)S(1)}, f32[4,21,8,128]{3,2,1,0:T(8,128)S(1)}, u32[]{:S(2)}, u32[]{:S(2)}) collective-permute-start(f32[4,21,8,128]{3,2,1,0:T(8,128)S(1)} %get-tuple-element.21), channel_id=1, source_target_pairs={{0,3},{1,0},{2,1},{3,2},{4,7},{5,4},{6,5},{7,6},{8,11},{9,8},{10,9... | collective-permute-start | bytes 1032200 | tf_op jit(solution)/shard_map/ppermute | solution.py:519
  54.4 0.2 convert_reduce_fusion
  54.6 6.6 %collective-permute-done.refs_1_ = f32[4,21,8,128]{3,2,1,0:T(8,128)S(1)} collective-permute-done((f32[4,21,8,128]{3,2,1,0:T(8,128)S(1)}, f32[4,21,8,128]{3,2,1,0:T(8,128)S(1)}, u32[]{:S(2)}, u32[]{:S(2)}) %collective-permute-start) | collective-permute-done | bytes 344096 | tf_op jit(solution)/shard_map/ppermute | solution.py:519
  61.2 0.2 fusion.3
  61.3 1.0 collective-permute-done.1.refs_2_
  62.4 0.2 fusion.2
  62.5 5.6 %collective-permute-done.2.refs_3_ = f32[4,21,8,128]{3,2,1,0:T(8,128)S(1)} collective-permute-done((f32[4,21,8,128]{3,2,1,0:T(8,128)S(1)}, f32[4,21,8,128]{3,2,1,0:T(8,128)S(1)}, u32[]{:S(2)}, u32[]{:S(2)}) %collective-permute-start.2) | collective-permute-done | bytes 344096 | tf_op jit(solution)/shard_map/ppermute | solution.py:519
  68.2 0.2 fusion.1
  68.4 2.5 %post.1 = (f32[27,16,8,128]{3,2,1,0:T(8,128)S(1)}, f32[9,2,8,128]{3,2,1,0:T(8,128)S(1)}, f32[9,2,8,128]{3,2,1,0:T(8,128)S(1)}, f32[9,2,8,128]{3,2,1,0:T(8,128)S(1)}, f32[9,2,8,128]{3,2,1,0:T(8,128)S(1)}) custom-call(s32[16]{0:T(128)S(1)} %pad_add_fusion.tags_ref, f32[4,21,8,128]{3,2,1,0:T(8,128)S(1)} %get-tuple-element.18.refs_0_, ...), custom_call_target="tpu_custom_call" | custom-call | flops 10000000 | bytes 3000000 | tf_op jit(solution)/shard_map/post/pallas_call | solution.py:373
  70.9 1.2 %copy-done = f32[27,16,8,128]{3,2,1,0:T(8,128)} copy-done((f32[27,16,8,128]{3,2,1,0:T(8,128)}, f32[27,16,8,128]{3,2,1,0:T(8,128)S(1)}, u32[]{:S(2)}) %copy-start) | copy-done | bytes 1769496
  72.1 0.8 collective-permute-start.6
  72.9 5.9 %all-to-all-done.1.in_ref = f32[16,18,8,128]{3,2,1,0:T(8,128)S(1)} async-done(((f32[16,18,8,128]{3,2,1,0:T(8,128)}), f32[16,18,8,128]{3,2,1,0:T(8,128)S(1)}, u32[]{:S(2)}, u32[]{:S(2)}) %all-to-all-start.1) | async-done | bytes 1179680 | tf_op jit(solution)/shard_map/all_to_all | solution.py:534
  78.9 0.8 repack_1.1
  79.7 1.6 %collective-permute-start.4 = (f32[4,18,8,128]{3,2,1,0:T(8,128)S(1)}, f32[4,18,8,128]{3,2,1,0:T(8,128)S(1)}, u32[]{:S(2)}, u32[]{:S(2)}) collective-permute-start(f32[4,18,8,128]{3,2,1,0:T(8,128)S(1)} %get-tuple-element.24), channel_id=1, source_target_pairs={{0,2},{1,3},{2,0},{3,1},{4,6},{5,7},{6,4},{7,5},{8,10},{9,11},{10,... | collective-permute-start | bytes 884744 | tf_op jit(solution)/shard_map/ppermute | solution.py:519
  81.3 1.4 %collective-permute-start.5 = (f32[4,18,8,128]{3,2,1,0:T(8,128)S(1)}, f32[4,18,8,128]{3,2,1,0:T(8,128)S(1)}, u32[]{:S(2)}, u32[]{:S(2)}) collective-permute-start(f32[4,18,8,128]{3,2,1,0:T(8,128)S(1)} %get-tuple-element.25), channel_id=1, source_target_pairs={{0,3},{1,0},{2,1},{3,2},{4,7},{5,4},{6,5},{7,6},{8,11},{9,8},{10,9... | collective-permute-start | bytes 884744 | tf_op jit(solution)/shard_map/ppermute | solution.py:519
  82.7 12.4 %collective-permute-done.7.refs_8_ = f32[9,2,8,128]{3,2,1,0:T(8,128)S(1)} collective-permute-done((f32[9,2,8,128]{3,2,1,0:T(8,128)S(1)}, f32[9,2,8,128]{3,2,1,0:T(8,128)S(1)}, u32[]{:S(2)}, u32[]{:S(2)}) %collective-permute-start.7) | collective-permute-done | bytes 73760 | tf_op jit(solution)/shard_map/ppermute | solution.py:519
  95.2 1.5 %collective-permute-start.8 = (f32[24,8,128]{2,1,0:T(8,128)S(1)}, f32[24,8,128]{2,1,0:T(8,128)S(1)}, u32[]{:S(2)}, u32[]{:S(2)}) collective-permute-start(f32[24,8,128]{2,1,0:T(8,128)S(1)} %pad_maximum_fusion), channel_id=1, source_target_pairs={{0,4},{4,8},{8,12},{12,16},{16,20},{20,24},{24,28},{28,0},{1,5},{5... | collective-permute-start | bytes 294920 | tf_op jit(solution)/shard_map/ppermute | solution.py:519
  96.6 3.4 %collective-permute-start.9 = (f32[24,8,128]{2,1,0:T(8,128)S(1)}, f32[24,8,128]{2,1,0:T(8,128)S(1)}, u32[]{:S(2)}, u32[]{:S(2)}) collective-permute-start(f32[24,8,128]{2,1,0:T(8,128)S(1)} %pad_maximum_fusion.1), channel_id=1, source_target_pairs={{0,28},{4,0},{8,4},{12,8},{16,12},{20,16},{24,20},{28,24},{1,29},{... | collective-permute-start | bytes 294920 | tf_op jit(solution)/shard_map/ppermute | solution.py:519
  100.0 3.5 %collective-permute-done.8.refs_5_ = f32[24,8,128]{2,1,0:T(8,128)S(1)} collective-permute-done((f32[24,8,128]{2,1,0:T(8,128)S(1)}, f32[24,8,128]{2,1,0:T(8,128)S(1)}, u32[]{:S(2)}, u32[]{:S(2)}) %collective-permute-start.8) | collective-permute-done | bytes 98336 | tf_op jit(solution)/shard_map/ppermute | solution.py:519
  103.5 0.5 collective-permute-done.9.refs_6_
  104.0 1.5 %copy-done.1 = f32[27,16,8,128]{3,2,1,0:T(8,128)S(1)} copy-done((f32[27,16,8,128]{3,2,1,0:T(8,128)S(1)}, f32[27,16,8,128]{3,2,1,0:T(8,128)}, u32[]{:S(2)}) %copy-start.1) | copy-done | bytes 1769496
  105.5 5.1 %finish.1 = f32[27,8,4096]{2,1,0:T(8,128)} custom-call(s32[16]{0:T(128)S(1)} %pad_add_fusion.tags_ref, f32[4,18,8,128]{3,2,1,0:T(8,128)S(1)} %get-tuple-element.22.refs_0_, f32[4,18,8,128]{3,2,1,0:T(8,128)S(1)} %collective-permute-done.3.refs_1_, f32[4,18,8,128]{3,2,1,0:T(8,128)S(1)} %collective-permute-done.4.refs_2_, ...), custom_call_target="tpu_custom_call" | custom-call | flops 10000000 | bytes 8000000 | tf_op jit(solution)/shard_map/finish/pallas_call | solution.py:492
  (21 shorter events, 0.3 us)
Async XLA Ops:
  0.0 0.7 copy-start.2
  0.7 0.7 copy-start.4
  6.3 7.4 %copy-start.3 = (s32[8]{0:T(128)S(1)}, s32[8]{0:T(128)}, u32[]{:S(2)}) copy-start(s32[8]{0:T(128)} %dest_ref.3) | copy-start | bytes 100
  6.3 7.4 %copy-start.5 = (s32[8]{0:T(128)S(1)}, s32[8]{0:T(128)}, u32[]{:S(2)}) copy-start(s32[8]{0:T(128)} %level_ref.3) | copy-start | bytes 100
  6.3 40.2 %all-to-all-start = ((f32[16,21,8,128]{3,2,1,0:T(8,128)}), f32[16,21,8,128]{3,2,1,0:T(8,128)S(1)}, u32[]{:S(2)}, u32[]{:S(2)}) async-start(f32[16,21,8,128]{3,2,1,0:T(8,128)} %pre_0.1), calls=%async_computation | async-start | bytes 2752512 | tf_op jit(solution)/shard_map/all_to_all | solution.py:534
  46.5 32.4 %all-to-all-start.1 = ((f32[16,18,8,128]{3,2,1,0:T(8,128)}), f32[16,18,8,128]{3,2,1,0:T(8,128)S(1)}, u32[]{:S(2)}, u32[]{:S(2)}) async-start(f32[16,18,8,128]{3,2,1,0:T(8,128)} %pre_1.1), calls=%async_computation.1 | async-start | bytes 2359296 | tf_op jit(solution)/shard_map/all_to_all | solution.py:534
  51.4 9.8 %collective-permute-start = (f32[4,21,8,128]{3,2,1,0:T(8,128)S(1)}, f32[4,21,8,128]{3,2,1,0:T(8,128)S(1)}, u32[]{:S(2)}, u32[]{:S(2)}) collective-permute-start(f32[4,21,8,128]{3,2,1,0:T(8,128)S(1)} %get-tuple-element.19), channel_id=1, source_target_pairs={{0,1},{1,2},{2,3},{3,0},{4,5},{5,6},{6,7},{7,4},{8,9},{9,10},{10,1... | collective-permute-start | bytes 1032200 | tf_op jit(solution)/shard_map/ppermute | solution.py:519
  51.4 11.0 %collective-permute-start.1 = (f32[4,21,8,128]{3,2,1,0:T(8,128)S(1)}, f32[4,21,8,128]{3,2,1,0:T(8,128)S(1)}, u32[]{:S(2)}, u32[]{:S(2)}) collective-permute-start(f32[4,21,8,128]{3,2,1,0:T(8,128)S(1)} %get-tuple-element.20), channel_id=1, source_target_pairs={{0,2},{1,3},{2,0},{3,1},{4,6},{5,7},{6,4},{7,5},{8,10},{9,11},{10,... | collective-permute-start | bytes 1032200 | tf_op jit(solution)/shard_map/ppermute | solution.py:519
  53.0 15.2 %collective-permute-start.2 = (f32[4,21,8,128]{3,2,1,0:T(8,128)S(1)}, f32[4,21,8,128]{3,2,1,0:T(8,128)S(1)}, u32[]{:S(2)}, u32[]{:S(2)}) collective-permute-start(f32[4,21,8,128]{3,2,1,0:T(8,128)S(1)} %get-tuple-element.21), channel_id=1, source_target_pairs={{0,3},{1,0},{2,1},{3,2},{4,7},{5,4},{6,5},{7,6},{8,11},{9,8},{10,9... | collective-permute-start | bytes 1032200 | tf_op jit(solution)/shard_map/ppermute | solution.py:519
  70.9 1.2 %copy-start = (f32[27,16,8,128]{3,2,1,0:T(8,128)}, f32[27,16,8,128]{3,2,1,0:T(8,128)S(1)}, u32[]{:S(2)}) copy-start(f32[27,16,8,128]{3,2,1,0:T(8,128)S(1)} %get-tuple-element.26.refs_4_) | copy-start | bytes 5308420
  72.1 10.6 %collective-permute-start.6 = (f32[9,2,8,128]{3,2,1,0:T(8,128)S(1)}, f32[9,2,8,128]{3,2,1,0:T(8,128)S(1)}, u32[]{:S(2)}, u32[]{:S(2)}) collective-permute-start(f32[9,2,8,128]{3,2,1,0:T(8,128)S(1)} %get-tuple-element.28), channel_id=1, source_target_pairs={{0,1},{1,2},{2,3},{3,0},{4,5},{5,6},{6,7},{7,4},{8,9},{9,10},{10,1... | collective-permute-start | bytes 221192 | tf_op jit(solution)/shard_map/ppermute | solution.py:519
  79.6 20.4 %collective-permute-start.3 = (f32[4,18,8,128]{3,2,1,0:T(8,128)S(1)}, f32[4,18,8,128]{3,2,1,0:T(8,128)S(1)}, u32[]{:S(2)}, u32[]{:S(2)}) collective-permute-start(f32[4,18,8,128]{3,2,1,0:T(8,128)S(1)} %get-tuple-element.23), channel_id=1, source_target_pairs={{0,1},{1,2},{2,3},{3,0},{4,5},{5,6},{6,7},{7,4},{8,9},{9,10},{10,1... | collective-permute-start | bytes 884744 | tf_op jit(solution)/shard_map/ppermute | solution.py:519
  79.7 20.3 %collective-permute-start.4 = (f32[4,18,8,128]{3,2,1,0:T(8,128)S(1)}, f32[4,18,8,128]{3,2,1,0:T(8,128)S(1)}, u32[]{:S(2)}, u32[]{:S(2)}) collective-permute-start(f32[4,18,8,128]{3,2,1,0:T(8,128)S(1)} %get-tuple-element.24), channel_id=1, source_target_pairs={{0,2},{1,3},{2,0},{3,1},{4,6},{5,7},{6,4},{7,5},{8,10},{9,11},{10,... | collective-permute-start | bytes 884744 | tf_op jit(solution)/shard_map/ppermute | solution.py:519
  81.3 18.7 %collective-permute-start.5 = (f32[4,18,8,128]{3,2,1,0:T(8,128)S(1)}, f32[4,18,8,128]{3,2,1,0:T(8,128)S(1)}, u32[]{:S(2)}, u32[]{:S(2)}) collective-permute-start(f32[4,18,8,128]{3,2,1,0:T(8,128)S(1)} %get-tuple-element.25), channel_id=1, source_target_pairs={{0,3},{1,0},{2,1},{3,2},{4,7},{5,4},{6,5},{7,6},{8,11},{9,8},{10,9... | collective-permute-start | bytes 884744 | tf_op jit(solution)/shard_map/ppermute | solution.py:519
  82.7 12.5 %collective-permute-start.7 = (f32[9,2,8,128]{3,2,1,0:T(8,128)S(1)}, f32[9,2,8,128]{3,2,1,0:T(8,128)S(1)}, u32[]{:S(2)}, u32[]{:S(2)}) collective-permute-start(f32[9,2,8,128]{3,2,1,0:T(8,128)S(1)} %get-tuple-element.29), channel_id=1, source_target_pairs={{0,3},{1,0},{2,1},{3,2},{4,7},{5,4},{6,5},{7,6},{8,11},{9,8},{10,9... | collective-permute-start | bytes 221192 | tf_op jit(solution)/shard_map/ppermute | solution.py:519
  95.2 8.3 %collective-permute-start.8 = (f32[24,8,128]{2,1,0:T(8,128)S(1)}, f32[24,8,128]{2,1,0:T(8,128)S(1)}, u32[]{:S(2)}, u32[]{:S(2)}) collective-permute-start(f32[24,8,128]{2,1,0:T(8,128)S(1)} %pad_maximum_fusion), channel_id=1, source_target_pairs={{0,4},{4,8},{8,12},{12,16},{16,20},{20,24},{24,28},{28,0},{1,5},{5... | collective-permute-start | bytes 294920 | tf_op jit(solution)/shard_map/ppermute | solution.py:519
  96.6 7.4 %collective-permute-start.9 = (f32[24,8,128]{2,1,0:T(8,128)S(1)}, f32[24,8,128]{2,1,0:T(8,128)S(1)}, u32[]{:S(2)}, u32[]{:S(2)}) collective-permute-start(f32[24,8,128]{2,1,0:T(8,128)S(1)} %pad_maximum_fusion.1), channel_id=1, source_target_pairs={{0,28},{4,0},{8,4},{12,8},{16,12},{20,16},{24,20},{28,24},{1,29},{... | collective-permute-start | bytes 294920 | tf_op jit(solution)/shard_map/ppermute | solution.py:519
  104.0 1.5 %copy-start.1 = (f32[27,16,8,128]{3,2,1,0:T(8,128)S(1)}, f32[27,16,8,128]{3,2,1,0:T(8,128)}, u32[]{:S(2)}) copy-start(f32[27,16,8,128]{3,2,1,0:T(8,128)} %copy-done) | copy-start | bytes 5308420

commit v4 on v3

--- a/solution.py
+++ b/solution.py
@@ -17,7 +17,7 @@
 WIDTH = EDGE // GROUPS
 CHUNKS = ((0, 3), (1, 2))
 SIDE_TILES = 3
-VMEM_LIMIT = 50 * 1024 * 1024
+VMEM_LIMIT = 20 * 1024 * 1024
 
 
 def velocity(q):
@@ -551,6 +551,7 @@
     up = jnp.concatenate([xhi.reshape(18, SUB, LANES), below[6:, 1], above[6:, 1]])
     down = jnp.concatenate([xlo.reshape(18, SUB, LANES), below[:3, 0], above[:3, 0]])
     xlo, xhi = shifted(up, "row", 1), shifted(down, "row", -1)
+    in_row[1], below, above = lax.optimization_barrier((in_row[1], below, above))
     homes = to_columns(1)
     return jnp.transpose(finish(tags, homes, early, xlo, xhi, below, above), (1, 0, 2))
 

time: 111 us -> 100 us (0.901)
  waiting for transfers between devices: 65.3 us -> 54.9 us
  Pallas kernels: 17.3 us -> 13.2 us
  starting transfers between devices: 22.7 us -> 24.2 us
  local copies, waits for them, and re-layouts: 4 us -> 5.41 us
    ppermute x10, waiting for transfers between devices: 29.7 us -> 20.1 us  [shifted(): lax.ppermute(value, axis, [(i, (i + step) % count) for i in range(count)])]
    pallas_call x2, Pallas kernels: 8.14 us -> 3.19 us  [pre(): pl.pallas_call(functools.partial(pre_kernel, cap, per_row, part), grid_sp...]
    ppermute x10, starting transfers between devices: 11.7 us -> 13.2 us  [shifted(): lax.ppermute(value, axis, [(i, (i + step) % count) for i in range(count)])]
    unnamed x12 -> x16, local copies, waits for them, and re-layouts: 3.99 us -> 5.4 us
  transfers between devices with their start and end apart: 12 -> 12, of which waited for: 8 -> 8; matrix products, arithmetic and copies ran while one was open for 1% -> 2% of each run, Pallas kernels for 7% -> 5%
where the time goes in v4:
time: 100 us; the launch traced here: 99.8 us
  waiting for transfers between devices  54.9 us (55%)
  starting transfers between devices  24.2 us (24%)
  Pallas kernels  13.2 us (13%)
  local copies, waits for them, and re-layouts  5.41 us (5%)
  other arithmetic  1.98 us (2%)
    all_to_all x2, waiting for transfers between devices, on_device(): lax.all_to_all(pre(ordered, destination, refinement, part, row_count, cap...  34.8 us
    ppermute x10, waiting for transfers between devices, shifted(): lax.ppermute(value, axis, [(i, (i + step) % count) for i in range(count)])  20.1 us
    ppermute x10, starting transfers between devices, shifted(): lax.ppermute(value, axis, [(i, (i + step) % count) for i in range(count)])  13.2 us
    all_to_all x2, starting transfers between devices, on_device(): lax.all_to_all(pre(ordered, destination, refinement, part, row_count, cap...  11 us
    unnamed x16, local copies, waits for them, and re-layouts  5.4 us
    pallas_call x1, Pallas kernels, finish(): pl.pallas_call(functools.partial(finish_kernel, len(homes)), grid_spec=pl...  5.06 us
    pallas_call x2, Pallas kernels, pre(): pl.pallas_call(functools.partial(pre_kernel, cap, per_row, part), grid_sp...  3.19 us
    pallas_call x1, Pallas kernels, post(): pl.pallas_call(functools.partial(post_kernel, len(homes)), grid_spec=pltp...  2.48 us
  transfers between devices with their start and end apart: 12, of which 8 were waited for; matrix products, arithmetic and copies ran while one was open for 2% of the time, Pallas kernels for 5%

profile of v4, /device:TPU:0, one launch (start us, length us, event | category | flops | bytes accessed | tf_op | source)
XLA Modules:
  0.0 99.8 jit_solution(17075053187564609131)
XLA Ops:
  0.0 2.0 %copy-done = f32[8,27,4096]{2,0,1:T(8,128)S(1)} copy-done((f32[8,27,4096]{2,0,1:T(8,128)S(1)}, f32[8,27,4096]{2,0,1:T(8,128)}, u32[]{:S(2)}) %copy-start) | copy-done | bytes 3538968
  2.0 0.7 copy-done.4
  2.7 0.7 copy-done.6
  3.3 2.1 %pre_0.1 = f32[16,21,8,128]{3,2,1,0:T(8,128)S(1)} custom-call(s32[8]{0:T(128)S(1)} %copy-done.4, s32[8]{0:T(128)S(1)} %copy-done.6, f32[27,8,4096]{2,1,0:T(8,128)S(1)} %bitcast.12), custom_call_target="tpu_custom_call" | custom-call | flops 10000000 | bytes 4000000 | tf_op jit(solution)/shard_map/pre_0/pallas_call | solution.py:171
  5.5 1.1 %copy-done.2 = f32[16,21,8,128]{3,2,1,0:T(8,128)} copy-done((f32[16,21,8,128]{3,2,1,0:T(8,128)}, f32[16,21,8,128]{3,2,1,0:T(8,128)S(1)}, u32[]{:S(2)}) %copy-start.2) | copy-done | bytes 1376280
  6.5 7.4 %all-to-all-start = ((f32[16,21,8,128]{3,2,1,0:T(8,128)}), f32[16,21,8,128]{3,2,1,0:T(8,128)}, u32[]{:S(2)}, u32[]{:S(2)}) async-start(f32[16,21,8,128]{3,2,1,0:T(8,128)} %copy-done.2), calls=%async_computation | async-start | bytes 2752512 | tf_op jit(solution)/shard_map/all_to_all | solution.py:534
  13.9 1.1 %pre_1.1 = f32[16,18,8,128]{3,2,1,0:T(8,128)S(1)} custom-call(s32[8]{0:T(128)S(1)} %copy-done.5, s32[8]{0:T(128)S(1)} %copy-done.7, f32[27,8,4096]{2,1,0:T(8,128)S(1)} %bitcast.13), custom_call_target="tpu_custom_call" | custom-call | flops 10000000 | bytes 4000000 | tf_op jit(solution)/shard_map/pre_1/pallas_call | solution.py:171
  15.0 1.0 %copy-done.3 = f32[16,18,8,128]{3,2,1,0:T(8,128)} copy-done((f32[16,18,8,128]{3,2,1,0:T(8,128)}, f32[16,18,8,128]{3,2,1,0:T(8,128)S(1)}, u32[]{:S(2)}) %copy-start.3) | copy-done | bytes 1179672
  16.0 30.8 %all-to-all-done.in_ref = f32[16,21,8,128]{3,2,1,0:T(8,128)} async-done(((f32[16,21,8,128]{3,2,1,0:T(8,128)}), f32[16,21,8,128]{3,2,1,0:T(8,128)}, u32[]{:S(2)}, u32[]{:S(2)}) %all-to-all-start) | async-done | bytes 1376288 | tf_op jit(solution)/shard_map/all_to_all | solution.py:534
  46.8 3.6 %all-to-all-start.1 = ((f32[16,18,8,128]{3,2,1,0:T(8,128)}), f32[16,18,8,128]{3,2,1,0:T(8,128)S(1)}, u32[]{:S(2)}, u32[]{:S(2)}) async-start(f32[16,18,8,128]{3,2,1,0:T(8,128)} %copy-done.3), calls=%async_computation.1 | async-start | bytes 2359296 | tf_op jit(solution)/shard_map/all_to_all | solution.py:534
  50.5 1.2 %fusion = s32[16]{0:T(128)S(1)} fusion(f32[16,21,8,128]{3,2,1,0:T(8,128)} %all-to-all-done.in_ref), kind=kLoop, calls=%fused_computation.7 | loop fusion | flops 16 | bytes 128 | tf_op jit(solution)/shard_map/convert_element_type | solution.py:523
  51.7 1.7 %repack_0.1 = (f32[4,21,8,128]{3,2,1,0:T(8,128)S(1)}, f32[4,21,8,128]{3,2,1,0:T(8,128)S(1)}, f32[4,21,8,128]{3,2,1,0:T(8,128)S(1)}, f32[4,21,8,128]{3,2,1,0:T(8,128)S(1)}) custom-call(s32[16]{0:T(128)S(1)} %compare_select_fusion.2.away_ref, f32[16,21,8,128]{3,2,1,0:T(8,128)} %all-to-all-done.in_ref), custom_call_target="tpu_custom_call" | custom-call | bytes 3000000 | tf_op jit(solution)/shard_map/repack_0/pallas_call | solution.py:219
  53.4 1.6 %collective-permute-start.1 = (f32[4,21,8,128]{3,2,1,0:T(8,128)S(1)}, f32[4,21,8,128]{3,2,1,0:T(8,128)S(1)}, u32[]{:S(2)}, u32[]{:S(2)}) collective-permute-start(f32[4,21,8,128]{3,2,1,0:T(8,128)S(1)} %get-tuple-element.23), channel_id=1, source_target_pairs={{0,2},{1,3},{2,0},{3,1},{4,6},{5,7},{6,4},{7,5},{8,10},{9,11},{10,... | collective-permute-start | bytes 1032200 | tf_op jit(solution)/shard_map/ppermute | solution.py:519
  55.0 1.4 %collective-permute-start.2 = (f32[4,21,8,128]{3,2,1,0:T(8,128)S(1)}, f32[4,21,8,128]{3,2,1,0:T(8,128)S(1)}, u32[]{:S(2)}, u32[]{:S(2)}) collective-permute-start(f32[4,21,8,128]{3,2,1,0:T(8,128)S(1)} %get-tuple-element.24), channel_id=1, source_target_pairs={{0,3},{1,0},{2,1},{3,2},{4,7},{5,4},{6,5},{7,6},{8,11},{9,8},{10,9... | collective-permute-start | bytes 1032200 | tf_op jit(solution)/shard_map/ppermute | solution.py:519
  56.4 0.2 convert_reduce_fusion
  56.6 6.6 %collective-permute-done.refs_1_ = f32[4,21,8,128]{3,2,1,0:T(8,128)S(1)} collective-permute-done((f32[4,21,8,128]{3,2,1,0:T(8,128)S(1)}, f32[4,21,8,128]{3,2,1,0:T(8,128)S(1)}, u32[]{:S(2)}, u32[]{:S(2)}) %collective-permute-start) | collective-permute-done | bytes 344096 | tf_op jit(solution)/shard_map/ppermute | solution.py:519
  63.2 0.2 fusion.3
  63.3 1.0 %collective-permute-done.1.refs_2_ = f32[4,21,8,128]{3,2,1,0:T(8,128)S(1)} collective-permute-done((f32[4,21,8,128]{3,2,1,0:T(8,128)S(1)}, f32[4,21,8,128]{3,2,1,0:T(8,128)S(1)}, u32[]{:S(2)}, u32[]{:S(2)}) %collective-permute-start.1) | collective-permute-done | bytes 344096 | tf_op jit(solution)/shard_map/ppermute | solution.py:519
  64.4 0.2 fusion.2
  64.6 5.6 %collective-permute-done.2.refs_3_ = f32[4,21,8,128]{3,2,1,0:T(8,128)S(1)} collective-permute-done((f32[4,21,8,128]{3,2,1,0:T(8,128)S(1)}, f32[4,21,8,128]{3,2,1,0:T(8,128)S(1)}, u32[]{:S(2)}, u32[]{:S(2)}) %collective-permute-start.2) | collective-permute-done | bytes 344096 | tf_op jit(solution)/shard_map/ppermute | solution.py:519
  70.4 2.5 %post.1 = (f32[27,16,8,128]{3,2,1,0:T(8,128)S(1)}, f32[9,2,8,128]{3,2,1,0:T(8,128)S(1)}, f32[9,2,8,128]{3,2,1,0:T(8,128)S(1)}, f32[9,2,8,128]{3,2,1,0:T(8,128)S(1)}, f32[9,2,8,128]{3,2,1,0:T(8,128)S(1)}) custom-call(s32[16]{0:T(128)S(1)} %pad_add_fusion.tags_ref, f32[4,21,8,128]{3,2,1,0:T(8,128)S(1)} %get-tuple-element.21.refs_0_, ...), custom_call_target="tpu_custom_call" | custom-call | flops 10000000 | bytes 3000000 | tf_op jit(solution)/shard_map/post/pallas_call | solution.py:373
  72.9 1.1 %collective-permute-start.3 = (f32[9,2,8,128]{3,2,1,0:T(8,128)S(1)}, f32[9,2,8,128]{3,2,1,0:T(8,128)S(1)}, u32[]{:S(2)}, u32[]{:S(2)}) collective-permute-start(f32[9,2,8,128]{3,2,1,0:T(8,128)S(1)} %get-tuple-element.25), channel_id=1, source_target_pairs={{0,1},{1,2},{2,3},{3,0},{4,5},{5,6},{6,7},{7,4},{8,9},{9,10},{10,1... | collective-permute-start | bytes 221192 | tf_op jit(solution)/shard_map/ppermute | solution.py:519
  74.1 1.2 %collective-permute-start.4 = (f32[9,2,8,128]{3,2,1,0:T(8,128)S(1)}, f32[9,2,8,128]{3,2,1,0:T(8,128)S(1)}, u32[]{:S(2)}, u32[]{:S(2)}) collective-permute-start(f32[9,2,8,128]{3,2,1,0:T(8,128)S(1)} %get-tuple-element.26), channel_id=1, source_target_pairs={{0,3},{1,0},{2,1},{3,2},{4,7},{5,4},{6,5},{7,6},{8,11},{9,8},{10,9... | collective-permute-start | bytes 221192 | tf_op jit(solution)/shard_map/ppermute | solution.py:519
  75.2 4.0 %all-to-all-done.1.in_ref = f32[16,18,8,128]{3,2,1,0:T(8,128)S(1)} async-done(((f32[16,18,8,128]{3,2,1,0:T(8,128)}), f32[16,18,8,128]{3,2,1,0:T(8,128)S(1)}, u32[]{:S(2)}, u32[]{:S(2)}) %all-to-all-start.1) | async-done | bytes 1179680 | tf_op jit(solution)/shard_map/all_to_all | solution.py:534
  79.2 0.8 repack_1.1
  80.1 1.6 %collective-permute-start.6 = (f32[4,18,8,128]{3,2,1,0:T(8,128)S(1)}, f32[4,18,8,128]{3,2,1,0:T(8,128)S(1)}, u32[]{:S(2)}, u32[]{:S(2)}) collective-permute-start(f32[4,18,8,128]{3,2,1,0:T(8,128)S(1)} %get-tuple-element.30), channel_id=1, source_target_pairs={{0,2},{1,3},{2,0},{3,1},{4,6},{5,7},{6,4},{7,5},{8,10},{9,11},{10,... | collective-permute-start | bytes 884744 | tf_op jit(solution)/shard_map/ppermute | solution.py:519
  81.7 1.4 %collective-permute-start.7 = (f32[4,18,8,128]{3,2,1,0:T(8,128)S(1)}, f32[4,18,8,128]{3,2,1,0:T(8,128)S(1)}, u32[]{:S(2)}, u32[]{:S(2)}) collective-permute-start(f32[4,18,8,128]{3,2,1,0:T(8,128)S(1)} %get-tuple-element.31), channel_id=1, source_target_pairs={{0,3},{1,0},{2,1},{3,2},{4,7},{5,4},{6,5},{7,6},{8,11},{9,8},{10,9... | collective-permute-start | bytes 884744 | tf_op jit(solution)/shard_map/ppermute | solution.py:519
  83.1 1.5 %collective-permute-start.8 = (f32[24,8,128]{2,1,0:T(8,128)S(1)}, f32[24,8,128]{2,1,0:T(8,128)S(1)}, u32[]{:S(2)}, u32[]{:S(2)}) collective-permute-start(f32[24,8,128]{2,1,0:T(8,128)S(1)} %pad_maximum_fusion), channel_id=1, source_target_pairs={{0,4},{4,8},{8,12},{12,16},{16,20},{20,24},{24,28},{28,0},{1,5},{5... | collective-permute-start | bytes 294920 | tf_op jit(solution)/shard_map/ppermute | solution.py:519
  84.5 3.4 %collective-permute-start.9 = (f32[24,8,128]{2,1,0:T(8,128)S(1)}, f32[24,8,128]{2,1,0:T(8,128)S(1)}, u32[]{:S(2)}, u32[]{:S(2)}) collective-permute-start(f32[24,8,128]{2,1,0:T(8,128)S(1)} %pad_maximum_fusion.1), channel_id=1, source_target_pairs={{0,28},{4,0},{8,4},{12,8},{16,12},{20,16},{24,20},{28,24},{1,29},{... | collective-permute-start | bytes 294920 | tf_op jit(solution)/shard_map/ppermute | solution.py:519
  87.9 2.6 %collective-permute-done.8.refs_5_ = f32[24,8,128]{2,1,0:T(8,128)S(1)} collective-permute-done((f32[24,8,128]{2,1,0:T(8,128)S(1)}, f32[24,8,128]{2,1,0:T(8,128)S(1)}, u32[]{:S(2)}, u32[]{:S(2)}) %collective-permute-start.8) | collective-permute-done | bytes 98336 | tf_op jit(solution)/shard_map/ppermute | solution.py:519
  90.7 4.0 %collective-permute-done.7.refs_3_ = f32[4,18,8,128]{3,2,1,0:T(8,128)S(1)} collective-permute-done((f32[4,18,8,128]{3,2,1,0:T(8,128)S(1)}, f32[4,18,8,128]{3,2,1,0:T(8,128)S(1)}, u32[]{:S(2)}, u32[]{:S(2)}) %collective-permute-start.7) | collective-permute-done | bytes 294944 | tf_op jit(solution)/shard_map/ppermute | solution.py:519
  94.7 5.1 %finish.1 = f32[27,8,4096]{2,1,0:T(8,128)} custom-call(s32[16]{0:T(128)S(1)} %pad_add_fusion.tags_ref, f32[4,18,8,128]{3,2,1,0:T(8,128)S(1)} %get-tuple-element.28.refs_0_, f32[4,18,8,128]{3,2,1,0:T(8,128)S(1)} %collective-permute-done.5.refs_1_, f32[4,18,8,128]{3,2,1,0:T(8,128)S(1)} %collective-permute-done.6.refs_2_, ...), custom_call_target="tpu_custom_call" | custom-call | flops 10000000 | bytes 8000000 | tf_op jit(solution)/shard_map/finish/pallas_call | solution.py:492
  (25 shorter events, 0.6 us)
Async XLA Ops:
  0.0 2.0 %copy-start = (f32[8,27,4096]{2,0,1:T(8,128)S(1)}, f32[8,27,4096]{2,0,1:T(8,128)}, u32[]{:S(2)}) copy-start(f32[8,27,4096]{2,0,1:T(8,128)} %param.3) | copy-start | bytes 10616836
  2.0 0.7 copy-start.4
  2.7 0.7 copy-start.6
  3.3 10.6 %copy-start.1 = (f32[8,27,4096]{2,0,1:T(8,128)S(1)}, f32[8,27,4096]{2,0,1:T(8,128)}, u32[]{:S(2)}) copy-start(f32[8,27,4096]{2,0,1:T(8,128)} %param.3) | copy-start | bytes 10616836
  5.5 1.1 %copy-start.2 = (f32[16,21,8,128]{3,2,1,0:T(8,128)}, f32[16,21,8,128]{3,2,1,0:T(8,128)S(1)}, u32[]{:S(2)}) copy-start(f32[16,21,8,128]{3,2,1,0:T(8,128)S(1)} %pre_0.1) | copy-start | bytes 4128772
  6.5 7.4 %copy-start.5 = (s32[8]{0:T(128)S(1)}, s32[8]{0:T(128)}, u32[]{:S(2)}) copy-start(s32[8]{0:T(128)} %dest_ref.3) | copy-start | bytes 100
  6.5 7.4 %copy-start.7 = (s32[8]{0:T(128)S(1)}, s32[8]{0:T(128)}, u32[]{:S(2)}) copy-start(s32[8]{0:T(128)} %level_ref.3) | copy-start | bytes 100
  6.5 40.3 %all-to-all-start = ((f32[16,21,8,128]{3,2,1,0:T(8,128)}), f32[16,21,8,128]{3,2,1,0:T(8,128)}, u32[]{:S(2)}, u32[]{:S(2)}) async-start(f32[16,21,8,128]{3,2,1,0:T(8,128)} %copy-done.2), calls=%async_computation | async-start | bytes 2752512 | tf_op jit(solution)/shard_map/all_to_all | solution.py:534
  15.0 1.0 %copy-start.3 = (f32[16,18,8,128]{3,2,1,0:T(8,128)}, f32[16,18,8,128]{3,2,1,0:T(8,128)S(1)}, u32[]{:S(2)}) copy-start(f32[16,18,8,128]{3,2,1,0:T(8,128)S(1)} %pre_1.1) | copy-start | bytes 3538948
  46.8 32.4 %all-to-all-start.1 = ((f32[16,18,8,128]{3,2,1,0:T(8,128)}), f32[16,18,8,128]{3,2,1,0:T(8,128)S(1)}, u32[]{:S(2)}, u32[]{:S(2)}) async-start(f32[16,18,8,128]{3,2,1,0:T(8,128)} %copy-done.3), calls=%async_computation.1 | async-start | bytes 2359296 | tf_op jit(solution)/shard_map/all_to_all | solution.py:534
  53.4 9.8 %collective-permute-start = (f32[4,21,8,128]{3,2,1,0:T(8,128)S(1)}, f32[4,21,8,128]{3,2,1,0:T(8,128)S(1)}, u32[]{:S(2)}, u32[]{:S(2)}) collective-permute-start(f32[4,21,8,128]{3,2,1,0:T(8,128)S(1)} %get-tuple-element.22), channel_id=1, source_target_pairs={{0,1},{1,2},{2,3},{3,0},{4,5},{5,6},{6,7},{7,4},{8,9},{9,10},{10,1... | collective-permute-start | bytes 1032200 | tf_op jit(solution)/shard_map/ppermute | solution.py:519
  53.4 11.0 %collective-permute-start.1 = (f32[4,21,8,128]{3,2,1,0:T(8,128)S(1)}, f32[4,21,8,128]{3,2,1,0:T(8,128)S(1)}, u32[]{:S(2)}, u32[]{:S(2)}) collective-permute-start(f32[4,21,8,128]{3,2,1,0:T(8,128)S(1)} %get-tuple-element.23), channel_id=1, source_target_pairs={{0,2},{1,3},{2,0},{3,1},{4,6},{5,7},{6,4},{7,5},{8,10},{9,11},{10,... | collective-permute-start | bytes 1032200 | tf_op jit(solution)/shard_map/ppermute | solution.py:519
  55.0 15.2 %collective-permute-start.2 = (f32[4,21,8,128]{3,2,1,0:T(8,128)S(1)}, f32[4,21,8,128]{3,2,1,0:T(8,128)S(1)}, u32[]{:S(2)}, u32[]{:S(2)}) collective-permute-start(f32[4,21,8,128]{3,2,1,0:T(8,128)S(1)} %get-tuple-element.24), channel_id=1, source_target_pairs={{0,3},{1,0},{2,1},{3,2},{4,7},{5,4},{6,5},{7,6},{8,11},{9,8},{10,9... | collective-permute-start | bytes 1032200 | tf_op jit(solution)/shard_map/ppermute | solution.py:519
  72.9 6.3 %collective-permute-start.3 = (f32[9,2,8,128]{3,2,1,0:T(8,128)S(1)}, f32[9,2,8,128]{3,2,1,0:T(8,128)S(1)}, u32[]{:S(2)}, u32[]{:S(2)}) collective-permute-start(f32[9,2,8,128]{3,2,1,0:T(8,128)S(1)} %get-tuple-element.25), channel_id=1, source_target_pairs={{0,1},{1,2},{2,3},{3,0},{4,5},{5,6},{6,7},{7,4},{8,9},{9,10},{10,1... | collective-permute-start | bytes 221192 | tf_op jit(solution)/shard_map/ppermute | solution.py:519
  74.1 5.2 %collective-permute-start.4 = (f32[9,2,8,128]{3,2,1,0:T(8,128)S(1)}, f32[9,2,8,128]{3,2,1,0:T(8,128)S(1)}, u32[]{:S(2)}, u32[]{:S(2)}) collective-permute-start(f32[9,2,8,128]{3,2,1,0:T(8,128)S(1)} %get-tuple-element.26), channel_id=1, source_target_pairs={{0,3},{1,0},{2,1},{3,2},{4,7},{5,4},{6,5},{7,6},{8,11},{9,8},{10,9... | collective-permute-start | bytes 221192 | tf_op jit(solution)/shard_map/ppermute | solution.py:519
  80.0 10.7 %collective-permute-start.5 = (f32[4,18,8,128]{3,2,1,0:T(8,128)S(1)}, f32[4,18,8,128]{3,2,1,0:T(8,128)S(1)}, u32[]{:S(2)}, u32[]{:S(2)}) collective-permute-start(f32[4,18,8,128]{3,2,1,0:T(8,128)S(1)} %get-tuple-element.29), channel_id=1, source_target_pairs={{0,1},{1,2},{2,3},{3,0},{4,5},{5,6},{6,7},{7,4},{8,9},{9,10},{10,1... | collective-permute-start | bytes 884744 | tf_op jit(solution)/shard_map/ppermute | solution.py:519
  80.1 10.6 %collective-permute-start.6 = (f32[4,18,8,128]{3,2,1,0:T(8,128)S(1)}, f32[4,18,8,128]{3,2,1,0:T(8,128)S(1)}, u32[]{:S(2)}, u32[]{:S(2)}) collective-permute-start(f32[4,18,8,128]{3,2,1,0:T(8,128)S(1)} %get-tuple-element.30), channel_id=1, source_target_pairs={{0,2},{1,3},{2,0},{3,1},{4,6},{5,7},{6,4},{7,5},{8,10},{9,11},{10,... | collective-permute-start | bytes 884744 | tf_op jit(solution)/shard_map/ppermute | solution.py:519
  81.7 13.1 %collective-permute-start.7 = (f32[4,18,8,128]{3,2,1,0:T(8,128)S(1)}, f32[4,18,8,128]{3,2,1,0:T(8,128)S(1)}, u32[]{:S(2)}, u32[]{:S(2)}) collective-permute-start(f32[4,18,8,128]{3,2,1,0:T(8,128)S(1)} %get-tuple-element.31), channel_id=1, source_target_pairs={{0,3},{1,0},{2,1},{3,2},{4,7},{5,4},{6,5},{7,6},{8,11},{9,8},{10,9... | collective-permute-start | bytes 884744 | tf_op jit(solution)/shard_map/ppermute | solution.py:519
  83.1 7.5 %collective-permute-start.8 = (f32[24,8,128]{2,1,0:T(8,128)S(1)}, f32[24,8,128]{2,1,0:T(8,128)S(1)}, u32[]{:S(2)}, u32[]{:S(2)}) collective-permute-start(f32[24,8,128]{2,1,0:T(8,128)S(1)} %pad_maximum_fusion), channel_id=1, source_target_pairs={{0,4},{4,8},{8,12},{12,16},{16,20},{20,24},{24,28},{28,0},{1,5},{5... | collective-permute-start | bytes 294920 | tf_op jit(solution)/shard_map/ppermute | solution.py:519
  84.5 6.1 %collective-permute-start.9 = (f32[24,8,128]{2,1,0:T(8,128)S(1)}, f32[24,8,128]{2,1,0:T(8,128)S(1)}, u32[]{:S(2)}, u32[]{:S(2)}) collective-permute-start(f32[24,8,128]{2,1,0:T(8,128)S(1)} %pad_maximum_fusion.1), channel_id=1, source_target_pairs={{0,28},{4,0},{8,4},{12,8},{16,12},{20,16},{24,20},{28,24},{1,29},{... | collective-permute-start | bytes 294920 | tf_op jit(solution)/shard_map/ppermute | solution.py:519

commit v5 on v4

--- a/solution.py
+++ b/solution.py
@@ -17,7 +17,10 @@
 WIDTH = EDGE // GROUPS
 CHUNKS = ((0, 3), (1, 2))
 SIDE_TILES = 3
+START_AFTER = 1
+TAG_ROW = 2 * NFIELD - (SIDE_TILES - 1) * SUB
 VMEM_LIMIT = 20 * 1024 * 1024
+PRE_VMEM_LIMIT = 60 * 1024 * 1024
 
 
 def velocity(q):
@@ -26,6 +29,33 @@
 
 def tiles_of(part):
     return len(CHUNKS[part]) * NFIELD + (0 if part else SIDE_TILES)
+
+
+def step_to(target, here, count):
+    if count & (count - 1) == 0:
+        return target ^ here
+    return lax.rem(target - here + count, count)
+
+
+def origin_of(step, here, count):
+    if count & (count - 1) == 0:
+        return here ^ step
+    return lax.rem(here - step + count, count)
+
+
+def issue_order(count):
+    near = list(range(1, count // 2))
+    far = list(range(count - 1, count // 2 - 1, -1))
+    return near[:2] + far + near[2:] + [0]
+
+
+def exchanged(value, axis, step):
+    count = lax.axis_size(axis)
+    if count & (count - 1) == 0:
+        pairs = [(i, i ^ step) for i in range(count)]
+    else:
+        pairs = [(i, (i + step) % count) for i in range(count)]
+    return lax.ppermute(value, axis, pairs)
 
 
 def raw_moments(f):
@@ -73,162 +103,227 @@
     )
 
 
-def pre_kernel(cap, per_row, part, dest_ref, level_ref, x_ref, out_ref, swap_ref, *more):
-    g = pl.program_id(0)
+def pre_kernel(cap, row_count, per_row, part, dest_hbm, level_hbm, x_hbm, *refs):
+    outs = refs[:-8]
+    x_ref, swap_ref, packed_ref, side_ref, dest_ref, level_ref, source_ref, sems = refs[-8:]
+    order = CHUNKS[1] if part else CHUNKS[0] + CHUNKS[1]
     steps = len(CHUNKS[part])
-    blocks = x_ref.shape[1]
-    chunks = x_ref.shape[2] // LANES
+    blocks = x_ref.shape[2]
+    cells = x_ref.shape[3]
+    chunks = cells // LANES
+    small = [
+        pltpu.make_async_copy(dest_hbm, dest_ref, sems.at[0]),
+        pltpu.make_async_copy(level_hbm, level_ref, sems.at[1]),
+    ]
+    large = [
+        pltpu.make_async_copy(
+            x_hbm.at[:, :, pl.ds(group * cells, cells)], x_ref.at[step], sems.at[2 + step]
+        )
+        for step, group in enumerate(order)
+    ]
+    for copy in small + large:
+        copy.start()
+    for copy in small:
+        copy.wait()
+
     which = lax.broadcasted_iota(jnp.int32, (SUB, LANES), 0)
     spot = lax.broadcasted_iota(jnp.int32, (SUB, LANES), 1) // EDGE
     scale = jnp.zeros((SUB, LANES), jnp.int32)
+    tag = jnp.zeros((SUB, LANES), jnp.int32)
     for t in range(blocks):
         scale = jnp.where(which == t, jnp.left_shift(1, level_ref[t]), scale)
+        tag = jnp.where(which == t, dest_ref[t], tag)
     rate = 1.0 / (3.0 * VISCOSITY * scale.astype(jnp.float32) + 0.5)
     keep = 1.0 - rate
+
+    here = lax.axis_index("row")
+    for e in range(row_count * cap):
+        source_ref[e] = -1
     rows = [dest_ref[t] // per_row for t in range(blocks)]
-    slots = []
     for t in range(blocks):
-        slot = rows[t] * cap
+        e = (rows[t] if part else step_to(rows[t], here, row_count)) * cap
         for other in range(t):
-            slot = slot + jnp.where(rows[other] == rows[t], 1, 0)
-        slots.append(slot)
-
-    def full():
-        for c in range(chunks):
-            fields = collided([x_ref[q, :, c * LANES : (c + 1) * LANES] for q in range(NQ)], keep)
-            for n, field in enumerate(fields):
-                base = (n * chunks + c) * SUB
-                swap_ref[base : base + SUB, :] = field
-        for t in range(blocks):
-            for n in range(NFIELD):
-                moved = swap_ref[pl.ds(n * chunks * SUB + t, SUB, stride=SUB), :]
-                out_ref[slots[t], g * NFIELD + n] = moved
-
-    if part == 1:
-        full()
-        return
-    pl.when(g < steps)(full)
-    packed_ref, side_ref = more
-
-    def pack(step):
-        first_x = CHUNKS[1][step] * WIDTH
+            e = e + jnp.where(rows[other] == rows[t], 1, 0)
+        source_ref[e] = t
+
+    def spread(ref, first, count):
+        for e in range(row_count * cap):
+            t = source_ref[e]
+
+            @pl.when(t >= 0)
+            def _():
+                for n in range(count):
+                    moved = ref[pl.ds(n * SUB * SUB + t, SUB, stride=SUB), :]
+                    if part:
+                        outs[0][e, first + n] = moved
+                    else:
+                        outs[e // cap][e % cap, first + n] = moved
+
+    for step, group in enumerate(order):
+        large[step].wait()
+        if step < steps:
+            for c in range(chunks):
+                fields = collided(
+                    [x_ref[step, q, :, c * LANES : (c + 1) * LANES] for q in range(NQ)], keep
+                )
+                for n, field in enumerate(fields):
+                    base = (n * chunks + c) * SUB
+                    swap_ref[base : base + SUB, :] = field
+            spread(swap_ref, step * NFIELD, NFIELD)
+            continue
         for q in range(NQ):
             for half in range(2):
-                value = packed_ref[half * NQ + q] if step else None
+                value = packed_ref[half * NQ + q] if step > steps else None
                 for x in range(WIDTH):
                     c = x * 2 + half
-                    at = (first_x + x) % SUB
-                    moved = x_ref[q, :, c * LANES : (c + 1) * LANES]
+                    at = (group * WIDTH + x) % SUB
+                    moved = x_ref[step, q, :, c * LANES : (c + 1) * LANES]
                     turn = (at + half) * EDGE % LANES
                     if turn:
                         moved = pltpu.roll(moved, turn, axis=1)
                     value = moved if value is None else jnp.where(spot == at, moved, value)
                 packed_ref[half * NQ + q] = value
 
-    for step in range(len(CHUNKS[1])):
-        pl.when(g == steps + step)(functools.partial(pack, step))
-
-    @pl.when(g == pl.num_programs(0) - 1)
-    def _():
-        tag = jnp.zeros((SUB, LANES), jnp.int32)
-        for t in range(blocks):
-            tag = jnp.where(which == t, dest_ref[t], tag)
-        tag = tag.astype(jnp.float32)
+    if part == 0:
         for half in range(2):
             fields = collided([packed_ref[half * NQ + q] for q in range(NQ)], keep)
             for n, field in enumerate(fields):
                 base = (half * NFIELD + n) * SUB
                 side_ref[base : base + SUB, :] = field
         for row in range(2 * NFIELD, SIDE_TILES * SUB):
-            side_ref[row * SUB : (row + 1) * SUB, :] = tag
-        first = steps * NFIELD
-        for slot in range(out_ref.shape[0]):
-            out_ref[slot, first + SIDE_TILES - 1] = jnp.full((SUB, LANES), -1.0, jnp.float32)
-        for t in range(blocks):
-            for tile in range(SIDE_TILES):
-                moved = side_ref[pl.ds(tile * SUB * SUB + t, SUB, stride=SUB), :]
-                out_ref[slots[t], first + tile] = moved
+            side_ref[row * SUB : (row + 1) * SUB, :] = tag.astype(jnp.float32)
+        for out in outs:
+            for k in range(cap):
+                out[k, tiles_of(0) - 1] = jnp.full((SUB, LANES), -1.0, jnp.float32)
+        spread(side_ref, steps * NFIELD, SIDE_TILES)
 
 
 def pre(populations, destination, refinement, part, row_count, cap, per_row):
     blocks = populations.shape[1]
     cells = populations.shape[2] // GROUPS
-    order = CHUNKS[1] if part else CHUNKS[0] + CHUNKS[1]
-    shape = (row_count * cap, tiles_of(part), SUB, LANES)
-
-    def place(g, *_):
-        index = order[-1]
-        for step in range(len(order) - 1):
-            index = jnp.where(g == step, order[step], index)
-        return (0, 0, index)
-
-    scratch = [pltpu.VMEM((NFIELD * cells // LANES * SUB, LANES), jnp.float32)]
-    if part == 0:
-        scratch += [
+    loaded = len(CHUNKS[part]) + (0 if part else len(CHUNKS[1]))
+    arrays = 1 if part else row_count
+    slots = row_count * cap // arrays
+    out = jax.ShapeDtypeStruct((slots, tiles_of(part), SUB, LANES), jnp.float32)
+    return pl.pallas_call(
+        functools.partial(pre_kernel, cap, row_count, per_row, part),
+        in_specs=[pl.BlockSpec(memory_space=pltpu.HBM)] * 3,
+        out_specs=[pl.BlockSpec(memory_space=pltpu.VMEM)] * arrays,
+        out_shape=[out] * arrays,
+        scratch_shapes=[
+            pltpu.VMEM((loaded, NQ, blocks, cells), jnp.float32),
+            pltpu.VMEM((NFIELD * cells // LANES * SUB, LANES), jnp.float32),
             pltpu.VMEM((2 * NQ, SUB, LANES), jnp.float32),
             pltpu.VMEM((SIDE_TILES * SUB * SUB, LANES), jnp.float32),
-        ]
-    return pl.pallas_call(
-        functools.partial(pre_kernel, cap, per_row, part),
-        grid_spec=pltpu.PrefetchScalarGridSpec(
-            num_scalar_prefetch=2,
-            grid=(len(order),),
-            in_specs=[pl.BlockSpec((NQ, blocks, cells), place)],
-            out_specs=pl.BlockSpec(shape, lambda g, *_: (0, 0, 0, 0)),
-            scratch_shapes=scratch,
-        ),
-        out_shape=jax.ShapeDtypeStruct(shape, jnp.float32),
-        compiler_params=pltpu.CompilerParams(vmem_limit_bytes=VMEM_LIMIT),
+            pltpu.SMEM((blocks,), jnp.int32),
+            pltpu.SMEM((blocks,), jnp.int32),
+            pltpu.SMEM((row_count * cap,), jnp.int32),
+            pltpu.SemaphoreType.DMA((2 + loaded,)),
+        ],
+        compiler_params=pltpu.CompilerParams(vmem_limit_bytes=PRE_VMEM_LIMIT),
         cost_estimate=pl.CostEstimate(flops=10**7, bytes_accessed=4 * 10**6, transcendentals=0),
         name="pre_%d" % part,
     )(destination, refinement, populations)
 
 
-def repack_kernel(cap, col_count, tagged, away_ref, in_ref, *refs):
-    outs, (source_ref, count_ref) = refs[:col_count], refs[col_count:]
-    for d in range(col_count):
-        count_ref[d] = 0
-        for k in range(cap):
-            source_ref[d * cap + k] = -1
-    for slot in range(in_ref.shape[0]):
-
-        @pl.when(away_ref[slot] >= 0)
+def read_tags(ins, tag_ref, sems):
+    cap, tiles = ins[0].shape[:2]
+    copies = [
+        pltpu.make_async_copy(in_ref.at[k, tiles - 1], tag_ref.at[d * cap + k], sems.at[d * cap + k])
+        for d, in_ref in enumerate(ins)
+        for k in range(cap)
+    ]
+    for copy in copies:
+        copy.start()
+    for copy in copies:
+        copy.wait()
+    return lambda e: tag_ref[e, TAG_ROW, 0].astype(jnp.int32)
+
+
+def tag_scratch(slots):
+    return [pltpu.SMEM((slots, SUB, LANES), jnp.float32), pltpu.SemaphoreType.DMA((slots,))]
+
+
+def repack_kernel(cap, cap_in, row_count, col_count, blocks, part, *refs):
+    refs = list(refs)
+    if part == 0:
+        tag_ref, sems, block_ref, count_ref = refs[-4:]
+        ins, outs, plan_ref = refs[: -5 - col_count], refs[-5 - col_count : -5], refs[-5]
+    else:
+        plan_ref, block_ref = refs[0], refs[-1]
+        ins, outs = refs[1 : -1 - col_count], refs[-1 - col_count : -1]
+    tiles = ins[0].shape[1]
+    slots_in = row_count * cap_in
+    order = issue_order(row_count)
+    if part == 0:
+        tag_at = read_tags(ins, tag_ref, sems)
+        here = lax.axis_index("col")
+        for d in range(col_count + 1):
+            count_ref[d] = 0
+        for e in range(col_count * cap):
+            plan_ref[slots_in + e] = -1
+        for e in range(slots_in):
+            tag = tag_at(e)
+            plan_ref[e] = -1
+
+            @pl.when(tag >= 0)
+            def _():
+                d = step_to(lax.rem(tag // blocks, col_count), here, col_count)
+                k = count_ref[d]
+                count_ref[d] = k + 1
+                j = count_ref[col_count]
+                count_ref[col_count] = j + 1
+                plan_ref[e] = j
+                plan_ref[slots_in + d * cap + k] = j
+
+    row = lax.axis_index("row")
+    for e in range(slots_in):
+        j = plan_ref[e]
+
+        @pl.when(j >= 0)
         def _():
-            d = away_ref[slot]
-            k = count_ref[d]
-            count_ref[d] = k + 1
-            source_ref[d * cap + k] = slot
-
-    for d in range(col_count):
-        for k in range(cap):
-            slot = source_ref[d * cap + k]
-
-            @pl.when(slot >= 0)
+            if part:
+                origin = origin_of(order[e // cap_in], row, row_count)
+                block_ref[j] = ins[0][origin * cap_in + e % cap_in]
+            else:
+                block_ref[j] = ins[e // cap_in][e % cap_in]
+
+    for e in range(col_count * cap):
+        j = plan_ref[slots_in + e]
+        out = outs[e // cap]
+
+        @pl.when(j >= 0)
+        def _():
+            out[e % cap] = block_ref[j]
+
+        if part == 0:
+
+            @pl.when(j < 0)
             def _():
-                outs[d][k] = in_ref[slot]
-
-            if tagged:
-
-                @pl.when(slot < 0)
-                def _():
-                    outs[d][k, in_ref.shape[1] - 1] = jnp.full((SUB, LANES), -1.0, jnp.float32)
-
-
-def repack(away, landed, part, col_count, cap):
-    out = jax.ShapeDtypeStruct((cap,) + landed.shape[1:], jnp.float32)
-    return pl.pallas_call(
-        functools.partial(repack_kernel, cap, col_count, part == 0),
-        in_specs=[pl.BlockSpec(memory_space=pltpu.SMEM), pl.BlockSpec(memory_space=pltpu.VMEM)],
-        out_specs=[pl.BlockSpec(memory_space=pltpu.VMEM)] * col_count,
-        scratch_shapes=[
-            pltpu.SMEM((col_count * cap,), jnp.int32),
-            pltpu.SMEM((col_count,), jnp.int32),
-        ],
-        out_shape=[out] * col_count,
+                out[e % cap, tiles - 1] = jnp.full((SUB, LANES), -1.0, jnp.float32)
+
+
+def repack(landed, plan, part, row_count, col_count, cap, cap_in, blocks):
+    slots_in = row_count * cap_in
+    tiles = landed[0].shape[1:]
+    whole = pl.BlockSpec(memory_space=pltpu.VMEM)
+    scalars = pl.BlockSpec(memory_space=pltpu.SMEM)
+    length = slots_in + col_count * cap
+    scratch = [pltpu.VMEM((blocks,) + tiles, jnp.float32)]
+    if part == 0:
+        scratch = tag_scratch(slots_in) + scratch + [pltpu.SMEM((col_count + 1,), jnp.int32)]
+    *packed, last = pl.pallas_call(
+        functools.partial(repack_kernel, cap, cap_in, row_count, col_count, blocks, part),
+        in_specs=([scalars] if part else []) + [whole] * len(landed),
+        out_specs=[whole] * col_count + ([] if part else [scalars]),
+        scratch_shapes=scratch,
+        out_shape=[jax.ShapeDtypeStruct((cap,) + tiles, jnp.float32)] * col_count
+        + ([] if part else [jax.ShapeDtypeStruct((length,), jnp.int32)]),
         compiler_params=pltpu.CompilerParams(vmem_limit_bytes=VMEM_LIMIT),
         cost_estimate=pl.CostEstimate(flops=0, bytes_accessed=3 * 10**6, transcendentals=0),
         name="repack_%d" % part,
-    )(away, landed)
+    )(*([plan] if part else []), *landed)
+    return (packed + [last], plan) if part else (packed, last)
 
 
 def backward(zeroth, first, second, u):
@@ -286,31 +381,37 @@
     return result
 
 
-def unload(tags_ref, ins, block_ref):
+def unload(plan_ref, ins, block_ref):
     cap = ins[0].shape[0]
-    for d, in_ref in enumerate(ins):
-        for k in range(cap):
-            tag = tags_ref[d * cap + k]
-
-            @pl.when(tag >= 0)
-            def _():
-                block_ref[tag % SUB] = in_ref[k]
+    for e in range(len(ins) * cap):
+        t = plan_ref[e]
+
+        @pl.when(t >= 0)
+        def _():
+            block_ref[t] = ins[e // cap][e % cap]
 
 
 def side_spot(lane, x):
     return (lane // EDGE) == x % SUB
 
 
-def post_kernel(count, tags_ref, *refs):
+def post_kernel(count, *refs):
     ins = refs[:count]
-    post_ref, ylo_ref, yhi_ref, xlo_ref, xhi_ref, block_ref, swap_ref, side_ref = refs[count:]
+    (
+        post_ref, ylo_ref, yhi_ref, xlo_ref, xhi_ref, plan_ref,
+        block_ref, swap_ref, side_ref, tag_ref, sems,
+    ) = refs[count:]
     g = pl.program_id(0)
     steps = len(CHUNKS[0])
     lane = lax.broadcasted_iota(jnp.int32, (SUB, LANES), 1)
 
     @pl.when(g == 0)
     def _():
-        unload(tags_ref, ins, block_ref)
+        tag_at = read_tags(ins, tag_ref, sems)
+        for e in range(count * ins[0].shape[0]):
+            tag = tag_at(e)
+            plan_ref[e] = jnp.where(tag >= 0, lax.rem(tag, SUB), -1)
+        unload(plan_ref, ins, block_ref)
         for t in range(SUB):
             for tile in range(SIDE_TILES):
                 side_ref[pl.ds(tile * SUB * SUB + t, SUB, stride=SUB), :] = block_ref[
@@ -365,33 +466,35 @@
                     xhi_ref[q, half] = result[18 + q]
 
 
-def post(tags, homes):
+def post(homes):
     shape = jax.ShapeDtypeStruct
     face = (9, 2, SUB, LANES)
     steps = len(CHUNKS[0])
-    spec = pl.BlockSpec(face, lambda g, *_: (0, 0, 0, 0))
+    slots = len(homes) * homes[0].shape[0]
+    spec = pl.BlockSpec(face, lambda g: (0, 0, 0, 0))
     return pl.pallas_call(
         functools.partial(post_kernel, len(homes)),
-        grid_spec=pltpu.PrefetchScalarGridSpec(
-            num_scalar_prefetch=1,
-            grid=(steps,),
-            in_specs=[pl.BlockSpec(homes[0].shape, lambda g, *_: (0, 0, 0, 0))] * len(homes),
-            out_specs=[pl.BlockSpec((NQ, SUB, SUB, LANES), lambda g, *_: (0, g, 0, 0))] + [spec] * 4,
-            scratch_shapes=[
-                pltpu.VMEM((SUB, tiles_of(0), SUB, LANES), jnp.float32),
-                pltpu.VMEM((NFIELD * SUB * SUB, LANES), jnp.float32),
-                pltpu.VMEM((SIDE_TILES * SUB * SUB, LANES), jnp.float32),
-            ],
-        ),
+        grid=(steps,),
+        in_specs=[pl.BlockSpec(homes[0].shape, lambda g: (0, 0, 0, 0))] * len(homes),
+        out_specs=[pl.BlockSpec((NQ, SUB, SUB, LANES), lambda g: (0, g, 0, 0))]
+        + [spec] * 4
+        + [pl.BlockSpec(memory_space=pltpu.SMEM)],
+        scratch_shapes=[
+            pltpu.VMEM((SUB, tiles_of(0), SUB, LANES), jnp.float32),
+            pltpu.VMEM((NFIELD * SUB * SUB, LANES), jnp.float32),
+            pltpu.VMEM((SIDE_TILES * SUB * SUB, LANES), jnp.float32),
+        ]
+        + tag_scratch(slots),
         out_shape=[shape((NQ, steps * SUB, SUB, LANES), jnp.float32)]
-        + [shape(face, jnp.float32)] * 4,
+        + [shape(face, jnp.float32)] * 4
+        + [shape((slots,), jnp.int32)],
         compiler_params=pltpu.CompilerParams(vmem_limit_bytes=VMEM_LIMIT),
         cost_estimate=pl.CostEstimate(flops=10**7, bytes_accessed=3 * 10**6, transcendentals=0),
         name="post",
-    )(tags, *homes)
-
-
-def finish_kernel(count, tags_ref, *refs):
+    )(*homes)
+
+
+def finish_kernel(count, plan_ref, *refs):
     ins = refs[:count]
     (
         early_ref, xlo_ref, xhi_ref, below_in, above_in,
@@ -411,7 +514,7 @@
         ]
         for copy in copies:
             copy.start()
-        unload(tags_ref, ins, block_ref)
+        unload(plan_ref, ins, block_ref)
         for step, group in enumerate(CHUNKS[1]):
             for t in range(SUB):
                 for n in range(NFIELD):
@@ -484,7 +587,7 @@
                 out_ref[q, :, c * LANES : (c + 1) * LANES] = value
 
 
-def finish(tags, homes, early, xlo, xhi, below, above):
+def finish(plan, homes, early, xlo, xhi, below, above):
     def whole(value):
         rank = len(value.shape)
         return pl.BlockSpec(value.shape, lambda g, *_: (0,) * rank)
@@ -511,16 +614,12 @@
         compiler_params=pltpu.CompilerParams(vmem_limit_bytes=VMEM_LIMIT),
         cost_estimate=pl.CostEstimate(flops=10**7, bytes_accessed=8 * 10**6, transcendentals=0),
         name="finish",
-    )(tags, *homes, early, xlo, xhi, below, above)
+    )(plan, *homes, early, xlo, xhi, below, above)
 
 
 def shifted(value, axis, step):
     count = lax.axis_size(axis)
     return lax.ppermute(value, axis, [(i, (i + step) % count) for i in range(count)])
-
-
-def tags_of(landed):
-    return landed[:, -1, 2 * NFIELD - (SIDE_TILES - 1) * SUB, 0].astype(jnp.int32)
 
 
 def on_device(populations, destination, refinement):
@@ -530,30 +629,27 @@
     cap_row = 2 * ((blocks + row_count - 1) // row_count)
     cap_col = 2 * ((blocks + col_count - 1) // col_count)
     ordered = jnp.transpose(populations, (1, 0, 2))
-    in_row = [
-        lax.all_to_all(
-            pre(ordered, destination, refinement, part, row_count, cap_row, blocks * col_count),
-            "row", split_axis=0, concat_axis=0, tiled=True,
-        )
-        for part in range(2)
-    ]
-    tags = tags_of(in_row[0])
-    away = jnp.where(tags >= 0, (tags // blocks - lax.axis_index("col")) % col_count, -1)
-
-    def to_columns(part):
-        packed = repack(away, in_row[part], part, col_count, cap_col)
-        return [packed[d] if d == 0 else shifted(packed[d], "col", d) for d in range(col_count)]
-
-    homes = to_columns(0)
-    tags = jnp.concatenate([tags_of(value) for value in homes])
-    early, ylo, yhi, xlo, xhi = post(tags, homes)
+
+    def travel(packed, axis):
+        return [exchanged(packed[d], axis, d) if d else packed[0] for d in issue_order(len(packed))]
+
+    early_row = travel(
+        pre(ordered, destination, refinement, 0, row_count, cap_row, blocks * col_count), "row"
+    )
+    waited = START_AFTER
+    destination, early_row[waited] = lax.optimization_barrier((destination, early_row[waited]))
+    (late,) = pre(ordered, destination, refinement, 1, row_count, cap_row, blocks * col_count)
+    late_row = lax.all_to_all(late, "row", split_axis=0, concat_axis=0, tiled=True)
+    packed, plan = repack(early_row, None, 0, row_count, col_count, cap_col, cap_row, blocks)
+    early, ylo, yhi, xlo, xhi, picked = post(travel(packed, "col"))
     below, above = shifted(yhi, "col", 1), shifted(ylo, "col", -1)
     up = jnp.concatenate([xhi.reshape(18, SUB, LANES), below[6:, 1], above[6:, 1]])
     down = jnp.concatenate([xlo.reshape(18, SUB, LANES), below[:3, 0], above[:3, 0]])
     xlo, xhi = shifted(up, "row", 1), shifted(down, "row", -1)
-    in_row[1], below, above = lax.optimization_barrier((in_row[1], below, above))
-    homes = to_columns(1)
-    return jnp.transpose(finish(tags, homes, early, xlo, xhi, below, above), (1, 0, 2))
+    late_row, below, above = lax.optimization_barrier((late_row, below, above))
+    packed, _ = repack([late_row], plan, 1, row_count, col_count, cap_col, cap_row, blocks)
+    homes = travel(packed, "col")
+    return jnp.transpose(finish(picked, homes, early, xlo, xhi, below, above), (1, 0, 2))
 
 
 def solution(mesh):

time: 100 us -> 130 us (1.30)
  waiting for transfers between devices: 54.9 us -> 77 us
  starting transfers between devices: 24.2 us -> 33.2 us
  Pallas kernels: 13.2 us -> 19.5 us
  local copies, waits for them, and re-layouts: 5.41 us -> 0.03 us
  other arithmetic: 1.98 us -> 0.02 us
    ppermute x0 -> x13, waiting for transfers between devices: none -> 71.7 us  [exchanged(): return lax.ppermute(value, axis, pairs)]
    all_to_all x2 -> x1, waiting for transfers between devices: 34.8 us -> 0.01 us  [on_device(): lax.all_to_all(late, 'row', split_axis=0, concat_axis=0, tiled=True)]
    ppermute x0 -> x13, starting transfers between devices: none -> 20.5 us  [exchanged(): return lax.ppermute(value, axis, pairs)]
    ppermute x10 -> x4, waiting for transfers between devices: 20.1 us -> 5.23 us  [shifted(): lax.ppermute(value, axis, [(i, (i + step) % count) for i in range(count)])]
    ppermute x10 -> x4, starting transfers between devices: 13.2 us -> 6.61 us  [shifted(): lax.ppermute(value, axis, [(i, (i + step) % count) for i in range(count)])]
    pallas_call x5, Pallas kernels: 8.12 us -> 14.5 us  [the longest x2 6.38 us: pre(): pl.pallas_call(functools.partial(pre_kernel, cap, row_count, per_row, par...]
    unnamed x16 -> x14, local copies, waits for them, and re-layouts: 5.4 us -> 0.03 us
    all_to_all x2 -> x1, starting transfers between devices: 11 us -> 6.12 us  [on_device(): lax.all_to_all(late, 'row', split_axis=0, concat_axis=0, tiled=True)]
  transfers between devices with their start and end apart: 12 -> 18, of which waited for: 8 -> 12; matrix products, arithmetic and copies ran while one was open for 2% -> 0% of each run, Pallas kernels for 5% -> 6%
where the time goes in v5:
time: 130 us
  waiting for transfers between devices  77 us (59%)
  starting transfers between devices  33.2 us (26%)
  Pallas kernels  19.5 us (15%)
    ppermute x13, waiting for transfers between devices, exchanged(): return lax.ppermute(value, axis, pairs)  71.7 us
    ppermute x13, starting transfers between devices, exchanged(): return lax.ppermute(value, axis, pairs)  20.5 us
    ppermute x4, starting transfers between devices, shifted(): lax.ppermute(value, axis, [(i, (i + step) % count) for i in range(count)])  6.61 us
    pallas_call x2, Pallas kernels, pre(): pl.pallas_call(functools.partial(pre_kernel, cap, row_count, per_row, par...  6.38 us
    all_to_all x1, starting transfers between devices, on_device(): lax.all_to_all(late, 'row', split_axis=0, concat_axis=0, tiled=True)  6.12 us
    ppermute x4, waiting for transfers between devices, shifted(): lax.ppermute(value, axis, [(i, (i + step) % count) for i in range(count)])  5.23 us
    pallas_call x1, Pallas kernels, finish(): pl.pallas_call(functools.partial(finish_kernel, len(homes)), grid_spec=pl...  5.03 us
    pallas_call x1, Pallas kernels, post(): pl.pallas_call(functools.partial(post_kernel, len(homes)), grid=(steps,),...  4.27 us
  transfers between devices with their start and end apart: 18, of which 12 were waited for; matrix products, arithmetic and copies ran while one was open for 0% of the time, Pallas kernels for 6%

profile of v5, /device:TPU:0, one launch (start us, length us, event | category | flops | bytes accessed | tf_op | source)
XLA Modules:
  0.0 129.9 jit_solution(4756630009991521162)
XLA Ops:
  0.0 3.6 %pre_0.1 = (f32[2,21,8,128]{3,2,1,0:T(8,128)}, f32[2,21,8,128]{3,2,1,0:T(8,128)}, f32[2,21,8,128]{3,2,1,0:T(8,128)}, f32[2,21,8,128]{3,2,1,0:T(8,128)}, f32[2,21...) custom-call(s32[8]{0:T(128)} %dest_hbm.2, s32[8]{0:T(128)} %level_hbm.3, ...), custom_call_target="tpu_custom_call" | custom-call | flops 10000000 | bytes 4000000 | tf_op jit(solution)/shard_map/pre_0/pallas_call | solution.py:208
  3.6 3.1 %collective-permute-start.1 = (f32[2,21,8,128]{3,2,1,0:T(8,128)}, f32[2,21,8,128]{3,2,1,0:T(8,128)S(1)}, u32[]{:S(2)}, u32[]{:S(2)}) collective-permute-start(f32[2,21,8,128]{3,2,1,0:T(8,128)} %get-tuple-element.34), channel_id=1, source_target_pairs={{0,8},{4,12},{8,0},{12,4},{16,24},{20,28},{24,16},{28,20},{1,9},{5... | collective-permute-start | bytes 516104 | tf_op jit(solution)/shard_map/ppermute | solution.py:58
  6.7 4.6 %collective-permute-done.1.refs_1_ = f32[2,21,8,128]{3,2,1,0:T(8,128)S(1)} collective-permute-done((f32[2,21,8,128]{3,2,1,0:T(8,128)}, f32[2,21,8,128]{3,2,1,0:T(8,128)S(1)}, u32[]{:S(2)}, u32[]{:S(2)}) %collective-permute-start.1) | collective-permute-done | bytes 172064 | tf_op jit(solution)/shard_map/ppermute | solution.py:58
  11.3 2.8 %pre_1.1 = f32[16,18,8,128]{3,2,1,0:T(8,128)} custom-call(s32[8]{0:T(128)} %dest_hbm.2, s32[8]{0:T(128)} %level_hbm.3, f32[27,8,4096]{2,1,0:T(8,128)} %bitcast.15), custom_call_target="tpu_custom_call" | custom-call | flops 10000000 | bytes 4000000 | tf_op jit(solution)/shard_map/pre_1/pallas_call | solution.py:208
  14.1 6.1 %all-to-all-start = ((f32[16,18,8,128]{3,2,1,0:T(8,128)}), f32[16,18,8,128]{3,2,1,0:T(8,128)S(1)}, u32[]{:S(2)}, u32[]{:S(2)}) async-start(f32[16,18,8,128]{3,2,1,0:T(8,128)} %pre_1.1), calls=%async_computation | async-start | bytes 2359296 | tf_op jit(solution)/shard_map/all_to_all | solution.py:642
  20.3 2.0 %collective-permute-start = (f32[2,21,8,128]{3,2,1,0:T(8,128)S(1)}, f32[2,21,8,128]{3,2,1,0:T(8,128)S(1)}, u32[]{:S(2)}, u32[]{:S(2)}) collective-permute-start(f32[2,21,8,128]{3,2,1,0:T(8,128)S(1)} %copy-done.6), channel_id=1, source_target_pairs={{0,4},{4,0},{8,12},{12,8},{16,20},{20,16},{24,28},{28,24},{1,5},{5... | collective-permute-start | bytes 516104 | tf_op jit(solution)/shard_map/ppermute | solution.py:58
  22.3 3.3 %collective-permute-start.2 = (f32[2,21,8,128]{3,2,1,0:T(8,128)S(1)}, f32[2,21,8,128]{3,2,1,0:T(8,128)S(1)}, u32[]{:S(2)}, u32[]{:S(2)}) collective-permute-start(f32[2,21,8,128]{3,2,1,0:T(8,128)S(1)} %copy-done.5), channel_id=1, source_target_pairs={{0,28},{4,24},{8,20},{12,16},{16,12},{20,8},{24,4},{28,0},{1,29},{... | collective-permute-start | bytes 516104 | tf_op jit(solution)/shard_map/ppermute | solution.py:58
  25.6 2.0 %collective-permute-start.4 = (f32[2,21,8,128]{3,2,1,0:T(8,128)S(1)}, f32[2,21,8,128]{3,2,1,0:T(8,128)S(1)}, u32[]{:S(2)}, u32[]{:S(2)}) collective-permute-start(f32[2,21,8,128]{3,2,1,0:T(8,128)S(1)} %copy-done.3), channel_id=1, source_target_pairs={{0,20},{4,16},{8,28},{12,24},{16,4},{20,0},{24,12},{28,8},{1,21},{... | collective-permute-start | bytes 516104 | tf_op jit(solution)/shard_map/ppermute | solution.py:58
  27.6 2.4 %collective-permute-start.5 = (f32[2,21,8,128]{3,2,1,0:T(8,128)S(1)}, f32[2,21,8,128]{3,2,1,0:T(8,128)S(1)}, u32[]{:S(2)}, u32[]{:S(2)}) collective-permute-start(f32[2,21,8,128]{3,2,1,0:T(8,128)S(1)} %copy-done.2), channel_id=1, source_target_pairs={{0,16},{4,20},{8,24},{12,28},{16,0},{20,4},{24,8},{28,12},{1,17},{... | collective-permute-start | bytes 516104 | tf_op jit(solution)/shard_map/ppermute | solution.py:58
  29.9 5.0 %collective-permute-done.refs_0_ = f32[2,21,8,128]{3,2,1,0:T(8,128)S(1)} collective-permute-done((f32[2,21,8,128]{3,2,1,0:T(8,128)S(1)}, f32[2,21,8,128]{3,2,1,0:T(8,128)S(1)}, u32[]{:S(2)}, u32[]{:S(2)}) %collective-permute-start) | collective-permute-done | bytes 172064 | tf_op jit(solution)/shard_map/ppermute | solution.py:58
  34.9 2.1 %collective-permute-start.6 = (f32[2,21,8,128]{3,2,1,0:T(8,128)S(1)}, f32[2,21,8,128]{3,2,1,0:T(8,128)S(1)}, u32[]{:S(2)}, u32[]{:S(2)}) collective-permute-start(f32[2,21,8,128]{3,2,1,0:T(8,128)S(1)} %copy-done.1), channel_id=1, source_target_pairs={{0,12},{4,8},{8,4},{12,0},{16,28},{20,24},{24,20},{28,16},{1,13},{... | collective-permute-start | bytes 516104 | tf_op jit(solution)/shard_map/ppermute | solution.py:58
  37.0 12.5 %collective-permute-done.2.refs_2_ = f32[2,21,8,128]{3,2,1,0:T(8,128)S(1)} collective-permute-done((f32[2,21,8,128]{3,2,1,0:T(8,128)S(1)}, f32[2,21,8,128]{3,2,1,0:T(8,128)S(1)}, u32[]{:S(2)}, u32[]{:S(2)}) %collective-permute-start.2) | collective-permute-done | bytes 172064 | tf_op jit(solution)/shard_map/ppermute | solution.py:58
  49.6 2.7 %collective-permute-done.3.refs_3_ = f32[2,21,8,128]{3,2,1,0:T(8,128)S(1)} collective-permute-done((f32[2,21,8,128]{3,2,1,0:T(8,128)S(1)}, f32[2,21,8,128]{3,2,1,0:T(8,128)S(1)}, u32[]{:S(2)}, u32[]{:S(2)}) %collective-permute-start.3) | collective-permute-done | bytes 172064 | tf_op jit(solution)/shard_map/ppermute | solution.py:58
  52.3 23.4 %collective-permute-done.4.refs_4_ = f32[2,21,8,128]{3,2,1,0:T(8,128)S(1)} collective-permute-done((f32[2,21,8,128]{3,2,1,0:T(8,128)S(1)}, f32[2,21,8,128]{3,2,1,0:T(8,128)S(1)}, u32[]{:S(2)}, u32[]{:S(2)}) %collective-permute-start.4) | collective-permute-done | bytes 172064 | tf_op jit(solution)/shard_map/ppermute | solution.py:58
  75.7 2.0 %collective-permute-done.5.refs_5_ = f32[2,21,8,128]{3,2,1,0:T(8,128)S(1)} collective-permute-done((f32[2,21,8,128]{3,2,1,0:T(8,128)S(1)}, f32[2,21,8,128]{3,2,1,0:T(8,128)S(1)}, u32[]{:S(2)}, u32[]{:S(2)}) %collective-permute-start.5) | collective-permute-done | bytes 172064 | tf_op jit(solution)/shard_map/ppermute | solution.py:58
  77.7 3.0 %repack_0.1 = (f32[4,21,8,128]{3,2,1,0:T(8,128)S(1)}, f32[4,21,8,128]{3,2,1,0:T(8,128)S(1)}, f32[4,21,8,128]{3,2,1,0:T(8,128)S(1)}, f32[4,21,8,128]{3,2,1,0:T(8,128)S(1)}, s32[32]{0:T(128)S(1)}) custom-call(f32[2,21,8,128]{3,2,1,0:T(8,128)S(1)} %collective-permute-done.refs_0_, f32[2,21,8,128]{3,2,1,0:T(8,128)S(1)} %collective-permute-done.1.refs_1_, ...), custom_call_target="tpu_custom_call" | custom-call | bytes 3000000 | tf_op jit(solution)/shard_map/repack_0/pallas_call | solution.py:315
  80.8 1.7 %collective-permute-start.8 = (f32[4,21,8,128]{3,2,1,0:T(8,128)S(1)}, f32[4,21,8,128]{3,2,1,0:T(8,128)S(1)}, u32[]{:S(2)}, u32[]{:S(2)}) collective-permute-start(f32[4,21,8,128]{3,2,1,0:T(8,128)S(1)} %get-tuple-element.43), channel_id=1, source_target_pairs={{0,3},{1,2},{2,1},{3,0},{4,7},{5,6},{6,5},{7,4},{8,11},{9,10},{10,... | collective-permute-start | bytes 1032200 | tf_op jit(solution)/shard_map/ppermute | solution.py:58
  82.4 0.5 collective-permute-start.9
  82.9 7.9 %collective-permute-done.8.refs_1_ = f32[4,21,8,128]{3,2,1,0:T(8,128)S(1)} collective-permute-done((f32[4,21,8,128]{3,2,1,0:T(8,128)S(1)}, f32[4,21,8,128]{3,2,1,0:T(8,128)S(1)}, u32[]{:S(2)}, u32[]{:S(2)}) %collective-permute-start.8) | collective-permute-done | bytes 344096 | tf_op jit(solution)/shard_map/ppermute | solution.py:58
  90.8 7.7 %collective-permute-done.9.refs_2_ = f32[4,21,8,128]{3,2,1,0:T(8,128)S(1)} collective-permute-done((f32[4,21,8,128]{3,2,1,0:T(8,128)S(1)}, f32[4,21,8,128]{3,2,1,0:T(8,128)S(1)}, u32[]{:S(2)}, u32[]{:S(2)}) %collective-permute-start.9) | collective-permute-done | bytes 344096 | tf_op jit(solution)/shard_map/ppermute | solution.py:58
  98.6 4.3 %post.1 = (f32[27,16,8,128]{3,2,1,0:T(8,128)S(1)}, f32[9,2,8,128]{3,2,1,0:T(8,128)S(1)}, f32[9,2,8,128]{3,2,1,0:T(8,128)S(1)}, f32[9,2,8,128]{3,2,1,0:T(8,128)S(...) custom-call(f32[4,21,8,128]{3,2,1,0:T(8,128)S(1)} %collective-permute-done.7.refs_0_, ...), custom_call_target="tpu_custom_call" | custom-call | flops 10000000 | bytes 3000000 | tf_op jit(solution)/shard_map/post/pallas_call | solution.py:475
  102.9 1.7 %collective-permute-start.11 = (f32[9,2,8,128]{3,2,1,0:T(8,128)S(1)}, f32[9,2,8,128]{3,2,1,0:T(8,128)S(1)}, u32[]{:S(2)}, u32[]{:S(2)}) collective-permute-start(f32[9,2,8,128]{3,2,1,0:T(8,128)S(1)} %get-tuple-element.50), channel_id=1, source_target_pairs={{0,3},{1,0},{2,1},{3,2},{4,7},{5,4},{6,5},{7,6},{8,11},{9,8},{10,9... | collective-permute-start | bytes 221192 | tf_op jit(solution)/shard_map/ppermute | solution.py:622
  104.6 2.0 %collective-permute-done.10.refs_7_ = f32[9,2,8,128]{3,2,1,0:T(8,128)S(1)} collective-permute-done((f32[9,2,8,128]{3,2,1,0:T(8,128)S(1)}, f32[9,2,8,128]{3,2,1,0:T(8,128)S(1)}, u32[]{:S(2)}, u32[]{:S(2)}) %collective-permute-start.10) | collective-permute-done | bytes 73760 | tf_op jit(solution)/shard_map/ppermute | solution.py:622
  106.7 0.9 repack_1.1
  107.6 1.7 %collective-permute-start.12 = (f32[4,18,8,128]{3,2,1,0:T(8,128)S(1)}, f32[4,18,8,128]{3,2,1,0:T(8,128)S(1)}, u32[]{:S(2)}, u32[]{:S(2)}) collective-permute-start(f32[4,18,8,128]{3,2,1,0:T(8,128)S(1)} %get-tuple-element.52), channel_id=1, source_target_pairs={{0,1},{1,0},{2,3},{3,2},{4,5},{5,4},{6,7},{7,6},{8,9},{9,8},{10,11... | collective-permute-start | bytes 884744 | tf_op jit(solution)/shard_map/ppermute | solution.py:58
  109.5 1.5 %collective-permute-start.14 = (f32[4,18,8,128]{3,2,1,0:T(8,128)S(1)}, f32[4,18,8,128]{3,2,1,0:T(8,128)S(1)}, u32[]{:S(2)}, u32[]{:S(2)}) collective-permute-start(f32[4,18,8,128]{3,2,1,0:T(8,128)S(1)} %get-tuple-element.54), channel_id=1, source_target_pairs={{0,2},{1,3},{2,0},{3,1},{4,6},{5,7},{6,4},{7,5},{8,10},{9,11},{10,... | collective-permute-start | bytes 884744 | tf_op jit(solution)/shard_map/ppermute | solution.py:58
  111.0 1.2 collective-permute-start.15
  112.3 3.6 %collective-permute-start.16 = (f32[24,8,128]{2,1,0:T(8,128)S(1)}, f32[24,8,128]{2,1,0:T(8,128)S(1)}, u32[]{:S(2)}, u32[]{:S(2)}) collective-permute-start(f32[24,8,128]{2,1,0:T(8,128)S(1)} %pad_maximum_fusion.1), channel_id=1, source_target_pairs={{0,28},{4,0},{8,4},{12,8},{16,12},{20,16},{24,20},{28,24},{1,29},{... | collective-permute-start | bytes 294920 | tf_op jit(solution)/shard_map/ppermute | solution.py:622
  115.8 2.9 %collective-permute-done.15.refs_5_ = f32[24,8,128]{2,1,0:T(8,128)S(1)} collective-permute-done((f32[24,8,128]{2,1,0:T(8,128)S(1)}, f32[24,8,128]{2,1,0:T(8,128)S(1)}, u32[]{:S(2)}, u32[]{:S(2)}) %collective-permute-start.15) | collective-permute-done | bytes 98336 | tf_op jit(solution)/shard_map/ppermute | solution.py:622
  118.7 0.3 collective-permute-done.16.refs_6_
  119.0 5.9 %collective-permute-done.14.refs_2_ = f32[4,18,8,128]{3,2,1,0:T(8,128)S(1)} collective-permute-done((f32[4,18,8,128]{3,2,1,0:T(8,128)S(1)}, f32[4,18,8,128]{3,2,1,0:T(8,128)S(1)}, u32[]{:S(2)}, u32[]{:S(2)}) %collective-permute-start.14) | collective-permute-done | bytes 294944 | tf_op jit(solution)/shard_map/ppermute | solution.py:58
  124.9 5.0 %finish.1 = f32[27,8,4096]{2,1,0:T(8,128)} custom-call(s32[16]{0:T(128)S(1)} %get-tuple-element.46.plan_ref, f32[4,18,8,128]{3,2,1,0:T(8,128)S(1)} %collective-permute-done.12.refs_0_, f32[4,18,8,128]{3,2,1,0:T(8,128)S(1)} %collective-permute-done.13.refs_1_, f32[4,18,8,128]{3,2,1,0:T(8,128)S(1)} %collective-permute-done.14.refs_2_, ...), custom_call_target="tpu_custom_call" | custom-call | flops 10000000 | bytes 8000000 | tf_op jit(solution)/shard_map/finish/pallas_call | solution.py:595
  (28 shorter events, 0.4 us)
Async XLA Ops:
  3.6 7.7 %collective-permute-start.1 = (f32[2,21,8,128]{3,2,1,0:T(8,128)}, f32[2,21,8,128]{3,2,1,0:T(8,128)S(1)}, u32[]{:S(2)}, u32[]{:S(2)}) collective-permute-start(f32[2,21,8,128]{3,2,1,0:T(8,128)} %get-tuple-element.34), channel_id=1, source_target_pairs={{0,8},{4,12},{8,0},{12,4},{16,24},{20,28},{24,16},{28,20},{1,9},{5... | collective-permute-start | bytes 516104 | tf_op jit(solution)/shard_map/ppermute | solution.py:58
  14.1 6.2 %copy-start.6 = (f32[2,21,8,128]{3,2,1,0:T(8,128)S(1)}, f32[2,21,8,128]{3,2,1,0:T(8,128)}, u32[]{:S(2)}) copy-start(f32[2,21,8,128]{3,2,1,0:T(8,128)} %get-tuple-element.33) | copy-start | bytes 516100
  14.1 8.2 %copy-start.5 = (f32[2,21,8,128]{3,2,1,0:T(8,128)S(1)}, f32[2,21,8,128]{3,2,1,0:T(8,128)}, u32[]{:S(2)}) copy-start(f32[2,21,8,128]{3,2,1,0:T(8,128)} %get-tuple-element.36) | copy-start | bytes 516100
  14.1 11.5 %copy-start.4 = (f32[2,21,8,128]{3,2,1,0:T(8,128)S(1)}, f32[2,21,8,128]{3,2,1,0:T(8,128)}, u32[]{:S(2)}) copy-start(f32[2,21,8,128]{3,2,1,0:T(8,128)} %get-tuple-element.37) | copy-start | bytes 516100
  14.1 11.5 %copy-start.3 = (f32[2,21,8,128]{3,2,1,0:T(8,128)S(1)}, f32[2,21,8,128]{3,2,1,0:T(8,128)}, u32[]{:S(2)}) copy-start(f32[2,21,8,128]{3,2,1,0:T(8,128)} %get-tuple-element.38) | copy-start | bytes 516100
  14.1 13.5 %copy-start.2 = (f32[2,21,8,128]{3,2,1,0:T(8,128)S(1)}, f32[2,21,8,128]{3,2,1,0:T(8,128)}, u32[]{:S(2)}) copy-start(f32[2,21,8,128]{3,2,1,0:T(8,128)} %get-tuple-element.39) | copy-start | bytes 516100
  14.1 20.8 %copy-start.1 = (f32[2,21,8,128]{3,2,1,0:T(8,128)S(1)}, f32[2,21,8,128]{3,2,1,0:T(8,128)}, u32[]{:S(2)}) copy-start(f32[2,21,8,128]{3,2,1,0:T(8,128)} %get-tuple-element.40) | copy-start | bytes 516100
  14.1 63.6 %copy-start = (f32[2,21,8,128]{3,2,1,0:T(8,128)S(1)}, f32[2,21,8,128]{3,2,1,0:T(8,128)}, u32[]{:S(2)}) copy-start(f32[2,21,8,128]{3,2,1,0:T(8,128)} %get-tuple-element.41.refs_7_) | copy-start | bytes 516100
  14.1 92.6 %all-to-all-start = ((f32[16,18,8,128]{3,2,1,0:T(8,128)}), f32[16,18,8,128]{3,2,1,0:T(8,128)S(1)}, u32[]{:S(2)}, u32[]{:S(2)}) async-start(f32[16,18,8,128]{3,2,1,0:T(8,128)} %pre_1.1), calls=%async_computation | async-start | bytes 2359296 | tf_op jit(solution)/shard_map/all_to_all | solution.py:642
  20.3 14.6 %collective-permute-start = (f32[2,21,8,128]{3,2,1,0:T(8,128)S(1)}, f32[2,21,8,128]{3,2,1,0:T(8,128)S(1)}, u32[]{:S(2)}, u32[]{:S(2)}) collective-permute-start(f32[2,21,8,128]{3,2,1,0:T(8,128)S(1)} %copy-done.6), channel_id=1, source_target_pairs={{0,4},{4,0},{8,12},{12,8},{16,20},{20,16},{24,28},{28,24},{1,5},{5... | collective-permute-start | bytes 516104 | tf_op jit(solution)/shard_map/ppermute | solution.py:58
  22.3 27.3 %collective-permute-start.2 = (f32[2,21,8,128]{3,2,1,0:T(8,128)S(1)}, f32[2,21,8,128]{3,2,1,0:T(8,128)S(1)}, u32[]{:S(2)}, u32[]{:S(2)}) collective-permute-start(f32[2,21,8,128]{3,2,1,0:T(8,128)S(1)} %copy-done.5), channel_id=1, source_target_pairs={{0,28},{4,24},{8,20},{12,16},{16,12},{20,8},{24,4},{28,0},{1,29},{... | collective-permute-start | bytes 516104 | tf_op jit(solution)/shard_map/ppermute | solution.py:58
  25.6 26.7 %collective-permute-start.3 = (f32[2,21,8,128]{3,2,1,0:T(8,128)S(1)}, f32[2,21,8,128]{3,2,1,0:T(8,128)S(1)}, u32[]{:S(2)}, u32[]{:S(2)}) collective-permute-start(f32[2,21,8,128]{3,2,1,0:T(8,128)S(1)} %copy-done.4), channel_id=1, source_target_pairs={{0,24},{4,28},{8,16},{12,20},{16,8},{20,12},{24,0},{28,4},{1,25},{... | collective-permute-start | bytes 516104 | tf_op jit(solution)/shard_map/ppermute | solution.py:58
  25.6 50.1 %collective-permute-start.4 = (f32[2,21,8,128]{3,2,1,0:T(8,128)S(1)}, f32[2,21,8,128]{3,2,1,0:T(8,128)S(1)}, u32[]{:S(2)}, u32[]{:S(2)}) collective-permute-start(f32[2,21,8,128]{3,2,1,0:T(8,128)S(1)} %copy-done.3), channel_id=1, source_target_pairs={{0,20},{4,16},{8,28},{12,24},{16,4},{20,0},{24,12},{28,8},{1,21},{... | collective-permute-start | bytes 516104 | tf_op jit(solution)/shard_map/ppermute | solution.py:58
  27.6 50.1 %collective-permute-start.5 = (f32[2,21,8,128]{3,2,1,0:T(8,128)S(1)}, f32[2,21,8,128]{3,2,1,0:T(8,128)S(1)}, u32[]{:S(2)}, u32[]{:S(2)}) collective-permute-start(f32[2,21,8,128]{3,2,1,0:T(8,128)S(1)} %copy-done.2), channel_id=1, source_target_pairs={{0,16},{4,20},{8,24},{12,28},{16,0},{20,4},{24,8},{28,12},{1,17},{... | collective-permute-start | bytes 516104 | tf_op jit(solution)/shard_map/ppermute | solution.py:58
  34.9 42.8 %collective-permute-start.6 = (f32[2,21,8,128]{3,2,1,0:T(8,128)S(1)}, f32[2,21,8,128]{3,2,1,0:T(8,128)S(1)}, u32[]{:S(2)}, u32[]{:S(2)}) collective-permute-start(f32[2,21,8,128]{3,2,1,0:T(8,128)S(1)} %copy-done.1), channel_id=1, source_target_pairs={{0,12},{4,8},{8,4},{12,0},{16,28},{20,24},{24,20},{28,16},{1,13},{... | collective-permute-start | bytes 516104 | tf_op jit(solution)/shard_map/ppermute | solution.py:58
  80.7 2.2 %collective-permute-start.7 = (f32[4,21,8,128]{3,2,1,0:T(8,128)S(1)}, f32[4,21,8,128]{3,2,1,0:T(8,128)S(1)}, u32[]{:S(2)}, u32[]{:S(2)}) collective-permute-start(f32[4,21,8,128]{3,2,1,0:T(8,128)S(1)} %get-tuple-element.42), channel_id=1, source_target_pairs={{0,1},{1,0},{2,3},{3,2},{4,5},{5,4},{6,7},{7,6},{8,9},{9,8},{10,11... | collective-permute-start | bytes 1032200 | tf_op jit(solution)/shard_map/ppermute | solution.py:58
  80.8 10.1 %collective-permute-start.8 = (f32[4,21,8,128]{3,2,1,0:T(8,128)S(1)}, f32[4,21,8,128]{3,2,1,0:T(8,128)S(1)}, u32[]{:S(2)}, u32[]{:S(2)}) collective-permute-start(f32[4,21,8,128]{3,2,1,0:T(8,128)S(1)} %get-tuple-element.43), channel_id=1, source_target_pairs={{0,3},{1,2},{2,1},{3,0},{4,7},{5,6},{6,5},{7,4},{8,11},{9,10},{10,... | collective-permute-start | bytes 1032200 | tf_op jit(solution)/shard_map/ppermute | solution.py:58
  82.4 16.1 %collective-permute-start.9 = (f32[4,21,8,128]{3,2,1,0:T(8,128)S(1)}, f32[4,21,8,128]{3,2,1,0:T(8,128)S(1)}, u32[]{:S(2)}, u32[]{:S(2)}) collective-permute-start(f32[4,21,8,128]{3,2,1,0:T(8,128)S(1)} %get-tuple-element.44), channel_id=1, source_target_pairs={{0,2},{1,3},{2,0},{3,1},{4,6},{5,7},{6,4},{7,5},{8,10},{9,11},{10,... | collective-permute-start | bytes 1032200 | tf_op jit(solution)/shard_map/ppermute | solution.py:58
  102.8 3.8 %collective-permute-start.10 = (f32[9,2,8,128]{3,2,1,0:T(8,128)S(1)}, f32[9,2,8,128]{3,2,1,0:T(8,128)S(1)}, u32[]{:S(2)}, u32[]{:S(2)}) collective-permute-start(f32[9,2,8,128]{3,2,1,0:T(8,128)S(1)} %get-tuple-element.49), channel_id=1, source_target_pairs={{0,1},{1,2},{2,3},{3,0},{4,5},{5,6},{6,7},{7,4},{8,9},{9,10},{10,1... | collective-permute-start | bytes 221192 | tf_op jit(solution)/shard_map/ppermute | solution.py:622
  102.9 3.8 %collective-permute-start.11 = (f32[9,2,8,128]{3,2,1,0:T(8,128)S(1)}, f32[9,2,8,128]{3,2,1,0:T(8,128)S(1)}, u32[]{:S(2)}, u32[]{:S(2)}) collective-permute-start(f32[9,2,8,128]{3,2,1,0:T(8,128)S(1)} %get-tuple-element.50), channel_id=1, source_target_pairs={{0,3},{1,0},{2,1},{3,2},{4,7},{5,4},{6,5},{7,6},{8,11},{9,8},{10,9... | collective-permute-start | bytes 221192 | tf_op jit(solution)/shard_map/ppermute | solution.py:622
  107.6 11.5 %collective-permute-start.12 = (f32[4,18,8,128]{3,2,1,0:T(8,128)S(1)}, f32[4,18,8,128]{3,2,1,0:T(8,128)S(1)}, u32[]{:S(2)}, u32[]{:S(2)}) collective-permute-start(f32[4,18,8,128]{3,2,1,0:T(8,128)S(1)} %get-tuple-element.52), channel_id=1, source_target_pairs={{0,1},{1,0},{2,3},{3,2},{4,5},{5,4},{6,7},{7,6},{8,9},{9,8},{10,11... | collective-permute-start | bytes 884744 | tf_op jit(solution)/shard_map/ppermute | solution.py:58
  109.3 9.7 %collective-permute-start.13 = (f32[4,18,8,128]{3,2,1,0:T(8,128)S(1)}, f32[4,18,8,128]{3,2,1,0:T(8,128)S(1)}, u32[]{:S(2)}, u32[]{:S(2)}) collective-permute-start(f32[4,18,8,128]{3,2,1,0:T(8,128)S(1)} %get-tuple-element.53), channel_id=1, source_target_pairs={{0,3},{1,2},{2,1},{3,0},{4,7},{5,6},{6,5},{7,4},{8,11},{9,10},{10,... | collective-permute-start | bytes 884744 | tf_op jit(solution)/shard_map/ppermute | solution.py:58
  109.5 15.5 %collective-permute-start.14 = (f32[4,18,8,128]{3,2,1,0:T(8,128)S(1)}, f32[4,18,8,128]{3,2,1,0:T(8,128)S(1)}, u32[]{:S(2)}, u32[]{:S(2)}) collective-permute-start(f32[4,18,8,128]{3,2,1,0:T(8,128)S(1)} %get-tuple-element.54), channel_id=1, source_target_pairs={{0,2},{1,3},{2,0},{3,1},{4,6},{5,7},{6,4},{7,5},{8,10},{9,11},{10,... | collective-permute-start | bytes 884744 | tf_op jit(solution)/shard_map/ppermute | solution.py:58
  111.0 7.7 %collective-permute-start.15 = (f32[24,8,128]{2,1,0:T(8,128)S(1)}, f32[24,8,128]{2,1,0:T(8,128)S(1)}, u32[]{:S(2)}, u32[]{:S(2)}) collective-permute-start(f32[24,8,128]{2,1,0:T(8,128)S(1)} %pad_maximum_fusion), channel_id=1, source_target_pairs={{0,4},{4,8},{8,12},{12,16},{16,20},{20,24},{24,28},{28,0},{1,5},{5... | collective-permute-start | bytes 294920 | tf_op jit(solution)/shard_map/ppermute | solution.py:622
  112.3 6.8 %collective-permute-start.16 = (f32[24,8,128]{2,1,0:T(8,128)S(1)}, f32[24,8,128]{2,1,0:T(8,128)S(1)}, u32[]{:S(2)}, u32[]{:S(2)}) collective-permute-start(f32[24,8,128]{2,1,0:T(8,128)S(1)} %pad_maximum_fusion.1), channel_id=1, source_target_pairs={{0,28},{4,0},{8,4},{12,8},{16,12},{20,16},{24,20},{28,24},{1,29},{... | collective-permute-start | bytes 294920 | tf_op jit(solution)/shard_map/ppermute | solution.py:622

commit v6 on v5

--- a/solution.py
+++ b/solution.py
@@ -17,8 +17,7 @@
 WIDTH = EDGE // GROUPS
 CHUNKS = ((0, 3), (1, 2))
 SIDE_TILES = 3
-START_AFTER = 1
-TAG_ROW = 2 * NFIELD - (SIDE_TILES - 1) * SUB
+LATE_TILES = -(-2 * NFIELD * (SUB - 1) // SUB)
 VMEM_LIMIT = 20 * 1024 * 1024
 PRE_VMEM_LIMIT = 60 * 1024 * 1024
 
@@ -28,25 +27,17 @@
 
 
 def tiles_of(part):
-    return len(CHUNKS[part]) * NFIELD + (0 if part else SIDE_TILES)
+    return LATE_TILES if part else len(CHUNKS[0]) * NFIELD + SIDE_TILES
+
+
+def free_place(c):
+    return (c % 2) * (SUB - 1)
 
 
 def step_to(target, here, count):
     if count & (count - 1) == 0:
         return target ^ here
     return lax.rem(target - here + count, count)
-
-
-def origin_of(step, here, count):
-    if count & (count - 1) == 0:
-        return here ^ step
-    return lax.rem(here - step + count, count)
-
-
-def issue_order(count):
-    near = list(range(1, count // 2))
-    far = list(range(count - 1, count // 2 - 1, -1))
-    return near[:2] + far + near[2:] + [0]
 
 
 def exchanged(value, axis, step):
@@ -103,9 +94,8 @@
     )
 
 
-def pre_kernel(cap, row_count, per_row, part, dest_hbm, level_hbm, x_hbm, *refs):
-    outs = refs[:-8]
-    x_ref, swap_ref, packed_ref, side_ref, dest_ref, level_ref, source_ref, sems = refs[-8:]
+def pre_kernel(cap, row_count, per_row, part, dest_hbm, level_hbm, x_hbm, out_ref, *refs):
+    x_ref, swap_ref, packed_ref, side_ref, dest_ref, level_ref, sems = refs
     order = CHUNKS[1] if part else CHUNKS[0] + CHUNKS[1]
     steps = len(CHUNKS[part])
     blocks = x_ref.shape[2]
@@ -136,40 +126,41 @@
     rate = 1.0 / (3.0 * VISCOSITY * scale.astype(jnp.float32) + 0.5)
     keep = 1.0 - rate
 
-    here = lax.axis_index("row")
-    for e in range(row_count * cap):
-        source_ref[e] = -1
     rows = [dest_ref[t] // per_row for t in range(blocks)]
+    slots = []
     for t in range(blocks):
-        e = (rows[t] if part else step_to(rows[t], here, row_count)) * cap
+        slot = rows[t] * cap
         for other in range(t):
-            e = e + jnp.where(rows[other] == rows[t], 1, 0)
-        source_ref[e] = t
+            slot = slot + jnp.where(rows[other] == rows[t], 1, 0)
+        slots.append(slot)
 
     def spread(ref, first, count):
-        for e in range(row_count * cap):
-            t = source_ref[e]
-
-            @pl.when(t >= 0)
-            def _():
-                for n in range(count):
-                    moved = ref[pl.ds(n * SUB * SUB + t, SUB, stride=SUB), :]
-                    if part:
-                        outs[0][e, first + n] = moved
-                    else:
-                        outs[e // cap][e % cap, first + n] = moved
+        for t in range(blocks):
+            for n in range(count):
+                moved = ref[pl.ds(n * SUB * SUB + t, SUB, stride=SUB), :]
+                out_ref[slots[t], first + n] = moved
+
+    def fields_at(step, c):
+        return collided([x_ref[step, q, :, c * LANES : (c + 1) * LANES] for q in range(NQ)], keep)
 
     for step, group in enumerate(order):
         large[step].wait()
+        if part:
+            last = fields_at(step, chunks - 1)
+            for c in range(chunks - 1):
+                place = free_place(c)
+                turn = (place - c) * EDGE % LANES
+                for n, field in enumerate(fields_at(step, c)):
+                    other = pltpu.roll(last[n], turn, axis=1) if turn else last[n]
+                    base = ((step * NFIELD + n) * (chunks - 1) + c) * SUB
+                    swap_ref[base : base + SUB, :] = jnp.where(spot == place, other, field)
+            continue
         if step < steps:
             for c in range(chunks):
-                fields = collided(
-                    [x_ref[step, q, :, c * LANES : (c + 1) * LANES] for q in range(NQ)], keep
-                )
-                for n, field in enumerate(fields):
+                for n, field in enumerate(fields_at(step, c)):
                     base = (n * chunks + c) * SUB
                     swap_ref[base : base + SUB, :] = field
-            spread(swap_ref, step * NFIELD, NFIELD)
+            spread(swap_ref, SIDE_TILES + step * NFIELD, NFIELD)
             continue
         for q in range(NQ):
             for half in range(2):
@@ -184,40 +175,41 @@
                     value = moved if value is None else jnp.where(spot == at, moved, value)
                 packed_ref[half * NQ + q] = value
 
-    if part == 0:
-        for half in range(2):
-            fields = collided([packed_ref[half * NQ + q] for q in range(NQ)], keep)
-            for n, field in enumerate(fields):
-                base = (half * NFIELD + n) * SUB
-                side_ref[base : base + SUB, :] = field
-        for row in range(2 * NFIELD, SIDE_TILES * SUB):
+    if part:
+        for row in range(steps * NFIELD * (chunks - 1), LATE_TILES * SUB):
+            swap_ref[row * SUB : (row + 1) * SUB, :] = tag.astype(jnp.float32)
+        spread(swap_ref, 0, LATE_TILES)
+        return
+    for row in range(SIDE_TILES * SUB):
+        if not 1 <= row <= 2 * NFIELD:
             side_ref[row * SUB : (row + 1) * SUB, :] = tag.astype(jnp.float32)
-        for out in outs:
-            for k in range(cap):
-                out[k, tiles_of(0) - 1] = jnp.full((SUB, LANES), -1.0, jnp.float32)
-        spread(side_ref, steps * NFIELD, SIDE_TILES)
+    for half in range(2):
+        fields = collided([packed_ref[half * NQ + q] for q in range(NQ)], keep)
+        for n, field in enumerate(fields):
+            base = (1 + half * NFIELD + n) * SUB
+            side_ref[base : base + SUB, :] = field
+    for slot in range(row_count * cap):
+        out_ref[slot, 0] = jnp.full((SUB, LANES), -1.0, jnp.float32)
+    spread(side_ref, 0, SIDE_TILES)
 
 
 def pre(populations, destination, refinement, part, row_count, cap, per_row):
     blocks = populations.shape[1]
     cells = populations.shape[2] // GROUPS
     loaded = len(CHUNKS[part]) + (0 if part else len(CHUNKS[1]))
-    arrays = 1 if part else row_count
-    slots = row_count * cap // arrays
-    out = jax.ShapeDtypeStruct((slots, tiles_of(part), SUB, LANES), jnp.float32)
+    rows = LATE_TILES * SUB if part else NFIELD * cells // LANES
     return pl.pallas_call(
         functools.partial(pre_kernel, cap, row_count, per_row, part),
         in_specs=[pl.BlockSpec(memory_space=pltpu.HBM)] * 3,
-        out_specs=[pl.BlockSpec(memory_space=pltpu.VMEM)] * arrays,
-        out_shape=[out] * arrays,
+        out_specs=pl.BlockSpec(memory_space=pltpu.VMEM),
+        out_shape=jax.ShapeDtypeStruct((row_count * cap, tiles_of(part), SUB, LANES), jnp.float32),
         scratch_shapes=[
             pltpu.VMEM((loaded, NQ, blocks, cells), jnp.float32),
-            pltpu.VMEM((NFIELD * cells // LANES * SUB, LANES), jnp.float32),
+            pltpu.VMEM((rows * SUB, LANES), jnp.float32),
             pltpu.VMEM((2 * NQ, SUB, LANES), jnp.float32),
             pltpu.VMEM((SIDE_TILES * SUB * SUB, LANES), jnp.float32),
             pltpu.SMEM((blocks,), jnp.int32),
             pltpu.SMEM((blocks,), jnp.int32),
-            pltpu.SMEM((row_count * cap,), jnp.int32),
             pltpu.SemaphoreType.DMA((2 + loaded,)),
         ],
         compiler_params=pltpu.CompilerParams(vmem_limit_bytes=PRE_VMEM_LIMIT),
@@ -227,103 +219,76 @@
 
 
 def read_tags(ins, tag_ref, sems):
-    cap, tiles = ins[0].shape[:2]
+    cap = ins[0].shape[0]
     copies = [
-        pltpu.make_async_copy(in_ref.at[k, tiles - 1], tag_ref.at[d * cap + k], sems.at[d * cap + k])
+        pltpu.make_async_copy(in_ref.at[:, 0, pl.ds(0, 1)], tag_ref.at[pl.ds(d * cap, cap)], sems.at[d])
         for d, in_ref in enumerate(ins)
-        for k in range(cap)
     ]
     for copy in copies:
         copy.start()
     for copy in copies:
         copy.wait()
-    return lambda e: tag_ref[e, TAG_ROW, 0].astype(jnp.int32)
-
-
-def tag_scratch(slots):
-    return [pltpu.SMEM((slots, SUB, LANES), jnp.float32), pltpu.SemaphoreType.DMA((slots,))]
-
-
-def repack_kernel(cap, cap_in, row_count, col_count, blocks, part, *refs):
-    refs = list(refs)
-    if part == 0:
-        tag_ref, sems, block_ref, count_ref = refs[-4:]
-        ins, outs, plan_ref = refs[: -5 - col_count], refs[-5 - col_count : -5], refs[-5]
+    return lambda e: tag_ref[e, 0, 0].astype(jnp.int32)
+
+
+def tag_scratch(arrays, slots):
+    return [pltpu.SMEM((slots, 1, LANES), jnp.float32), pltpu.SemaphoreType.DMA((arrays,))]
+
+
+def repack_kernel(cap, col_count, blocks, part, *refs):
+    if part:
+        plan_ref, in_ref, *outs = refs
     else:
-        plan_ref, block_ref = refs[0], refs[-1]
-        ins, outs = refs[1 : -1 - col_count], refs[-1 - col_count : -1]
-    tiles = ins[0].shape[1]
-    slots_in = row_count * cap_in
-    order = issue_order(row_count)
-    if part == 0:
-        tag_at = read_tags(ins, tag_ref, sems)
+        in_ref, *outs, plan_ref, tag_ref, sems, count_ref = refs
+        tag_at = read_tags([in_ref], tag_ref, sems)
         here = lax.axis_index("col")
-        for d in range(col_count + 1):
+        for d in range(col_count):
             count_ref[d] = 0
         for e in range(col_count * cap):
-            plan_ref[slots_in + e] = -1
-        for e in range(slots_in):
+            plan_ref[e] = -1
+        for e in range(in_ref.shape[0]):
             tag = tag_at(e)
-            plan_ref[e] = -1
 
             @pl.when(tag >= 0)
             def _():
                 d = step_to(lax.rem(tag // blocks, col_count), here, col_count)
                 k = count_ref[d]
                 count_ref[d] = k + 1
-                j = count_ref[col_count]
-                count_ref[col_count] = j + 1
-                plan_ref[e] = j
-                plan_ref[slots_in + d * cap + k] = j
-
-    row = lax.axis_index("row")
-    for e in range(slots_in):
-        j = plan_ref[e]
-
-        @pl.when(j >= 0)
-        def _():
-            if part:
-                origin = origin_of(order[e // cap_in], row, row_count)
-                block_ref[j] = ins[0][origin * cap_in + e % cap_in]
-            else:
-                block_ref[j] = ins[e // cap_in][e % cap_in]
-
-    for e in range(col_count * cap):
-        j = plan_ref[slots_in + e]
-        out = outs[e // cap]
-
-        @pl.when(j >= 0)
-        def _():
-            out[e % cap] = block_ref[j]
-
-        if part == 0:
-
-            @pl.when(j < 0)
+                plan_ref[d * cap + k] = e
+
+    for d, out in enumerate(outs):
+        for k in range(cap):
+            e = plan_ref[d * cap + k]
+
+            @pl.when(e >= 0)
             def _():
-                out[e % cap, tiles - 1] = jnp.full((SUB, LANES), -1.0, jnp.float32)
-
-
-def repack(landed, plan, part, row_count, col_count, cap, cap_in, blocks):
-    slots_in = row_count * cap_in
-    tiles = landed[0].shape[1:]
+                out[k] = in_ref[e]
+
+            if part == 0:
+
+                @pl.when(e < 0)
+                def _():
+                    out[k, 0] = jnp.full((SUB, LANES), -1.0, jnp.float32)
+
+
+def repack(landed, plan, part, col_count, cap, blocks):
     whole = pl.BlockSpec(memory_space=pltpu.VMEM)
     scalars = pl.BlockSpec(memory_space=pltpu.SMEM)
-    length = slots_in + col_count * cap
-    scratch = [pltpu.VMEM((blocks,) + tiles, jnp.float32)]
+    scratch = []
     if part == 0:
-        scratch = tag_scratch(slots_in) + scratch + [pltpu.SMEM((col_count + 1,), jnp.int32)]
-    *packed, last = pl.pallas_call(
-        functools.partial(repack_kernel, cap, cap_in, row_count, col_count, blocks, part),
-        in_specs=([scalars] if part else []) + [whole] * len(landed),
+        scratch = tag_scratch(1, landed.shape[0]) + [pltpu.SMEM((col_count,), jnp.int32)]
+    packed = pl.pallas_call(
+        functools.partial(repack_kernel, cap, col_count, blocks, part),
+        in_specs=([scalars] if part else []) + [whole],
         out_specs=[whole] * col_count + ([] if part else [scalars]),
         scratch_shapes=scratch,
-        out_shape=[jax.ShapeDtypeStruct((cap,) + tiles, jnp.float32)] * col_count
-        + ([] if part else [jax.ShapeDtypeStruct((length,), jnp.int32)]),
+        out_shape=[jax.ShapeDtypeStruct((cap,) + landed.shape[1:], jnp.float32)] * col_count
+        + ([] if part else [jax.ShapeDtypeStruct((col_count * cap,), jnp.int32)]),
         compiler_params=pltpu.CompilerParams(vmem_limit_bytes=VMEM_LIMIT),
         cost_estimate=pl.CostEstimate(flops=0, bytes_accessed=3 * 10**6, transcendentals=0),
         name="repack_%d" % part,
-    )(*([plan] if part else []), *landed)
-    return (packed + [last], plan) if part else (packed, last)
+    )(*([plan] if part else []), landed)
+    return packed if part else (packed[:-1], packed[-1])
 
 
 def backward(zeroth, first, second, u):
@@ -398,8 +363,8 @@
 def post_kernel(count, *refs):
     ins = refs[:count]
     (
-        post_ref, ylo_ref, yhi_ref, xlo_ref, xhi_ref, plan_ref,
-        block_ref, swap_ref, side_ref, tag_ref, sems,
+        post_ref, ylo_ref, yhi_ref, xlo_ref, xhi_ref, plan_ref, side_ref,
+        block_ref, swap_ref, tag_ref, sems,
     ) = refs[count:]
     g = pl.program_id(0)
     steps = len(CHUNKS[0])
@@ -414,14 +379,14 @@
         unload(plan_ref, ins, block_ref)
         for t in range(SUB):
             for tile in range(SIDE_TILES):
-                side_ref[pl.ds(tile * SUB * SUB + t, SUB, stride=SUB), :] = block_ref[
-                    t, steps * NFIELD + tile
-                ]
+                swap_ref[pl.ds(tile * SUB * SUB + t, SUB, stride=SUB), :] = block_ref[t, tile]
         for half in range(2):
-            fields = [
-                side_ref[(half * NFIELD + n) * SUB : (half * NFIELD + n + 1) * SUB, :]
-                for n in range(NFIELD)
-            ]
+            fields = []
+            for n in range(NFIELD):
+                base = (1 + half * NFIELD + n) * SUB
+                field = swap_ref[base : base + SUB, :]
+                side_ref[half, n] = field
+                fields.append(field)
             result = post_populations(*fields)
             for i in range(3):
                 for k in range(3):
@@ -431,7 +396,9 @@
 
     for t in range(SUB):
         for n in range(NFIELD):
-            swap_ref[pl.ds(n * SUB * SUB + t, SUB, stride=SUB), :] = block_ref[t, g * NFIELD + n]
+            swap_ref[pl.ds(n * SUB * SUB + t, SUB, stride=SUB), :] = block_ref[
+                t, SIDE_TILES + g * NFIELD + n
+            ]
     group = CHUNKS[0][0]
     for step in range(1, steps):
         group = jnp.where(g == step, CHUNKS[0][step], group)
@@ -478,16 +445,18 @@
         in_specs=[pl.BlockSpec(homes[0].shape, lambda g: (0, 0, 0, 0))] * len(homes),
         out_specs=[pl.BlockSpec((NQ, SUB, SUB, LANES), lambda g: (0, g, 0, 0))]
         + [spec] * 4
-        + [pl.BlockSpec(memory_space=pltpu.SMEM)],
+        + [
+            pl.BlockSpec(memory_space=pltpu.SMEM),
+            pl.BlockSpec((2, NFIELD, SUB, LANES), lambda g: (0, 0, 0, 0)),
+        ],
         scratch_shapes=[
             pltpu.VMEM((SUB, tiles_of(0), SUB, LANES), jnp.float32),
             pltpu.VMEM((NFIELD * SUB * SUB, LANES), jnp.float32),
-            pltpu.VMEM((SIDE_TILES * SUB * SUB, LANES), jnp.float32),
         ]
-        + tag_scratch(slots),
+        + tag_scratch(len(homes), slots),
         out_shape=[shape((NQ, steps * SUB, SUB, LANES), jnp.float32)]
         + [shape(face, jnp.float32)] * 4
-        + [shape((slots,), jnp.int32)],
+        + [shape((slots,), jnp.int32), shape((2, NFIELD, SUB, LANES), jnp.float32)],
         compiler_params=pltpu.CompilerParams(vmem_limit_bytes=VMEM_LIMIT),
         cost_estimate=pl.CostEstimate(flops=10**7, bytes_accessed=3 * 10**6, transcendentals=0),
         name="post",
@@ -497,7 +466,7 @@
 def finish_kernel(count, plan_ref, *refs):
     ins = refs[:count]
     (
-        early_ref, xlo_ref, xhi_ref, below_in, above_in,
+        early_ref, side_ref, xlo_ref, xhi_ref, below_in, above_in,
         out_ref, main_ref, below_ref, above_ref, block_ref, swap_ref, sems,
     ) = refs[count:]
     g = pl.program_id(0)
@@ -515,16 +484,31 @@
         for copy in copies:
             copy.start()
         unload(plan_ref, ins, block_ref)
+        for t in range(SUB):
+            for tile in range(LATE_TILES):
+                swap_ref[pl.ds(tile * SUB * SUB + t, SUB, stride=SUB), :] = block_ref[t, tile]
+        spot = lax.broadcasted_iota(jnp.int32, (SUB, LANES), 1) // EDGE
+
+        def turned(value, places):
+            turn = places * EDGE % LANES
+            return pltpu.roll(value, turn, axis=1) if turn else value
+
         for step, group in enumerate(CHUNKS[1]):
-            for t in range(SUB):
+            last = [None] * NFIELD
+            for c in range(SUB):
+                at = (group * WIDTH + c // 2) % SUB
+                place = free_place(c)
+                fields = []
                 for n in range(NFIELD):
-                    swap_ref[pl.ds(n * SUB * SUB + t, SUB, stride=SUB), :] = block_ref[
-                        t, step * NFIELD + n
-                    ]
-            for c in range(SUB):
-                fields = [
-                    swap_ref[(n * SUB + c) * SUB : (n * SUB + c + 1) * SUB, :] for n in range(NFIELD)
-                ]
+                    if c < SUB - 1:
+                        base = ((step * NFIELD + n) * (SUB - 1) + c) * SUB
+                        row = swap_ref[base : base + SUB, :]
+                        part = turned(row, c - place)
+                        last[n] = part if c == 0 else jnp.where(spot == c, part, last[n])
+                    else:
+                        row = last[n]
+                    side = turned(side_ref[c % 2, n], place - at)
+                    fields.append(jnp.where(spot == place, side, row))
                 for q, value in enumerate(post_populations(*fields)):
                     main_ref[q, group * SUB + c] = value
         for x in range(EDGE):
@@ -587,7 +571,7 @@
                 out_ref[q, :, c * LANES : (c + 1) * LANES] = value
 
 
-def finish(plan, homes, early, xlo, xhi, below, above):
+def finish(plan, homes, early, sides, xlo, xhi, below, above):
     def whole(value):
         rank = len(value.shape)
         return pl.BlockSpec(value.shape, lambda g, *_: (0,) * rank)
@@ -599,14 +583,14 @@
             grid=(GROUPS,),
             in_specs=[whole(value) for value in homes]
             + [pl.BlockSpec(memory_space=pl.ANY)]
-            + [whole(value) for value in (xlo, xhi, below, above)],
+            + [whole(value) for value in (sides, xlo, xhi, below, above)],
             out_specs=pl.BlockSpec((NQ, SUB, SUB * LANES), lambda g, *_: (0, 0, g)),
             scratch_shapes=[
                 pltpu.VMEM((NQ, GROUPS * SUB, SUB, LANES), jnp.float32),
                 pltpu.VMEM((9, EDGE + 2, SUB, LANES), jnp.float32),
                 pltpu.VMEM((9, EDGE + 2, SUB, LANES), jnp.float32),
-                pltpu.VMEM((SUB, tiles_of(1), SUB, LANES), jnp.float32),
-                pltpu.VMEM((NFIELD * SUB * SUB, LANES), jnp.float32),
+                pltpu.VMEM((SUB, LATE_TILES, SUB, LANES), jnp.float32),
+                pltpu.VMEM((LATE_TILES * SUB * SUB, LANES), jnp.float32),
                 pltpu.SemaphoreType.DMA((len(CHUNKS[0]),)),
             ],
         ),
@@ -614,7 +598,7 @@
         compiler_params=pltpu.CompilerParams(vmem_limit_bytes=VMEM_LIMIT),
         cost_estimate=pl.CostEstimate(flops=10**7, bytes_accessed=8 * 10**6, transcendentals=0),
         name="finish",
-    )(plan, *homes, early, xlo, xhi, below, above)
+    )(plan, *homes, early, sides, xlo, xhi, below, above)
 
 
 def shifted(value, axis, step):
@@ -630,26 +614,26 @@
     cap_col = 2 * ((blocks + col_count - 1) // col_count)
     ordered = jnp.transpose(populations, (1, 0, 2))
 
-    def travel(packed, axis):
-        return [exchanged(packed[d], axis, d) if d else packed[0] for d in issue_order(len(packed))]
-
-    early_row = travel(
-        pre(ordered, destination, refinement, 0, row_count, cap_row, blocks * col_count), "row"
-    )
-    waited = START_AFTER
-    destination, early_row[waited] = lax.optimization_barrier((destination, early_row[waited]))
-    (late,) = pre(ordered, destination, refinement, 1, row_count, cap_row, blocks * col_count)
-    late_row = lax.all_to_all(late, "row", split_axis=0, concat_axis=0, tiled=True)
-    packed, plan = repack(early_row, None, 0, row_count, col_count, cap_col, cap_row, blocks)
-    early, ylo, yhi, xlo, xhi, picked = post(travel(packed, "col"))
+    in_row = [
+        lax.all_to_all(
+            pre(ordered, destination, refinement, part, row_count, cap_row, blocks * col_count),
+            "row", split_axis=0, concat_axis=0, tiled=True,
+        )
+        for part in range(2)
+    ]
+
+    def to_columns(packed):
+        return [exchanged(packed[d], "col", d) for d in range(col_count - 1, 0, -1)] + [packed[0]]
+
+    packed, plan = repack(in_row[0], None, 0, col_count, cap_col, blocks)
+    early, ylo, yhi, xlo, xhi, picked, sides = post(to_columns(packed))
     below, above = shifted(yhi, "col", 1), shifted(ylo, "col", -1)
     up = jnp.concatenate([xhi.reshape(18, SUB, LANES), below[6:, 1], above[6:, 1]])
     down = jnp.concatenate([xlo.reshape(18, SUB, LANES), below[:3, 0], above[:3, 0]])
     xlo, xhi = shifted(up, "row", 1), shifted(down, "row", -1)
-    late_row, below, above = lax.optimization_barrier((late_row, below, above))
-    packed, _ = repack([late_row], plan, 1, row_count, col_count, cap_col, cap_row, blocks)
-    homes = travel(packed, "col")
-    return jnp.transpose(finish(picked, homes, early, xlo, xhi, below, above), (1, 0, 2))
+    in_row[1], below, above = lax.optimization_barrier((in_row[1], below, above))
+    homes = to_columns(repack(in_row[1], plan, 1, col_count, cap_col, blocks))
+    return jnp.transpose(finish(picked, homes, early, sides, xlo, xhi, below, above), (1, 0, 2))
 
 
 def solution(mesh):

time: 130 us -> 96.7 us (0.74)
  waiting for transfers between devices: 77 us -> 54.2 us
  starting transfers between devices: 33.2 us -> 22.6 us
  local copies, waits for them, and re-layouts: 0.03 us -> 2.68 us
  Pallas kernels: 19.5 us -> 16.9 us
    ppermute x13 -> x6, waiting for transfers between devices: 71.7 us -> 18.3 us  [exchanged(): return lax.ppermute(value, axis, pairs)]
    all_to_all x1 -> x2, waiting for transfers between devices: 0.01 us -> 30.3 us  [on_device(): lax.all_to_all(pre(ordered, destination, refinement, part, row_count, cap...]
    ppermute x13 -> x6, starting transfers between devices: 20.5 us -> 5.08 us  [exchanged(): return lax.ppermute(value, axis, pairs)]
    all_to_all x1 -> x2, starting transfers between devices: 6.12 us -> 10.9 us  [on_device(): lax.all_to_all(pre(ordered, destination, refinement, part, row_count, cap...]
    unnamed x14 -> x4, local copies, waits for them, and re-layouts: 0.03 us -> 2.68 us
    pallas_call x2, Pallas kernels: 3.86 us -> 2.36 us  [repack(): pl.pallas_call(functools.partial(repack_kernel, cap, col_count, blocks, p...]
  transfers between devices with their start and end apart: 18 -> 12, of which waited for: 12 -> 8; matrix products, arithmetic and copies ran while one was open for 0% -> 0% of each run, Pallas kernels for 6% -> 8%
where the time goes in v6:
time: 96.7 us; the launch traced here: 96.4 us
  waiting for transfers between devices  54.2 us (56%)
  starting transfers between devices  22.6 us (23%)
  Pallas kernels  16.9 us (17%)
  local copies, waits for them, and re-layouts  2.68 us (3%)
    all_to_all x2, waiting for transfers between devices, on_device(): lax.all_to_all(pre(ordered, destination, refinement, part, row_count, cap...  30.3 us
    ppermute x6, waiting for transfers between devices, exchanged(): return lax.ppermute(value, axis, pairs)  18.3 us
    all_to_all x2, starting transfers between devices, on_device(): lax.all_to_all(pre(ordered, destination, refinement, part, row_count, cap...  10.9 us
    ppermute x4, starting transfers between devices, shifted(): lax.ppermute(value, axis, [(i, (i + step) % count) for i in range(count)])  6.57 us
    pallas_call x2, Pallas kernels, pre(): pl.pallas_call(functools.partial(pre_kernel, cap, row_count, per_row, par...  6.12 us
    ppermute x4, waiting for transfers between devices, shifted(): lax.ppermute(value, axis, [(i, (i + step) % count) for i in range(count)])  5.62 us
    pallas_call x1, Pallas kernels, finish(): pl.pallas_call(functools.partial(finish_kernel, len(homes)), grid_spec=pl...  5.14 us
    ppermute x6, starting transfers between devices, exchanged(): return lax.ppermute(value, axis, pairs)  5.08 us
  transfers between devices with their start and end apart: 12, of which 8 were waited for; matrix products, arithmetic and copies ran while one was open for 0% of the time, Pallas kernels for 8%

profile of v6, /device:TPU:0, one launch (start us, length us, event | category | flops | bytes accessed | tf_op | source)
XLA Modules:
  0.0 96.4 jit_solution(13261069955737402752)
XLA Ops:
  0.0 3.4 %pre_0.1 = f32[16,21,8,128]{3,2,1,0:T(8,128)} custom-call(s32[8]{0:T(128)} %dest_hbm.3, s32[8]{0:T(128)} %level_hbm.3, f32[27,8,4096]{2,1,0:T(8,128)} %bitcast.14), custom_call_target="tpu_custom_call" | custom-call | flops 10000000 | bytes 4000000 | tf_op jit(solution)/shard_map/pre_0/pallas_call | solution.py:201
  3.4 7.3 %all-to-all-start = ((f32[16,21,8,128]{3,2,1,0:T(8,128)}), f32[16,21,8,128]{3,2,1,0:T(8,128)S(1)}, u32[]{:S(2)}, u32[]{:S(2)}) async-start(f32[16,21,8,128]{3,2,1,0:T(8,128)} %pre_0.1), calls=%async_computation | async-start | bytes 2752512 | tf_op jit(solution)/shard_map/all_to_all | solution.py:618
  10.7 2.7 %pre_1.1 = f32[16,16,8,128]{3,2,1,0:T(8,128)} custom-call(s32[8]{0:T(128)} %dest_hbm.3, s32[8]{0:T(128)} %level_hbm.3, f32[27,8,4096]{2,1,0:T(8,128)} %bitcast.15), custom_call_target="tpu_custom_call" | custom-call | flops 10000000 | bytes 4000000 | tf_op jit(solution)/shard_map/pre_1/pallas_call | solution.py:201
  13.4 30.1 %all-to-all-done.refs_0_ = f32[16,21,8,128]{3,2,1,0:T(8,128)S(1)} async-done(((f32[16,21,8,128]{3,2,1,0:T(8,128)}), f32[16,21,8,128]{3,2,1,0:T(8,128)S(1)}, u32[]{:S(2)}, u32[]{:S(2)}) %all-to-all-start) | async-done | bytes 1376288 | tf_op jit(solution)/shard_map/all_to_all | solution.py:618
  43.5 3.6 %all-to-all-start.1 = ((f32[16,16,8,128]{3,2,1,0:T(8,128)}), f32[16,16,8,128]{3,2,1,0:T(8,128)S(1)}, u32[]{:S(2)}, u32[]{:S(2)}) async-start(f32[16,16,8,128]{3,2,1,0:T(8,128)} %pre_1.1), calls=%async_computation.1 | async-start | bytes 2097152 | tf_op jit(solution)/shard_map/all_to_all | solution.py:618
  47.1 1.7 %repack_0.1 = (f32[4,21,8,128]{3,2,1,0:T(8,128)S(1)}, f32[4,21,8,128]{3,2,1,0:T(8,128)S(1)}, f32[4,21,8,128]{3,2,1,0:T(8,128)S(1)}, f32[4,21,8,128]{3,2,1,0:T(8,128)S(1)}, s32[16]{0:T(128)S(1)}) custom-call(f32[16,21,8,128]{3,2,1,0:T(8,128)S(1)} %all-to-all-done.refs_0_), custom_call_target="tpu_custom_call" | custom-call | bytes 3000000 | tf_op jit(solution)/shard_map/repack_0/pallas_call | solution.py:280
  48.8 0.9 collective-permute-start
  49.7 0.7 collective-permute-start.1
  50.4 0.3 collective-permute-start.2
  50.7 8.4 %collective-permute-done.refs_0_ = f32[4,21,8,128]{3,2,1,0:T(8,128)S(1)} collective-permute-done((f32[4,21,8,128]{3,2,1,0:T(8,128)S(1)}, f32[4,21,8,128]{3,2,1,0:T(8,128)S(1)}, u32[]{:S(2)}, u32[]{:S(2)}) %collective-permute-start) | collective-permute-done | bytes 344096 | tf_op jit(solution)/shard_map/ppermute | solution.py:49
  59.1 7.4 %collective-permute-done.1.refs_1_ = f32[4,21,8,128]{3,2,1,0:T(8,128)S(1)} collective-permute-done((f32[4,21,8,128]{3,2,1,0:T(8,128)S(1)}, f32[4,21,8,128]{3,2,1,0:T(8,128)S(1)}, u32[]{:S(2)}, u32[]{:S(2)}) %collective-permute-start.1) | collective-permute-done | bytes 344096 | tf_op jit(solution)/shard_map/ppermute | solution.py:49
  66.6 0.0 collective-permute-done.2.refs_2_
  66.6 3.2 %post.1 = (f32[27,16,8,128]{3,2,1,0:T(8,128)S(1)}, f32[9,2,8,128]{3,2,1,0:T(8,128)S(1)}, f32[9,2,8,128]{3,2,1,0:T(8,128)S(1)}, f32[9,2,8,128]{3,2,1,0:T(8,128)S(...) custom-call(f32[4,21,8,128]{3,2,1,0:T(8,128)S(1)} %collective-permute-done.refs_0_, ...), custom_call_target="tpu_custom_call" | custom-call | flops 10000000 | bytes 3000000 | tf_op jit(solution)/shard_map/post/pallas_call | solution.py:442
  69.8 0.0 copy-start
  69.8 1.2 %copy-done = f32[27,16,8,128]{3,2,1,0:T(8,128)} copy-done((f32[27,16,8,128]{3,2,1,0:T(8,128)}, f32[27,16,8,128]{3,2,1,0:T(8,128)S(1)}, u32[]{:S(2)}) %copy-start) | copy-done | bytes 1769496
  71.0 0.0 collective-permute-start.3
  71.1 1.7 %collective-permute-start.4 = (f32[9,2,8,128]{3,2,1,0:T(8,128)S(1)}, f32[9,2,8,128]{3,2,1,0:T(8,128)S(1)}, u32[]{:S(2)}, u32[]{:S(2)}) collective-permute-start(f32[9,2,8,128]{3,2,1,0:T(8,128)S(1)} %get-tuple-element.31), channel_id=1, source_target_pairs={{0,3},{1,0},{2,1},{3,2},{4,7},{5,4},{6,5},{7,6},{8,11},{9,8},{10,9... | collective-permute-start | bytes 221192 | tf_op jit(solution)/shard_map/ppermute | solution.py:606
  72.8 0.3 all-to-all-done.1.refs_1_
  73.1 1.8 %collective-permute-done.3.refs_8_ = f32[9,2,8,128]{3,2,1,0:T(8,128)S(1)} collective-permute-done((f32[9,2,8,128]{3,2,1,0:T(8,128)S(1)}, f32[9,2,8,128]{3,2,1,0:T(8,128)S(1)}, u32[]{:S(2)}, u32[]{:S(2)}) %collective-permute-start.3) | collective-permute-done | bytes 73760 | tf_op jit(solution)/shard_map/ppermute | solution.py:606
  74.8 0.0 collective-permute-done.4.refs_9_
  74.8 0.7 repack_1.1
  75.5 1.8 %collective-permute-start.5 = (f32[4,16,8,128]{3,2,1,0:T(8,128)S(1)}, f32[4,16,8,128]{3,2,1,0:T(8,128)S(1)}, u32[]{:S(2)}, u32[]{:S(2)}) collective-permute-start(f32[4,16,8,128]{3,2,1,0:T(8,128)S(1)} %get-tuple-element.33), channel_id=1, source_target_pairs={{0,3},{1,2},{2,1},{3,0},{4,7},{5,6},{6,5},{7,4},{8,11},{9,10},{10,... | collective-permute-start | bytes 786440 | tf_op jit(solution)/shard_map/ppermute | solution.py:49
  77.3 1.3 %collective-permute-start.6 = (f32[4,16,8,128]{3,2,1,0:T(8,128)S(1)}, f32[4,16,8,128]{3,2,1,0:T(8,128)S(1)}, u32[]{:S(2)}, u32[]{:S(2)}) collective-permute-start(f32[4,16,8,128]{3,2,1,0:T(8,128)S(1)} %get-tuple-element.34), channel_id=1, source_target_pairs={{0,2},{1,3},{2,0},{3,1},{4,6},{5,7},{6,4},{7,5},{8,10},{9,11},{10,... | collective-permute-start | bytes 786440 | tf_op jit(solution)/shard_map/ppermute | solution.py:49
  78.7 1.6 %collective-permute-start.8 = (f32[24,8,128]{2,1,0:T(8,128)S(1)}, f32[24,8,128]{2,1,0:T(8,128)S(1)}, u32[]{:S(2)}, u32[]{:S(2)}) collective-permute-start(f32[24,8,128]{2,1,0:T(8,128)S(1)} %pad_maximum_fusion), channel_id=1, source_target_pairs={{0,4},{4,8},{8,12},{12,16},{16,20},{20,24},{24,28},{28,0},{1,5},{5... | collective-permute-start | bytes 294920 | tf_op jit(solution)/shard_map/ppermute | solution.py:606
  80.3 3.2 %collective-permute-start.9 = (f32[24,8,128]{2,1,0:T(8,128)S(1)}, f32[24,8,128]{2,1,0:T(8,128)S(1)}, u32[]{:S(2)}, u32[]{:S(2)}) collective-permute-start(f32[24,8,128]{2,1,0:T(8,128)S(1)} %pad_maximum_fusion.1), channel_id=1, source_target_pairs={{0,28},{4,0},{8,4},{12,8},{16,12},{20,16},{24,20},{28,24},{1,29},{... | collective-permute-start | bytes 294920 | tf_op jit(solution)/shard_map/ppermute | solution.py:606
  83.5 3.2 %collective-permute-done.8.refs_6_ = f32[24,8,128]{2,1,0:T(8,128)S(1)} collective-permute-done((f32[24,8,128]{2,1,0:T(8,128)S(1)}, f32[24,8,128]{2,1,0:T(8,128)S(1)}, u32[]{:S(2)}, u32[]{:S(2)}) %collective-permute-start.8) | collective-permute-done | bytes 98336 | tf_op jit(solution)/shard_map/ppermute | solution.py:606
  86.8 0.6 collective-permute-done.9.refs_7_
  87.4 0.0 collective-permute-done.5.refs_0_
  87.4 2.4 %collective-permute-done.6.refs_1_ = f32[4,16,8,128]{3,2,1,0:T(8,128)S(1)} collective-permute-done((f32[4,16,8,128]{3,2,1,0:T(8,128)S(1)}, f32[4,16,8,128]{3,2,1,0:T(8,128)S(1)}, u32[]{:S(2)}, u32[]{:S(2)}) %collective-permute-start.6) | collective-permute-done | bytes 262176 | tf_op jit(solution)/shard_map/ppermute | solution.py:49
  89.8 0.0 collective-permute-done.7.refs_2_
  89.8 1.5 %copy-done.1 = f32[27,16,8,128]{3,2,1,0:T(8,128)S(1)} copy-done((f32[27,16,8,128]{3,2,1,0:T(8,128)S(1)}, f32[27,16,8,128]{3,2,1,0:T(8,128)}, u32[]{:S(2)}) %copy-start.1) | copy-done | bytes 1769496
  91.3 5.1 %finish.1 = f32[27,8,4096]{2,1,0:T(8,128)} custom-call(s32[16]{0:T(128)S(1)} %get-tuple-element.28.plan_ref, f32[4,16,8,128]{3,2,1,0:T(8,128)S(1)} %collective-permute-done.5.refs_0_, f32[4,16,8,128]{3,2,1,0:T(8,128)S(1)} %collective-permute-done.6.refs_1_, f32[4,16,8,128]{3,2,1,0:T(8,128)S(1)} %collective-permute-done.7.refs_2_, ...), custom_call_target="tpu_custom_call" | custom-call | flops 10000000 | bytes 8000000 | tf_op jit(solution)/shard_map/finish/pallas_call | solution.py:579
  (6 shorter events, 0.0 us)
Async XLA Ops:
  3.4 40.1 %all-to-all-start = ((f32[16,21,8,128]{3,2,1,0:T(8,128)}), f32[16,21,8,128]{3,2,1,0:T(8,128)S(1)}, u32[]{:S(2)}, u32[]{:S(2)}) async-start(f32[16,21,8,128]{3,2,1,0:T(8,128)} %pre_0.1), calls=%async_computation | async-start | bytes 2752512 | tf_op jit(solution)/shard_map/all_to_all | solution.py:618
  43.5 29.6 %all-to-all-start.1 = ((f32[16,16,8,128]{3,2,1,0:T(8,128)}), f32[16,16,8,128]{3,2,1,0:T(8,128)S(1)}, u32[]{:S(2)}, u32[]{:S(2)}) async-start(f32[16,16,8,128]{3,2,1,0:T(8,128)} %pre_1.1), calls=%async_computation.1 | async-start | bytes 2097152 | tf_op jit(solution)/shard_map/all_to_all | solution.py:618
  48.8 10.4 %collective-permute-start = (f32[4,21,8,128]{3,2,1,0:T(8,128)S(1)}, f32[4,21,8,128]{3,2,1,0:T(8,128)S(1)}, u32[]{:S(2)}, u32[]{:S(2)}) collective-permute-start(f32[4,21,8,128]{3,2,1,0:T(8,128)S(1)} %get-tuple-element.24), channel_id=1, source_target_pairs={{0,3},{1,2},{2,1},{3,0},{4,7},{5,6},{6,5},{7,4},{8,11},{9,10},{10,... | collective-permute-start | bytes 1032200 | tf_op jit(solution)/shard_map/ppermute | solution.py:49
  49.7 16.9 %collective-permute-start.1 = (f32[4,21,8,128]{3,2,1,0:T(8,128)S(1)}, f32[4,21,8,128]{3,2,1,0:T(8,128)S(1)}, u32[]{:S(2)}, u32[]{:S(2)}) collective-permute-start(f32[4,21,8,128]{3,2,1,0:T(8,128)S(1)} %get-tuple-element.25), channel_id=1, source_target_pairs={{0,2},{1,3},{2,0},{3,1},{4,6},{5,7},{6,4},{7,5},{8,10},{9,11},{10,... | collective-permute-start | bytes 1032200 | tf_op jit(solution)/shard_map/ppermute | solution.py:49
  50.4 16.1 %collective-permute-start.2 = (f32[4,21,8,128]{3,2,1,0:T(8,128)S(1)}, f32[4,21,8,128]{3,2,1,0:T(8,128)S(1)}, u32[]{:S(2)}, u32[]{:S(2)}) collective-permute-start(f32[4,21,8,128]{3,2,1,0:T(8,128)S(1)} %get-tuple-element.26), channel_id=1, source_target_pairs={{0,1},{1,0},{2,3},{3,2},{4,5},{5,4},{6,7},{7,6},{8,9},{9,8},{10,11... | collective-permute-start | bytes 1032200 | tf_op jit(solution)/shard_map/ppermute | solution.py:49
  69.8 1.2 %copy-start = (f32[27,16,8,128]{3,2,1,0:T(8,128)}, f32[27,16,8,128]{3,2,1,0:T(8,128)S(1)}, u32[]{:S(2)}) copy-start(f32[27,16,8,128]{3,2,1,0:T(8,128)S(1)} %get-tuple-element.37.refs_4_) | copy-start | bytes 5308420
  71.0 3.8 %collective-permute-start.3 = (f32[9,2,8,128]{3,2,1,0:T(8,128)S(1)}, f32[9,2,8,128]{3,2,1,0:T(8,128)S(1)}, u32[]{:S(2)}, u32[]{:S(2)}) collective-permute-start(f32[9,2,8,128]{3,2,1,0:T(8,128)S(1)} %get-tuple-element.30), channel_id=1, source_target_pairs={{0,1},{1,2},{2,3},{3,0},{4,5},{5,6},{6,7},{7,4},{8,9},{9,10},{10,1... | collective-permute-start | bytes 221192 | tf_op jit(solution)/shard_map/ppermute | solution.py:606
  71.1 3.7 %collective-permute-start.4 = (f32[9,2,8,128]{3,2,1,0:T(8,128)S(1)}, f32[9,2,8,128]{3,2,1,0:T(8,128)S(1)}, u32[]{:S(2)}, u32[]{:S(2)}) collective-permute-start(f32[9,2,8,128]{3,2,1,0:T(8,128)S(1)} %get-tuple-element.31), channel_id=1, source_target_pairs={{0,3},{1,0},{2,1},{3,2},{4,7},{5,4},{6,5},{7,6},{8,11},{9,8},{10,9... | collective-permute-start | bytes 221192 | tf_op jit(solution)/shard_map/ppermute | solution.py:606
  75.5 11.9 %collective-permute-start.5 = (f32[4,16,8,128]{3,2,1,0:T(8,128)S(1)}, f32[4,16,8,128]{3,2,1,0:T(8,128)S(1)}, u32[]{:S(2)}, u32[]{:S(2)}) collective-permute-start(f32[4,16,8,128]{3,2,1,0:T(8,128)S(1)} %get-tuple-element.33), channel_id=1, source_target_pairs={{0,3},{1,2},{2,1},{3,0},{4,7},{5,6},{6,5},{7,4},{8,11},{9,10},{10,... | collective-permute-start | bytes 786440 | tf_op jit(solution)/shard_map/ppermute | solution.py:49
  77.3 12.5 %collective-permute-start.6 = (f32[4,16,8,128]{3,2,1,0:T(8,128)S(1)}, f32[4,16,8,128]{3,2,1,0:T(8,128)S(1)}, u32[]{:S(2)}, u32[]{:S(2)}) collective-permute-start(f32[4,16,8,128]{3,2,1,0:T(8,128)S(1)} %get-tuple-element.34), channel_id=1, source_target_pairs={{0,2},{1,3},{2,0},{3,1},{4,6},{5,7},{6,4},{7,5},{8,10},{9,11},{10,... | collective-permute-start | bytes 786440 | tf_op jit(solution)/shard_map/ppermute | solution.py:49
  78.7 11.1 %collective-permute-start.7 = (f32[4,16,8,128]{3,2,1,0:T(8,128)S(1)}, f32[4,16,8,128]{3,2,1,0:T(8,128)S(1)}, u32[]{:S(2)}, u32[]{:S(2)}) collective-permute-start(f32[4,16,8,128]{3,2,1,0:T(8,128)S(1)} %get-tuple-element.35), channel_id=1, source_target_pairs={{0,1},{1,0},{2,3},{3,2},{4,5},{5,4},{6,7},{7,6},{8,9},{9,8},{10,11... | collective-permute-start | bytes 786440 | tf_op jit(solution)/shard_map/ppermute | solution.py:49
  78.7 8.1 %collective-permute-start.8 = (f32[24,8,128]{2,1,0:T(8,128)S(1)}, f32[24,8,128]{2,1,0:T(8,128)S(1)}, u32[]{:S(2)}, u32[]{:S(2)}) collective-permute-start(f32[24,8,128]{2,1,0:T(8,128)S(1)} %pad_maximum_fusion), channel_id=1, source_target_pairs={{0,4},{4,8},{8,12},{12,16},{16,20},{20,24},{24,28},{28,0},{1,5},{5... | collective-permute-start | bytes 294920 | tf_op jit(solution)/shard_map/ppermute | solution.py:606
  80.3 7.1 %collective-permute-start.9 = (f32[24,8,128]{2,1,0:T(8,128)S(1)}, f32[24,8,128]{2,1,0:T(8,128)S(1)}, u32[]{:S(2)}, u32[]{:S(2)}) collective-permute-start(f32[24,8,128]{2,1,0:T(8,128)S(1)} %pad_maximum_fusion.1), channel_id=1, source_target_pairs={{0,28},{4,0},{8,4},{12,8},{16,12},{20,16},{24,20},{28,24},{1,29},{... | collective-permute-start | bytes 294920 | tf_op jit(solution)/shard_map/ppermute | solution.py:606
  89.8 1.5 %copy-start.1 = (f32[27,16,8,128]{3,2,1,0:T(8,128)S(1)}, f32[27,16,8,128]{3,2,1,0:T(8,128)}, u32[]{:S(2)}) copy-start(f32[27,16,8,128]{3,2,1,0:T(8,128)} %copy-done) | copy-start | bytes 5308420

commit v7 on v6

--- a/solution.py
+++ b/solution.py
@@ -15,11 +15,12 @@
 NFIELD = 9
 GROUPS = 4
 WIDTH = EDGE // GROUPS
-CHUNKS = ((0, 3), (1, 2))
+CHUNKS = ((0, 3), (1,), (2,))
+INNER = (1, 2)
 SIDE_TILES = 3
-LATE_TILES = -(-2 * NFIELD * (SUB - 1) // SUB)
+LATE_TILES = -(-NFIELD * (SUB - 1) // SUB)
 VMEM_LIMIT = 20 * 1024 * 1024
-PRE_VMEM_LIMIT = 60 * 1024 * 1024
+LARGE_VMEM_LIMIT = 60 * 1024 * 1024
 
 
 def velocity(q):
@@ -96,7 +97,7 @@
 
 def pre_kernel(cap, row_count, per_row, part, dest_hbm, level_hbm, x_hbm, out_ref, *refs):
     x_ref, swap_ref, packed_ref, side_ref, dest_ref, level_ref, sems = refs
-    order = CHUNKS[1] if part else CHUNKS[0] + CHUNKS[1]
+    order = CHUNKS[part] if part else CHUNKS[0] + INNER
     steps = len(CHUNKS[part])
     blocks = x_ref.shape[2]
     cells = x_ref.shape[3]
@@ -196,7 +197,7 @@
 def pre(populations, destination, refinement, part, row_count, cap, per_row):
     blocks = populations.shape[1]
     cells = populations.shape[2] // GROUPS
-    loaded = len(CHUNKS[part]) + (0 if part else len(CHUNKS[1]))
+    loaded = len(CHUNKS[part]) + (0 if part else len(INNER))
     rows = LATE_TILES * SUB if part else NFIELD * cells // LANES
     return pl.pallas_call(
         functools.partial(pre_kernel, cap, row_count, per_row, part),
@@ -212,7 +213,7 @@
             pltpu.SMEM((blocks,), jnp.int32),
             pltpu.SemaphoreType.DMA((2 + loaded,)),
         ],
-        compiler_params=pltpu.CompilerParams(vmem_limit_bytes=PRE_VMEM_LIMIT),
+        compiler_params=pltpu.CompilerParams(vmem_limit_bytes=LARGE_VMEM_LIMIT),
         cost_estimate=pl.CostEstimate(flops=10**7, bytes_accessed=4 * 10**6, transcendentals=0),
         name="pre_%d" % part,
     )(destination, refinement, populations)
@@ -346,186 +347,75 @@
     return result
 
 
-def unload(plan_ref, ins, block_ref):
-    cap = ins[0].shape[0]
+def unload(plan_ref, ins, fields_ref):
+    cap, tiles = ins[0].shape[:2]
     for e in range(len(ins) * cap):
         t = plan_ref[e]
 
         @pl.when(t >= 0)
         def _():
-            block_ref[t] = ins[e // cap][e % cap]
-
-
-def side_spot(lane, x):
-    return (lane // EDGE) == x % SUB
-
-
-def post_kernel(count, *refs):
-    ins = refs[:count]
-    (
-        post_ref, ylo_ref, yhi_ref, xlo_ref, xhi_ref, plan_ref, side_ref,
-        block_ref, swap_ref, tag_ref, sems,
-    ) = refs[count:]
-    g = pl.program_id(0)
-    steps = len(CHUNKS[0])
-    lane = lax.broadcasted_iota(jnp.int32, (SUB, LANES), 1)
-
-    @pl.when(g == 0)
-    def _():
-        tag_at = read_tags(ins, tag_ref, sems)
-        for e in range(count * ins[0].shape[0]):
-            tag = tag_at(e)
-            plan_ref[e] = jnp.where(tag >= 0, lax.rem(tag, SUB), -1)
-        unload(plan_ref, ins, block_ref)
-        for t in range(SUB):
-            for tile in range(SIDE_TILES):
-                swap_ref[pl.ds(tile * SUB * SUB + t, SUB, stride=SUB), :] = block_ref[t, tile]
-        for half in range(2):
-            fields = []
-            for n in range(NFIELD):
-                base = (1 + half * NFIELD + n) * SUB
-                field = swap_ref[base : base + SUB, :]
-                side_ref[half, n] = field
-                fields.append(field)
-            result = post_populations(*fields)
-            for i in range(3):
-                for k in range(3):
-                    value = result[i * 9 + 6 * half + k]
-                    for tile in range(2):
-                        (yhi_ref if half else ylo_ref)[i * 3 + k, tile] = value
-
-    for t in range(SUB):
+            for tile in range(tiles):
+                fields_ref[pl.ds(tile * SUB * SUB + t, SUB, stride=SUB), :] = ins[e // cap][e % cap, tile]
+
+
+def row_of(ref, row):
+    return ref[row * SUB : (row + 1) * SUB, :]
+
+
+def turned(value, places):
+    turn = places * EDGE % LANES
+    return pltpu.roll(value, turn, axis=1) if turn else value
+
+
+def places_y():
+    return lax.broadcasted_iota(jnp.int32, (SUB, LANES), 1) // EDGE
+
+
+def outer_fields(fields_ref, step, c):
+    first = (SIDE_TILES + step * NFIELD) * SUB
+    return [row_of(fields_ref, first + n * SUB + c) for n in range(NFIELD)]
+
+
+def side_fields(fields_ref, half):
+    return [row_of(fields_ref, 1 + half * NFIELD + n) for n in range(NFIELD)]
+
+
+def fill_outer(fields_ref, main_ref):
+    for step, group in enumerate(CHUNKS[0]):
+        for c in range(SUB):
+            for q, value in enumerate(post_populations(*outer_fields(fields_ref, step, c))):
+                main_ref[q, 2 + group * SUB + c] = value
+
+
+def fill_inner(fields_ref, late_ref, group, main_ref):
+    spot = places_y()
+    last = [None] * NFIELD
+    for c in range(SUB):
+        at = (group * WIDTH + c // 2) % SUB
+        place = free_place(c)
+        side = side_fields(fields_ref, c % 2)
+        fields = []
         for n in range(NFIELD):
-            swap_ref[pl.ds(n * SUB * SUB + t, SUB, stride=SUB), :] = block_ref[
-                t, SIDE_TILES + g * NFIELD + n
-            ]
-    group = CHUNKS[0][0]
-    for step in range(1, steps):
-        group = jnp.where(g == step, CHUNKS[0][step], group)
-    for c in range(SUB):
-        fields = [swap_ref[(n * SUB + c) * SUB : (n * SUB + c + 1) * SUB, :] for n in range(NFIELD)]
-        result = post_populations(*fields)
-        for q in range(NQ):
-            post_ref[q, c] = result[q]
-        x_in, half = c // 2, c % 2
-        x = group * WIDTH + x_in
-        inside = side_spot(lane, x)
-        face_ref, first, shift = ((ylo_ref, 0, 0), (yhi_ref, 6, EDGE))[half]
-        turn = ((x % SUB) * EDGE + shift) % LANES
-        for i in range(3):
-            for k in range(3):
-                value = pltpu.roll(result[i * 9 + first + k], turn, axis=1)
-                at = (i * 3 + k, x // SUB)
-                face_ref[at] = jnp.where(inside, value, face_ref[at])
-
-        if x_in == 0:
-
-            @pl.when(group == 0)
-            def _():
-                for q in range(9):
-                    xlo_ref[q, half] = result[q]
-
-        if x_in == WIDTH - 1:
-
-            @pl.when(group == GROUPS - 1)
-            def _():
-                for q in range(9):
-                    xhi_ref[q, half] = result[18 + q]
-
-
-def post(homes):
-    shape = jax.ShapeDtypeStruct
-    face = (9, 2, SUB, LANES)
-    steps = len(CHUNKS[0])
-    slots = len(homes) * homes[0].shape[0]
-    spec = pl.BlockSpec(face, lambda g: (0, 0, 0, 0))
-    return pl.pallas_call(
-        functools.partial(post_kernel, len(homes)),
-        grid=(steps,),
-        in_specs=[pl.BlockSpec(homes[0].shape, lambda g: (0, 0, 0, 0))] * len(homes),
-        out_specs=[pl.BlockSpec((NQ, SUB, SUB, LANES), lambda g: (0, g, 0, 0))]
-        + [spec] * 4
-        + [
-            pl.BlockSpec(memory_space=pltpu.SMEM),
-            pl.BlockSpec((2, NFIELD, SUB, LANES), lambda g: (0, 0, 0, 0)),
-        ],
-        scratch_shapes=[
-            pltpu.VMEM((SUB, tiles_of(0), SUB, LANES), jnp.float32),
-            pltpu.VMEM((NFIELD * SUB * SUB, LANES), jnp.float32),
-        ]
-        + tag_scratch(len(homes), slots),
-        out_shape=[shape((NQ, steps * SUB, SUB, LANES), jnp.float32)]
-        + [shape(face, jnp.float32)] * 4
-        + [shape((slots,), jnp.int32), shape((2, NFIELD, SUB, LANES), jnp.float32)],
-        compiler_params=pltpu.CompilerParams(vmem_limit_bytes=VMEM_LIMIT),
-        cost_estimate=pl.CostEstimate(flops=10**7, bytes_accessed=3 * 10**6, transcendentals=0),
-        name="post",
-    )(*homes)
-
-
-def finish_kernel(count, plan_ref, *refs):
-    ins = refs[:count]
-    (
-        early_ref, side_ref, xlo_ref, xhi_ref, below_in, above_in,
-        out_ref, main_ref, below_ref, above_ref, block_ref, swap_ref, sems,
-    ) = refs[count:]
-    g = pl.program_id(0)
-
-    @pl.when(g == 0)
-    def _():
-        copies = [
-            pltpu.make_async_copy(
-                early_ref.at[:, pl.ds(step * SUB, SUB)],
-                main_ref.at[:, pl.ds(group * SUB, SUB)],
-                sems.at[step],
-            )
-            for step, group in enumerate(CHUNKS[0])
-        ]
-        for copy in copies:
-            copy.start()
-        unload(plan_ref, ins, block_ref)
-        for t in range(SUB):
-            for tile in range(LATE_TILES):
-                swap_ref[pl.ds(tile * SUB * SUB + t, SUB, stride=SUB), :] = block_ref[t, tile]
-        spot = lax.broadcasted_iota(jnp.int32, (SUB, LANES), 1) // EDGE
-
-        def turned(value, places):
-            turn = places * EDGE % LANES
-            return pltpu.roll(value, turn, axis=1) if turn else value
-
-        for step, group in enumerate(CHUNKS[1]):
-            last = [None] * NFIELD
-            for c in range(SUB):
-                at = (group * WIDTH + c // 2) % SUB
-                place = free_place(c)
-                fields = []
-                for n in range(NFIELD):
-                    if c < SUB - 1:
-                        base = ((step * NFIELD + n) * (SUB - 1) + c) * SUB
-                        row = swap_ref[base : base + SUB, :]
-                        part = turned(row, c - place)
-                        last[n] = part if c == 0 else jnp.where(spot == c, part, last[n])
-                    else:
-                        row = last[n]
-                    side = turned(side_ref[c % 2, n], place - at)
-                    fields.append(jnp.where(spot == place, side, row))
-                for q, value in enumerate(post_populations(*fields)):
-                    main_ref[q, group * SUB + c] = value
-        for x in range(EDGE):
-            at = x % SUB
-            for k in range(9):
-                packed = below_in[k, x // SUB]
-                below_ref[k, x + 1] = pltpu.roll(packed, (LANES - EDGE - EDGE * at) % LANES, axis=1)
-                packed = above_in[k, x // SUB]
-                above_ref[k, x + 1] = pltpu.roll(packed, (LANES - EDGE * at) % LANES, axis=1)
-        for k in range(3):
-            below_ref[6 + k, 0] = xlo_ref[18 + k]
-            above_ref[6 + k, 0] = pltpu.roll(xlo_ref[21 + k], EDGE, axis=1)
-            below_ref[k, EDGE + 1] = pltpu.roll(xhi_ref[18 + k], LANES - EDGE, axis=1)
-            above_ref[k, EDGE + 1] = xhi_ref[21 + k]
-        for copy in copies:
-            copy.wait()
-
+            if c < SUB - 1:
+                row = row_of(late_ref, n * (SUB - 1) + c)
+                part = turned(row, c - place)
+                last[n] = part if c == 0 else jnp.where(spot == c, part, last[n])
+            else:
+                row = last[n]
+            fields.append(jnp.where(spot == place, turned(side[n], place - at), row))
+        for q, value in enumerate(post_populations(*fields)):
+            main_ref[q, 2 + group * SUB + c] = value
+
+
+def fill_sides(below_in, above_in, below_ref, above_ref, first, last):
+    for x in range(first, last):
+        at = x % SUB
+        for k in range(9):
+            below_ref[k, x + 1] = turned(below_in[k, x // SUB], SUB - 1 - at)
+            above_ref[k, x + 1] = turned(above_in[k, x // SUB], -at)
+
+
+def stream_pair(first_x, out_ref, main_ref, below_ref, above_ref):
     lane = lax.broadcasted_iota(jnp.int32, (SUB, LANES), 1)
     block = lax.broadcasted_iota(jnp.int32, (SUB, LANES), 0)
     along = lane % EDGE
@@ -533,72 +423,211 @@
     floor = first_z & (block == 0)
     ceiling = last_z & (block == SUB - 1)
     low_y, high_y = lane < EDGE, lane >= LANES - EDGE
-
-    for x in range(WIDTH):
-
-        def source(q, half):
-            at = x - velocity(q)[0]
-            row = (g * WIDTH + at) * 2 + half
-            if at < 0:
-                inside = main_ref[q, jnp.maximum(row, 0)]
-                return jnp.where(g == 0, xlo_ref[(q - 18) * 2 + half], inside)
-            if at >= WIDTH:
-                inside = main_ref[q, jnp.minimum(row, GROUPS * SUB - 1)]
-                return jnp.where(g == GROUPS - 1, xhi_ref[q * 2 + half], inside)
-            return main_ref[q, row]
-
+    for i in range(2):
         for half in range(2):
-            c = x * 2 + half
+            c = i * 2 + half
             for q in range(NQ):
                 cx, cy, cz = velocity(q)
-                a = source(q, half)
-                side = g * WIDTH + x - cx + 1
+                x = first_x + i - cx + 1
+                a = main_ref[q, x * 2 + half]
                 k = (cx + 1) * 3 + cz + 1
                 if cy == 1:
-                    a = jnp.where(high_y, below_ref[k, side] if half == 0 else source(q, 0), a)
+                    a = jnp.where(high_y, main_ref[q, x * 2] if half else below_ref[k, x], a)
                 elif cy == -1:
-                    a = jnp.where(low_y, above_ref[k, side] if half == 1 else source(q, 1), a)
+                    a = jnp.where(low_y, above_ref[k, x] if half else main_ref[q, x * 2 + 1], a)
                 shift = EDGE * cy + cz
                 value = a if shift == 0 else pltpu.roll(a, shift % LANES, axis=1)
-                if cz == 1:
-                    fill = pltpu.roll(pltpu.roll(a, 1, axis=0), (shift - EDGE) % LANES, axis=1)
-                    value = jnp.where(first_z, fill, value)
-                    value = jnp.where(floor, main_ref[26 - q, g * SUB + c], value)
-                elif cz == -1:
-                    fill = pltpu.roll(pltpu.roll(a, SUB - 1, axis=0), (shift + EDGE) % LANES, axis=1)
-                    value = jnp.where(last_z, fill, value)
-                    value = jnp.where(ceiling, main_ref[26 - q, g * SUB + c], value)
+                if cz:
+                    bounced = main_ref[26 - q, (first_x + i + 1) * 2 + half]
+                    turn = (1 if cz == 1 else SUB - 1)
+                    fill = pltpu.roll(pltpu.roll(a, turn, axis=0), (shift - cz * EDGE) % LANES, axis=1)
+                    value = jnp.where(first_z if cz == 1 else last_z, fill, value)
+                    value = jnp.where(floor if cz == 1 else ceiling, bounced, value)
                 out_ref[q, :, c * LANES : (c + 1) * LANES] = value
 
 
-def finish(plan, homes, early, sides, xlo, xhi, below, above):
-    def whole(value):
-        rank = len(value.shape)
-        return pl.BlockSpec(value.shape, lambda g, *_: (0,) * rank)
-
+def faces_kernel(count, *refs):
+    ins = refs[:count]
+    ylo_ref, yhi_ref, xlo_ref, xhi_ref, plan_ref, fields_ref, tag_ref, sems = refs[count:]
+    tag_at = read_tags(ins, tag_ref, sems)
+    for e in range(count * ins[0].shape[0]):
+        tag = tag_at(e)
+        plan_ref[e] = jnp.where(tag >= 0, lax.rem(tag, SUB), -1)
+    unload(plan_ref, ins, fields_ref)
+    spot = places_y()
+    for half in range(2):
+        packed = [side_fields(fields_ref, half)] * 2
+        place = half * (SUB - 1)
+        for step, group in enumerate(CHUNKS[0]):
+            tile = group * WIDTH // SUB
+            for x in range(group * WIDTH, (group + 1) * WIDTH):
+                c = (x - group * WIDTH) * 2 + half
+                packed[tile] = [
+                    jnp.where(spot == x % SUB, turned(value, x % SUB - place), old)
+                    for value, old in zip(outer_fields(fields_ref, step, c), packed[tile])
+                ]
+        for tile in range(2):
+            result = post_populations(*packed[tile])
+            for i in range(3):
+                for k in range(3):
+                    (yhi_ref if half else ylo_ref)[i * 3 + k, tile] = result[i * 9 + half * 6 + k]
+        low = post_populations(*outer_fields(fields_ref, CHUNKS[0].index(0), half))
+        high = post_populations(*outer_fields(fields_ref, CHUNKS[0].index(GROUPS - 1), SUB - 2 + half))
+        for q in range(9):
+            xlo_ref[q, half] = low[q]
+            xhi_ref[q, half] = high[18 + q]
+
+
+def faces(homes):
+    shape = jax.ShapeDtypeStruct
+    face = shape((9, 2, SUB, LANES), jnp.float32)
+    slots = len(homes) * homes[0].shape[0]
+    whole = pl.BlockSpec(memory_space=pltpu.VMEM)
+    return pl.pallas_call(
+        functools.partial(faces_kernel, len(homes)),
+        in_specs=[whole] * len(homes),
+        out_specs=[whole] * 4 + [pl.BlockSpec(memory_space=pltpu.SMEM), whole],
+        scratch_shapes=tag_scratch(len(homes), slots),
+        out_shape=[face] * 4
+        + [shape((slots,), jnp.int32), shape((tiles_of(0) * SUB * SUB, LANES), jnp.float32)],
+        compiler_params=pltpu.CompilerParams(vmem_limit_bytes=VMEM_LIMIT),
+        cost_estimate=pl.CostEstimate(flops=10**7, bytes_accessed=3 * 10**6, transcendentals=0),
+        name="faces",
+    )(*homes)
+
+
+PAIRS = ((0, 1, 2, 7), (3, 4, 5, 6))
+KEPT = ((5, 8), (12, 15))
+
+
+def advance_kernel(count, plan_ref, *refs):
+    ins = refs[:count]
+    (
+        fields_ref, xlo_ref, xhi_ref, below_in, above_in, out_ref, kept_ref,
+        main_ref, below_ref, above_ref, late_ref,
+    ) = refs[count:]
+    g = pl.program_id(0)
+
+    @pl.when(g == 0)
+    def _():
+        unload(plan_ref, ins, late_ref)
+        fill_outer(fields_ref, main_ref)
+        fill_inner(fields_ref, late_ref, CHUNKS[1][0], main_ref)
+        fill_sides(below_in, above_in, below_ref, above_ref, 0, 7)
+        fill_sides(below_in, above_in, below_ref, above_ref, 13, EDGE)
+        for k in range(3):
+            below_ref[6 + k, 0] = xlo_ref[18 + k]
+            above_ref[6 + k, 0] = turned(xlo_ref[21 + k], 1)
+            below_ref[k, EDGE + 1] = turned(xhi_ref[18 + k], -1)
+            above_ref[k, EDGE + 1] = xhi_ref[21 + k]
+        for q in range(9):
+            for half in range(2):
+                main_ref[18 + q, half] = xlo_ref[q * 2 + half]
+                main_ref[q, 2 * EDGE + 2 + half] = xhi_ref[q * 2 + half]
+        to = 0
+        for first, last in KEPT:
+            for row in range(2 * first + 2, 2 * last + 2):
+                for q in range(NQ):
+                    kept_ref[q, to] = main_ref[q, row]
+                to += 1
+
+    first_x = 2 * jnp.where(g == len(PAIRS[0]) - 1, PAIRS[0][-1], g)
+    stream_pair(first_x, out_ref, main_ref, below_ref, above_ref)
+
+
+def finish_kernel(count, plan_ref, *refs):
+    ins = refs[:count]
+    (
+        fields_ref, kept_ref, below_in, above_in, _, out_ref,
+        main_ref, below_ref, above_ref, late_ref, sems,
+    ) = refs[count:]
+    g = pl.program_id(0)
+
+    @pl.when(g == 0)
+    def _():
+        copies = []
+        to = 0
+        for first, last in KEPT:
+            rows = 2 * (last - first)
+            copies.append(
+                pltpu.make_async_copy(
+                    kept_ref.at[:, pl.ds(to, rows)],
+                    main_ref.at[:, pl.ds(2 * first + 2, rows)],
+                    sems.at[len(copies)],
+                )
+            )
+            to += rows
+        for copy in copies:
+            copy.start()
+        unload(plan_ref, ins, late_ref)
+        fill_inner(fields_ref, late_ref, CHUNKS[2][0], main_ref)
+        fill_sides(below_in, above_in, below_ref, above_ref, 5, 15)
+        for copy in copies:
+            copy.wait()
+
+    stream_pair(2 * (PAIRS[1][0] + g), out_ref, main_ref, below_ref, above_ref)
+
+
+def whole_of(value):
+    rank = len(value.shape)
+    return pl.BlockSpec(value.shape, lambda g, *_: (0,) * rank)
+
+
+def scratch_of_lattice():
+    side = pltpu.VMEM((9, EDGE + 2, SUB, LANES), jnp.float32)
+    return [
+        pltpu.VMEM((NQ, 2 * EDGE + 4, SUB, LANES), jnp.float32), side, side,
+        pltpu.VMEM((LATE_TILES * SUB * SUB, LANES), jnp.float32),
+    ]
+
+
+def advance(plan, homes, fields, xlo, xhi, below, above):
+    pairs = PAIRS[0]
+    inputs = [*homes, fields, xlo, xhi, below, above]
+    kept = jax.ShapeDtypeStruct(
+        (NQ, 2 * sum(last - first for first, last in KEPT), SUB, LANES), jnp.float32
+    )
+    return pl.pallas_call(
+        functools.partial(advance_kernel, len(homes)),
+        grid_spec=pltpu.PrefetchScalarGridSpec(
+            num_scalar_prefetch=1,
+            grid=(len(pairs),),
+            in_specs=[whole_of(value) for value in inputs],
+            out_specs=[
+                pl.BlockSpec(
+                    (NQ, SUB, 4 * LANES),
+                    lambda g, *_: (0, 0, jnp.where(g == len(pairs) - 1, pairs[-1], g)),
+                ),
+                whole_of(kept),
+            ],
+            scratch_shapes=scratch_of_lattice(),
+        ),
+        out_shape=[jax.ShapeDtypeStruct((NQ, SUB, GROUPS * SUB * LANES), jnp.float32), kept],
+        compiler_params=pltpu.CompilerParams(vmem_limit_bytes=LARGE_VMEM_LIMIT),
+        cost_estimate=pl.CostEstimate(flops=10**7, bytes_accessed=5 * 10**6, transcendentals=0),
+        name="advance",
+    )(plan, *inputs)
+
+
+def finish(plan, homes, fields, kept, below, above, out):
+    pairs = PAIRS[1]
+    anywhere = pl.BlockSpec(memory_space=pl.ANY)
     return pl.pallas_call(
         functools.partial(finish_kernel, len(homes)),
         grid_spec=pltpu.PrefetchScalarGridSpec(
             num_scalar_prefetch=1,
-            grid=(GROUPS,),
-            in_specs=[whole(value) for value in homes]
-            + [pl.BlockSpec(memory_space=pl.ANY)]
-            + [whole(value) for value in (sides, xlo, xhi, below, above)],
-            out_specs=pl.BlockSpec((NQ, SUB, SUB * LANES), lambda g, *_: (0, 0, g)),
-            scratch_shapes=[
-                pltpu.VMEM((NQ, GROUPS * SUB, SUB, LANES), jnp.float32),
-                pltpu.VMEM((9, EDGE + 2, SUB, LANES), jnp.float32),
-                pltpu.VMEM((9, EDGE + 2, SUB, LANES), jnp.float32),
-                pltpu.VMEM((SUB, LATE_TILES, SUB, LANES), jnp.float32),
-                pltpu.VMEM((LATE_TILES * SUB * SUB, LANES), jnp.float32),
-                pltpu.SemaphoreType.DMA((len(CHUNKS[0]),)),
-            ],
+            grid=(len(pairs),),
+            in_specs=[whole_of(value) for value in (*homes, fields)]
+            + [anywhere, whole_of(below), whole_of(above), anywhere],
+            out_specs=pl.BlockSpec((NQ, SUB, 4 * LANES), lambda g, *_: (0, 0, pairs[0] + g)),
+            scratch_shapes=scratch_of_lattice() + [pltpu.SemaphoreType.DMA((len(KEPT),))],
         ),
-        out_shape=jax.ShapeDtypeStruct((NQ, SUB, GROUPS * SUB * LANES), jnp.float32),
+        out_shape=jax.ShapeDtypeStruct(out.shape, jnp.float32),
+        input_output_aliases={len(homes) + 5: 0},
         compiler_params=pltpu.CompilerParams(vmem_limit_bytes=VMEM_LIMIT),
-        cost_estimate=pl.CostEstimate(flops=10**7, bytes_accessed=8 * 10**6, transcendentals=0),
+        cost_estimate=pl.CostEstimate(flops=10**7, bytes_accessed=5 * 10**6, transcendentals=0),
         name="finish",
-    )(plan, *homes, early, sides, xlo, xhi, below, above)
+    )(plan, *homes, fields, kept, below, above, out)
 
 
 def shifted(value, axis, step):
@@ -619,21 +648,24 @@
             pre(ordered, destination, refinement, part, row_count, cap_row, blocks * col_count),
             "row", split_axis=0, concat_axis=0, tiled=True,
         )
-        for part in range(2)
+        for part in range(len(CHUNKS))
     ]
 
     def to_columns(packed):
         return [exchanged(packed[d], "col", d) for d in range(col_count - 1, 0, -1)] + [packed[0]]
 
     packed, plan = repack(in_row[0], None, 0, col_count, cap_col, blocks)
-    early, ylo, yhi, xlo, xhi, picked, sides = post(to_columns(packed))
+    ylo, yhi, xlo, xhi, picked, fields = faces(to_columns(packed))
     below, above = shifted(yhi, "col", 1), shifted(ylo, "col", -1)
     up = jnp.concatenate([xhi.reshape(18, SUB, LANES), below[6:, 1], above[6:, 1]])
     down = jnp.concatenate([xlo.reshape(18, SUB, LANES), below[:3, 0], above[:3, 0]])
     xlo, xhi = shifted(up, "row", 1), shifted(down, "row", -1)
-    in_row[1], below, above = lax.optimization_barrier((in_row[1], below, above))
-    homes = to_columns(repack(in_row[1], plan, 1, col_count, cap_col, blocks))
-    return jnp.transpose(finish(picked, homes, early, sides, xlo, xhi, below, above), (1, 0, 2))
+    middle = to_columns(repack(in_row[1], plan, 1, col_count, cap_col, blocks))
+    packed = repack(in_row[2], plan, 2, col_count, cap_col, blocks)
+    picked, packed = lax.optimization_barrier((picked, list(packed)))
+    last = to_columns(packed)
+    out, kept = advance(picked, middle, fields, xlo, xhi, below, above)
+    return jnp.transpose(finish(picked, last, fields, kept, below, above, out), (1, 0, 2))
 
 
 def solution(mesh):

time: 96.7 us -> 122 us (1.26)
  waiting for transfers between devices: 54.2 us -> 66.3 us
  Pallas kernels: 16.9 us -> 22.3 us
  starting transfers between devices: 22.6 us -> 27.5 us
  local copies, waits for them, and re-layouts: 2.68 us -> 5.12 us
    all_to_all x2 -> x3, waiting for transfers between devices: 30.3 us -> 41.9 us  [on_device(): lax.all_to_all(pre(ordered, destination, refinement, part, row_count, cap...]
    pallas_call x1 -> x2, Pallas kernels: 3.22 us -> 7.9 us  [the longest x1 6.19 us: advance(): pl.pallas_call(functools.partial(advance_kernel, len(homes)), grid_spec=p...]
    all_to_all x2 -> x3, starting transfers between devices: 10.9 us -> 14.5 us  [on_device(): lax.all_to_all(pre(ordered, destination, refinement, part, row_count, cap...]
    ppermute x4, waiting for transfers between devices: 5.62 us -> 8.53 us  [shifted(): lax.ppermute(value, axis, [(i, (i + step) % count) for i in range(count)])]
    unnamed x4 -> x30, local copies, waits for them, and re-layouts: 2.68 us -> 5.12 us
    ppermute x6 -> x9, waiting for transfers between devices: 18.3 us -> 15.9 us  [exchanged(): return lax.ppermute(value, axis, pairs)]
    ppermute x6 -> x9, starting transfers between devices: 5.08 us -> 7.3 us  [exchanged(): return lax.ppermute(value, axis, pairs)]
    pallas_call x2 -> x3, Pallas kernels: 6.12 us -> 7.77 us  [pre(): pl.pallas_call(functools.partial(pre_kernel, cap, row_count, per_row, par...]
  transfers between devices with their start and end apart: 12 -> 16, of which waited for: 8 -> 7; matrix products, arithmetic and copies ran while one was open for 0% -> 0% of each run, Pallas kernels for 8% -> 14%
where the time goes in v7:
time: 122 us; the launch traced here: 121 us
  waiting for transfers between devices  66.3 us (54%)
  starting transfers between devices  27.5 us (23%)
  Pallas kernels  22.3 us (18%)
  local copies, waits for them, and re-layouts  5.12 us (4%)
    all_to_all x3, waiting for transfers between devices, on_device(): lax.all_to_all(pre(ordered, destination, refinement, part, row_count, cap...  41.9 us
    ppermute x9, waiting for transfers between devices, exchanged(): return lax.ppermute(value, axis, pairs)  15.9 us
    all_to_all x3, starting transfers between devices, on_device(): lax.all_to_all(pre(ordered, destination, refinement, part, row_count, cap...  14.5 us
    ppermute x4, waiting for transfers between devices, shifted(): lax.ppermute(value, axis, [(i, (i + step) % count) for i in range(count)])  8.53 us
    pallas_call x3, Pallas kernels, pre(): pl.pallas_call(functools.partial(pre_kernel, cap, row_count, per_row, par...  7.77 us
    ppermute x9, starting transfers between devices, exchanged(): return lax.ppermute(value, axis, pairs)  7.3 us
    pallas_call x1, Pallas kernels, advance(): pl.pallas_call(functools.partial(advance_kernel, len(homes)), grid_spec=p...  6.19 us
    ppermute x4, starting transfers between devices, shifted(): lax.ppermute(value, axis, [(i, (i + step) % count) for i in range(count)])  5.65 us
  transfers between devices with their start and end apart: 16, of which 7 were waited for; matrix products, arithmetic and copies ran while one was open for 0% of the time, Pallas kernels for 14%

profile of v7, /device:TPU:0, one launch (start us, length us, event | category | flops | bytes accessed | tf_op | source)
XLA Modules:
  0.0 121.4 jit_solution(7028398203977730268)
XLA Ops:
  0.0 2.2 %pre_1.1 = f32[16,8,8,128]{3,2,1,0:T(8,128)} custom-call(s32[8]{0:T(128)} %dest_hbm.5, s32[8]{0:T(128)} %level_hbm.5, f32[27,8,4096]{2,1,0:T(8,128)} %bitcast.14), custom_call_target="tpu_custom_call" | custom-call | flops 10000000 | bytes 4000000 | tf_op jit(solution)/shard_map/pre_1/pallas_call | solution.py:202
  2.2 7.3 %all-to-all-start.2 = ((f32[16,8,8,128]{3,2,1,0:T(8,128)}), f32[16,8,8,128]{3,2,1,0:T(8,128)S(1)}, u32[]{:S(2)}, u32[]{:S(2)}) async-start(f32[16,8,8,128]{3,2,1,0:T(8,128)} %pre_1.1), calls=%async_computation.2 | async-start | bytes 1048576 | tf_op jit(solution)/shard_map/all_to_all | solution.py:647
  9.5 3.4 %pre_0.1 = f32[16,21,8,128]{3,2,1,0:T(8,128)} custom-call(s32[8]{0:T(128)} %dest_hbm.5, s32[8]{0:T(128)} %level_hbm.5, f32[27,8,4096]{2,1,0:T(8,128)} %bitcast.15), custom_call_target="tpu_custom_call" | custom-call | flops 10000000 | bytes 4000000 | tf_op jit(solution)/shard_map/pre_0/pallas_call | solution.py:202
  12.9 11.1 %all-to-all-done.2.refs_1_ = f32[16,8,8,128]{3,2,1,0:T(8,128)S(1)} async-done(((f32[16,8,8,128]{3,2,1,0:T(8,128)}), f32[16,8,8,128]{3,2,1,0:T(8,128)S(1)}, u32[]{:S(2)}, u32[]{:S(2)}) %all-to-all-start.2) | async-done | bytes 524320 | tf_op jit(solution)/shard_map/all_to_all | solution.py:647
  23.9 3.6 %all-to-all-start = ((f32[16,21,8,128]{3,2,1,0:T(8,128)}), f32[16,21,8,128]{3,2,1,0:T(8,128)S(1)}, u32[]{:S(2)}, u32[]{:S(2)}) async-start(f32[16,21,8,128]{3,2,1,0:T(8,128)} %pre_0.1), calls=%async_computation | async-start | bytes 2752512 | tf_op jit(solution)/shard_map/all_to_all | solution.py:647
  27.6 2.2 %pre_2.1 = f32[16,8,8,128]{3,2,1,0:T(8,128)} custom-call(s32[8]{0:T(128)} %dest_hbm.5, s32[8]{0:T(128)} %level_hbm.5, f32[27,8,4096]{2,1,0:T(8,128)} %bitcast.16), custom_call_target="tpu_custom_call" | custom-call | flops 10000000 | bytes 4000000 | tf_op jit(solution)/shard_map/pre_2/pallas_call | solution.py:202
  29.8 30.8 %all-to-all-done.refs_0_ = f32[16,21,8,128]{3,2,1,0:T(8,128)S(1)} async-done(((f32[16,21,8,128]{3,2,1,0:T(8,128)}), f32[16,21,8,128]{3,2,1,0:T(8,128)S(1)}, u32[]{:S(2)}, u32[]{:S(2)}) %all-to-all-start) | async-done | bytes 1376288 | tf_op jit(solution)/shard_map/all_to_all | solution.py:647
  60.6 3.6 %all-to-all-start.1 = ((f32[16,8,8,128]{3,2,1,0:T(8,128)}), f32[16,8,8,128]{3,2,1,0:T(8,128)S(1)}, u32[]{:S(2)}, u32[]{:S(2)}) async-start(f32[16,8,8,128]{3,2,1,0:T(8,128)} %pre_2.1), calls=%async_computation.1 | async-start | bytes 1048576 | tf_op jit(solution)/shard_map/all_to_all | solution.py:647
  64.2 1.7 %repack_0.1 = (f32[4,21,8,128]{3,2,1,0:T(8,128)S(1)}, f32[4,21,8,128]{3,2,1,0:T(8,128)S(1)}, f32[4,21,8,128]{3,2,1,0:T(8,128)S(1)}, f32[4,21,8,128]{3,2,1,0:T(8,128)S(1)}, s32[16]{0:T(128)S(1)}) custom-call(f32[16,21,8,128]{3,2,1,0:T(8,128)S(1)} %all-to-all-done.refs_0_), custom_call_target="tpu_custom_call" | custom-call | bytes 3000000 | tf_op jit(solution)/shard_map/repack_0/pallas_call | solution.py:281
  65.9 0.9 collective-permute-start
  66.8 0.7 collective-permute-start.1
  67.8 8.4 %collective-permute-done.refs_0_ = f32[4,21,8,128]{3,2,1,0:T(8,128)S(1)} collective-permute-done((f32[4,21,8,128]{3,2,1,0:T(8,128)S(1)}, f32[4,21,8,128]{3,2,1,0:T(8,128)S(1)}, u32[]{:S(2)}, u32[]{:S(2)}) %collective-permute-start) | collective-permute-done | bytes 344096 | tf_op jit(solution)/shard_map/ppermute | solution.py:50
  76.2 7.4 %collective-permute-done.1.refs_1_ = f32[4,21,8,128]{3,2,1,0:T(8,128)S(1)} collective-permute-done((f32[4,21,8,128]{3,2,1,0:T(8,128)S(1)}, f32[4,21,8,128]{3,2,1,0:T(8,128)S(1)}, u32[]{:S(2)}, u32[]{:S(2)}) %collective-permute-start.1) | collective-permute-done | bytes 344096 | tf_op jit(solution)/shard_map/ppermute | solution.py:50
  83.7 1.7 %faces.1 = (f32[9,2,8,128]{3,2,1,0:T(8,128)S(1)}, f32[9,2,8,128]{3,2,1,0:T(8,128)S(1)}, f32[9,2,8,128]{3,2,1,0:T(8,128)S(1)}, f32[9,2,8,128]{3,2,1,0:T(8,128)S(1...) custom-call(f32[4,21,8,128]{3,2,1,0:T(8,128)S(1)} %collective-permute-done.refs_0_, ...), custom_call_target="tpu_custom_call" | custom-call | flops 10000000 | bytes 3000000 | tf_op jit(solution)/shard_map/faces/pallas_call | solution.py:486
  85.4 0.8 copy-done
  86.3 0.7 repack_1.1
  87.0 1.8 %collective-permute-start.6 = (f32[4,8,8,128]{3,2,1,0:T(8,128)S(1)}, f32[4,8,8,128]{3,2,1,0:T(8,128)S(1)}, u32[]{:S(2)}, u32[]{:S(2)}) collective-permute-start(f32[4,8,8,128]{3,2,1,0:T(8,128)S(1)} %get-tuple-element.47), channel_id=1, source_target_pairs={{0,3},{1,2},{2,1},{3,0},{4,7},{5,6},{6,5},{7,4},{8,11},{9,10},{10,... | collective-permute-start | bytes 393224 | tf_op jit(solution)/shard_map/ppermute | solution.py:50
  88.8 1.3 %collective-permute-start.7 = (f32[4,8,8,128]{3,2,1,0:T(8,128)S(1)}, f32[4,8,8,128]{3,2,1,0:T(8,128)S(1)}, u32[]{:S(2)}, u32[]{:S(2)}) collective-permute-start(f32[4,8,8,128]{3,2,1,0:T(8,128)S(1)} %get-tuple-element.48), channel_id=1, source_target_pairs={{0,2},{1,3},{2,0},{3,1},{4,6},{5,7},{6,4},{7,5},{8,10},{9,11},{10,... | collective-permute-start | bytes 393224 | tf_op jit(solution)/shard_map/ppermute | solution.py:50
  90.1 0.7 repack_2.1
  90.8 0.8 collective-permute-start.10
  91.7 5.0 %collective-permute-done.10.refs_8_.refs_7_ = f32[9,2,8,128]{3,2,1,0:T(8,128)S(1)} collective-permute-done((f32[9,2,8,128]{3,2,1,0:T(8,128)S(1)}, f32[9,2,8,128]{3,2,1,0:T(8,128)S(1)}, u32[]{:S(2)}, u32[]{:S(2)}) %collective-permute-start.10) | collective-permute-done | bytes 73760 | tf_op jit(solution)/shard_map/ppermute | solution.py:635
  96.8 0.6 collective-permute-start.4
  97.4 1.6 %collective-permute-start.5 = (f32[4,8,8,128]{3,2,1,0:T(8,128)S(1)}, f32[4,8,8,128]{3,2,1,0:T(8,128)S(1)}, u32[]{:S(2)}, u32[]{:S(2)}) collective-permute-start(f32[4,8,8,128]{3,2,1,0:T(8,128)S(1)} %get-tuple-element.44), channel_id=1, source_target_pairs={{0,1},{1,0},{2,3},{3,2},{4,5},{5,4},{6,7},{7,6},{8,9},{9,8},{10,11... | collective-permute-start | bytes 393224 | tf_op jit(solution)/shard_map/ppermute | solution.py:50
  99.0 1.5 %collective-permute-start.11 = (f32[24,8,128]{2,1,0:T(8,128)S(1)}, f32[24,8,128]{2,1,0:T(8,128)S(1)}, u32[]{:S(2)}, u32[]{:S(2)}) collective-permute-start(f32[24,8,128]{2,1,0:T(8,128)S(1)} %pad_maximum_fusion), channel_id=1, source_target_pairs={{0,4},{4,8},{8,12},{12,16},{16,20},{20,24},{24,28},{28,0},{1,5},{5... | collective-permute-start | bytes 294920 | tf_op jit(solution)/shard_map/ppermute | solution.py:635
  100.6 3.2 %collective-permute-start.12 = (f32[24,8,128]{2,1,0:T(8,128)S(1)}, f32[24,8,128]{2,1,0:T(8,128)S(1)}, u32[]{:S(2)}, u32[]{:S(2)}) collective-permute-start(f32[24,8,128]{2,1,0:T(8,128)S(1)} %pad_maximum_fusion.1), channel_id=1, source_target_pairs={{0,28},{4,0},{8,4},{12,8},{16,12},{20,16},{24,20},{28,24},{1,29},{... | collective-permute-start | bytes 294920 | tf_op jit(solution)/shard_map/ppermute | solution.py:635
  103.8 2.8 %collective-permute-done.11.refs_5_ = f32[24,8,128]{2,1,0:T(8,128)S(1)} collective-permute-done((f32[24,8,128]{2,1,0:T(8,128)S(1)}, f32[24,8,128]{2,1,0:T(8,128)S(1)}, u32[]{:S(2)}, u32[]{:S(2)}) %collective-permute-start.11) | collective-permute-done | bytes 98336 | tf_op jit(solution)/shard_map/ppermute | solution.py:635
  106.6 0.7 collective-permute-done.12.refs_6_
  107.9 6.2 %advance.1 = (f32[27,8,4096]{2,1,0:T(8,128)}, f32[27,12,8,128]{3,2,1,0:T(8,128)}) custom-call(s32[16]{0:T(128)} %copy-done.8, f32[4,8,8,128]{3,2,1,0:T(8,128)} %copy-done.10, f32[4,8,8,128]{3,2,1,0:T(8,128)} %copy-done.11, f32[4,8,8,128]{3,2,1,0:T(8,128)} %copy-done.12, f32[4,8,8,128]{3,2,1,0:T(8,128)} %copy-done.7, f32[1344,128]{1,0:T(8,128)} %copy-done, ...), custom_call_target="tpu_custom_call" | custom-call | flops 10000000 | bytes 5000000 | tf_op jit(solution)/shard_map/advance/pallas_call | solution.py:590
  114.2 1.3 %copy-done.2 = f32[27,12,8,128]{3,2,1,0:T(8,128)S(1)} copy-done((f32[27,12,8,128]{3,2,1,0:T(8,128)S(1)}, f32[27,12,8,128]{3,2,1,0:T(8,128)}, u32[]{:S(2)}) %copy-start.2) | copy-done | bytes 1327128
  115.5 0.9 copy-done.4
  116.4 0.9 copy-done.6
  117.8 3.6 %finish.1 = f32[27,8,4096]{2,1,0:T(8,128)} custom-call(s32[16]{0:T(128)S(1)} %copy-done.9, f32[4,8,8,128]{3,2,1,0:T(8,128)S(1)} %collective-permute-done.3.refs_0_, f32[4,8,8,128]{3,2,1,0:T(8,128)S(1)} %collective-permute-done.4.refs_1_, f32[4,8,8,128]{3,2,1,0:T(8,128)S(1)} %collective-permute-done.5.refs_2_, ...), custom_call_target="tpu_custom_call", output_to_operand_aliasing={{}: (9, {})} | custom-call | flops 10000000 | bytes 5000000 | tf_op jit(solution)/shard_map/finish/pallas_call | solution.py:615
  (43 shorter events, 1.6 us)
Async XLA Ops:
  2.2 21.8 %all-to-all-start.2 = ((f32[16,8,8,128]{3,2,1,0:T(8,128)}), f32[16,8,8,128]{3,2,1,0:T(8,128)S(1)}, u32[]{:S(2)}, u32[]{:S(2)}) async-start(f32[16,8,8,128]{3,2,1,0:T(8,128)} %pre_1.1), calls=%async_computation.2 | async-start | bytes 1048576 | tf_op jit(solution)/shard_map/all_to_all | solution.py:647
  23.9 36.6 %all-to-all-start = ((f32[16,21,8,128]{3,2,1,0:T(8,128)}), f32[16,21,8,128]{3,2,1,0:T(8,128)S(1)}, u32[]{:S(2)}, u32[]{:S(2)}) async-start(f32[16,21,8,128]{3,2,1,0:T(8,128)} %pre_0.1), calls=%async_computation | async-start | bytes 2752512 | tf_op jit(solution)/shard_map/all_to_all | solution.py:647
  60.6 29.6 %all-to-all-start.1 = ((f32[16,8,8,128]{3,2,1,0:T(8,128)}), f32[16,8,8,128]{3,2,1,0:T(8,128)S(1)}, u32[]{:S(2)}, u32[]{:S(2)}) async-start(f32[16,8,8,128]{3,2,1,0:T(8,128)} %pre_2.1), calls=%async_computation.1 | async-start | bytes 1048576 | tf_op jit(solution)/shard_map/all_to_all | solution.py:647
  65.9 10.4 %collective-permute-start = (f32[4,21,8,128]{3,2,1,0:T(8,128)S(1)}, f32[4,21,8,128]{3,2,1,0:T(8,128)S(1)}, u32[]{:S(2)}, u32[]{:S(2)}) collective-permute-start(f32[4,21,8,128]{3,2,1,0:T(8,128)S(1)} %get-tuple-element.31), channel_id=1, source_target_pairs={{0,3},{1,2},{2,1},{3,0},{4,7},{5,6},{6,5},{7,4},{8,11},{9,10},{10,... | collective-permute-start | bytes 1032200 | tf_op jit(solution)/shard_map/ppermute | solution.py:50
  66.8 16.9 %collective-permute-start.1 = (f32[4,21,8,128]{3,2,1,0:T(8,128)S(1)}, f32[4,21,8,128]{3,2,1,0:T(8,128)S(1)}, u32[]{:S(2)}, u32[]{:S(2)}) collective-permute-start(f32[4,21,8,128]{3,2,1,0:T(8,128)S(1)} %get-tuple-element.32), channel_id=1, source_target_pairs={{0,2},{1,3},{2,0},{3,1},{4,6},{5,7},{6,4},{7,5},{8,10},{9,11},{10,... | collective-permute-start | bytes 1032200 | tf_op jit(solution)/shard_map/ppermute | solution.py:50
  67.5 16.1 %collective-permute-start.2 = (f32[4,21,8,128]{3,2,1,0:T(8,128)S(1)}, f32[4,21,8,128]{3,2,1,0:T(8,128)S(1)}, u32[]{:S(2)}, u32[]{:S(2)}) collective-permute-start(f32[4,21,8,128]{3,2,1,0:T(8,128)S(1)} %get-tuple-element.33), channel_id=1, source_target_pairs={{0,1},{1,0},{2,3},{3,2},{4,5},{5,4},{6,7},{7,6},{8,9},{9,8},{10,11... | collective-permute-start | bytes 1032200 | tf_op jit(solution)/shard_map/ppermute | solution.py:50
  85.4 0.8 copy-start
  86.2 3.9 %copy-start.8 = (s32[16]{0:T(128)}, s32[16]{0:T(128)S(1)}, u32[]{:S(2)}) copy-start(s32[16]{0:T(128)S(1)} %get-tuple-element.41.plan_ref) | copy-start | bytes 196
  86.2 27.9 %copy-start.1 = (f32[1344,128]{1,0:T(8,128)S(1)}, f32[1344,128]{1,0:T(8,128)}, u32[]{:S(2)}) copy-start(f32[1344,128]{1,0:T(8,128)} %copy-done) | copy-start | bytes 2064388
  86.3 5.4 %collective-permute-start.9 = (f32[9,2,8,128]{3,2,1,0:T(8,128)S(1)}, f32[9,2,8,128]{3,2,1,0:T(8,128)S(1)}, u32[]{:S(2)}, u32[]{:S(2)}) collective-permute-start(f32[9,2,8,128]{3,2,1,0:T(8,128)S(1)} %get-tuple-element.52), channel_id=1, source_target_pairs={{0,1},{1,2},{2,3},{3,0},{4,5},{5,6},{6,7},{7,4},{8,9},{9,10},{10,1... | collective-permute-start | bytes 221192 | tf_op jit(solution)/shard_map/ppermute | solution.py:635
  87.0 10.4 %copy-start.7 = (f32[4,8,8,128]{3,2,1,0:T(8,128)}, f32[4,8,8,128]{3,2,1,0:T(8,128)S(1)}, u32[]{:S(2)}) copy-start(f32[4,8,8,128]{3,2,1,0:T(8,128)S(1)} %get-tuple-element.50.refs_3_) | copy-start | bytes 393220
  87.0 10.4 %collective-permute-start.6 = (f32[4,8,8,128]{3,2,1,0:T(8,128)S(1)}, f32[4,8,8,128]{3,2,1,0:T(8,128)S(1)}, u32[]{:S(2)}, u32[]{:S(2)}) collective-permute-start(f32[4,8,8,128]{3,2,1,0:T(8,128)S(1)} %get-tuple-element.47), channel_id=1, source_target_pairs={{0,3},{1,2},{2,1},{3,0},{4,7},{5,6},{6,5},{7,4},{8,11},{9,10},{10,... | collective-permute-start | bytes 393224 | tf_op jit(solution)/shard_map/ppermute | solution.py:50
  88.8 10.3 %collective-permute-start.7 = (f32[4,8,8,128]{3,2,1,0:T(8,128)S(1)}, f32[4,8,8,128]{3,2,1,0:T(8,128)S(1)}, u32[]{:S(2)}, u32[]{:S(2)}) collective-permute-start(f32[4,8,8,128]{3,2,1,0:T(8,128)S(1)} %get-tuple-element.48), channel_id=1, source_target_pairs={{0,2},{1,3},{2,0},{3,1},{4,6},{5,7},{6,4},{7,5},{8,10},{9,11},{10,... | collective-permute-start | bytes 393224 | tf_op jit(solution)/shard_map/ppermute | solution.py:50
  90.1 10.5 %collective-permute-start.8 = (f32[4,8,8,128]{3,2,1,0:T(8,128)S(1)}, f32[4,8,8,128]{3,2,1,0:T(8,128)S(1)}, u32[]{:S(2)}, u32[]{:S(2)}) collective-permute-start(f32[4,8,8,128]{3,2,1,0:T(8,128)S(1)} %get-tuple-element.49), channel_id=1, source_target_pairs={{0,1},{1,0},{2,3},{3,2},{4,5},{5,4},{6,7},{7,6},{8,9},{9,8},{10,11... | collective-permute-start | bytes 393224 | tf_op jit(solution)/shard_map/ppermute | solution.py:50
  90.8 6.0 %collective-permute-start.10 = (f32[9,2,8,128]{3,2,1,0:T(8,128)S(1)}, f32[9,2,8,128]{3,2,1,0:T(8,128)S(1)}, u32[]{:S(2)}, u32[]{:S(2)}) collective-permute-start(f32[9,2,8,128]{3,2,1,0:T(8,128)S(1)} %get-tuple-element.53), channel_id=1, source_target_pairs={{0,3},{1,0},{2,1},{3,2},{4,7},{5,4},{6,5},{7,6},{8,11},{9,8},{10,9... | collective-permute-start | bytes 221192 | tf_op jit(solution)/shard_map/ppermute | solution.py:635
  91.6 15.6 %copy-start.3 = (f32[9,2,8,128]{3,2,1,0:T(8,128)}, f32[9,2,8,128]{3,2,1,0:T(8,128)S(1)}, u32[]{:S(2)}) copy-start(f32[9,2,8,128]{3,2,1,0:T(8,128)S(1)} %collective-permute-done.9.refs_7_.refs_6_) | copy-start | bytes 221188
  91.6 22.5 %collective-permute-start.3 = (f32[4,8,8,128]{3,2,1,0:T(8,128)S(1)}, f32[4,8,8,128]{3,2,1,0:T(8,128)S(1)}, u32[]{:S(2)}, u32[]{:S(2)}) collective-permute-start(f32[4,8,8,128]{3,2,1,0:T(8,128)S(1)} %get-tuple-element.42), channel_id=1, source_target_pairs={{0,3},{1,2},{2,1},{3,0},{4,7},{5,6},{6,5},{7,4},{8,11},{9,10},{10,... | collective-permute-start | bytes 393224 | tf_op jit(solution)/shard_map/ppermute | solution.py:50
  96.8 10.5 %copy-start.5 = (f32[9,2,8,128]{3,2,1,0:T(8,128)}, f32[9,2,8,128]{3,2,1,0:T(8,128)S(1)}, u32[]{:S(2)}) copy-start(f32[9,2,8,128]{3,2,1,0:T(8,128)S(1)} %collective-permute-done.10.refs_8_.refs_7_) | copy-start | bytes 221188
  96.8 17.3 %collective-permute-start.4 = (f32[4,8,8,128]{3,2,1,0:T(8,128)S(1)}, f32[4,8,8,128]{3,2,1,0:T(8,128)S(1)}, u32[]{:S(2)}, u32[]{:S(2)}) collective-permute-start(f32[4,8,8,128]{3,2,1,0:T(8,128)S(1)} %get-tuple-element.43), channel_id=1, source_target_pairs={{0,2},{1,3},{2,0},{3,1},{4,6},{5,7},{6,4},{7,5},{8,10},{9,11},{10,... | collective-permute-start | bytes 393224 | tf_op jit(solution)/shard_map/ppermute | solution.py:50
  97.4 9.9 %copy-start.10 = (f32[4,8,8,128]{3,2,1,0:T(8,128)}, f32[4,8,8,128]{3,2,1,0:T(8,128)S(1)}, u32[]{:S(2)}) copy-start(f32[4,8,8,128]{3,2,1,0:T(8,128)S(1)} %collective-permute-done.6.refs_0_) | copy-start | bytes 393220
  97.4 16.7 %collective-permute-start.5 = (f32[4,8,8,128]{3,2,1,0:T(8,128)S(1)}, f32[4,8,8,128]{3,2,1,0:T(8,128)S(1)}, u32[]{:S(2)}, u32[]{:S(2)}) collective-permute-start(f32[4,8,8,128]{3,2,1,0:T(8,128)S(1)} %get-tuple-element.44), channel_id=1, source_target_pairs={{0,1},{1,0},{2,3},{3,2},{4,5},{5,4},{6,7},{7,6},{8,9},{9,8},{10,11... | collective-permute-start | bytes 393224 | tf_op jit(solution)/shard_map/ppermute | solution.py:50
  99.0 8.3 %copy-start.11 = (f32[4,8,8,128]{3,2,1,0:T(8,128)}, f32[4,8,8,128]{3,2,1,0:T(8,128)S(1)}, u32[]{:S(2)}) copy-start(f32[4,8,8,128]{3,2,1,0:T(8,128)S(1)} %collective-permute-done.7.refs_1_) | copy-start | bytes 393220
  99.0 7.6 %collective-permute-start.11 = (f32[24,8,128]{2,1,0:T(8,128)S(1)}, f32[24,8,128]{2,1,0:T(8,128)S(1)}, u32[]{:S(2)}, u32[]{:S(2)}) collective-permute-start(f32[24,8,128]{2,1,0:T(8,128)S(1)} %pad_maximum_fusion), channel_id=1, source_target_pairs={{0,4},{4,8},{8,12},{12,16},{16,20},{20,24},{24,28},{28,0},{1,5},{5... | collective-permute-start | bytes 294920 | tf_op jit(solution)/shard_map/ppermute | solution.py:635
  100.6 6.8 %copy-start.12 = (f32[4,8,8,128]{3,2,1,0:T(8,128)}, f32[4,8,8,128]{3,2,1,0:T(8,128)S(1)}, u32[]{:S(2)}) copy-start(f32[4,8,8,128]{3,2,1,0:T(8,128)S(1)} %collective-permute-done.8.refs_2_) | copy-start | bytes 393220
  100.6 6.7 %collective-permute-start.12 = (f32[24,8,128]{2,1,0:T(8,128)S(1)}, f32[24,8,128]{2,1,0:T(8,128)S(1)}, u32[]{:S(2)}, u32[]{:S(2)}) collective-permute-start(f32[24,8,128]{2,1,0:T(8,128)S(1)} %pad_maximum_fusion.1), channel_id=1, source_target_pairs={{0,28},{4,0},{8,4},{12,8},{16,12},{20,16},{24,20},{28,24},{1,29},{... | collective-permute-start | bytes 294920 | tf_op jit(solution)/shard_map/ppermute | solution.py:635
  106.6 0.7 copy-start.13
  107.3 0.6 copy-start.14
  114.1 1.3 %copy-start.2 = (f32[27,12,8,128]{3,2,1,0:T(8,128)S(1)}, f32[27,12,8,128]{3,2,1,0:T(8,128)}, u32[]{:S(2)}) copy-start(f32[27,12,8,128]{3,2,1,0:T(8,128)} %get-tuple-element.55.refs_5_) | copy-start | bytes 3981316
  115.5 0.9 copy-start.4
  116.3 0.9 copy-start.6
  117.2 0.6 copy-start.9

commit v8 on v7

--- a/solution.py
+++ b/solution.py
@@ -603,7 +603,7 @@
             scratch_shapes=scratch_of_lattice(),
         ),
         out_shape=[jax.ShapeDtypeStruct((NQ, SUB, GROUPS * SUB * LANES), jnp.float32), kept],
-        compiler_params=pltpu.CompilerParams(vmem_limit_bytes=LARGE_VMEM_LIMIT),
+        compiler_params=pltpu.CompilerParams(vmem_limit_bytes=VMEM_LIMIT),
         cost_estimate=pl.CostEstimate(flops=10**7, bytes_accessed=5 * 10**6, transcendentals=0),
         name="advance",
     )(plan, *inputs)
@@ -643,13 +643,14 @@
     cap_col = 2 * ((blocks + col_count - 1) // col_count)
     ordered = jnp.transpose(populations, (1, 0, 2))
 
-    in_row = [
-        lax.all_to_all(
-            pre(ordered, destination, refinement, part, row_count, cap_row, blocks * col_count),
-            "row", split_axis=0, concat_axis=0, tiled=True,
-        )
-        for part in range(len(CHUNKS))
-    ]
+    in_row = []
+    for part in range(len(CHUNKS)):
+        sent = pre(ordered, destination, refinement, part, row_count, cap_row, blocks * col_count)
+        if part:
+            sent, in_row[-1] = lax.optimization_barrier((sent, in_row[-1]))
+        else:
+            sent, destination = lax.optimization_barrier((sent, destination))
+        in_row.append(lax.all_to_all(sent, "row", split_axis=0, concat_axis=0, tiled=True))
 
     def to_columns(packed):
         return [exchanged(packed[d], "col", d) for d in range(col_count - 1, 0, -1)] + [packed[0]]
@@ -657,10 +658,11 @@
     packed, plan = repack(in_row[0], None, 0, col_count, cap_col, blocks)
     ylo, yhi, xlo, xhi, picked, fields = faces(to_columns(packed))
     below, above = shifted(yhi, "col", 1), shifted(ylo, "col", -1)
+    middle = to_columns(repack(in_row[1], plan, 1, col_count, cap_col, blocks))
+    in_row[2], below, above = lax.optimization_barrier((in_row[2], below, above))
     up = jnp.concatenate([xhi.reshape(18, SUB, LANES), below[6:, 1], above[6:, 1]])
     down = jnp.concatenate([xlo.reshape(18, SUB, LANES), below[:3, 0], above[:3, 0]])
     xlo, xhi = shifted(up, "row", 1), shifted(down, "row", -1)
-    middle = to_columns(repack(in_row[1], plan, 1, col_count, cap_col, blocks))
     packed = repack(in_row[2], plan, 2, col_count, cap_col, blocks)
     picked, packed = lax.optimization_barrier((picked, list(packed)))
     last = to_columns(packed)

time: 122 us -> 114 us (0.934)
  local copies, waits for them, and re-layouts: 5.12 us -> 0.01 us
  Pallas kernels: 22.3 us -> 20.4 us
    unnamed x30 -> x0, local copies, waits for them, and re-layouts: 5.12 us -> none
    ppermute x4, waiting for transfers between devices: 8.53 us -> 3.79 us  [shifted(): lax.ppermute(value, axis, [(i, (i + step) % count) for i in range(count)])]
    ppermute x9, waiting for transfers between devices: 15.9 us -> 19.2 us  [exchanged(): return lax.ppermute(value, axis, pairs)]
    pallas_call x1, Pallas kernels: 6.19 us -> 4.26 us  [advance(): pl.pallas_call(functools.partial(advance_kernel, len(homes)), grid_spec=p...]
  transfers between devices with their start and end apart: 16 -> 16, of which waited for: 7 -> 8; matrix products, arithmetic and copies ran while one was open for 0% -> 0% of each run, Pallas kernels for 14% -> 12%
where the time goes in v8:
time: 114 us
  waiting for transfers between devices  66.1 us (58%)
  starting transfers between devices  27.5 us (24%)
  Pallas kernels  20.4 us (18%)
    all_to_all x3, waiting for transfers between devices, on_device(): lax.all_to_all(sent, 'row', split_axis=0, concat_axis=0, tiled=True)  43.1 us
    ppermute x9, waiting for transfers between devices, exchanged(): return lax.ppermute(value, axis, pairs)  19.2 us
    all_to_all x3, starting transfers between devices, on_device(): lax.all_to_all(sent, 'row', split_axis=0, concat_axis=0, tiled=True)  14.5 us
    pallas_call x3, Pallas kernels, pre(): pl.pallas_call(functools.partial(pre_kernel, cap, row_count, per_row, par...  7.78 us
    ppermute x4, starting transfers between devices, shifted(): lax.ppermute(value, axis, [(i, (i + step) % count) for i in range(count)])  6.52 us
    ppermute x9, starting transfers between devices, exchanged(): return lax.ppermute(value, axis, pairs)  6.45 us
    pallas_call x1, Pallas kernels, advance(): pl.pallas_call(functools.partial(advance_kernel, len(homes)), grid_spec=p...  4.26 us
    ppermute x4, waiting for transfers between devices, shifted(): lax.ppermute(value, axis, [(i, (i + step) % count) for i in range(count)])  3.79 us
  transfers between devices with their start and end apart: 16, of which 8 were waited for; matrix products, arithmetic and copies ran while one was open for 0% of the time, Pallas kernels for 12%

profile of v8, /device:TPU:0, one launch (start us, length us, event | category | flops | bytes accessed | tf_op | source)
XLA Modules:
  0.0 114.1 jit_solution(10565388524041589927)
XLA Ops:
  0.0 3.4 %pre_0.1 = f32[16,21,8,128]{3,2,1,0:T(8,128)} custom-call(s32[8]{0:T(128)} %dest_hbm.3, s32[8]{0:T(128)} %level_hbm.5, f32[27,8,4096]{2,1,0:T(8,128)} %bitcast.14), custom_call_target="tpu_custom_call" | custom-call | flops 10000000 | bytes 4000000 | tf_op jit(solution)/shard_map/pre_0/pallas_call | solution.py:202
  3.4 7.3 %all-to-all-start = ((f32[16,21,8,128]{3,2,1,0:T(8,128)}), f32[16,21,8,128]{3,2,1,0:T(8,128)S(1)}, u32[]{:S(2)}, u32[]{:S(2)}) async-start(f32[16,21,8,128]{3,2,1,0:T(8,128)} %pre_0.1), calls=%async_computation | async-start | bytes 2752512 | tf_op jit(solution)/shard_map/all_to_all | solution.py:653
  10.7 2.2 %pre_1.1 = f32[16,8,8,128]{3,2,1,0:T(8,128)} custom-call(s32[8]{0:T(128)} %dest_hbm.3, s32[8]{0:T(128)} %level_hbm.5, f32[27,8,4096]{2,1,0:T(8,128)} %bitcast.15), custom_call_target="tpu_custom_call" | custom-call | flops 10000000 | bytes 4000000 | tf_op jit(solution)/shard_map/pre_1/pallas_call | solution.py:202
  12.9 30.6 %all-to-all-done.refs_0_ = f32[16,21,8,128]{3,2,1,0:T(8,128)S(1)} async-done(((f32[16,21,8,128]{3,2,1,0:T(8,128)}), f32[16,21,8,128]{3,2,1,0:T(8,128)S(1)}, u32[]{:S(2)}, u32[]{:S(2)}) %all-to-all-start) | async-done | bytes 1376288 | tf_op jit(solution)/shard_map/all_to_all | solution.py:653
  43.5 3.6 %all-to-all-start.1 = ((f32[16,8,8,128]{3,2,1,0:T(8,128)}), f32[16,8,8,128]{3,2,1,0:T(8,128)S(1)}, u32[]{:S(2)}, u32[]{:S(2)}) async-start(f32[16,8,8,128]{3,2,1,0:T(8,128)} %pre_1.1), calls=%async_computation.1 | async-start | bytes 1048576 | tf_op jit(solution)/shard_map/all_to_all | solution.py:653
  47.1 2.2 %pre_2.1 = f32[16,8,8,128]{3,2,1,0:T(8,128)} custom-call(s32[8]{0:T(128)} %dest_hbm.3, s32[8]{0:T(128)} %level_hbm.5, f32[27,8,4096]{2,1,0:T(8,128)} %bitcast.16), custom_call_target="tpu_custom_call" | custom-call | flops 10000000 | bytes 4000000 | tf_op jit(solution)/shard_map/pre_2/pallas_call | solution.py:202
  49.3 12.5 %all-to-all-done.1.refs_1_ = f32[16,8,8,128]{3,2,1,0:T(8,128)S(1)} async-done(((f32[16,8,8,128]{3,2,1,0:T(8,128)}), f32[16,8,8,128]{3,2,1,0:T(8,128)S(1)}, u32[]{:S(2)}, u32[]{:S(2)}) %all-to-all-start.1) | async-done | bytes 524320 | tf_op jit(solution)/shard_map/all_to_all | solution.py:653
  61.8 3.6 %all-to-all-start.2 = ((f32[16,8,8,128]{3,2,1,0:T(8,128)}), f32[16,8,8,128]{3,2,1,0:T(8,128)S(1)}, u32[]{:S(2)}, u32[]{:S(2)}) async-start(f32[16,8,8,128]{3,2,1,0:T(8,128)} %pre_2.1), calls=%async_computation.2 | async-start | bytes 1048576 | tf_op jit(solution)/shard_map/all_to_all | solution.py:653
  65.4 1.7 %repack_0.1 = (f32[4,21,8,128]{3,2,1,0:T(8,128)S(1)}, f32[4,21,8,128]{3,2,1,0:T(8,128)S(1)}, f32[4,21,8,128]{3,2,1,0:T(8,128)S(1)}, f32[4,21,8,128]{3,2,1,0:T(8,128)S(1)}, s32[16]{0:T(128)S(1)}) custom-call(f32[16,21,8,128]{3,2,1,0:T(8,128)S(1)} %all-to-all-done.refs_0_), custom_call_target="tpu_custom_call" | custom-call | bytes 3000000 | tf_op jit(solution)/shard_map/repack_0/pallas_call | solution.py:281
  67.1 0.9 collective-permute-start
  68.0 0.7 collective-permute-start.1
  68.8 0.3 collective-permute-start.2
  69.0 8.4 %collective-permute-done.refs_0_ = f32[4,21,8,128]{3,2,1,0:T(8,128)S(1)} collective-permute-done((f32[4,21,8,128]{3,2,1,0:T(8,128)S(1)}, f32[4,21,8,128]{3,2,1,0:T(8,128)S(1)}, u32[]{:S(2)}, u32[]{:S(2)}) %collective-permute-start) | collective-permute-done | bytes 344096 | tf_op jit(solution)/shard_map/ppermute | solution.py:50
  77.4 7.4 %collective-permute-done.1.refs_1_ = f32[4,21,8,128]{3,2,1,0:T(8,128)S(1)} collective-permute-done((f32[4,21,8,128]{3,2,1,0:T(8,128)S(1)}, f32[4,21,8,128]{3,2,1,0:T(8,128)S(1)}, u32[]{:S(2)}, u32[]{:S(2)}) %collective-permute-start.1) | collective-permute-done | bytes 344096 | tf_op jit(solution)/shard_map/ppermute | solution.py:50
  84.9 1.7 %faces.1 = (f32[9,2,8,128]{3,2,1,0:T(8,128)S(1)}, f32[9,2,8,128]{3,2,1,0:T(8,128)S(1)}, f32[9,2,8,128]{3,2,1,0:T(8,128)S(1)}, f32[9,2,8,128]{3,2,1,0:T(8,128)S(1...) custom-call(f32[4,21,8,128]{3,2,1,0:T(8,128)S(1)} %collective-permute-done.refs_0_, ...), custom_call_target="tpu_custom_call" | custom-call | flops 10000000 | bytes 3000000 | tf_op jit(solution)/shard_map/faces/pallas_call | solution.py:486
  86.6 0.1 collective-permute-start.3
  86.7 1.7 %collective-permute-start.4 = (f32[9,2,8,128]{3,2,1,0:T(8,128)S(1)}, f32[9,2,8,128]{3,2,1,0:T(8,128)S(1)}, u32[]{:S(2)}, u32[]{:S(2)}) collective-permute-start(f32[9,2,8,128]{3,2,1,0:T(8,128)S(1)} %get-tuple-element.52), channel_id=1, source_target_pairs={{0,3},{1,0},{2,1},{3,2},{4,7},{5,4},{6,5},{7,6},{8,11},{9,8},{10,9... | collective-permute-start | bytes 221192 | tf_op jit(solution)/shard_map/ppermute | solution.py:635
  88.4 0.7 repack_1.1
  89.1 0.1 collective-permute-start.8
  89.2 1.4 %collective-permute-start.9 = (f32[4,8,8,128]{3,2,1,0:T(8,128)S(1)}, f32[4,8,8,128]{3,2,1,0:T(8,128)S(1)}, u32[]{:S(2)}, u32[]{:S(2)}) collective-permute-start(f32[4,8,8,128]{3,2,1,0:T(8,128)S(1)} %get-tuple-element.66), channel_id=1, source_target_pairs={{0,2},{1,3},{2,0},{3,1},{4,6},{5,7},{6,4},{7,5},{8,10},{9,11},{10,... | collective-permute-start | bytes 393224 | tf_op jit(solution)/shard_map/ppermute | solution.py:50
  90.6 0.4 collective-permute-start.10
  91.0 0.7 repack_2.1
  91.7 1.2 %collective-permute-start.5 = (f32[4,8,8,128]{3,2,1,0:T(8,128)S(1)}, f32[4,8,8,128]{3,2,1,0:T(8,128)S(1)}, u32[]{:S(2)}, u32[]{:S(2)}) collective-permute-start(f32[4,8,8,128]{3,2,1,0:T(8,128)S(1)} %get-tuple-element.59), channel_id=1, source_target_pairs={{0,3},{1,2},{2,1},{3,0},{4,7},{5,6},{6,5},{7,4},{8,11},{9,10},{10,... | collective-permute-start | bytes 393224 | tf_op jit(solution)/shard_map/ppermute | solution.py:50
  92.9 1.3 %collective-permute-start.6 = (f32[4,8,8,128]{3,2,1,0:T(8,128)S(1)}, f32[4,8,8,128]{3,2,1,0:T(8,128)S(1)}, u32[]{:S(2)}, u32[]{:S(2)}) collective-permute-start(f32[4,8,8,128]{3,2,1,0:T(8,128)S(1)} %get-tuple-element.60), channel_id=1, source_target_pairs={{0,2},{1,3},{2,0},{3,1},{4,6},{5,7},{6,4},{7,5},{8,10},{9,11},{10,... | collective-permute-start | bytes 393224 | tf_op jit(solution)/shard_map/ppermute | solution.py:50
  94.3 0.6 collective-permute-done.8.refs_0_
  95.0 2.7 %collective-permute-done.9.refs_1_ = f32[4,8,8,128]{3,2,1,0:T(8,128)S(1)} collective-permute-done((f32[4,8,8,128]{3,2,1,0:T(8,128)S(1)}, f32[4,8,8,128]{3,2,1,0:T(8,128)S(1)}, u32[]{:S(2)}, u32[]{:S(2)}) %collective-permute-start.9) | collective-permute-done | bytes 131104 | tf_op jit(solution)/shard_map/ppermute | solution.py:50
  97.6 1.0 collective-permute-start.11
  98.7 3.7 %collective-permute-start.12 = (f32[24,8,128]{2,1,0:T(8,128)S(1)}, f32[24,8,128]{2,1,0:T(8,128)S(1)}, u32[]{:S(2)}, u32[]{:S(2)}) collective-permute-start(f32[24,8,128]{2,1,0:T(8,128)S(1)} %pad_maximum_fusion.1), channel_id=1, source_target_pairs={{0,28},{4,0},{8,4},{12,8},{16,12},{20,16},{24,20},{28,24},{1,29},{... | collective-permute-start | bytes 294920 | tf_op jit(solution)/shard_map/ppermute | solution.py:635
  102.4 3.0 %collective-permute-done.11.refs_5_ = f32[24,8,128]{2,1,0:T(8,128)S(1)} collective-permute-done((f32[24,8,128]{2,1,0:T(8,128)S(1)}, f32[24,8,128]{2,1,0:T(8,128)S(1)}, u32[]{:S(2)}, u32[]{:S(2)}) %collective-permute-start.11) | collective-permute-done | bytes 98336 | tf_op jit(solution)/shard_map/ppermute | solution.py:635
  105.4 0.7 collective-permute-done.12.refs_6_
  106.2 4.3 %advance.1 = (f32[27,8,4096]{2,1,0:T(8,128)}, f32[27,12,8,128]{3,2,1,0:T(8,128)S(1)}) custom-call(s32[16]{0:T(128)S(1)} %get-tuple-element.58.plan_ref, f32[4,8,8,128]{3,2,1,0:T(8,128)S(1)} %collective-permute-done.8.refs_0_, f32[4,8,8,128]{3,2,1,0:T(8,128)S(1)} %collective-permute-done.9.refs_1_, f32[4,8,8,128]{3,2,1,0:T(8,128)S(1)} %collective-permute-done.10.refs_2_, ...), custom_call_target="tpu_custom_call" | custom-call | flops 10000000 | bytes 5000000 | tf_op jit(solution)/shard_map/advance/pallas_call | solution.py:590
  110.4 3.7 %finish.1 = f32[27,8,4096]{2,1,0:T(8,128)} custom-call(s32[16]{0:T(128)S(1)} %get-tuple-element.58.plan_ref, f32[4,8,8,128]{3,2,1,0:T(8,128)S(1)} %collective-permute-done.5.refs_0_, f32[4,8,8,128]{3,2,1,0:T(8,128)S(1)} %collective-permute-done.6.refs_1_, f32[4,8,8,128]{3,2,1,0:T(8,128)S(1)} %collective-permute-done.7.refs_2_, ...), custom_call_target="tpu_custom_call", output_to_operand_aliasing={{}: (9, {})} | custom-call | flops 10000000 | bytes 5000000 | tf_op jit(solution)/shard_map/finish/pallas_call | solution.py:615
  (12 shorter events, 0.1 us)
Async XLA Ops:
  3.4 40.1 %all-to-all-start = ((f32[16,21,8,128]{3,2,1,0:T(8,128)}), f32[16,21,8,128]{3,2,1,0:T(8,128)S(1)}, u32[]{:S(2)}, u32[]{:S(2)}) async-start(f32[16,21,8,128]{3,2,1,0:T(8,128)} %pre_0.1), calls=%async_computation | async-start | bytes 2752512 | tf_op jit(solution)/shard_map/all_to_all | solution.py:653
  43.5 18.3 %all-to-all-start.1 = ((f32[16,8,8,128]{3,2,1,0:T(8,128)}), f32[16,8,8,128]{3,2,1,0:T(8,128)S(1)}, u32[]{:S(2)}, u32[]{:S(2)}) async-start(f32[16,8,8,128]{3,2,1,0:T(8,128)} %pre_1.1), calls=%async_computation.1 | async-start | bytes 1048576 | tf_op jit(solution)/shard_map/all_to_all | solution.py:653
  61.8 29.2 %all-to-all-start.2 = ((f32[16,8,8,128]{3,2,1,0:T(8,128)}), f32[16,8,8,128]{3,2,1,0:T(8,128)S(1)}, u32[]{:S(2)}, u32[]{:S(2)}) async-start(f32[16,8,8,128]{3,2,1,0:T(8,128)} %pre_2.1), calls=%async_computation.2 | async-start | bytes 1048576 | tf_op jit(solution)/shard_map/all_to_all | solution.py:653
  67.1 10.4 %collective-permute-start = (f32[4,21,8,128]{3,2,1,0:T(8,128)S(1)}, f32[4,21,8,128]{3,2,1,0:T(8,128)S(1)}, u32[]{:S(2)}, u32[]{:S(2)}) collective-permute-start(f32[4,21,8,128]{3,2,1,0:T(8,128)S(1)} %get-tuple-element.43), channel_id=1, source_target_pairs={{0,3},{1,2},{2,1},{3,0},{4,7},{5,6},{6,5},{7,4},{8,11},{9,10},{10,... | collective-permute-start | bytes 1032200 | tf_op jit(solution)/shard_map/ppermute | solution.py:50
  68.0 16.9 %collective-permute-start.1 = (f32[4,21,8,128]{3,2,1,0:T(8,128)S(1)}, f32[4,21,8,128]{3,2,1,0:T(8,128)S(1)}, u32[]{:S(2)}, u32[]{:S(2)}) collective-permute-start(f32[4,21,8,128]{3,2,1,0:T(8,128)S(1)} %get-tuple-element.44), channel_id=1, source_target_pairs={{0,2},{1,3},{2,0},{3,1},{4,6},{5,7},{6,4},{7,5},{8,10},{9,11},{10,... | collective-permute-start | bytes 1032200 | tf_op jit(solution)/shard_map/ppermute | solution.py:50
  68.8 16.1 %collective-permute-start.2 = (f32[4,21,8,128]{3,2,1,0:T(8,128)S(1)}, f32[4,21,8,128]{3,2,1,0:T(8,128)S(1)}, u32[]{:S(2)}, u32[]{:S(2)}) collective-permute-start(f32[4,21,8,128]{3,2,1,0:T(8,128)S(1)} %get-tuple-element.45), channel_id=1, source_target_pairs={{0,1},{1,0},{2,3},{3,2},{4,5},{5,4},{6,7},{7,6},{8,9},{9,8},{10,11... | collective-permute-start | bytes 1032200 | tf_op jit(solution)/shard_map/ppermute | solution.py:50
  86.6 4.4 %collective-permute-start.3 = (f32[9,2,8,128]{3,2,1,0:T(8,128)S(1)}, f32[9,2,8,128]{3,2,1,0:T(8,128)S(1)}, u32[]{:S(2)}, u32[]{:S(2)}) collective-permute-start(f32[9,2,8,128]{3,2,1,0:T(8,128)S(1)} %get-tuple-element.51), channel_id=1, source_target_pairs={{0,1},{1,2},{2,3},{3,0},{4,5},{5,6},{6,7},{7,4},{8,9},{9,10},{10,1... | collective-permute-start | bytes 221192 | tf_op jit(solution)/shard_map/ppermute | solution.py:635
  86.7 4.3 %collective-permute-start.4 = (f32[9,2,8,128]{3,2,1,0:T(8,128)S(1)}, f32[9,2,8,128]{3,2,1,0:T(8,128)S(1)}, u32[]{:S(2)}, u32[]{:S(2)}) collective-permute-start(f32[9,2,8,128]{3,2,1,0:T(8,128)S(1)} %get-tuple-element.52), channel_id=1, source_target_pairs={{0,3},{1,0},{2,1},{3,2},{4,7},{5,4},{6,5},{7,6},{8,11},{9,8},{10,9... | collective-permute-start | bytes 221192 | tf_op jit(solution)/shard_map/ppermute | solution.py:635
  89.1 5.8 %collective-permute-start.8 = (f32[4,8,8,128]{3,2,1,0:T(8,128)S(1)}, f32[4,8,8,128]{3,2,1,0:T(8,128)S(1)}, u32[]{:S(2)}, u32[]{:S(2)}) collective-permute-start(f32[4,8,8,128]{3,2,1,0:T(8,128)S(1)} %get-tuple-element.65), channel_id=1, source_target_pairs={{0,3},{1,2},{2,1},{3,0},{4,7},{5,6},{6,5},{7,4},{8,11},{9,10},{10,... | collective-permute-start | bytes 393224 | tf_op jit(solution)/shard_map/ppermute | solution.py:50
  89.2 8.5 %collective-permute-start.9 = (f32[4,8,8,128]{3,2,1,0:T(8,128)S(1)}, f32[4,8,8,128]{3,2,1,0:T(8,128)S(1)}, u32[]{:S(2)}, u32[]{:S(2)}) collective-permute-start(f32[4,8,8,128]{3,2,1,0:T(8,128)S(1)} %get-tuple-element.66), channel_id=1, source_target_pairs={{0,2},{1,3},{2,0},{3,1},{4,6},{5,7},{6,4},{7,5},{8,10},{9,11},{10,... | collective-permute-start | bytes 393224 | tf_op jit(solution)/shard_map/ppermute | solution.py:50
  90.6 8.1 %collective-permute-start.10 = (f32[4,8,8,128]{3,2,1,0:T(8,128)S(1)}, f32[4,8,8,128]{3,2,1,0:T(8,128)S(1)}, u32[]{:S(2)}, u32[]{:S(2)}) collective-permute-start(f32[4,8,8,128]{3,2,1,0:T(8,128)S(1)} %get-tuple-element.67), channel_id=1, source_target_pairs={{0,1},{1,0},{2,3},{3,2},{4,5},{5,4},{6,7},{7,6},{8,9},{9,8},{10,11... | collective-permute-start | bytes 393224 | tf_op jit(solution)/shard_map/ppermute | solution.py:50
  91.7 18.7 %collective-permute-start.5 = (f32[4,8,8,128]{3,2,1,0:T(8,128)S(1)}, f32[4,8,8,128]{3,2,1,0:T(8,128)S(1)}, u32[]{:S(2)}, u32[]{:S(2)}) collective-permute-start(f32[4,8,8,128]{3,2,1,0:T(8,128)S(1)} %get-tuple-element.59), channel_id=1, source_target_pairs={{0,3},{1,2},{2,1},{3,0},{4,7},{5,6},{6,5},{7,4},{8,11},{9,10},{10,... | collective-permute-start | bytes 393224 | tf_op jit(solution)/shard_map/ppermute | solution.py:50
  92.9 17.5 %collective-permute-start.6 = (f32[4,8,8,128]{3,2,1,0:T(8,128)S(1)}, f32[4,8,8,128]{3,2,1,0:T(8,128)S(1)}, u32[]{:S(2)}, u32[]{:S(2)}) collective-permute-start(f32[4,8,8,128]{3,2,1,0:T(8,128)S(1)} %get-tuple-element.60), channel_id=1, source_target_pairs={{0,2},{1,3},{2,0},{3,1},{4,6},{5,7},{6,4},{7,5},{8,10},{9,11},{10,... | collective-permute-start | bytes 393224 | tf_op jit(solution)/shard_map/ppermute | solution.py:50
  94.9 15.5 %collective-permute-start.7 = (f32[4,8,8,128]{3,2,1,0:T(8,128)S(1)}, f32[4,8,8,128]{3,2,1,0:T(8,128)S(1)}, u32[]{:S(2)}, u32[]{:S(2)}) collective-permute-start(f32[4,8,8,128]{3,2,1,0:T(8,128)S(1)} %get-tuple-element.61), channel_id=1, source_target_pairs={{0,1},{1,0},{2,3},{3,2},{4,5},{5,4},{6,7},{7,6},{8,9},{9,8},{10,11... | collective-permute-start | bytes 393224 | tf_op jit(solution)/shard_map/ppermute | solution.py:50
  97.6 7.8 %collective-permute-start.11 = (f32[24,8,128]{2,1,0:T(8,128)S(1)}, f32[24,8,128]{2,1,0:T(8,128)S(1)}, u32[]{:S(2)}, u32[]{:S(2)}) collective-permute-start(f32[24,8,128]{2,1,0:T(8,128)S(1)} %pad_maximum_fusion), channel_id=1, source_target_pairs={{0,4},{4,8},{8,12},{12,16},{16,20},{20,24},{24,28},{28,0},{1,5},{5... | collective-permute-start | bytes 294920 | tf_op jit(solution)/shard_map/ppermute | solution.py:635
  98.7 7.5 %collective-permute-start.12 = (f32[24,8,128]{2,1,0:T(8,128)S(1)}, f32[24,8,128]{2,1,0:T(8,128)S(1)}, u32[]{:S(2)}, u32[]{:S(2)}) collective-permute-start(f32[24,8,128]{2,1,0:T(8,128)S(1)} %pad_maximum_fusion.1), channel_id=1, source_target_pairs={{0,28},{4,0},{8,4},{12,8},{16,12},{20,16},{24,20},{28,24},{1,29},{... | collective-permute-start | bytes 294920 | tf_op jit(solution)/shard_map/ppermute | solution.py:635

commit v9 on v8

--- a/solution.py
+++ b/solution.py
@@ -635,6 +635,10 @@
     return lax.ppermute(value, axis, [(i, (i + step) % count) for i in range(count)])
 
 
+def after(value, *earlier):
+    return lax.optimization_barrier((value, *earlier))[0]
+
+
 def on_device(populations, destination, refinement):
     blocks = populations.shape[0]
     row_count = lax.axis_size("row")
@@ -643,19 +647,21 @@
     cap_col = 2 * ((blocks + col_count - 1) // col_count)
     ordered = jnp.transpose(populations, (1, 0, 2))
 
-    in_row = []
-    for part in range(len(CHUNKS)):
-        sent = pre(ordered, destination, refinement, part, row_count, cap_row, blocks * col_count)
-        if part:
-            sent, in_row[-1] = lax.optimization_barrier((sent, in_row[-1]))
-        else:
-            sent, destination = lax.optimization_barrier((sent, destination))
-        in_row.append(lax.all_to_all(sent, "row", split_axis=0, concat_axis=0, tiled=True))
+    def prepared(part, *earlier):
+        first = after(destination, *earlier)
+        return pre(ordered, first, refinement, part, row_count, cap_row, blocks * col_count)
+
+    def to_rows(sent):
+        return lax.all_to_all(sent, "row", split_axis=0, concat_axis=0, tiled=True)
 
     def to_columns(packed):
         return [exchanged(packed[d], "col", d) for d in range(col_count - 1, 0, -1)] + [packed[0]]
 
+    sent = prepared(0)
+    in_row = [to_rows(sent)]
+    in_row.append(to_rows(after(prepared(1, sent), in_row[0])))
     packed, plan = repack(in_row[0], None, 0, col_count, cap_col, blocks)
+    in_row.append(to_rows(prepared(2, packed[0])))
     ylo, yhi, xlo, xhi, picked, fields = faces(to_columns(packed))
     below, above = shifted(yhi, "col", 1), shifted(ylo, "col", -1)
     middle = to_columns(repack(in_row[1], plan, 1, col_count, cap_col, blocks))

time: 114 us -> 110 us (0.965)
  waiting for transfers between devices: 66.1 us -> 61.5 us
    all_to_all x3, waiting for transfers between devices: 43.1 us -> 41.4 us  [to_rows(): return lax.all_to_all(sent, 'row', split_axis=0, concat_axis=0, tiled=True)]
    ppermute x9, waiting for transfers between devices: 19.2 us -> 17.6 us  [exchanged(): return lax.ppermute(value, axis, pairs)]
    ppermute x4, waiting for transfers between devices: 3.79 us -> 2.5 us  [shifted(): lax.ppermute(value, axis, [(i, (i + step) % count) for i in range(count)])]
  transfers between devices with their start and end apart: 16 -> 16, of which waited for: 8 -> 9; matrix products, arithmetic and copies ran while one was open for 0% -> 0% of each run, Pallas kernels for 12% -> 12%
where the time goes in v9:
time: 110 us; the launch traced here: 109 us
  waiting for transfers between devices  61.5 us (56%)
  starting transfers between devices  27.1 us (25%)
  Pallas kernels  20.4 us (19%)
    all_to_all x3, waiting for transfers between devices, to_rows(): return lax.all_to_all(sent, 'row', split_axis=0, concat_axis=0, tiled=True)  41.4 us
    ppermute x9, waiting for transfers between devices, exchanged(): return lax.ppermute(value, axis, pairs)  17.6 us
    all_to_all x3, starting transfers between devices, to_rows(): return lax.all_to_all(sent, 'row', split_axis=0, concat_axis=0, tiled=True)  14.5 us
    pallas_call x3, Pallas kernels, pre(): pl.pallas_call(functools.partial(pre_kernel, cap, row_count, per_row, par...  7.78 us
    ppermute x4, starting transfers between devices, shifted(): lax.ppermute(value, axis, [(i, (i + step) % count) for i in range(count)])  6.62 us
    ppermute x9, starting transfers between devices, exchanged(): return lax.ppermute(value, axis, pairs)  5.93 us
    pallas_call x1, Pallas kernels, advance(): pl.pallas_call(functools.partial(advance_kernel, len(homes)), grid_spec=p...  4.27 us
    pallas_call x1, Pallas kernels, finish(): pl.pallas_call(functools.partial(finish_kernel, len(homes)), grid_spec=pl...  3.65 us
  transfers between devices with their start and end apart: 16, of which 9 were waited for; matrix products, arithmetic and copies ran while one was open for 0% of the time, Pallas kernels for 12%

profile of v9, /device:TPU:0, one launch (start us, length us, event | category | flops | bytes accessed | tf_op | source)
XLA Modules:
  0.0 109.1 jit_solution(5864807542230739466)
XLA Ops:
  0.0 3.4 %pre_0.1 = f32[16,21,8,128]{3,2,1,0:T(8,128)} custom-call(s32[8]{0:T(128)} %dest_hbm.2, s32[8]{0:T(128)} %level_hbm.5, f32[27,8,4096]{2,1,0:T(8,128)} %bitcast.14), custom_call_target="tpu_custom_call" | custom-call | flops 10000000 | bytes 4000000 | tf_op jit(solution)/shard_map/pre_0/pallas_call | solution.py:202
  3.4 7.3 %all-to-all-start = ((f32[16,21,8,128]{3,2,1,0:T(8,128)}), f32[16,21,8,128]{3,2,1,0:T(8,128)S(1)}, u32[]{:S(2)}, u32[]{:S(2)}) async-start(f32[16,21,8,128]{3,2,1,0:T(8,128)} %pre_0.1), calls=%async_computation | async-start | bytes 2752512 | tf_op jit(solution)/shard_map/all_to_all | solution.py:655
  10.7 2.2 %pre_1.1 = f32[16,8,8,128]{3,2,1,0:T(8,128)} custom-call(s32[8]{0:T(128)} %dest_hbm.2, s32[8]{0:T(128)} %level_hbm.5, f32[27,8,4096]{2,1,0:T(8,128)} %bitcast.15), custom_call_target="tpu_custom_call" | custom-call | flops 10000000 | bytes 4000000 | tf_op jit(solution)/shard_map/pre_1/pallas_call | solution.py:202
  12.9 30.6 %all-to-all-done.refs_0_ = f32[16,21,8,128]{3,2,1,0:T(8,128)S(1)} async-done(((f32[16,21,8,128]{3,2,1,0:T(8,128)}), f32[16,21,8,128]{3,2,1,0:T(8,128)S(1)}, u32[]{:S(2)}, u32[]{:S(2)}) %all-to-all-start) | async-done | bytes 1376288 | tf_op jit(solution)/shard_map/all_to_all | solution.py:655
  43.5 3.6 %all-to-all-start.2 = ((f32[16,8,8,128]{3,2,1,0:T(8,128)}), f32[16,8,8,128]{3,2,1,0:T(8,128)S(1)}, u32[]{:S(2)}, u32[]{:S(2)}) async-start(f32[16,8,8,128]{3,2,1,0:T(8,128)} %pre_1.1), calls=%async_computation.2 | async-start | bytes 1048576 | tf_op jit(solution)/shard_map/all_to_all | solution.py:655
  47.1 1.7 %repack_0.1 = (f32[4,21,8,128]{3,2,1,0:T(8,128)S(1)}, f32[4,21,8,128]{3,2,1,0:T(8,128)S(1)}, f32[4,21,8,128]{3,2,1,0:T(8,128)S(1)}, f32[4,21,8,128]{3,2,1,0:T(8,128)S(1)}, s32[16]{0:T(128)S(1)}) custom-call(f32[16,21,8,128]{3,2,1,0:T(8,128)S(1)} %all-to-all-done.refs_0_), custom_call_target="tpu_custom_call" | custom-call | bytes 3000000 | tf_op jit(solution)/shard_map/repack_0/pallas_call | solution.py:281
  48.8 2.2 %pre_2.1 = f32[16,8,8,128]{3,2,1,0:T(8,128)} custom-call(s32[8]{0:T(128)} %dest_hbm.2, s32[8]{0:T(128)} %level_hbm.5, f32[27,8,4096]{2,1,0:T(8,128)} %bitcast.16), custom_call_target="tpu_custom_call" | custom-call | flops 10000000 | bytes 4000000 | tf_op jit(solution)/shard_map/pre_2/pallas_call | solution.py:202
  51.0 10.8 %all-to-all-done.2.refs_1_ = f32[16,8,8,128]{3,2,1,0:T(8,128)S(1)} async-done(((f32[16,8,8,128]{3,2,1,0:T(8,128)}), f32[16,8,8,128]{3,2,1,0:T(8,128)S(1)}, u32[]{:S(2)}, u32[]{:S(2)}) %all-to-all-start.2) | async-done | bytes 524320 | tf_op jit(solution)/shard_map/all_to_all | solution.py:655
  61.8 3.6 %all-to-all-start.1 = ((f32[16,8,8,128]{3,2,1,0:T(8,128)}), f32[16,8,8,128]{3,2,1,0:T(8,128)S(1)}, u32[]{:S(2)}, u32[]{:S(2)}) async-start(f32[16,8,8,128]{3,2,1,0:T(8,128)} %pre_2.1), calls=%async_computation.1 | async-start | bytes 1048576 | tf_op jit(solution)/shard_map/all_to_all | solution.py:655
  65.4 0.9 collective-permute-start
  66.3 0.7 collective-permute-start.1
  67.0 0.3 collective-permute-start.2
  67.3 8.4 %collective-permute-done.refs_0_ = f32[4,21,8,128]{3,2,1,0:T(8,128)S(1)} collective-permute-done((f32[4,21,8,128]{3,2,1,0:T(8,128)S(1)}, f32[4,21,8,128]{3,2,1,0:T(8,128)S(1)}, u32[]{:S(2)}, u32[]{:S(2)}) %collective-permute-start) | collective-permute-done | bytes 344096 | tf_op jit(solution)/shard_map/ppermute | solution.py:50
  75.7 7.4 %collective-permute-done.1.refs_1_ = f32[4,21,8,128]{3,2,1,0:T(8,128)S(1)} collective-permute-done((f32[4,21,8,128]{3,2,1,0:T(8,128)S(1)}, f32[4,21,8,128]{3,2,1,0:T(8,128)S(1)}, u32[]{:S(2)}, u32[]{:S(2)}) %collective-permute-start.1) | collective-permute-done | bytes 344096 | tf_op jit(solution)/shard_map/ppermute | solution.py:50
  83.1 1.7 %faces.1 = (f32[9,2,8,128]{3,2,1,0:T(8,128)S(1)}, f32[9,2,8,128]{3,2,1,0:T(8,128)S(1)}, f32[9,2,8,128]{3,2,1,0:T(8,128)S(1)}, f32[9,2,8,128]{3,2,1,0:T(8,128)S(1...) custom-call(f32[4,21,8,128]{3,2,1,0:T(8,128)S(1)} %collective-permute-done.refs_0_, ...), custom_call_target="tpu_custom_call" | custom-call | flops 10000000 | bytes 3000000 | tf_op jit(solution)/shard_map/faces/pallas_call | solution.py:486
  84.9 0.1 collective-permute-start.3
  85.0 1.7 %collective-permute-start.4 = (f32[9,2,8,128]{3,2,1,0:T(8,128)S(1)}, f32[9,2,8,128]{3,2,1,0:T(8,128)S(1)}, u32[]{:S(2)}, u32[]{:S(2)}) collective-permute-start(f32[9,2,8,128]{3,2,1,0:T(8,128)S(1)} %get-tuple-element.45), channel_id=1, source_target_pairs={{0,3},{1,0},{2,1},{3,2},{4,7},{5,4},{6,5},{7,6},{8,11},{9,8},{10,9... | collective-permute-start | bytes 221192 | tf_op jit(solution)/shard_map/ppermute | solution.py:635
  86.7 0.7 repack_1.1
  87.4 1.3 %collective-permute-done.3.refs_7_.refs_6_ = f32[9,2,8,128]{3,2,1,0:T(8,128)S(1)} collective-permute-done((f32[9,2,8,128]{3,2,1,0:T(8,128)S(1)}, f32[9,2,8,128]{3,2,1,0:T(8,128)S(1)}, u32[]{:S(2)}, u32[]{:S(2)}) %collective-permute-start.3) | collective-permute-done | bytes 73760 | tf_op jit(solution)/shard_map/ppermute | solution.py:635
  88.7 2.1 %collective-permute-start.11 = (f32[24,8,128]{2,1,0:T(8,128)S(1)}, f32[24,8,128]{2,1,0:T(8,128)S(1)}, u32[]{:S(2)}, u32[]{:S(2)}) collective-permute-start(f32[24,8,128]{2,1,0:T(8,128)S(1)} %pad_maximum_fusion), channel_id=1, source_target_pairs={{0,4},{4,8},{8,12},{12,16},{16,20},{20,24},{24,28},{28,0},{1,5},{5... | collective-permute-start | bytes 294920 | tf_op jit(solution)/shard_map/ppermute | solution.py:635
  90.8 2.8 %collective-permute-start.12 = (f32[24,8,128]{2,1,0:T(8,128)S(1)}, f32[24,8,128]{2,1,0:T(8,128)S(1)}, u32[]{:S(2)}, u32[]{:S(2)}) collective-permute-start(f32[24,8,128]{2,1,0:T(8,128)S(1)} %pad_maximum_fusion.1), channel_id=1, source_target_pairs={{0,28},{4,0},{8,4},{12,8},{16,12},{20,16},{24,20},{28,24},{1,29},{... | collective-permute-start | bytes 294920 | tf_op jit(solution)/shard_map/ppermute | solution.py:635
  93.6 1.3 %collective-permute-start.9 = (f32[4,8,8,128]{3,2,1,0:T(8,128)S(1)}, f32[4,8,8,128]{3,2,1,0:T(8,128)S(1)}, u32[]{:S(2)}, u32[]{:S(2)}) collective-permute-start(f32[4,8,8,128]{3,2,1,0:T(8,128)S(1)} %get-tuple-element.60), channel_id=1, source_target_pairs={{0,2},{1,3},{2,0},{3,1},{4,6},{5,7},{6,4},{7,5},{8,10},{9,11},{10,... | collective-permute-start | bytes 393224 | tf_op jit(solution)/shard_map/ppermute | solution.py:50
  94.9 0.2 collective-permute-start.10
  95.1 0.7 repack_2.1
  95.8 1.0 collective-permute-done.11.refs_5_
  96.8 1.3 %collective-permute-start.5 = (f32[4,8,8,128]{3,2,1,0:T(8,128)S(1)}, f32[4,8,8,128]{3,2,1,0:T(8,128)S(1)}, u32[]{:S(2)}, u32[]{:S(2)}) collective-permute-start(f32[4,8,8,128]{3,2,1,0:T(8,128)S(1)} %get-tuple-element.52), channel_id=1, source_target_pairs={{0,3},{1,2},{2,1},{3,0},{4,7},{5,6},{6,5},{7,4},{8,11},{9,10},{10,... | collective-permute-start | bytes 393224 | tf_op jit(solution)/shard_map/ppermute | solution.py:50
  98.1 0.2 collective-permute-done.12.refs_6_
  98.4 1.1 %collective-permute-start.6 = (f32[4,8,8,128]{3,2,1,0:T(8,128)S(1)}, f32[4,8,8,128]{3,2,1,0:T(8,128)S(1)}, u32[]{:S(2)}, u32[]{:S(2)}) collective-permute-start(f32[4,8,8,128]{3,2,1,0:T(8,128)S(1)} %get-tuple-element.53), channel_id=1, source_target_pairs={{0,2},{1,3},{2,0},{3,1},{4,6},{5,7},{6,4},{7,5},{8,10},{9,11},{10,... | collective-permute-start | bytes 393224 | tf_op jit(solution)/shard_map/ppermute | solution.py:50
  99.5 0.4 collective-permute-done.9.refs_1_
  99.9 4.3 %advance.1 = (f32[27,8,4096]{2,1,0:T(8,128)}, f32[27,12,8,128]{3,2,1,0:T(8,128)S(1)}) custom-call(s32[16]{0:T(128)S(1)} %get-tuple-element.51.plan_ref, f32[4,8,8,128]{3,2,1,0:T(8,128)S(1)} %collective-permute-done.8.refs_0_, f32[4,8,8,128]{3,2,1,0:T(8,128)S(1)} %collective-permute-done.9.refs_1_, f32[4,8,8,128]{3,2,1,0:T(8,128)S(1)} %collective-permute-done.10.refs_2_, ...), custom_call_target="tpu_custom_call" | custom-call | flops 10000000 | bytes 5000000 | tf_op jit(solution)/shard_map/advance/pallas_call | solution.py:590
  104.1 1.3 %collective-permute-done.6.refs_1_ = f32[4,8,8,128]{3,2,1,0:T(8,128)S(1)} collective-permute-done((f32[4,8,8,128]{3,2,1,0:T(8,128)S(1)}, f32[4,8,8,128]{3,2,1,0:T(8,128)S(1)}, u32[]{:S(2)}, u32[]{:S(2)}) %collective-permute-start.6) | collective-permute-done | bytes 131104 | tf_op jit(solution)/shard_map/ppermute | solution.py:50
  105.5 3.6 %finish.1 = f32[27,8,4096]{2,1,0:T(8,128)} custom-call(s32[16]{0:T(128)S(1)} %get-tuple-element.51.plan_ref, f32[4,8,8,128]{3,2,1,0:T(8,128)S(1)} %collective-permute-done.5.refs_0_, f32[4,8,8,128]{3,2,1,0:T(8,128)S(1)} %collective-permute-done.6.refs_1_, f32[4,8,8,128]{3,2,1,0:T(8,128)S(1)} %collective-permute-done.7.refs_2_, ...), custom_call_target="tpu_custom_call", output_to_operand_aliasing={{}: (9, {})} | custom-call | flops 10000000 | bytes 5000000 | tf_op jit(solution)/shard_map/finish/pallas_call | solution.py:615
  (12 shorter events, 0.1 us)
Async XLA Ops:
  3.4 40.1 %all-to-all-start = ((f32[16,21,8,128]{3,2,1,0:T(8,128)}), f32[16,21,8,128]{3,2,1,0:T(8,128)S(1)}, u32[]{:S(2)}, u32[]{:S(2)}) async-start(f32[16,21,8,128]{3,2,1,0:T(8,128)} %pre_0.1), calls=%async_computation | async-start | bytes 2752512 | tf_op jit(solution)/shard_map/all_to_all | solution.py:655
  43.5 18.3 %all-to-all-start.2 = ((f32[16,8,8,128]{3,2,1,0:T(8,128)}), f32[16,8,8,128]{3,2,1,0:T(8,128)S(1)}, u32[]{:S(2)}, u32[]{:S(2)}) async-start(f32[16,8,8,128]{3,2,1,0:T(8,128)} %pre_1.1), calls=%async_computation.2 | async-start | bytes 1048576 | tf_op jit(solution)/shard_map/all_to_all | solution.py:655
  61.8 26.9 %all-to-all-start.1 = ((f32[16,8,8,128]{3,2,1,0:T(8,128)}), f32[16,8,8,128]{3,2,1,0:T(8,128)S(1)}, u32[]{:S(2)}, u32[]{:S(2)}) async-start(f32[16,8,8,128]{3,2,1,0:T(8,128)} %pre_2.1), calls=%async_computation.1 | async-start | bytes 1048576 | tf_op jit(solution)/shard_map/all_to_all | solution.py:655
  65.4 10.3 %collective-permute-start = (f32[4,21,8,128]{3,2,1,0:T(8,128)S(1)}, f32[4,21,8,128]{3,2,1,0:T(8,128)S(1)}, u32[]{:S(2)}, u32[]{:S(2)}) collective-permute-start(f32[4,21,8,128]{3,2,1,0:T(8,128)S(1)} %get-tuple-element.37), channel_id=1, source_target_pairs={{0,3},{1,2},{2,1},{3,0},{4,7},{5,6},{6,5},{7,4},{8,11},{9,10},{10,... | collective-permute-start | bytes 1032200 | tf_op jit(solution)/shard_map/ppermute | solution.py:50
  66.3 16.9 %collective-permute-start.1 = (f32[4,21,8,128]{3,2,1,0:T(8,128)S(1)}, f32[4,21,8,128]{3,2,1,0:T(8,128)S(1)}, u32[]{:S(2)}, u32[]{:S(2)}) collective-permute-start(f32[4,21,8,128]{3,2,1,0:T(8,128)S(1)} %get-tuple-element.38), channel_id=1, source_target_pairs={{0,2},{1,3},{2,0},{3,1},{4,6},{5,7},{6,4},{7,5},{8,10},{9,11},{10,... | collective-permute-start | bytes 1032200 | tf_op jit(solution)/shard_map/ppermute | solution.py:50
  67.0 16.1 %collective-permute-start.2 = (f32[4,21,8,128]{3,2,1,0:T(8,128)S(1)}, f32[4,21,8,128]{3,2,1,0:T(8,128)S(1)}, u32[]{:S(2)}, u32[]{:S(2)}) collective-permute-start(f32[4,21,8,128]{3,2,1,0:T(8,128)S(1)} %get-tuple-element.39), channel_id=1, source_target_pairs={{0,1},{1,0},{2,3},{3,2},{4,5},{5,4},{6,7},{7,6},{8,9},{9,8},{10,11... | collective-permute-start | bytes 1032200 | tf_op jit(solution)/shard_map/ppermute | solution.py:50
  84.9 3.8 %collective-permute-start.3 = (f32[9,2,8,128]{3,2,1,0:T(8,128)S(1)}, f32[9,2,8,128]{3,2,1,0:T(8,128)S(1)}, u32[]{:S(2)}, u32[]{:S(2)}) collective-permute-start(f32[9,2,8,128]{3,2,1,0:T(8,128)S(1)} %get-tuple-element.44), channel_id=1, source_target_pairs={{0,1},{1,2},{2,3},{3,0},{4,5},{5,6},{6,7},{7,4},{8,9},{9,10},{10,1... | collective-permute-start | bytes 221192 | tf_op jit(solution)/shard_map/ppermute | solution.py:635
  85.0 3.7 %collective-permute-start.4 = (f32[9,2,8,128]{3,2,1,0:T(8,128)S(1)}, f32[9,2,8,128]{3,2,1,0:T(8,128)S(1)}, u32[]{:S(2)}, u32[]{:S(2)}) collective-permute-start(f32[9,2,8,128]{3,2,1,0:T(8,128)S(1)} %get-tuple-element.45), channel_id=1, source_target_pairs={{0,3},{1,0},{2,1},{3,2},{4,7},{5,4},{6,5},{7,6},{8,11},{9,8},{10,9... | collective-permute-start | bytes 221192 | tf_op jit(solution)/shard_map/ppermute | solution.py:635
  87.3 12.1 %collective-permute-start.8 = (f32[4,8,8,128]{3,2,1,0:T(8,128)S(1)}, f32[4,8,8,128]{3,2,1,0:T(8,128)S(1)}, u32[]{:S(2)}, u32[]{:S(2)}) collective-permute-start(f32[4,8,8,128]{3,2,1,0:T(8,128)S(1)} %get-tuple-element.59), channel_id=1, source_target_pairs={{0,3},{1,2},{2,1},{3,0},{4,7},{5,6},{6,5},{7,4},{8,11},{9,10},{10,... | collective-permute-start | bytes 393224 | tf_op jit(solution)/shard_map/ppermute | solution.py:50
  88.7 8.1 %collective-permute-start.11 = (f32[24,8,128]{2,1,0:T(8,128)S(1)}, f32[24,8,128]{2,1,0:T(8,128)S(1)}, u32[]{:S(2)}, u32[]{:S(2)}) collective-permute-start(f32[24,8,128]{2,1,0:T(8,128)S(1)} %pad_maximum_fusion), channel_id=1, source_target_pairs={{0,4},{4,8},{8,12},{12,16},{16,20},{20,24},{24,28},{28,0},{1,5},{5... | collective-permute-start | bytes 294920 | tf_op jit(solution)/shard_map/ppermute | solution.py:635
  90.8 7.6 %collective-permute-start.12 = (f32[24,8,128]{2,1,0:T(8,128)S(1)}, f32[24,8,128]{2,1,0:T(8,128)S(1)}, u32[]{:S(2)}, u32[]{:S(2)}) collective-permute-start(f32[24,8,128]{2,1,0:T(8,128)S(1)} %pad_maximum_fusion.1), channel_id=1, source_target_pairs={{0,28},{4,0},{8,4},{12,8},{16,12},{20,16},{24,20},{28,24},{1,29},{... | collective-permute-start | bytes 294920 | tf_op jit(solution)/shard_map/ppermute | solution.py:635
  93.6 6.3 %collective-permute-start.9 = (f32[4,8,8,128]{3,2,1,0:T(8,128)S(1)}, f32[4,8,8,128]{3,2,1,0:T(8,128)S(1)}, u32[]{:S(2)}, u32[]{:S(2)}) collective-permute-start(f32[4,8,8,128]{3,2,1,0:T(8,128)S(1)} %get-tuple-element.60), channel_id=1, source_target_pairs={{0,2},{1,3},{2,0},{3,1},{4,6},{5,7},{6,4},{7,5},{8,10},{9,11},{10,... | collective-permute-start | bytes 393224 | tf_op jit(solution)/shard_map/ppermute | solution.py:50
  94.9 5.0 %collective-permute-start.10 = (f32[4,8,8,128]{3,2,1,0:T(8,128)S(1)}, f32[4,8,8,128]{3,2,1,0:T(8,128)S(1)}, u32[]{:S(2)}, u32[]{:S(2)}) collective-permute-start(f32[4,8,8,128]{3,2,1,0:T(8,128)S(1)} %get-tuple-element.61), channel_id=1, source_target_pairs={{0,1},{1,0},{2,3},{3,2},{4,5},{5,4},{6,7},{7,6},{8,9},{9,8},{10,11... | collective-permute-start | bytes 393224 | tf_op jit(solution)/shard_map/ppermute | solution.py:50
  96.8 7.3 %collective-permute-start.5 = (f32[4,8,8,128]{3,2,1,0:T(8,128)S(1)}, f32[4,8,8,128]{3,2,1,0:T(8,128)S(1)}, u32[]{:S(2)}, u32[]{:S(2)}) collective-permute-start(f32[4,8,8,128]{3,2,1,0:T(8,128)S(1)} %get-tuple-element.52), channel_id=1, source_target_pairs={{0,3},{1,2},{2,1},{3,0},{4,7},{5,6},{6,5},{7,4},{8,11},{9,10},{10,... | collective-permute-start | bytes 393224 | tf_op jit(solution)/shard_map/ppermute | solution.py:50
  98.4 7.1 %collective-permute-start.6 = (f32[4,8,8,128]{3,2,1,0:T(8,128)S(1)}, f32[4,8,8,128]{3,2,1,0:T(8,128)S(1)}, u32[]{:S(2)}, u32[]{:S(2)}) collective-permute-start(f32[4,8,8,128]{3,2,1,0:T(8,128)S(1)} %get-tuple-element.53), channel_id=1, source_target_pairs={{0,2},{1,3},{2,0},{3,1},{4,6},{5,7},{6,4},{7,5},{8,10},{9,11},{10,... | collective-permute-start | bytes 393224 | tf_op jit(solution)/shard_map/ppermute | solution.py:50
  99.5 6.0 %collective-permute-start.7 = (f32[4,8,8,128]{3,2,1,0:T(8,128)S(1)}, f32[4,8,8,128]{3,2,1,0:T(8,128)S(1)}, u32[]{:S(2)}, u32[]{:S(2)}) collective-permute-start(f32[4,8,8,128]{3,2,1,0:T(8,128)S(1)} %get-tuple-element.54), channel_id=1, source_target_pairs={{0,1},{1,0},{2,3},{3,2},{4,5},{5,4},{6,7},{7,6},{8,9},{9,8},{10,11... | collective-permute-start | bytes 393224 | tf_op jit(solution)/shard_map/ppermute | solution.py:50

commit v10 on v9

--- a/solution.py
+++ b/solution.py
@@ -15,8 +15,8 @@
 NFIELD = 9
 GROUPS = 4
 WIDTH = EDGE // GROUPS
-CHUNKS = ((0, 3), (1,), (2,))
-INNER = (1, 2)
+CHUNKS = ((0, 3), (1, 2))
+INNER = CHUNKS[1]
 SIDE_TILES = 3
 LATE_TILES = -(-NFIELD * (SUB - 1) // SUB)
 VMEM_LIMIT = 20 * 1024 * 1024
@@ -28,7 +28,7 @@
 
 
 def tiles_of(part):
-    return LATE_TILES if part else len(CHUNKS[0]) * NFIELD + SIDE_TILES
+    return len(INNER) * LATE_TILES if part else len(CHUNKS[0]) * NFIELD + SIDE_TILES
 
 
 def free_place(c):
@@ -153,7 +153,7 @@
                 turn = (place - c) * EDGE % LANES
                 for n, field in enumerate(fields_at(step, c)):
                     other = pltpu.roll(last[n], turn, axis=1) if turn else last[n]
-                    base = ((step * NFIELD + n) * (chunks - 1) + c) * SUB
+                    base = (step * LATE_TILES * SUB + n * (chunks - 1) + c) * SUB
                     swap_ref[base : base + SUB, :] = jnp.where(spot == place, other, field)
             continue
         if step < steps:
@@ -177,9 +177,11 @@
                 packed_ref[half * NQ + q] = value
 
     if part:
-        for row in range(steps * NFIELD * (chunks - 1), LATE_TILES * SUB):
-            swap_ref[row * SUB : (row + 1) * SUB, :] = tag.astype(jnp.float32)
-        spread(swap_ref, 0, LATE_TILES)
+        for step in range(steps):
+            for row in range(NFIELD * (chunks - 1), LATE_TILES * SUB):
+                base = (step * LATE_TILES * SUB + row) * SUB
+                swap_ref[base : base + SUB, :] = tag.astype(jnp.float32)
+        spread(swap_ref, 0, steps * LATE_TILES)
         return
     for row in range(SIDE_TILES * SUB):
         if not 1 <= row <= 2 * NFIELD:
@@ -198,7 +200,7 @@
     blocks = populations.shape[1]
     cells = populations.shape[2] // GROUPS
     loaded = len(CHUNKS[part]) + (0 if part else len(INNER))
-    rows = LATE_TILES * SUB if part else NFIELD * cells // LANES
+    rows = tiles_of(1) * SUB if part else NFIELD * cells // LANES
     return pl.pallas_call(
         functools.partial(pre_kernel, cap, row_count, per_row, part),
         in_specs=[pl.BlockSpec(memory_space=pltpu.HBM)] * 3,
@@ -257,13 +259,15 @@
                 count_ref[d] = k + 1
                 plan_ref[d * cap + k] = e
 
-    for d, out in enumerate(outs):
+    tiles = outs[0].shape[1]
+    for place, out in enumerate(outs):
+        quarter, d = divmod(place, col_count)
         for k in range(cap):
             e = plan_ref[d * cap + k]
 
             @pl.when(e >= 0)
             def _():
-                out[k] = in_ref[e]
+                out[k] = in_ref[e, quarter * tiles : (quarter + 1) * tiles]
 
             if part == 0:
 
@@ -278,12 +282,14 @@
     scratch = []
     if part == 0:
         scratch = tag_scratch(1, landed.shape[0]) + [pltpu.SMEM((col_count,), jnp.int32)]
+    quarters = len(INNER) if part else 1
+    shape = (cap, landed.shape[1] // quarters) + landed.shape[2:]
     packed = pl.pallas_call(
         functools.partial(repack_kernel, cap, col_count, blocks, part),
         in_specs=([scalars] if part else []) + [whole],
-        out_specs=[whole] * col_count + ([] if part else [scalars]),
+        out_specs=[whole] * (quarters * col_count) + ([] if part else [scalars]),
         scratch_shapes=scratch,
-        out_shape=[jax.ShapeDtypeStruct((cap,) + landed.shape[1:], jnp.float32)] * col_count
+        out_shape=[jax.ShapeDtypeStruct(shape, jnp.float32)] * (quarters * col_count)
         + ([] if part else [jax.ShapeDtypeStruct((col_count * cap,), jnp.int32)]),
         compiler_params=pltpu.CompilerParams(vmem_limit_bytes=VMEM_LIMIT),
         cost_estimate=pl.CostEstimate(flops=0, bytes_accessed=3 * 10**6, transcendentals=0),
@@ -512,7 +518,7 @@
     def _():
         unload(plan_ref, ins, late_ref)
         fill_outer(fields_ref, main_ref)
-        fill_inner(fields_ref, late_ref, CHUNKS[1][0], main_ref)
+        fill_inner(fields_ref, late_ref, INNER[0], main_ref)
         fill_sides(below_in, above_in, below_ref, above_ref, 0, 7)
         fill_sides(below_in, above_in, below_ref, above_ref, 13, EDGE)
         for k in range(3):
@@ -560,7 +566,7 @@
         for copy in copies:
             copy.start()
         unload(plan_ref, ins, late_ref)
-        fill_inner(fields_ref, late_ref, CHUNKS[2][0], main_ref)
+        fill_inner(fields_ref, late_ref, INNER[1], main_ref)
         fill_sides(below_in, above_in, below_ref, above_ref, 5, 15)
         for copy in copies:
             copy.wait()
@@ -658,20 +664,17 @@
         return [exchanged(packed[d], "col", d) for d in range(col_count - 1, 0, -1)] + [packed[0]]
 
     sent = prepared(0)
-    in_row = [to_rows(sent)]
-    in_row.append(to_rows(after(prepared(1, sent), in_row[0])))
-    packed, plan = repack(in_row[0], None, 0, col_count, cap_col, blocks)
-    in_row.append(to_rows(prepared(2, packed[0])))
+    early_row = to_rows(sent)
+    late_row = to_rows(prepared(1, sent))
+    packed, plan = repack(early_row, None, 0, col_count, cap_col, blocks)
     ylo, yhi, xlo, xhi, picked, fields = faces(to_columns(packed))
     below, above = shifted(yhi, "col", 1), shifted(ylo, "col", -1)
-    middle = to_columns(repack(in_row[1], plan, 1, col_count, cap_col, blocks))
-    in_row[2], below, above = lax.optimization_barrier((in_row[2], below, above))
+    late_row, below, above = lax.optimization_barrier((late_row, below, above))
     up = jnp.concatenate([xhi.reshape(18, SUB, LANES), below[6:, 1], above[6:, 1]])
     down = jnp.concatenate([xlo.reshape(18, SUB, LANES), below[:3, 0], above[:3, 0]])
     xlo, xhi = shifted(up, "row", 1), shifted(down, "row", -1)
-    packed = repack(in_row[2], plan, 2, col_count, cap_col, blocks)
-    picked, packed = lax.optimization_barrier((picked, list(packed)))
-    last = to_columns(packed)
+    packed = repack(late_row, plan, 1, col_count, cap_col, blocks)
+    middle, last = to_columns(packed[:col_count]), to_columns(packed[col_count:])
     out, kept = advance(picked, middle, fields, xlo, xhi, below, above)
     return jnp.transpose(finish(picked, last, fields, kept, below, above, out), (1, 0, 2))
 

time: 110 us -> 95.1 us (0.86)
  waiting for transfers between devices: 61.5 us -> 53.5 us
  starting transfers between devices: 27.1 us -> 23 us
  Pallas kernels: 20.4 us -> 18.3 us
    all_to_all x3 -> x2, waiting for transfers between devices: 41.4 us -> 33 us  [to_rows(): return lax.all_to_all(sent, 'row', split_axis=0, concat_axis=0, tiled=True)]
    all_to_all x3 -> x2, starting transfers between devices: 14.5 us -> 10.9 us  [to_rows(): return lax.all_to_all(sent, 'row', split_axis=0, concat_axis=0, tiled=True)]
    pallas_call x3 -> x2, Pallas kernels: 7.78 us -> 6.11 us  [pre(): pl.pallas_call(functools.partial(pre_kernel, cap, row_count, per_row, par...]
    pallas_call x3 -> x2, Pallas kernels: 3.02 us -> 2.48 us  [repack(): pl.pallas_call(functools.partial(repack_kernel, cap, col_count, blocks, p...]
  transfers between devices with their start and end apart: 16 -> 15, of which waited for: 9 -> 8; matrix products, arithmetic and copies ran while one was open for 0% -> 0% of each run, Pallas kernels for 12% -> 12%
where the time goes in v10:
time: 95.1 us; the launch traced here: 94.8 us
  waiting for transfers between devices  53.5 us (56%)
  starting transfers between devices  23 us (24%)
  Pallas kernels  18.3 us (19%)
    all_to_all x2, waiting for transfers between devices, to_rows(): return lax.all_to_all(sent, 'row', split_axis=0, concat_axis=0, tiled=True)  33 us
    ppermute x9, waiting for transfers between devices, exchanged(): return lax.ppermute(value, axis, pairs)  18.6 us
    all_to_all x2, starting transfers between devices, to_rows(): return lax.all_to_all(sent, 'row', split_axis=0, concat_axis=0, tiled=True)  10.9 us
    ppermute x4, starting transfers between devices, shifted(): lax.ppermute(value, axis, [(i, (i + step) % count) for i in range(count)])  6.34 us
    pallas_call x2, Pallas kernels, pre(): pl.pallas_call(functools.partial(pre_kernel, cap, row_count, per_row, par...  6.11 us
    ppermute x9, starting transfers between devices, exchanged(): return lax.ppermute(value, axis, pairs)  5.75 us
    pallas_call x1, Pallas kernels, advance(): pl.pallas_call(functools.partial(advance_kernel, len(homes)), grid_spec=p...  4.34 us
    pallas_call x1, Pallas kernels, finish(): pl.pallas_call(functools.partial(finish_kernel, len(homes)), grid_spec=pl...  3.64 us
  transfers between devices with their start and end apart: 15, of which 8 were waited for; matrix products, arithmetic and copies ran while one was open for 0% of the time, Pallas kernels for 12%

profile of v10, /device:TPU:0, one launch (start us, length us, event | category | flops | bytes accessed | tf_op | source)
XLA Modules:
  0.0 94.8 jit_solution(11331796762004868596)
XLA Ops:
  0.0 3.4 %pre_0.1 = f32[16,21,8,128]{3,2,1,0:T(8,128)} custom-call(s32[8]{0:T(128)} %dest_hbm.1, s32[8]{0:T(128)} %level_hbm.3, f32[27,8,4096]{2,1,0:T(8,128)} %bitcast.14), custom_call_target="tpu_custom_call" | custom-call | flops 10000000 | bytes 4000000 | tf_op jit(solution)/shard_map/pre_0/pallas_call | solution.py:204
  3.4 7.3 %all-to-all-start = ((f32[16,21,8,128]{3,2,1,0:T(8,128)}), f32[16,21,8,128]{3,2,1,0:T(8,128)S(1)}, u32[]{:S(2)}, u32[]{:S(2)}) async-start(f32[16,21,8,128]{3,2,1,0:T(8,128)} %pre_0.1), calls=%async_computation | async-start | bytes 2752512 | tf_op jit(solution)/shard_map/all_to_all | solution.py:661
  10.7 2.7 %pre_1.1 = f32[16,16,8,128]{3,2,1,0:T(8,128)} custom-call(s32[8]{0:T(128)} %dest_hbm.1, s32[8]{0:T(128)} %level_hbm.3, f32[27,8,4096]{2,1,0:T(8,128)} %bitcast.15), custom_call_target="tpu_custom_call" | custom-call | flops 10000000 | bytes 4000000 | tf_op jit(solution)/shard_map/pre_1/pallas_call | solution.py:204
  13.4 30.1 %all-to-all-done.refs_0_ = f32[16,21,8,128]{3,2,1,0:T(8,128)S(1)} async-done(((f32[16,21,8,128]{3,2,1,0:T(8,128)}), f32[16,21,8,128]{3,2,1,0:T(8,128)S(1)}, u32[]{:S(2)}, u32[]{:S(2)}) %all-to-all-start) | async-done | bytes 1376288 | tf_op jit(solution)/shard_map/all_to_all | solution.py:661
  43.5 3.6 %all-to-all-start.1 = ((f32[16,16,8,128]{3,2,1,0:T(8,128)}), f32[16,16,8,128]{3,2,1,0:T(8,128)S(1)}, u32[]{:S(2)}, u32[]{:S(2)}) async-start(f32[16,16,8,128]{3,2,1,0:T(8,128)} %pre_1.1), calls=%async_computation.1 | async-start | bytes 2097152 | tf_op jit(solution)/shard_map/all_to_all | solution.py:661
  47.1 1.7 %repack_0.1 = (f32[4,21,8,128]{3,2,1,0:T(8,128)S(1)}, f32[4,21,8,128]{3,2,1,0:T(8,128)S(1)}, f32[4,21,8,128]{3,2,1,0:T(8,128)S(1)}, f32[4,21,8,128]{3,2,1,0:T(8,128)S(1)}, s32[16]{0:T(128)S(1)}) custom-call(f32[16,21,8,128]{3,2,1,0:T(8,128)S(1)} %all-to-all-done.refs_0_), custom_call_target="tpu_custom_call" | custom-call | bytes 3000000 | tf_op jit(solution)/shard_map/repack_0/pallas_call | solution.py:287
  48.8 0.9 collective-permute-start
  49.7 0.7 collective-permute-start.1
  50.4 0.3 collective-permute-start.2
  50.7 8.4 %collective-permute-done.refs_0_ = f32[4,21,8,128]{3,2,1,0:T(8,128)S(1)} collective-permute-done((f32[4,21,8,128]{3,2,1,0:T(8,128)S(1)}, f32[4,21,8,128]{3,2,1,0:T(8,128)S(1)}, u32[]{:S(2)}, u32[]{:S(2)}) %collective-permute-start) | collective-permute-done | bytes 344096 | tf_op jit(solution)/shard_map/ppermute | solution.py:50
  59.1 7.4 %collective-permute-done.1.refs_1_ = f32[4,21,8,128]{3,2,1,0:T(8,128)S(1)} collective-permute-done((f32[4,21,8,128]{3,2,1,0:T(8,128)S(1)}, f32[4,21,8,128]{3,2,1,0:T(8,128)S(1)}, u32[]{:S(2)}, u32[]{:S(2)}) %collective-permute-start.1) | collective-permute-done | bytes 344096 | tf_op jit(solution)/shard_map/ppermute | solution.py:50
  66.6 0.0 collective-permute-done.2.refs_2_
  66.6 1.7 %faces.1 = (f32[9,2,8,128]{3,2,1,0:T(8,128)S(1)}, f32[9,2,8,128]{3,2,1,0:T(8,128)S(1)}, f32[9,2,8,128]{3,2,1,0:T(8,128)S(1)}, f32[9,2,8,128]{3,2,1,0:T(8,128)S(1...) custom-call(f32[4,21,8,128]{3,2,1,0:T(8,128)S(1)} %collective-permute-done.refs_0_, ...), custom_call_target="tpu_custom_call" | custom-call | flops 10000000 | bytes 3000000 | tf_op jit(solution)/shard_map/faces/pallas_call | solution.py:492
  68.3 0.1 collective-permute-start.3
  68.4 1.7 %collective-permute-start.4 = (f32[9,2,8,128]{3,2,1,0:T(8,128)S(1)}, f32[9,2,8,128]{3,2,1,0:T(8,128)S(1)}, u32[]{:S(2)}, u32[]{:S(2)}) collective-permute-start(f32[9,2,8,128]{3,2,1,0:T(8,128)S(1)} %get-tuple-element.38), channel_id=1, source_target_pairs={{0,3},{1,0},{2,1},{3,2},{4,7},{5,4},{6,5},{7,6},{8,11},{9,8},{10,9... | collective-permute-start | bytes 221192 | tf_op jit(solution)/shard_map/ppermute | solution.py:641
  70.1 3.0 %all-to-all-done.1.refs_1_ = f32[16,16,8,128]{3,2,1,0:T(8,128)S(1)} async-done(((f32[16,16,8,128]{3,2,1,0:T(8,128)}), f32[16,16,8,128]{3,2,1,0:T(8,128)S(1)}, u32[]{:S(2)}, u32[]{:S(2)}) %all-to-all-start.1) | async-done | bytes 1048608 | tf_op jit(solution)/shard_map/all_to_all | solution.py:661
  73.1 0.0 collective-permute-done.3.refs_7_.refs_6_
  73.1 0.0 collective-permute-done.4.refs_8_.refs_7_
  73.1 1.5 %collective-permute-start.11 = (f32[24,8,128]{2,1,0:T(8,128)S(1)}, f32[24,8,128]{2,1,0:T(8,128)S(1)}, u32[]{:S(2)}, u32[]{:S(2)}) collective-permute-start(f32[24,8,128]{2,1,0:T(8,128)S(1)} %pad_maximum_fusion), channel_id=1, source_target_pairs={{0,4},{4,8},{8,12},{12,16},{16,20},{20,24},{24,28},{28,0},{1,5},{5... | collective-permute-start | bytes 294920 | tf_op jit(solution)/shard_map/ppermute | solution.py:641
  74.6 0.8 repack_1.1
  75.4 1.2 %collective-permute-start.8 = (f32[4,8,8,128]{3,2,1,0:T(8,128)S(1)}, f32[4,8,8,128]{3,2,1,0:T(8,128)S(1)}, u32[]{:S(2)}, u32[]{:S(2)}) collective-permute-start(f32[4,8,8,128]{3,2,1,0:T(8,128)S(1)} %get-tuple-element.45), channel_id=1, source_target_pairs={{0,3},{1,2},{2,1},{3,0},{4,7},{5,6},{6,5},{7,4},{8,11},{9,10},{10,... | collective-permute-start | bytes 393224 | tf_op jit(solution)/shard_map/ppermute | solution.py:50
  76.6 3.1 %collective-permute-start.12 = (f32[24,8,128]{2,1,0:T(8,128)S(1)}, f32[24,8,128]{2,1,0:T(8,128)S(1)}, u32[]{:S(2)}, u32[]{:S(2)}) collective-permute-start(f32[24,8,128]{2,1,0:T(8,128)S(1)} %pad_maximum_fusion.1), channel_id=1, source_target_pairs={{0,28},{4,0},{8,4},{12,8},{16,12},{20,16},{24,20},{28,24},{1,29},{... | collective-permute-start | bytes 294920 | tf_op jit(solution)/shard_map/ppermute | solution.py:641
  79.6 1.0 %collective-permute-start.9 = (f32[4,8,8,128]{3,2,1,0:T(8,128)S(1)}, f32[4,8,8,128]{3,2,1,0:T(8,128)S(1)}, u32[]{:S(2)}, u32[]{:S(2)}) collective-permute-start(f32[4,8,8,128]{3,2,1,0:T(8,128)S(1)} %get-tuple-element.46), channel_id=1, source_target_pairs={{0,2},{1,3},{2,0},{3,1},{4,6},{5,7},{6,4},{7,5},{8,10},{9,11},{10,... | collective-permute-start | bytes 393224 | tf_op jit(solution)/shard_map/ppermute | solution.py:50
  80.7 0.5 collective-permute-done.11.refs_5_
  81.2 0.6 collective-permute-start.5
  81.8 1.4 %collective-permute-done.12.refs_6_ = f32[24,8,128]{2,1,0:T(8,128)S(1)} collective-permute-done((f32[24,8,128]{2,1,0:T(8,128)S(1)}, f32[24,8,128]{2,1,0:T(8,128)S(1)}, u32[]{:S(2)}, u32[]{:S(2)}) %collective-permute-start.12) | collective-permute-done | bytes 98336 | tf_op jit(solution)/shard_map/ppermute | solution.py:641
  83.2 1.0 %collective-permute-start.6 = (f32[4,8,8,128]{3,2,1,0:T(8,128)S(1)}, f32[4,8,8,128]{3,2,1,0:T(8,128)S(1)}, u32[]{:S(2)}, u32[]{:S(2)}) collective-permute-start(f32[4,8,8,128]{3,2,1,0:T(8,128)S(1)} %get-tuple-element.41), channel_id=1, source_target_pairs={{0,2},{1,3},{2,0},{3,1},{4,6},{5,7},{6,4},{7,5},{8,10},{9,11},{10,... | collective-permute-start | bytes 393224 | tf_op jit(solution)/shard_map/ppermute | solution.py:50
  84.1 0.0 collective-permute-start.7
  84.1 1.8 %collective-permute-done.9.refs_1_ = f32[4,8,8,128]{3,2,1,0:T(8,128)S(1)} collective-permute-done((f32[4,8,8,128]{3,2,1,0:T(8,128)S(1)}, f32[4,8,8,128]{3,2,1,0:T(8,128)S(1)}, u32[]{:S(2)}, u32[]{:S(2)}) %collective-permute-start.9) | collective-permute-done | bytes 131104 | tf_op jit(solution)/shard_map/ppermute | solution.py:50
  85.9 4.3 %advance.1 = (f32[27,8,4096]{2,1,0:T(8,128)}, f32[27,12,8,128]{3,2,1,0:T(8,128)S(1)}) custom-call(s32[16]{0:T(128)S(1)} %get-tuple-element.34.plan_ref, f32[4,8,8,128]{3,2,1,0:T(8,128)S(1)} %collective-permute-done.8.refs_0_, f32[4,8,8,128]{3,2,1,0:T(8,128)S(1)} %collective-permute-done.9.refs_1_, f32[4,8,8,128]{3,2,1,0:T(8,128)S(1)} %collective-permute-done.10.refs_2_, ...), custom_call_target="tpu_custom_call" | custom-call | flops 10000000 | bytes 5000000 | tf_op jit(solution)/shard_map/advance/pallas_call | solution.py:596
  90.3 0.9 collective-permute-done.6.refs_1_
  91.2 3.6 %finish.1 = f32[27,8,4096]{2,1,0:T(8,128)} custom-call(s32[16]{0:T(128)S(1)} %get-tuple-element.34.plan_ref, f32[4,8,8,128]{3,2,1,0:T(8,128)S(1)} %collective-permute-done.5.refs_0_, f32[4,8,8,128]{3,2,1,0:T(8,128)S(1)} %collective-permute-done.6.refs_1_, f32[4,8,8,128]{3,2,1,0:T(8,128)S(1)} %collective-permute-done.7.refs_2_, ...), custom_call_target="tpu_custom_call", output_to_operand_aliasing={{}: (9, {})} | custom-call | flops 10000000 | bytes 5000000 | tf_op jit(solution)/shard_map/finish/pallas_call | solution.py:621
  (8 shorter events, 0.0 us)
Async XLA Ops:
  3.4 40.1 %all-to-all-start = ((f32[16,21,8,128]{3,2,1,0:T(8,128)}), f32[16,21,8,128]{3,2,1,0:T(8,128)S(1)}, u32[]{:S(2)}, u32[]{:S(2)}) async-start(f32[16,21,8,128]{3,2,1,0:T(8,128)} %pre_0.1), calls=%async_computation | async-start | bytes 2752512 | tf_op jit(solution)/shard_map/all_to_all | solution.py:661
  43.5 29.6 %all-to-all-start.1 = ((f32[16,16,8,128]{3,2,1,0:T(8,128)}), f32[16,16,8,128]{3,2,1,0:T(8,128)S(1)}, u32[]{:S(2)}, u32[]{:S(2)}) async-start(f32[16,16,8,128]{3,2,1,0:T(8,128)} %pre_1.1), calls=%async_computation.1 | async-start | bytes 2097152 | tf_op jit(solution)/shard_map/all_to_all | solution.py:661
  48.8 10.4 %collective-permute-start = (f32[4,21,8,128]{3,2,1,0:T(8,128)S(1)}, f32[4,21,8,128]{3,2,1,0:T(8,128)S(1)}, u32[]{:S(2)}, u32[]{:S(2)}) collective-permute-start(f32[4,21,8,128]{3,2,1,0:T(8,128)S(1)} %get-tuple-element.30), channel_id=1, source_target_pairs={{0,3},{1,2},{2,1},{3,0},{4,7},{5,6},{6,5},{7,4},{8,11},{9,10},{10,... | collective-permute-start | bytes 1032200 | tf_op jit(solution)/shard_map/ppermute | solution.py:50
  49.7 16.9 %collective-permute-start.1 = (f32[4,21,8,128]{3,2,1,0:T(8,128)S(1)}, f32[4,21,8,128]{3,2,1,0:T(8,128)S(1)}, u32[]{:S(2)}, u32[]{:S(2)}) collective-permute-start(f32[4,21,8,128]{3,2,1,0:T(8,128)S(1)} %get-tuple-element.31), channel_id=1, source_target_pairs={{0,2},{1,3},{2,0},{3,1},{4,6},{5,7},{6,4},{7,5},{8,10},{9,11},{10,... | collective-permute-start | bytes 1032200 | tf_op jit(solution)/shard_map/ppermute | solution.py:50
  50.4 16.1 %collective-permute-start.2 = (f32[4,21,8,128]{3,2,1,0:T(8,128)S(1)}, f32[4,21,8,128]{3,2,1,0:T(8,128)S(1)}, u32[]{:S(2)}, u32[]{:S(2)}) collective-permute-start(f32[4,21,8,128]{3,2,1,0:T(8,128)S(1)} %get-tuple-element.32), channel_id=1, source_target_pairs={{0,1},{1,0},{2,3},{3,2},{4,5},{5,4},{6,7},{7,6},{8,9},{9,8},{10,11... | collective-permute-start | bytes 1032200 | tf_op jit(solution)/shard_map/ppermute | solution.py:50
  68.3 4.8 %collective-permute-start.3 = (f32[9,2,8,128]{3,2,1,0:T(8,128)S(1)}, f32[9,2,8,128]{3,2,1,0:T(8,128)S(1)}, u32[]{:S(2)}, u32[]{:S(2)}) collective-permute-start(f32[9,2,8,128]{3,2,1,0:T(8,128)S(1)} %get-tuple-element.37), channel_id=1, source_target_pairs={{0,1},{1,2},{2,3},{3,0},{4,5},{5,6},{6,7},{7,4},{8,9},{9,10},{10,1... | collective-permute-start | bytes 221192 | tf_op jit(solution)/shard_map/ppermute | solution.py:641
  68.4 4.7 %collective-permute-start.4 = (f32[9,2,8,128]{3,2,1,0:T(8,128)S(1)}, f32[9,2,8,128]{3,2,1,0:T(8,128)S(1)}, u32[]{:S(2)}, u32[]{:S(2)}) collective-permute-start(f32[9,2,8,128]{3,2,1,0:T(8,128)S(1)} %get-tuple-element.38), channel_id=1, source_target_pairs={{0,3},{1,0},{2,1},{3,2},{4,7},{5,4},{6,5},{7,6},{8,11},{9,8},{10,9... | collective-permute-start | bytes 221192 | tf_op jit(solution)/shard_map/ppermute | solution.py:641
  73.1 8.1 %collective-permute-start.11 = (f32[24,8,128]{2,1,0:T(8,128)S(1)}, f32[24,8,128]{2,1,0:T(8,128)S(1)}, u32[]{:S(2)}, u32[]{:S(2)}) collective-permute-start(f32[24,8,128]{2,1,0:T(8,128)S(1)} %pad_maximum_fusion), channel_id=1, source_target_pairs={{0,4},{4,8},{8,12},{12,16},{16,20},{20,24},{24,28},{28,0},{1,5},{5... | collective-permute-start | bytes 294920 | tf_op jit(solution)/shard_map/ppermute | solution.py:641
  75.4 8.8 %collective-permute-start.8 = (f32[4,8,8,128]{3,2,1,0:T(8,128)S(1)}, f32[4,8,8,128]{3,2,1,0:T(8,128)S(1)}, u32[]{:S(2)}, u32[]{:S(2)}) collective-permute-start(f32[4,8,8,128]{3,2,1,0:T(8,128)S(1)} %get-tuple-element.45), channel_id=1, source_target_pairs={{0,3},{1,2},{2,1},{3,0},{4,7},{5,6},{6,5},{7,4},{8,11},{9,10},{10,... | collective-permute-start | bytes 393224 | tf_op jit(solution)/shard_map/ppermute | solution.py:50
  76.6 6.6 %collective-permute-start.12 = (f32[24,8,128]{2,1,0:T(8,128)S(1)}, f32[24,8,128]{2,1,0:T(8,128)S(1)}, u32[]{:S(2)}, u32[]{:S(2)}) collective-permute-start(f32[24,8,128]{2,1,0:T(8,128)S(1)} %pad_maximum_fusion.1), channel_id=1, source_target_pairs={{0,28},{4,0},{8,4},{12,8},{16,12},{20,16},{24,20},{28,24},{1,29},{... | collective-permute-start | bytes 294920 | tf_op jit(solution)/shard_map/ppermute | solution.py:641
  79.6 6.3 %collective-permute-start.9 = (f32[4,8,8,128]{3,2,1,0:T(8,128)S(1)}, f32[4,8,8,128]{3,2,1,0:T(8,128)S(1)}, u32[]{:S(2)}, u32[]{:S(2)}) collective-permute-start(f32[4,8,8,128]{3,2,1,0:T(8,128)S(1)} %get-tuple-element.46), channel_id=1, source_target_pairs={{0,2},{1,3},{2,0},{3,1},{4,6},{5,7},{6,4},{7,5},{8,10},{9,11},{10,... | collective-permute-start | bytes 393224 | tf_op jit(solution)/shard_map/ppermute | solution.py:50
  80.7 5.3 %collective-permute-start.10 = (f32[4,8,8,128]{3,2,1,0:T(8,128)S(1)}, f32[4,8,8,128]{3,2,1,0:T(8,128)S(1)}, u32[]{:S(2)}, u32[]{:S(2)}) collective-permute-start(f32[4,8,8,128]{3,2,1,0:T(8,128)S(1)} %get-tuple-element.47), channel_id=1, source_target_pairs={{0,1},{1,0},{2,3},{3,2},{4,5},{5,4},{6,7},{7,6},{8,9},{9,8},{10,11... | collective-permute-start | bytes 393224 | tf_op jit(solution)/shard_map/ppermute | solution.py:50
  81.2 9.1 %collective-permute-start.5 = (f32[4,8,8,128]{3,2,1,0:T(8,128)S(1)}, f32[4,8,8,128]{3,2,1,0:T(8,128)S(1)}, u32[]{:S(2)}, u32[]{:S(2)}) collective-permute-start(f32[4,8,8,128]{3,2,1,0:T(8,128)S(1)} %get-tuple-element.40), channel_id=1, source_target_pairs={{0,3},{1,2},{2,1},{3,0},{4,7},{5,6},{6,5},{7,4},{8,11},{9,10},{10,... | collective-permute-start | bytes 393224 | tf_op jit(solution)/shard_map/ppermute | solution.py:50
  83.2 8.0 %collective-permute-start.6 = (f32[4,8,8,128]{3,2,1,0:T(8,128)S(1)}, f32[4,8,8,128]{3,2,1,0:T(8,128)S(1)}, u32[]{:S(2)}, u32[]{:S(2)}) collective-permute-start(f32[4,8,8,128]{3,2,1,0:T(8,128)S(1)} %get-tuple-element.41), channel_id=1, source_target_pairs={{0,2},{1,3},{2,0},{3,1},{4,6},{5,7},{6,4},{7,5},{8,10},{9,11},{10,... | collective-permute-start | bytes 393224 | tf_op jit(solution)/shard_map/ppermute | solution.py:50
  84.1 7.0 %collective-permute-start.7 = (f32[4,8,8,128]{3,2,1,0:T(8,128)S(1)}, f32[4,8,8,128]{3,2,1,0:T(8,128)S(1)}, u32[]{:S(2)}, u32[]{:S(2)}) collective-permute-start(f32[4,8,8,128]{3,2,1,0:T(8,128)S(1)} %get-tuple-element.42), channel_id=1, source_target_pairs={{0,1},{1,0},{2,3},{3,2},{4,5},{5,4},{6,7},{7,6},{8,9},{9,8},{10,11... | collective-permute-start | bytes 393224 | tf_op jit(solution)/shard_map/ppermute | solution.py:50

commit v11 on v10

--- a/solution.py
+++ b/solution.py
@@ -452,6 +452,21 @@
                 out_ref[q, :, c * LANES : (c + 1) * LANES] = value
 
 
+def stream_pairs(pairs, out_hbm, pair_ref, sems, *lattice):
+    span = pair_ref.shape[3]
+
+    def copy(i):
+        return pltpu.make_async_copy(
+            pair_ref.at[i], out_hbm.at[:, :, pl.ds(pairs[i] * span, span)], sems.at[i]
+        )
+
+    for i, pair in enumerate(pairs):
+        stream_pair(2 * pair, pair_ref.at[i], *lattice)
+        copy(i).start()
+    for i in range(len(pairs)):
+        copy(i).wait()
+
+
 def faces_kernel(count, *refs):
     ins = refs[:count]
     ylo_ref, yhi_ref, xlo_ref, xhi_ref, plan_ref, fields_ref, tag_ref, sems = refs[count:]
@@ -510,73 +525,59 @@
     ins = refs[:count]
     (
         fields_ref, xlo_ref, xhi_ref, below_in, above_in, out_ref, kept_ref,
-        main_ref, below_ref, above_ref, late_ref,
+        main_ref, below_ref, above_ref, late_ref, pair_ref, sems,
     ) = refs[count:]
-    g = pl.program_id(0)
-
-    @pl.when(g == 0)
-    def _():
-        unload(plan_ref, ins, late_ref)
-        fill_outer(fields_ref, main_ref)
-        fill_inner(fields_ref, late_ref, INNER[0], main_ref)
-        fill_sides(below_in, above_in, below_ref, above_ref, 0, 7)
-        fill_sides(below_in, above_in, below_ref, above_ref, 13, EDGE)
-        for k in range(3):
-            below_ref[6 + k, 0] = xlo_ref[18 + k]
-            above_ref[6 + k, 0] = turned(xlo_ref[21 + k], 1)
-            below_ref[k, EDGE + 1] = turned(xhi_ref[18 + k], -1)
-            above_ref[k, EDGE + 1] = xhi_ref[21 + k]
-        for q in range(9):
-            for half in range(2):
-                main_ref[18 + q, half] = xlo_ref[q * 2 + half]
-                main_ref[q, 2 * EDGE + 2 + half] = xhi_ref[q * 2 + half]
-        to = 0
-        for first, last in KEPT:
-            for row in range(2 * first + 2, 2 * last + 2):
-                for q in range(NQ):
-                    kept_ref[q, to] = main_ref[q, row]
-                to += 1
-
-    first_x = 2 * jnp.where(g == len(PAIRS[0]) - 1, PAIRS[0][-1], g)
-    stream_pair(first_x, out_ref, main_ref, below_ref, above_ref)
+    unload(plan_ref, ins, late_ref)
+    fill_outer(fields_ref, main_ref)
+    fill_inner(fields_ref, late_ref, INNER[0], main_ref)
+    fill_sides(below_in, above_in, below_ref, above_ref, 0, 7)
+    fill_sides(below_in, above_in, below_ref, above_ref, 13, EDGE)
+    for k in range(3):
+        below_ref[6 + k, 0] = xlo_ref[18 + k]
+        above_ref[6 + k, 0] = turned(xlo_ref[21 + k], 1)
+        below_ref[k, EDGE + 1] = turned(xhi_ref[18 + k], -1)
+        above_ref[k, EDGE + 1] = xhi_ref[21 + k]
+    for q in range(9):
+        for half in range(2):
+            main_ref[18 + q, half] = xlo_ref[q * 2 + half]
+            main_ref[q, 2 * EDGE + 2 + half] = xhi_ref[q * 2 + half]
+    to = 0
+    for first, last in KEPT:
+        for row in range(2 * first + 2, 2 * last + 2):
+            for q in range(NQ):
+                kept_ref[q, to] = main_ref[q, row]
+            to += 1
+
+    stream_pairs(PAIRS[0], out_ref, pair_ref, sems, main_ref, below_ref, above_ref)
 
 
 def finish_kernel(count, plan_ref, *refs):
     ins = refs[:count]
     (
         fields_ref, kept_ref, below_in, above_in, _, out_ref,
-        main_ref, below_ref, above_ref, late_ref, sems,
+        main_ref, below_ref, above_ref, late_ref, pair_ref, sems,
     ) = refs[count:]
-    g = pl.program_id(0)
-
-    @pl.when(g == 0)
-    def _():
-        copies = []
-        to = 0
-        for first, last in KEPT:
-            rows = 2 * (last - first)
-            copies.append(
-                pltpu.make_async_copy(
-                    kept_ref.at[:, pl.ds(to, rows)],
-                    main_ref.at[:, pl.ds(2 * first + 2, rows)],
-                    sems.at[len(copies)],
-                )
+    copies = []
+    to = 0
+    for first, last in KEPT:
+        rows = 2 * (last - first)
+        copies.append(
+            pltpu.make_async_copy(
+                kept_ref.at[:, pl.ds(to, rows)],
+                main_ref.at[:, pl.ds(2 * first + 2, rows)],
+                sems.at[len(PAIRS[1]) + len(copies)],
             )
-            to += rows
-        for copy in copies:
-            copy.start()
-        unload(plan_ref, ins, late_ref)
-        fill_inner(fields_ref, late_ref, INNER[1], main_ref)
-        fill_sides(below_in, above_in, below_ref, above_ref, 5, 15)
-        for copy in copies:
-            copy.wait()
-
-    stream_pair(2 * (PAIRS[1][0] + g), out_ref, main_ref, below_ref, above_ref)
-
-
-def whole_of(value):
-    rank = len(value.shape)
-    return pl.BlockSpec(value.shape, lambda g, *_: (0,) * rank)
+        )
+        to += rows
+    for copy in copies:
+        copy.start()
+    unload(plan_ref, ins, late_ref)
+    fill_inner(fields_ref, late_ref, INNER[1], main_ref)
+    fill_sides(below_in, above_in, below_ref, above_ref, 5, 15)
+    for copy in copies:
+        copy.wait()
+
+    stream_pairs(PAIRS[1], out_ref, pair_ref, sems, main_ref, below_ref, above_ref)
 
 
 def scratch_of_lattice():
@@ -584,31 +585,24 @@
     return [
         pltpu.VMEM((NQ, 2 * EDGE + 4, SUB, LANES), jnp.float32), side, side,
         pltpu.VMEM((LATE_TILES * SUB * SUB, LANES), jnp.float32),
+        pltpu.VMEM((len(PAIRS[0]), NQ, SUB, 4 * LANES), jnp.float32),
+        pltpu.SemaphoreType.DMA((len(PAIRS[0]) + len(KEPT),)),
     ]
 
 
 def advance(plan, homes, fields, xlo, xhi, below, above):
-    pairs = PAIRS[0]
     inputs = [*homes, fields, xlo, xhi, below, above]
-    kept = jax.ShapeDtypeStruct(
-        (NQ, 2 * sum(last - first for first, last in KEPT), SUB, LANES), jnp.float32
-    )
+    whole = pl.BlockSpec(memory_space=pltpu.VMEM)
+    kept = 2 * sum(last - first for first, last in KEPT)
     return pl.pallas_call(
         functools.partial(advance_kernel, len(homes)),
-        grid_spec=pltpu.PrefetchScalarGridSpec(
-            num_scalar_prefetch=1,
-            grid=(len(pairs),),
-            in_specs=[whole_of(value) for value in inputs],
-            out_specs=[
-                pl.BlockSpec(
-                    (NQ, SUB, 4 * LANES),
-                    lambda g, *_: (0, 0, jnp.where(g == len(pairs) - 1, pairs[-1], g)),
-                ),
-                whole_of(kept),
-            ],
-            scratch_shapes=scratch_of_lattice(),
-        ),
-        out_shape=[jax.ShapeDtypeStruct((NQ, SUB, GROUPS * SUB * LANES), jnp.float32), kept],
+        in_specs=[pl.BlockSpec(memory_space=pltpu.SMEM)] + [whole] * len(inputs),
+        out_specs=[pl.BlockSpec(memory_space=pltpu.HBM), whole],
+        scratch_shapes=scratch_of_lattice(),
+        out_shape=[
+            jax.ShapeDtypeStruct((NQ, SUB, GROUPS * SUB * LANES), jnp.float32),
+            jax.ShapeDtypeStruct((NQ, kept, SUB, LANES), jnp.float32),
+        ],
         compiler_params=pltpu.CompilerParams(vmem_limit_bytes=VMEM_LIMIT),
         cost_estimate=pl.CostEstimate(flops=10**7, bytes_accessed=5 * 10**6, transcendentals=0),
         name="advance",
@@ -616,24 +610,20 @@
 
 
 def finish(plan, homes, fields, kept, below, above, out):
-    pairs = PAIRS[1]
-    anywhere = pl.BlockSpec(memory_space=pl.ANY)
+    inputs = [*homes, fields, kept, below, above]
+    whole = pl.BlockSpec(memory_space=pltpu.VMEM)
+    target = pl.BlockSpec(memory_space=pltpu.HBM)
     return pl.pallas_call(
         functools.partial(finish_kernel, len(homes)),
-        grid_spec=pltpu.PrefetchScalarGridSpec(
-            num_scalar_prefetch=1,
-            grid=(len(pairs),),
-            in_specs=[whole_of(value) for value in (*homes, fields)]
-            + [anywhere, whole_of(below), whole_of(above), anywhere],
-            out_specs=pl.BlockSpec((NQ, SUB, 4 * LANES), lambda g, *_: (0, 0, pairs[0] + g)),
-            scratch_shapes=scratch_of_lattice() + [pltpu.SemaphoreType.DMA((len(KEPT),))],
-        ),
+        in_specs=[pl.BlockSpec(memory_space=pltpu.SMEM)] + [whole] * len(inputs) + [target],
+        out_specs=target,
+        scratch_shapes=scratch_of_lattice(),
         out_shape=jax.ShapeDtypeStruct(out.shape, jnp.float32),
-        input_output_aliases={len(homes) + 5: 0},
+        input_output_aliases={1 + len(inputs): 0},
         compiler_params=pltpu.CompilerParams(vmem_limit_bytes=VMEM_LIMIT),
         cost_estimate=pl.CostEstimate(flops=10**7, bytes_accessed=5 * 10**6, transcendentals=0),
         name="finish",
-    )(plan, *homes, fields, kept, below, above, out)
+    )(plan, *inputs, out)
 
 
 def shifted(value, axis, step):
@@ -669,11 +659,10 @@
     packed, plan = repack(early_row, None, 0, col_count, cap_col, blocks)
     ylo, yhi, xlo, xhi, picked, fields = faces(to_columns(packed))
     below, above = shifted(yhi, "col", 1), shifted(ylo, "col", -1)
-    late_row, below, above = lax.optimization_barrier((late_row, below, above))
     up = jnp.concatenate([xhi.reshape(18, SUB, LANES), below[6:, 1], above[6:, 1]])
     down = jnp.concatenate([xlo.reshape(18, SUB, LANES), below[:3, 0], above[:3, 0]])
     xlo, xhi = shifted(up, "row", 1), shifted(down, "row", -1)
-    packed = repack(late_row, plan, 1, col_count, cap_col, blocks)
+    packed = repack(after(late_row, up, down), plan, 1, col_count, cap_col, blocks)
     middle, last = to_columns(packed[:col_count]), to_columns(packed[col_count:])
     out, kept = advance(picked, middle, fields, xlo, xhi, below, above)
     return jnp.transpose(finish(picked, last, fields, kept, below, above, out), (1, 0, 2))

time: 95.1 us -> 94.3 us (level)
  Pallas kernels: 18.3 us -> 16.3 us
  waiting for transfers between devices: 53.5 us -> 54.6 us
    ppermute x4, waiting for transfers between devices: 1.87 us -> 4.71 us  [shifted(): lax.ppermute(value, axis, [(i, (i + step) % count) for i in range(count)])]
    all_to_all x2, waiting for transfers between devices: 33 us -> 30.9 us  [to_rows(): return lax.all_to_all(sent, 'row', split_axis=0, concat_axis=0, tiled=True)]
    pallas_call x2, Pallas kernels: 7.98 us -> 6 us  [the longest x1 3.14 us: advance(): pl.pallas_call(functools.partial(advance_kernel, len(homes)), in_specs=[p...]
  transfers between devices with their start and end apart: 15 -> 15, of which waited for: 8 -> 10; matrix products, arithmetic and copies ran while one was open for 0% -> 0% of each run, Pallas kernels for 12% -> 10%
where the time goes in v11:
time: 94.3 us; the launch traced here: 94.1 us
  waiting for transfers between devices  54.6 us (58%)
  starting transfers between devices  23 us (24%)
  Pallas kernels  16.3 us (17%)
    all_to_all x2, waiting for transfers between devices, to_rows(): return lax.all_to_all(sent, 'row', split_axis=0, concat_axis=0, tiled=True)  30.9 us
    ppermute x9, waiting for transfers between devices, exchanged(): return lax.ppermute(value, axis, pairs)  19 us
    all_to_all x2, starting transfers between devices, to_rows(): return lax.all_to_all(sent, 'row', split_axis=0, concat_axis=0, tiled=True)  10.9 us
    ppermute x4, starting transfers between devices, shifted(): lax.ppermute(value, axis, [(i, (i + step) % count) for i in range(count)])  6.52 us
    pallas_call x2, Pallas kernels, pre(): pl.pallas_call(functools.partial(pre_kernel, cap, row_count, per_row, par...  6.13 us
    ppermute x9, starting transfers between devices, exchanged(): return lax.ppermute(value, axis, pairs)  5.59 us
    ppermute x4, waiting for transfers between devices, shifted(): lax.ppermute(value, axis, [(i, (i + step) % count) for i in range(count)])  4.71 us
    pallas_call x1, Pallas kernels, advance(): pl.pallas_call(functools.partial(advance_kernel, len(homes)), in_specs=[p...  3.14 us
  transfers between devices with their start and end apart: 15, of which 10 were waited for; matrix products, arithmetic and copies ran while one was open for 0% of the time, Pallas kernels for 10%

profile of v11, /device:TPU:0, one launch (start us, length us, event | category | flops | bytes accessed | tf_op | source)
XLA Modules:
  0.0 94.1 jit_solution(13414939009109176743)
XLA Ops:
  0.0 3.4 %pre_0.1 = f32[16,21,8,128]{3,2,1,0:T(8,128)} custom-call(s32[8]{0:T(128)} %dest_hbm.1, s32[8]{0:T(128)} %level_hbm.3, f32[27,8,4096]{2,1,0:T(8,128)} %bitcast.14), custom_call_target="tpu_custom_call" | custom-call | flops 10000000 | bytes 4000000 | tf_op jit(solution)/shard_map/pre_0/pallas_call | solution.py:204
  3.4 7.3 %all-to-all-start = ((f32[16,21,8,128]{3,2,1,0:T(8,128)}), f32[16,21,8,128]{3,2,1,0:T(8,128)S(1)}, u32[]{:S(2)}, u32[]{:S(2)}) async-start(f32[16,21,8,128]{3,2,1,0:T(8,128)} %pre_0.1), calls=%async_computation | async-start | bytes 2752512 | tf_op jit(solution)/shard_map/all_to_all | solution.py:651
  10.7 2.7 %pre_1.1 = f32[16,16,8,128]{3,2,1,0:T(8,128)} custom-call(s32[8]{0:T(128)} %dest_hbm.1, s32[8]{0:T(128)} %level_hbm.3, f32[27,8,4096]{2,1,0:T(8,128)} %bitcast.15), custom_call_target="tpu_custom_call" | custom-call | flops 10000000 | bytes 4000000 | tf_op jit(solution)/shard_map/pre_1/pallas_call | solution.py:204
  13.4 30.1 %all-to-all-done.refs_0_ = f32[16,21,8,128]{3,2,1,0:T(8,128)S(1)} async-done(((f32[16,21,8,128]{3,2,1,0:T(8,128)}), f32[16,21,8,128]{3,2,1,0:T(8,128)S(1)}, u32[]{:S(2)}, u32[]{:S(2)}) %all-to-all-start) | async-done | bytes 1376288 | tf_op jit(solution)/shard_map/all_to_all | solution.py:651
  43.5 3.6 %all-to-all-start.1 = ((f32[16,16,8,128]{3,2,1,0:T(8,128)}), f32[16,16,8,128]{3,2,1,0:T(8,128)S(1)}, u32[]{:S(2)}, u32[]{:S(2)}) async-start(f32[16,16,8,128]{3,2,1,0:T(8,128)} %pre_1.1), calls=%async_computation.1 | async-start | bytes 2097152 | tf_op jit(solution)/shard_map/all_to_all | solution.py:651
  47.1 1.7 %repack_0.1 = (f32[4,21,8,128]{3,2,1,0:T(8,128)S(1)}, f32[4,21,8,128]{3,2,1,0:T(8,128)S(1)}, f32[4,21,8,128]{3,2,1,0:T(8,128)S(1)}, f32[4,21,8,128]{3,2,1,0:T(8,128)S(1)}, s32[16]{0:T(128)S(1)}) custom-call(f32[16,21,8,128]{3,2,1,0:T(8,128)S(1)} %all-to-all-done.refs_0_), custom_call_target="tpu_custom_call" | custom-call | bytes 3000000 | tf_op jit(solution)/shard_map/repack_0/pallas_call | solution.py:287
  48.8 0.9 collective-permute-start
  49.7 0.7 collective-permute-start.1
  50.4 0.3 collective-permute-start.2
  50.7 8.4 %collective-permute-done.refs_0_ = f32[4,21,8,128]{3,2,1,0:T(8,128)S(1)} collective-permute-done((f32[4,21,8,128]{3,2,1,0:T(8,128)S(1)}, f32[4,21,8,128]{3,2,1,0:T(8,128)S(1)}, u32[]{:S(2)}, u32[]{:S(2)}) %collective-permute-start) | collective-permute-done | bytes 344096 | tf_op jit(solution)/shard_map/ppermute | solution.py:50
  59.1 7.4 %collective-permute-done.1.refs_1_ = f32[4,21,8,128]{3,2,1,0:T(8,128)S(1)} collective-permute-done((f32[4,21,8,128]{3,2,1,0:T(8,128)S(1)}, f32[4,21,8,128]{3,2,1,0:T(8,128)S(1)}, u32[]{:S(2)}, u32[]{:S(2)}) %collective-permute-start.1) | collective-permute-done | bytes 344096 | tf_op jit(solution)/shard_map/ppermute | solution.py:50
  66.6 0.0 collective-permute-done.2.refs_2_
  66.6 1.7 %faces.1 = (f32[9,2,8,128]{3,2,1,0:T(8,128)S(1)}, f32[9,2,8,128]{3,2,1,0:T(8,128)S(1)}, f32[9,2,8,128]{3,2,1,0:T(8,128)S(1)}, f32[9,2,8,128]{3,2,1,0:T(8,128)S(1...) custom-call(f32[4,21,8,128]{3,2,1,0:T(8,128)S(1)} %collective-permute-done.refs_0_, ...), custom_call_target="tpu_custom_call" | custom-call | flops 10000000 | bytes 3000000 | tf_op jit(solution)/shard_map/faces/pallas_call | solution.py:507
  68.3 0.1 collective-permute-start.3
  68.4 1.7 %collective-permute-start.4 = (f32[9,2,8,128]{3,2,1,0:T(8,128)S(1)}, f32[9,2,8,128]{3,2,1,0:T(8,128)S(1)}, u32[]{:S(2)}, u32[]{:S(2)}) collective-permute-start(f32[9,2,8,128]{3,2,1,0:T(8,128)S(1)} %get-tuple-element.37), channel_id=1, source_target_pairs={{0,3},{1,0},{2,1},{3,2},{4,7},{5,4},{6,5},{7,6},{8,11},{9,8},{10,9... | collective-permute-start | bytes 221192 | tf_op jit(solution)/shard_map/ppermute | solution.py:631
  70.1 2.0 %collective-permute-done.3.refs_7_.refs_6_ = f32[9,2,8,128]{3,2,1,0:T(8,128)S(1)} collective-permute-done((f32[9,2,8,128]{3,2,1,0:T(8,128)S(1)}, f32[9,2,8,128]{3,2,1,0:T(8,128)S(1)}, u32[]{:S(2)}, u32[]{:S(2)}) %collective-permute-start.3) | collective-permute-done | bytes 73760 | tf_op jit(solution)/shard_map/ppermute | solution.py:631
  72.2 0.9 all-to-all-done.1.refs_1_
  73.1 0.8 repack_1.1
  73.9 1.2 %collective-permute-start.8 = (f32[4,8,8,128]{3,2,1,0:T(8,128)S(1)}, f32[4,8,8,128]{3,2,1,0:T(8,128)S(1)}, u32[]{:S(2)}, u32[]{:S(2)}) collective-permute-start(f32[4,8,8,128]{3,2,1,0:T(8,128)S(1)} %get-tuple-element.45), channel_id=1, source_target_pairs={{0,3},{1,2},{2,1},{3,0},{4,7},{5,6},{6,5},{7,4},{8,11},{9,10},{10,... | collective-permute-start | bytes 393224 | tf_op jit(solution)/shard_map/ppermute | solution.py:50
  75.1 1.7 %collective-permute-start.11 = (f32[24,8,128]{2,1,0:T(8,128)S(1)}, f32[24,8,128]{2,1,0:T(8,128)S(1)}, u32[]{:S(2)}, u32[]{:S(2)}) collective-permute-start(f32[24,8,128]{2,1,0:T(8,128)S(1)} %pad_maximum_fusion), channel_id=1, source_target_pairs={{0,4},{4,8},{8,12},{12,16},{16,20},{20,24},{24,28},{28,0},{1,5},{5... | collective-permute-start | bytes 294920 | tf_op jit(solution)/shard_map/ppermute | solution.py:631
  76.8 3.0 %collective-permute-start.12 = (f32[24,8,128]{2,1,0:T(8,128)S(1)}, f32[24,8,128]{2,1,0:T(8,128)S(1)}, u32[]{:S(2)}, u32[]{:S(2)}) collective-permute-start(f32[24,8,128]{2,1,0:T(8,128)S(1)} %pad_maximum_fusion.1), channel_id=1, source_target_pairs={{0,28},{4,0},{8,4},{12,8},{16,12},{20,16},{24,20},{28,24},{1,29},{... | collective-permute-start | bytes 294920 | tf_op jit(solution)/shard_map/ppermute | solution.py:631
  79.8 1.1 %collective-permute-start.9 = (f32[4,8,8,128]{3,2,1,0:T(8,128)S(1)}, f32[4,8,8,128]{3,2,1,0:T(8,128)S(1)}, u32[]{:S(2)}, u32[]{:S(2)}) collective-permute-start(f32[4,8,8,128]{3,2,1,0:T(8,128)S(1)} %get-tuple-element.46), channel_id=1, source_target_pairs={{0,2},{1,3},{2,0},{3,1},{4,6},{5,7},{6,4},{7,5},{8,10},{9,11},{10,... | collective-permute-start | bytes 393224 | tf_op jit(solution)/shard_map/ppermute | solution.py:50
  80.9 0.0 collective-permute-start.10
  80.9 2.2 %collective-permute-done.11.refs_5_ = f32[24,8,128]{2,1,0:T(8,128)S(1)} collective-permute-done((f32[24,8,128]{2,1,0:T(8,128)S(1)}, f32[24,8,128]{2,1,0:T(8,128)S(1)}, u32[]{:S(2)}, u32[]{:S(2)}) %collective-permute-start.11) | collective-permute-done | bytes 98336 | tf_op jit(solution)/shard_map/ppermute | solution.py:631
  83.1 0.5 collective-permute-done.12.refs_6_
  83.6 0.9 collective-permute-start.6
  84.4 0.5 collective-permute-start.7
  84.9 0.2 collective-permute-done.9.refs_1_
  85.1 3.1 %advance.1 = (f32[27,8,4096]{2,1,0:T(8,128)}, f32[27,12,8,128]{3,2,1,0:T(8,128)S(1)}) custom-call(s32[16]{0:T(128)S(1)} %get-tuple-element.32.plan_ref, f32[4,8,8,128]{3,2,1,0:T(8,128)S(1)} %collective-permute-done.8.refs_0_, f32[4,8,8,128]{3,2,1,0:T(8,128)S(1)} %collective-permute-done.9.refs_1_, f32[4,8,8,128]{3,2,1,0:T(8,128)S(1)} %collective-permute-done.10.refs_2_, ...), custom_call_target="tpu_custom_call" | custom-call | flops 10000000 | bytes 5000000 | tf_op jit(solution)/shard_map/advance/pallas_call | solution.py:597
  88.3 0.6 collective-permute-done.5.refs_0_
  88.9 2.3 %collective-permute-done.6.refs_1_ = f32[4,8,8,128]{3,2,1,0:T(8,128)S(1)} collective-permute-done((f32[4,8,8,128]{3,2,1,0:T(8,128)S(1)}, f32[4,8,8,128]{3,2,1,0:T(8,128)S(1)}, u32[]{:S(2)}, u32[]{:S(2)}) %collective-permute-start.6) | collective-permute-done | bytes 131104 | tf_op jit(solution)/shard_map/ppermute | solution.py:50
  91.2 2.9 %finish.1 = f32[27,8,4096]{2,1,0:T(8,128)} custom-call(s32[16]{0:T(128)S(1)} %get-tuple-element.32.plan_ref, f32[4,8,8,128]{3,2,1,0:T(8,128)S(1)} %collective-permute-done.5.refs_0_, f32[4,8,8,128]{3,2,1,0:T(8,128)S(1)} %collective-permute-done.6.refs_1_, f32[4,8,8,128]{3,2,1,0:T(8,128)S(1)} %collective-permute-done.7.refs_2_, ...), custom_call_target="tpu_custom_call", output_to_operand_aliasing={{}: (9, {})} | custom-call | flops 10000000 | bytes 5000000 | tf_op jit(solution)/shard_map/finish/pallas_call | solution.py:616
  (9 shorter events, 0.0 us)
Async XLA Ops:
  3.4 40.1 %all-to-all-start = ((f32[16,21,8,128]{3,2,1,0:T(8,128)}), f32[16,21,8,128]{3,2,1,0:T(8,128)S(1)}, u32[]{:S(2)}, u32[]{:S(2)}) async-start(f32[16,21,8,128]{3,2,1,0:T(8,128)} %pre_0.1), calls=%async_computation | async-start | bytes 2752512 | tf_op jit(solution)/shard_map/all_to_all | solution.py:651
  43.5 29.6 %all-to-all-start.1 = ((f32[16,16,8,128]{3,2,1,0:T(8,128)}), f32[16,16,8,128]{3,2,1,0:T(8,128)S(1)}, u32[]{:S(2)}, u32[]{:S(2)}) async-start(f32[16,16,8,128]{3,2,1,0:T(8,128)} %pre_1.1), calls=%async_computation.1 | async-start | bytes 2097152 | tf_op jit(solution)/shard_map/all_to_all | solution.py:651
  48.8 10.4 %collective-permute-start = (f32[4,21,8,128]{3,2,1,0:T(8,128)S(1)}, f32[4,21,8,128]{3,2,1,0:T(8,128)S(1)}, u32[]{:S(2)}, u32[]{:S(2)}) collective-permute-start(f32[4,21,8,128]{3,2,1,0:T(8,128)S(1)} %get-tuple-element.28), channel_id=1, source_target_pairs={{0,3},{1,2},{2,1},{3,0},{4,7},{5,6},{6,5},{7,4},{8,11},{9,10},{10,... | collective-permute-start | bytes 1032200 | tf_op jit(solution)/shard_map/ppermute | solution.py:50
  49.7 16.9 %collective-permute-start.1 = (f32[4,21,8,128]{3,2,1,0:T(8,128)S(1)}, f32[4,21,8,128]{3,2,1,0:T(8,128)S(1)}, u32[]{:S(2)}, u32[]{:S(2)}) collective-permute-start(f32[4,21,8,128]{3,2,1,0:T(8,128)S(1)} %get-tuple-element.29), channel_id=1, source_target_pairs={{0,2},{1,3},{2,0},{3,1},{4,6},{5,7},{6,4},{7,5},{8,10},{9,11},{10,... | collective-permute-start | bytes 1032200 | tf_op jit(solution)/shard_map/ppermute | solution.py:50
  50.4 16.1 %collective-permute-start.2 = (f32[4,21,8,128]{3,2,1,0:T(8,128)S(1)}, f32[4,21,8,128]{3,2,1,0:T(8,128)S(1)}, u32[]{:S(2)}, u32[]{:S(2)}) collective-permute-start(f32[4,21,8,128]{3,2,1,0:T(8,128)S(1)} %get-tuple-element.30), channel_id=1, source_target_pairs={{0,1},{1,0},{2,3},{3,2},{4,5},{5,4},{6,7},{7,6},{8,9},{9,8},{10,11... | collective-permute-start | bytes 1032200 | tf_op jit(solution)/shard_map/ppermute | solution.py:50
  68.3 3.8 %collective-permute-start.3 = (f32[9,2,8,128]{3,2,1,0:T(8,128)S(1)}, f32[9,2,8,128]{3,2,1,0:T(8,128)S(1)}, u32[]{:S(2)}, u32[]{:S(2)}) collective-permute-start(f32[9,2,8,128]{3,2,1,0:T(8,128)S(1)} %get-tuple-element.36), channel_id=1, source_target_pairs={{0,1},{1,2},{2,3},{3,0},{4,5},{5,6},{6,7},{7,4},{8,9},{9,10},{10,1... | collective-permute-start | bytes 221192 | tf_op jit(solution)/shard_map/ppermute | solution.py:631
  68.4 3.7 %collective-permute-start.4 = (f32[9,2,8,128]{3,2,1,0:T(8,128)S(1)}, f32[9,2,8,128]{3,2,1,0:T(8,128)S(1)}, u32[]{:S(2)}, u32[]{:S(2)}) collective-permute-start(f32[9,2,8,128]{3,2,1,0:T(8,128)S(1)} %get-tuple-element.37), channel_id=1, source_target_pairs={{0,3},{1,0},{2,1},{3,2},{4,7},{5,4},{6,5},{7,6},{8,11},{9,8},{10,9... | collective-permute-start | bytes 221192 | tf_op jit(solution)/shard_map/ppermute | solution.py:631
  73.9 10.6 %collective-permute-start.8 = (f32[4,8,8,128]{3,2,1,0:T(8,128)S(1)}, f32[4,8,8,128]{3,2,1,0:T(8,128)S(1)}, u32[]{:S(2)}, u32[]{:S(2)}) collective-permute-start(f32[4,8,8,128]{3,2,1,0:T(8,128)S(1)} %get-tuple-element.45), channel_id=1, source_target_pairs={{0,3},{1,2},{2,1},{3,0},{4,7},{5,6},{6,5},{7,4},{8,11},{9,10},{10,... | collective-permute-start | bytes 393224 | tf_op jit(solution)/shard_map/ppermute | solution.py:50
  75.1 8.0 %collective-permute-start.11 = (f32[24,8,128]{2,1,0:T(8,128)S(1)}, f32[24,8,128]{2,1,0:T(8,128)S(1)}, u32[]{:S(2)}, u32[]{:S(2)}) collective-permute-start(f32[24,8,128]{2,1,0:T(8,128)S(1)} %pad_maximum_fusion), channel_id=1, source_target_pairs={{0,4},{4,8},{8,12},{12,16},{16,20},{20,24},{24,28},{28,0},{1,5},{5... | collective-permute-start | bytes 294920 | tf_op jit(solution)/shard_map/ppermute | solution.py:631
  76.8 6.7 %collective-permute-start.12 = (f32[24,8,128]{2,1,0:T(8,128)S(1)}, f32[24,8,128]{2,1,0:T(8,128)S(1)}, u32[]{:S(2)}, u32[]{:S(2)}) collective-permute-start(f32[24,8,128]{2,1,0:T(8,128)S(1)} %pad_maximum_fusion.1), channel_id=1, source_target_pairs={{0,28},{4,0},{8,4},{12,8},{16,12},{20,16},{24,20},{28,24},{1,29},{... | collective-permute-start | bytes 294920 | tf_op jit(solution)/shard_map/ppermute | solution.py:631
  79.8 5.3 %collective-permute-start.9 = (f32[4,8,8,128]{3,2,1,0:T(8,128)S(1)}, f32[4,8,8,128]{3,2,1,0:T(8,128)S(1)}, u32[]{:S(2)}, u32[]{:S(2)}) collective-permute-start(f32[4,8,8,128]{3,2,1,0:T(8,128)S(1)} %get-tuple-element.46), channel_id=1, source_target_pairs={{0,2},{1,3},{2,0},{3,1},{4,6},{5,7},{6,4},{7,5},{8,10},{9,11},{10,... | collective-permute-start | bytes 393224 | tf_op jit(solution)/shard_map/ppermute | solution.py:50
  80.9 4.3 %collective-permute-start.10 = (f32[4,8,8,128]{3,2,1,0:T(8,128)S(1)}, f32[4,8,8,128]{3,2,1,0:T(8,128)S(1)}, u32[]{:S(2)}, u32[]{:S(2)}) collective-permute-start(f32[4,8,8,128]{3,2,1,0:T(8,128)S(1)} %get-tuple-element.47), channel_id=1, source_target_pairs={{0,1},{1,0},{2,3},{3,2},{4,5},{5,4},{6,7},{7,6},{8,9},{9,8},{10,11... | collective-permute-start | bytes 393224 | tf_op jit(solution)/shard_map/ppermute | solution.py:50
  83.1 5.8 %collective-permute-start.5 = (f32[4,8,8,128]{3,2,1,0:T(8,128)S(1)}, f32[4,8,8,128]{3,2,1,0:T(8,128)S(1)}, u32[]{:S(2)}, u32[]{:S(2)}) collective-permute-start(f32[4,8,8,128]{3,2,1,0:T(8,128)S(1)} %get-tuple-element.40), channel_id=1, source_target_pairs={{0,3},{1,2},{2,1},{3,0},{4,7},{5,6},{6,5},{7,4},{8,11},{9,10},{10,... | collective-permute-start | bytes 393224 | tf_op jit(solution)/shard_map/ppermute | solution.py:50
  83.6 7.6 %collective-permute-start.6 = (f32[4,8,8,128]{3,2,1,0:T(8,128)S(1)}, f32[4,8,8,128]{3,2,1,0:T(8,128)S(1)}, u32[]{:S(2)}, u32[]{:S(2)}) collective-permute-start(f32[4,8,8,128]{3,2,1,0:T(8,128)S(1)} %get-tuple-element.41), channel_id=1, source_target_pairs={{0,2},{1,3},{2,0},{3,1},{4,6},{5,7},{6,4},{7,5},{8,10},{9,11},{10,... | collective-permute-start | bytes 393224 | tf_op jit(solution)/shard_map/ppermute | solution.py:50
  84.4 6.8 %collective-permute-start.7 = (f32[4,8,8,128]{3,2,1,0:T(8,128)S(1)}, f32[4,8,8,128]{3,2,1,0:T(8,128)S(1)}, u32[]{:S(2)}, u32[]{:S(2)}) collective-permute-start(f32[4,8,8,128]{3,2,1,0:T(8,128)S(1)} %get-tuple-element.42), channel_id=1, source_target_pairs={{0,1},{1,0},{2,3},{3,2},{4,5},{5,4},{6,7},{7,6},{8,9},{9,8},{10,11... | collective-permute-start | bytes 393224 | tf_op jit(solution)/shard_map/ppermute | solution.py:50

commit v12 on v11

--- a/solution.py
+++ b/solution.py
@@ -390,10 +390,10 @@
     for step, group in enumerate(CHUNKS[0]):
         for c in range(SUB):
             for q, value in enumerate(post_populations(*outer_fields(fields_ref, step, c))):
-                main_ref[q, 2 + group * SUB + c] = value
-
-
-def fill_inner(fields_ref, late_ref, group, main_ref):
+                main_ref[q, group * SUB + c] = value
+
+
+def fill_inner(fields_ref, late_ref, group, main_ref, first_row):
     spot = places_y()
     last = [None] * NFIELD
     for c in range(SUB):
@@ -410,18 +410,18 @@
                 row = last[n]
             fields.append(jnp.where(spot == place, turned(side[n], place - at), row))
         for q, value in enumerate(post_populations(*fields)):
-            main_ref[q, 2 + group * SUB + c] = value
-
-
-def fill_sides(below_in, above_in, below_ref, above_ref, first, last):
-    for x in range(first, last):
+            main_ref[q, first_row + c] = value
+
+
+def fill_sides(below_in, above_in, below_ref, above_ref):
+    for x in range(EDGE):
         at = x % SUB
         for k in range(9):
-            below_ref[k, x + 1] = turned(below_in[k, x // SUB], SUB - 1 - at)
-            above_ref[k, x + 1] = turned(above_in[k, x // SUB], -at)
-
-
-def stream_pair(first_x, out_ref, main_ref, below_ref, above_ref):
+            below_ref[k, x] = turned(below_in[k, x // SUB], SUB - 1 - at)
+            above_ref[k, x] = turned(above_in[k, x // SUB], -at)
+
+
+def stream_pair(first_x, out_ref, main, below, above):
     lane = lax.broadcasted_iota(jnp.int32, (SUB, LANES), 1)
     block = lax.broadcasted_iota(jnp.int32, (SUB, LANES), 0)
     along = lane % EDGE
@@ -434,17 +434,17 @@
             c = i * 2 + half
             for q in range(NQ):
                 cx, cy, cz = velocity(q)
-                x = first_x + i - cx + 1
-                a = main_ref[q, x * 2 + half]
+                x = first_x + i - cx
+                a = main(q, x, half)
                 k = (cx + 1) * 3 + cz + 1
                 if cy == 1:
-                    a = jnp.where(high_y, main_ref[q, x * 2] if half else below_ref[k, x], a)
+                    a = jnp.where(high_y, main(q, x, 0) if half else below(k, x), a)
                 elif cy == -1:
-                    a = jnp.where(low_y, above_ref[k, x] if half else main_ref[q, x * 2 + 1], a)
+                    a = jnp.where(low_y, above(k, x) if half else main(q, x, 1), a)
                 shift = EDGE * cy + cz
                 value = a if shift == 0 else pltpu.roll(a, shift % LANES, axis=1)
                 if cz:
-                    bounced = main_ref[26 - q, (first_x + i + 1) * 2 + half]
+                    bounced = main(26 - q, first_x + i, half)
                     turn = (1 if cz == 1 else SUB - 1)
                     fill = pltpu.roll(pltpu.roll(a, turn, axis=0), (shift - cz * EDGE) % LANES, axis=1)
                     value = jnp.where(first_z if cz == 1 else last_z, fill, value)
@@ -517,91 +517,81 @@
     )(*homes)
 
 
-PAIRS = ((0, 1, 2, 7), (3, 4, 5, 6))
-KEPT = ((5, 8), (12, 15))
+PAIRS = ((1, 2), (0, 3, 4, 5, 6, 7))
 
 
 def advance_kernel(count, plan_ref, *refs):
     ins = refs[:count]
     (
-        fields_ref, xlo_ref, xhi_ref, below_in, above_in, out_ref, kept_ref,
-        main_ref, below_ref, above_ref, late_ref, pair_ref, sems,
+        fields_ref, below_in, above_in, out_ref, main_ref, below_ref, above_ref,
+        late_ref, pair_ref, sems,
     ) = refs[count:]
     unload(plan_ref, ins, late_ref)
     fill_outer(fields_ref, main_ref)
-    fill_inner(fields_ref, late_ref, INNER[0], main_ref)
-    fill_sides(below_in, above_in, below_ref, above_ref, 0, 7)
-    fill_sides(below_in, above_in, below_ref, above_ref, 13, EDGE)
-    for k in range(3):
-        below_ref[6 + k, 0] = xlo_ref[18 + k]
-        above_ref[6 + k, 0] = turned(xlo_ref[21 + k], 1)
-        below_ref[k, EDGE + 1] = turned(xhi_ref[18 + k], -1)
-        above_ref[k, EDGE + 1] = xhi_ref[21 + k]
-    for q in range(9):
-        for half in range(2):
-            main_ref[18 + q, half] = xlo_ref[q * 2 + half]
-            main_ref[q, 2 * EDGE + 2 + half] = xhi_ref[q * 2 + half]
-    to = 0
-    for first, last in KEPT:
-        for row in range(2 * first + 2, 2 * last + 2):
-            for q in range(NQ):
-                kept_ref[q, to] = main_ref[q, row]
-            to += 1
-
-    stream_pairs(PAIRS[0], out_ref, pair_ref, sems, main_ref, below_ref, above_ref)
+    fill_inner(fields_ref, late_ref, INNER[0], main_ref, INNER[0] * SUB)
+    fill_sides(below_in, above_in, below_ref, above_ref)
+    stream_pairs(
+        PAIRS[0], out_ref, pair_ref, sems,
+        lambda q, x, half: main_ref[q, x * 2 + half],
+        lambda k, x: below_ref[k, x],
+        lambda k, x: above_ref[k, x],
+    )
 
 
 def finish_kernel(count, plan_ref, *refs):
     ins = refs[:count]
     (
-        fields_ref, kept_ref, below_in, above_in, _, out_ref,
-        main_ref, below_ref, above_ref, late_ref, pair_ref, sems,
+        fields_ref, main_ref, below_ref, above_ref, xlo_ref, xhi_ref, _, out_ref,
+        own_ref, late_ref, pair_ref, sems,
     ) = refs[count:]
-    copies = []
-    to = 0
-    for first, last in KEPT:
-        rows = 2 * (last - first)
-        copies.append(
-            pltpu.make_async_copy(
-                kept_ref.at[:, pl.ds(to, rows)],
-                main_ref.at[:, pl.ds(2 * first + 2, rows)],
-                sems.at[len(PAIRS[1]) + len(copies)],
-            )
-        )
-        to += rows
-    for copy in copies:
-        copy.start()
     unload(plan_ref, ins, late_ref)
-    fill_inner(fields_ref, late_ref, INNER[1], main_ref)
-    fill_sides(below_in, above_in, below_ref, above_ref, 5, 15)
-    for copy in copies:
-        copy.wait()
-
-    stream_pairs(PAIRS[1], out_ref, pair_ref, sems, main_ref, below_ref, above_ref)
-
-
-def scratch_of_lattice():
-    side = pltpu.VMEM((9, EDGE + 2, SUB, LANES), jnp.float32)
+    fill_inner(fields_ref, late_ref, INNER[1], own_ref, 0)
+    first = INNER[1] * WIDTH
+
+    def main(q, x, half):
+        if x < 0:
+            return xlo_ref[(q - 18) * 2 + half]
+        if x == EDGE:
+            return xhi_ref[q * 2 + half]
+        if first <= x < first + WIDTH:
+            return own_ref[q, (x - first) * 2 + half]
+        return main_ref[q, x * 2 + half]
+
+    def below(k, x):
+        if x < 0:
+            return xlo_ref[18 + k - 6]
+        return turned(xhi_ref[18 + k], -1) if x == EDGE else below_ref[k, x]
+
+    def above(k, x):
+        if x < 0:
+            return turned(xlo_ref[21 + k - 6], 1)
+        return xhi_ref[21 + k] if x == EDGE else above_ref[k, x]
+
+    stream_pairs(PAIRS[1], out_ref, pair_ref, sems, main, below, above)
+
+
+def scratch_of(pairs):
     return [
-        pltpu.VMEM((NQ, 2 * EDGE + 4, SUB, LANES), jnp.float32), side, side,
         pltpu.VMEM((LATE_TILES * SUB * SUB, LANES), jnp.float32),
-        pltpu.VMEM((len(PAIRS[0]), NQ, SUB, 4 * LANES), jnp.float32),
-        pltpu.SemaphoreType.DMA((len(PAIRS[0]) + len(KEPT),)),
+        pltpu.VMEM((len(pairs), NQ, SUB, 4 * LANES), jnp.float32),
+        pltpu.SemaphoreType.DMA((len(pairs),)),
     ]
 
 
-def advance(plan, homes, fields, xlo, xhi, below, above):
-    inputs = [*homes, fields, xlo, xhi, below, above]
+def advance(plan, homes, fields, below, above):
+    inputs = [*homes, fields, below, above]
     whole = pl.BlockSpec(memory_space=pltpu.VMEM)
-    kept = 2 * sum(last - first for first, last in KEPT)
+    shape = jax.ShapeDtypeStruct
     return pl.pallas_call(
         functools.partial(advance_kernel, len(homes)),
         in_specs=[pl.BlockSpec(memory_space=pltpu.SMEM)] + [whole] * len(inputs),
-        out_specs=[pl.BlockSpec(memory_space=pltpu.HBM), whole],
-        scratch_shapes=scratch_of_lattice(),
+        out_specs=[pl.BlockSpec(memory_space=pltpu.HBM), whole, whole, whole],
+        scratch_shapes=scratch_of(PAIRS[0]),
         out_shape=[
-            jax.ShapeDtypeStruct((NQ, SUB, GROUPS * SUB * LANES), jnp.float32),
-            jax.ShapeDtypeStruct((NQ, kept, SUB, LANES), jnp.float32),
+            shape((NQ, SUB, GROUPS * SUB * LANES), jnp.float32),
+            shape((NQ, 2 * EDGE, SUB, LANES), jnp.float32),
+            shape((9, EDGE, SUB, LANES), jnp.float32),
+            shape((9, EDGE, SUB, LANES), jnp.float32),
         ],
         compiler_params=pltpu.CompilerParams(vmem_limit_bytes=VMEM_LIMIT),
         cost_estimate=pl.CostEstimate(flops=10**7, bytes_accessed=5 * 10**6, transcendentals=0),
@@ -609,15 +599,15 @@
     )(plan, *inputs)
 
 
-def finish(plan, homes, fields, kept, below, above, out):
-    inputs = [*homes, fields, kept, below, above]
+def finish(plan, homes, fields, main, below, above, xlo, xhi, out):
+    inputs = [*homes, fields, main, below, above, xlo, xhi]
     whole = pl.BlockSpec(memory_space=pltpu.VMEM)
     target = pl.BlockSpec(memory_space=pltpu.HBM)
     return pl.pallas_call(
         functools.partial(finish_kernel, len(homes)),
         in_specs=[pl.BlockSpec(memory_space=pltpu.SMEM)] + [whole] * len(inputs) + [target],
         out_specs=target,
-        scratch_shapes=scratch_of_lattice(),
+        scratch_shapes=[pltpu.VMEM((NQ, SUB, SUB, LANES), jnp.float32)] + scratch_of(PAIRS[1]),
         out_shape=jax.ShapeDtypeStruct(out.shape, jnp.float32),
         input_output_aliases={1 + len(inputs): 0},
         compiler_params=pltpu.CompilerParams(vmem_limit_bytes=VMEM_LIMIT),
@@ -659,13 +649,15 @@
     packed, plan = repack(early_row, None, 0, col_count, cap_col, blocks)
     ylo, yhi, xlo, xhi, picked, fields = faces(to_columns(packed))
     below, above = shifted(yhi, "col", 1), shifted(ylo, "col", -1)
+    packed = repack(after(late_row, below, above), plan, 1, col_count, cap_col, blocks)
+    middle = to_columns(packed[:col_count])
+    last = to_columns([after(value, middle[-2]) for value in packed[col_count:]])
     up = jnp.concatenate([xhi.reshape(18, SUB, LANES), below[6:, 1], above[6:, 1]])
     down = jnp.concatenate([xlo.reshape(18, SUB, LANES), below[:3, 0], above[:3, 0]])
+    up, down = after(up, middle[-2]), after(down, middle[-2])
     xlo, xhi = shifted(up, "row", 1), shifted(down, "row", -1)
-    packed = repack(after(late_row, up, down), plan, 1, col_count, cap_col, blocks)
-    middle, last = to_columns(packed[:col_count]), to_columns(packed[col_count:])
-    out, kept = advance(picked, middle, fields, xlo, xhi, below, above)
-    return jnp.transpose(finish(picked, last, fields, kept, below, above, out), (1, 0, 2))
+    out, *lattice = advance(picked, middle, fields, below, above)
+    return jnp.transpose(finish(picked, last, fields, *lattice, xlo, xhi, out), (1, 0, 2))
 
 
 def solution(mesh):

time: 94.3 us -> 94.4 us (level)
  starting transfers between devices: 23 us -> 24.6 us
  waiting for transfers between devices: 54.6 us -> 53 us
    ppermute x4, waiting for transfers between devices: 4.71 us -> 0.26 us  [shifted(): lax.ppermute(value, axis, [(i, (i + step) % count) for i in range(count)])]
    all_to_all x2, waiting for transfers between devices: 30.9 us -> 33.6 us  [to_rows(): return lax.all_to_all(sent, 'row', split_axis=0, concat_axis=0, tiled=True)]
    ppermute x4, starting transfers between devices: 6.52 us -> 7.66 us  [shifted(): lax.ppermute(value, axis, [(i, (i + step) % count) for i in range(count)])]
  transfers between devices with their start and end apart: 15 -> 15, of which waited for: 10 -> 7; matrix products, arithmetic and copies ran while one was open for 0% -> 0% of each run, Pallas kernels for 10% -> 10%
where the time goes in v12:
time: 94.4 us; the launch traced here: 94.1 us
  waiting for transfers between devices  53 us (56%)
  starting transfers between devices  24.6 us (26%)
  Pallas kernels  16.3 us (17%)
    all_to_all x2, waiting for transfers between devices, to_rows(): return lax.all_to_all(sent, 'row', split_axis=0, concat_axis=0, tiled=True)  33.6 us
    ppermute x9, waiting for transfers between devices, exchanged(): return lax.ppermute(value, axis, pairs)  19.1 us
    all_to_all x2, starting transfers between devices, to_rows(): return lax.all_to_all(sent, 'row', split_axis=0, concat_axis=0, tiled=True)  10.9 us
    ppermute x4, starting transfers between devices, shifted(): lax.ppermute(value, axis, [(i, (i + step) % count) for i in range(count)])  7.66 us
    pallas_call x2, Pallas kernels, pre(): pl.pallas_call(functools.partial(pre_kernel, cap, row_count, per_row, par...  6.12 us
    ppermute x9, starting transfers between devices, exchanged(): return lax.ppermute(value, axis, pairs)  6.07 us
    pallas_call x1, Pallas kernels, finish(): pl.pallas_call(functools.partial(finish_kernel, len(homes)), in_specs=[pl...  3.1 us
    pallas_call x1, Pallas kernels, advance(): pl.pallas_call(functools.partial(advance_kernel, len(homes)), in_specs=[p...  2.94 us
  transfers between devices with their start and end apart: 15, of which 7 were waited for; matrix products, arithmetic and copies ran while one was open for 0% of the time, Pallas kernels for 10%

profile of v12, /device:TPU:0, one launch (start us, length us, event | category | flops | bytes accessed | tf_op | source)
XLA Modules:
  0.0 94.1 jit_solution(12738256344650642586)
XLA Ops:
  0.0 3.4 %pre_0.1 = f32[16,21,8,128]{3,2,1,0:T(8,128)} custom-call(s32[8]{0:T(128)} %dest_hbm.1, s32[8]{0:T(128)} %level_hbm.3, f32[27,8,4096]{2,1,0:T(8,128)} %bitcast.14), custom_call_target="tpu_custom_call" | custom-call | flops 10000000 | bytes 4000000 | tf_op jit(solution)/shard_map/pre_0/pallas_call | solution.py:204
  3.4 7.3 %all-to-all-start = ((f32[16,21,8,128]{3,2,1,0:T(8,128)}), f32[16,21,8,128]{3,2,1,0:T(8,128)S(1)}, u32[]{:S(2)}, u32[]{:S(2)}) async-start(f32[16,21,8,128]{3,2,1,0:T(8,128)} %pre_0.1), calls=%async_computation | async-start | bytes 2752512 | tf_op jit(solution)/shard_map/all_to_all | solution.py:641
  10.7 2.7 %pre_1.1 = f32[16,16,8,128]{3,2,1,0:T(8,128)} custom-call(s32[8]{0:T(128)} %dest_hbm.1, s32[8]{0:T(128)} %level_hbm.3, f32[27,8,4096]{2,1,0:T(8,128)} %bitcast.15), custom_call_target="tpu_custom_call" | custom-call | flops 10000000 | bytes 4000000 | tf_op jit(solution)/shard_map/pre_1/pallas_call | solution.py:204
  13.4 30.1 %all-to-all-done.refs_0_ = f32[16,21,8,128]{3,2,1,0:T(8,128)S(1)} async-done(((f32[16,21,8,128]{3,2,1,0:T(8,128)}), f32[16,21,8,128]{3,2,1,0:T(8,128)S(1)}, u32[]{:S(2)}, u32[]{:S(2)}) %all-to-all-start) | async-done | bytes 1376288 | tf_op jit(solution)/shard_map/all_to_all | solution.py:641
  43.5 3.6 %all-to-all-start.1 = ((f32[16,16,8,128]{3,2,1,0:T(8,128)}), f32[16,16,8,128]{3,2,1,0:T(8,128)S(1)}, u32[]{:S(2)}, u32[]{:S(2)}) async-start(f32[16,16,8,128]{3,2,1,0:T(8,128)} %pre_1.1), calls=%async_computation.1 | async-start | bytes 2097152 | tf_op jit(solution)/shard_map/all_to_all | solution.py:641
  47.1 1.7 %repack_0.1 = (f32[4,21,8,128]{3,2,1,0:T(8,128)S(1)}, f32[4,21,8,128]{3,2,1,0:T(8,128)S(1)}, f32[4,21,8,128]{3,2,1,0:T(8,128)S(1)}, f32[4,21,8,128]{3,2,1,0:T(8,128)S(1)}, s32[16]{0:T(128)S(1)}) custom-call(f32[16,21,8,128]{3,2,1,0:T(8,128)S(1)} %all-to-all-done.refs_0_), custom_call_target="tpu_custom_call" | custom-call | bytes 3000000 | tf_op jit(solution)/shard_map/repack_0/pallas_call | solution.py:287
  48.8 0.9 collective-permute-start
  49.7 0.7 collective-permute-start.1
  50.4 0.3 collective-permute-start.2
  50.7 8.4 %collective-permute-done.refs_0_ = f32[4,21,8,128]{3,2,1,0:T(8,128)S(1)} collective-permute-done((f32[4,21,8,128]{3,2,1,0:T(8,128)S(1)}, f32[4,21,8,128]{3,2,1,0:T(8,128)S(1)}, u32[]{:S(2)}, u32[]{:S(2)}) %collective-permute-start) | collective-permute-done | bytes 344096 | tf_op jit(solution)/shard_map/ppermute | solution.py:50
  59.1 7.4 %collective-permute-done.1.refs_1_ = f32[4,21,8,128]{3,2,1,0:T(8,128)S(1)} collective-permute-done((f32[4,21,8,128]{3,2,1,0:T(8,128)S(1)}, f32[4,21,8,128]{3,2,1,0:T(8,128)S(1)}, u32[]{:S(2)}, u32[]{:S(2)}) %collective-permute-start.1) | collective-permute-done | bytes 344096 | tf_op jit(solution)/shard_map/ppermute | solution.py:50
  66.6 1.7 %faces.1 = (f32[9,2,8,128]{3,2,1,0:T(8,128)S(1)}, f32[9,2,8,128]{3,2,1,0:T(8,128)S(1)}, f32[9,2,8,128]{3,2,1,0:T(8,128)S(1)}, f32[9,2,8,128]{3,2,1,0:T(8,128)S(1...) custom-call(f32[4,21,8,128]{3,2,1,0:T(8,128)S(1)} %collective-permute-done.refs_0_, ...), custom_call_target="tpu_custom_call" | custom-call | flops 10000000 | bytes 3000000 | tf_op jit(solution)/shard_map/faces/pallas_call | solution.py:507
  68.3 1.2 %collective-permute-start.4 = (f32[9,2,8,128]{3,2,0,1:T(8,128)S(1)}, f32[9,2,8,128]{3,2,0,1:T(8,128)S(1)}, u32[]{:S(2)}, u32[]{:S(2)}) collective-permute-start(f32[9,2,8,128]{3,2,0,1:T(8,128)S(1)} %copy.6), channel_id=1, source_target_pairs={{0,3},{1,0},{2,1},{3,2},{4,7},{5,4},{6,5},{7,6},{8,11},{9,8},{10,9... | collective-permute-start | bytes 221192 | tf_op jit(solution)/shard_map/ppermute | solution.py:621
  69.5 3.5 %all-to-all-done.1.refs_1_ = f32[16,16,8,128]{3,2,1,0:T(8,128)S(1)} async-done(((f32[16,16,8,128]{3,2,1,0:T(8,128)}), f32[16,16,8,128]{3,2,1,0:T(8,128)S(1)}, u32[]{:S(2)}, u32[]{:S(2)}) %all-to-all-start.1) | async-done | bytes 1048608 | tf_op jit(solution)/shard_map/all_to_all | solution.py:641
  73.1 0.0 collective-permute-done.4
  73.1 0.3 collective-permute-done.3
  73.3 0.8 repack_1.1
  74.1 0.1 collective-permute-start.5
  74.2 1.4 %collective-permute-start.9 = (f32[4,8,8,128]{3,2,1,0:T(8,128)S(1)}, f32[4,8,8,128]{3,2,1,0:T(8,128)S(1)}, u32[]{:S(2)}, u32[]{:S(2)}) collective-permute-start(f32[4,8,8,128]{3,2,1,0:T(8,128)S(1)} %get-tuple-element.56), channel_id=1, source_target_pairs={{0,3},{1,2},{2,1},{3,0},{4,7},{5,6},{6,5},{7,4},{8,11},{9,10},{10,... | collective-permute-start | bytes 393224 | tf_op jit(solution)/shard_map/ppermute | solution.py:50
  75.6 0.7 collective-permute-start.10
  76.4 0.0 collective-permute-done.5.refs_2_
  76.4 0.8 collective-permute-start.6
  77.1 0.7 collective-permute-start.7
  77.8 0.4 collective-permute-start.8
  78.3 1.2 %collective-permute-done.9.refs_0_ = f32[4,8,8,128]{3,2,1,0:T(8,128)S(1)} collective-permute-done((f32[4,8,8,128]{3,2,1,0:T(8,128)S(1)}, f32[4,8,8,128]{3,2,1,0:T(8,128)S(1)}, u32[]{:S(2)}, u32[]{:S(2)}) %collective-permute-start.9) | collective-permute-done | bytes 131104 | tf_op jit(solution)/shard_map/ppermute | solution.py:50
  79.5 1.9 %collective-permute-start.11 = (f32[24,8,128]{2,1,0:T(8,128)S(1)}, f32[24,8,128]{2,1,0:T(8,128)S(1)}, u32[]{:S(2)}, u32[]{:S(2)}) collective-permute-start(f32[24,8,128]{2,1,0:T(8,128)S(1)} %get-tuple-element.63), channel_id=1, source_target_pairs={{0,4},{4,8},{8,12},{12,16},{16,20},{20,24},{24,28},{28,0},{1,5},{5... | collective-permute-start | bytes 294920 | tf_op jit(solution)/shard_map/ppermute | solution.py:621
  81.4 2.1 %collective-permute-done.10.refs_1_ = f32[4,8,8,128]{3,2,1,0:T(8,128)S(1)} collective-permute-done((f32[4,8,8,128]{3,2,1,0:T(8,128)S(1)}, f32[4,8,8,128]{3,2,1,0:T(8,128)S(1)}, u32[]{:S(2)}, u32[]{:S(2)}) %collective-permute-start.10) | collective-permute-done | bytes 131104 | tf_op jit(solution)/shard_map/ppermute | solution.py:50
  83.4 4.6 %collective-permute-start.12 = (f32[24,8,128]{2,1,0:T(8,128)S(1)}, f32[24,8,128]{2,1,0:T(8,128)S(1)}, u32[]{:S(2)}, u32[]{:S(2)}) collective-permute-start(f32[24,8,128]{2,1,0:T(8,128)S(1)} %get-tuple-element.65), channel_id=1, source_target_pairs={{0,28},{4,0},{8,4},{12,8},{16,12},{20,16},{24,20},{28,24},{1,29},{... | collective-permute-start | bytes 294920 | tf_op jit(solution)/shard_map/ppermute | solution.py:621
  88.0 2.9 %advance.1 = (f32[27,8,4096]{2,1,0:T(8,128)}, f32[27,32,8,128]{3,2,1,0:T(8,128)S(1)}, f32[9,16,8,128]{3,2,1,0:T(8,128)S(1)}, f32[9,16,8,128]{3,2,1,0:T(8,128)S(1)}) custom-call(s32[16]{0:T(128)S(1)} %get-tuple-element.40.plan_ref, f32[4,8,8,128]{3,2,1,0:T(8,128)S(1)} %collective-permute-done.9.refs_0_, f32[4,8,8,128]{3,2,1,0:T(8,128)S(1)} %collective-permute-done.10.refs_1_, ...), custom_call_target="tpu_custom_call" | custom-call | flops 10000000 | bytes 5000000 | tf_op jit(solution)/shard_map/advance/pallas_call | solution.py:585
  91.0 0.0 collective-permute-done.12.refs_9_
  91.0 0.0 collective-permute-done.6.refs_0_
  91.0 3.1 %finish.1 = f32[27,8,4096]{2,1,0:T(8,128)} custom-call(s32[16]{0:T(128)S(1)} %get-tuple-element.40.plan_ref, f32[4,8,8,128]{3,2,1,0:T(8,128)S(1)} %collective-permute-done.6.refs_0_, f32[4,8,8,128]{3,2,1,0:T(8,128)S(1)} %collective-permute-done.7.refs_1_, f32[4,8,8,128]{3,2,1,0:T(8,128)S(1)} %collective-permute-done.8.refs_2_, ...), custom_call_target="tpu_custom_call", output_to_operand_aliasing={{}: (11, {})} | custom-call | flops 10000000 | bytes 5000000 | tf_op jit(solution)/shard_map/finish/pallas_call | solution.py:606
  (12 shorter events, 0.1 us)
Async XLA Ops:
  3.4 40.1 %all-to-all-start = ((f32[16,21,8,128]{3,2,1,0:T(8,128)}), f32[16,21,8,128]{3,2,1,0:T(8,128)S(1)}, u32[]{:S(2)}, u32[]{:S(2)}) async-start(f32[16,21,8,128]{3,2,1,0:T(8,128)} %pre_0.1), calls=%async_computation | async-start | bytes 2752512 | tf_op jit(solution)/shard_map/all_to_all | solution.py:641
  43.5 29.6 %all-to-all-start.1 = ((f32[16,16,8,128]{3,2,1,0:T(8,128)}), f32[16,16,8,128]{3,2,1,0:T(8,128)S(1)}, u32[]{:S(2)}, u32[]{:S(2)}) async-start(f32[16,16,8,128]{3,2,1,0:T(8,128)} %pre_1.1), calls=%async_computation.1 | async-start | bytes 2097152 | tf_op jit(solution)/shard_map/all_to_all | solution.py:641
  48.8 10.4 %collective-permute-start = (f32[4,21,8,128]{3,2,1,0:T(8,128)S(1)}, f32[4,21,8,128]{3,2,1,0:T(8,128)S(1)}, u32[]{:S(2)}, u32[]{:S(2)}) collective-permute-start(f32[4,21,8,128]{3,2,1,0:T(8,128)S(1)} %get-tuple-element.36), channel_id=1, source_target_pairs={{0,3},{1,2},{2,1},{3,0},{4,7},{5,6},{6,5},{7,4},{8,11},{9,10},{10,... | collective-permute-start | bytes 1032200 | tf_op jit(solution)/shard_map/ppermute | solution.py:50
  49.7 16.9 %collective-permute-start.1 = (f32[4,21,8,128]{3,2,1,0:T(8,128)S(1)}, f32[4,21,8,128]{3,2,1,0:T(8,128)S(1)}, u32[]{:S(2)}, u32[]{:S(2)}) collective-permute-start(f32[4,21,8,128]{3,2,1,0:T(8,128)S(1)} %get-tuple-element.37), channel_id=1, source_target_pairs={{0,2},{1,3},{2,0},{3,1},{4,6},{5,7},{6,4},{7,5},{8,10},{9,11},{10,... | collective-permute-start | bytes 1032200 | tf_op jit(solution)/shard_map/ppermute | solution.py:50
  50.4 16.1 %collective-permute-start.2 = (f32[4,21,8,128]{3,2,1,0:T(8,128)S(1)}, f32[4,21,8,128]{3,2,1,0:T(8,128)S(1)}, u32[]{:S(2)}, u32[]{:S(2)}) collective-permute-start(f32[4,21,8,128]{3,2,1,0:T(8,128)S(1)} %get-tuple-element.38), channel_id=1, source_target_pairs={{0,1},{1,0},{2,3},{3,2},{4,5},{5,4},{6,7},{7,6},{8,9},{9,8},{10,11... | collective-permute-start | bytes 1032200 | tf_op jit(solution)/shard_map/ppermute | solution.py:50
  68.3 4.7 %collective-permute-start.4 = (f32[9,2,8,128]{3,2,0,1:T(8,128)S(1)}, f32[9,2,8,128]{3,2,0,1:T(8,128)S(1)}, u32[]{:S(2)}, u32[]{:S(2)}) collective-permute-start(f32[9,2,8,128]{3,2,0,1:T(8,128)S(1)} %copy.6), channel_id=1, source_target_pairs={{0,3},{1,0},{2,1},{3,2},{4,7},{5,4},{6,5},{7,6},{8,11},{9,8},{10,9... | collective-permute-start | bytes 221192 | tf_op jit(solution)/shard_map/ppermute | solution.py:621
  69.5 3.8 %collective-permute-start.3 = (f32[9,2,8,128]{3,2,0,1:T(8,128)S(1)}, f32[9,2,8,128]{3,2,0,1:T(8,128)S(1)}, u32[]{:S(2)}, u32[]{:S(2)}) collective-permute-start(f32[9,2,8,128]{3,2,0,1:T(8,128)S(1)} %copy.5), channel_id=1, source_target_pairs={{0,1},{1,2},{2,3},{3,0},{4,5},{5,6},{6,7},{7,4},{8,9},{9,10},{10,1... | collective-permute-start | bytes 221192 | tf_op jit(solution)/shard_map/ppermute | solution.py:621
  74.1 2.2 %collective-permute-start.5 = (f32[4,8,8,128]{3,2,1,0:T(8,128)S(1)}, f32[4,8,8,128]{3,2,1,0:T(8,128)S(1)}, u32[]{:S(2)}, u32[]{:S(2)}) collective-permute-start(f32[4,8,8,128]{3,2,1,0:T(8,128)S(1)} %get-tuple-element.47), channel_id=1, source_target_pairs={{0,1},{1,0},{2,3},{3,2},{4,5},{5,4},{6,7},{7,6},{8,9},{9,8},{10,11... | collective-permute-start | bytes 393224 | tf_op jit(solution)/shard_map/ppermute | solution.py:50
  74.2 5.3 %collective-permute-start.9 = (f32[4,8,8,128]{3,2,1,0:T(8,128)S(1)}, f32[4,8,8,128]{3,2,1,0:T(8,128)S(1)}, u32[]{:S(2)}, u32[]{:S(2)}) collective-permute-start(f32[4,8,8,128]{3,2,1,0:T(8,128)S(1)} %get-tuple-element.56), channel_id=1, source_target_pairs={{0,3},{1,2},{2,1},{3,0},{4,7},{5,6},{6,5},{7,4},{8,11},{9,10},{10,... | collective-permute-start | bytes 393224 | tf_op jit(solution)/shard_map/ppermute | solution.py:50
  75.6 7.8 %collective-permute-start.10 = (f32[4,8,8,128]{3,2,1,0:T(8,128)S(1)}, f32[4,8,8,128]{3,2,1,0:T(8,128)S(1)}, u32[]{:S(2)}, u32[]{:S(2)}) collective-permute-start(f32[4,8,8,128]{3,2,1,0:T(8,128)S(1)} %get-tuple-element.57), channel_id=1, source_target_pairs={{0,2},{1,3},{2,0},{3,1},{4,6},{5,7},{6,4},{7,5},{8,10},{9,11},{10,... | collective-permute-start | bytes 393224 | tf_op jit(solution)/shard_map/ppermute | solution.py:50
  76.4 14.6 %collective-permute-start.6 = (f32[4,8,8,128]{3,2,1,0:T(8,128)S(1)}, f32[4,8,8,128]{3,2,1,0:T(8,128)S(1)}, u32[]{:S(2)}, u32[]{:S(2)}) collective-permute-start(f32[4,8,8,128]{3,2,1,0:T(8,128)S(1)} %get-tuple-element.48), channel_id=1, source_target_pairs={{0,3},{1,2},{2,1},{3,0},{4,7},{5,6},{6,5},{7,4},{8,11},{9,10},{10,... | collective-permute-start | bytes 393224 | tf_op jit(solution)/shard_map/ppermute | solution.py:50
  77.1 13.9 %collective-permute-start.7 = (f32[4,8,8,128]{3,2,1,0:T(8,128)S(1)}, f32[4,8,8,128]{3,2,1,0:T(8,128)S(1)}, u32[]{:S(2)}, u32[]{:S(2)}) collective-permute-start(f32[4,8,8,128]{3,2,1,0:T(8,128)S(1)} %get-tuple-element.50), channel_id=1, source_target_pairs={{0,2},{1,3},{2,0},{3,1},{4,6},{5,7},{6,4},{7,5},{8,10},{9,11},{10,... | collective-permute-start | bytes 393224 | tf_op jit(solution)/shard_map/ppermute | solution.py:50
  77.8 13.2 %collective-permute-start.8 = (f32[4,8,8,128]{3,2,1,0:T(8,128)S(1)}, f32[4,8,8,128]{3,2,1,0:T(8,128)S(1)}, u32[]{:S(2)}, u32[]{:S(2)}) collective-permute-start(f32[4,8,8,128]{3,2,1,0:T(8,128)S(1)} %get-tuple-element.52), channel_id=1, source_target_pairs={{0,1},{1,0},{2,3},{3,2},{4,5},{5,4},{6,7},{7,6},{8,9},{9,8},{10,11... | collective-permute-start | bytes 393224 | tf_op jit(solution)/shard_map/ppermute | solution.py:50
  79.5 11.5 %collective-permute-start.11 = (f32[24,8,128]{2,1,0:T(8,128)S(1)}, f32[24,8,128]{2,1,0:T(8,128)S(1)}, u32[]{:S(2)}, u32[]{:S(2)}) collective-permute-start(f32[24,8,128]{2,1,0:T(8,128)S(1)} %get-tuple-element.63), channel_id=1, source_target_pairs={{0,4},{4,8},{8,12},{12,16},{16,20},{20,24},{24,28},{28,0},{1,5},{5... | collective-permute-start | bytes 294920 | tf_op jit(solution)/shard_map/ppermute | solution.py:621
  83.4 7.6 %collective-permute-start.12 = (f32[24,8,128]{2,1,0:T(8,128)S(1)}, f32[24,8,128]{2,1,0:T(8,128)S(1)}, u32[]{:S(2)}, u32[]{:S(2)}) collective-permute-start(f32[24,8,128]{2,1,0:T(8,128)S(1)} %get-tuple-element.65), channel_id=1, source_target_pairs={{0,28},{4,0},{8,4},{12,8},{16,12},{20,16},{24,20},{28,24},{1,29},{... | collective-permute-start | bytes 294920 | tf_op jit(solution)/shard_map/ppermute | solution.py:621

commit v13 on v12

--- a/solution.py
+++ b/solution.py
@@ -652,11 +652,11 @@
     packed = repack(after(late_row, below, above), plan, 1, col_count, cap_col, blocks)
     middle = to_columns(packed[:col_count])
     last = to_columns([after(value, middle[-2]) for value in packed[col_count:]])
+    out, *lattice = advance(picked, middle, fields, below, above)
     up = jnp.concatenate([xhi.reshape(18, SUB, LANES), below[6:, 1], above[6:, 1]])
     down = jnp.concatenate([xlo.reshape(18, SUB, LANES), below[:3, 0], above[:3, 0]])
-    up, down = after(up, middle[-2]), after(down, middle[-2])
+    up, down = after(up, lattice[1]), after(down, lattice[1])
     xlo, xhi = shifted(up, "row", 1), shifted(down, "row", -1)
-    out, *lattice = advance(picked, middle, fields, below, above)
     return jnp.transpose(finish(picked, last, fields, *lattice, xlo, xhi, out), (1, 0, 2))
 
 

time: 94.4 us -> 97.4 us (1.032)
  waiting for transfers between devices: 53 us -> 57.7 us
  starting transfers between devices: 24.6 us -> 23 us
    ppermute x4, waiting for transfers between devices: 0.26 us -> 3.09 us  [shifted(): lax.ppermute(value, axis, [(i, (i + step) % count) for i in range(count)])]
    ppermute x9, waiting for transfers between devices: 19.1 us -> 21 us  [exchanged(): return lax.ppermute(value, axis, pairs)]
    ppermute x4, starting transfers between devices: 7.66 us -> 5.99 us  [shifted(): lax.ppermute(value, axis, [(i, (i + step) % count) for i in range(count)])]
  transfers between devices with their start and end apart: 15 -> 15, of which waited for: 7 -> 9; matrix products, arithmetic and copies ran while one was open for 0% -> 0% of each run, Pallas kernels for 10% -> 9%
where the time goes in v13:
time: 97.4 us; the launch traced here: 97.1 us
  waiting for transfers between devices  57.7 us (59%)
  starting transfers between devices  23 us (24%)
  Pallas kernels  16.3 us (17%)
    all_to_all x2, waiting for transfers between devices, to_rows(): return lax.all_to_all(sent, 'row', split_axis=0, concat_axis=0, tiled=True)  33.6 us
    ppermute x9, waiting for transfers between devices, exchanged(): return lax.ppermute(value, axis, pairs)  21 us
    all_to_all x2, starting transfers between devices, to_rows(): return lax.all_to_all(sent, 'row', split_axis=0, concat_axis=0, tiled=True)  10.9 us
    pallas_call x2, Pallas kernels, pre(): pl.pallas_call(functools.partial(pre_kernel, cap, row_count, per_row, par...  6.12 us
    ppermute x9, starting transfers between devices, exchanged(): return lax.ppermute(value, axis, pairs)  6.07 us
    ppermute x4, starting transfers between devices, shifted(): lax.ppermute(value, axis, [(i, (i + step) % count) for i in range(count)])  5.99 us
    pallas_call x1, Pallas kernels, finish(): pl.pallas_call(functools.partial(finish_kernel, len(homes)), in_specs=[pl...  3.1 us
    ppermute x4, waiting for transfers between devices, shifted(): lax.ppermute(value, axis, [(i, (i + step) % count) for i in range(count)])  3.09 us
  transfers between devices with their start and end apart: 15, of which 9 were waited for; matrix products, arithmetic and copies ran while one was open for 0% of the time, Pallas kernels for 9%

profile of v13, /device:TPU:0, one launch (start us, length us, event | category | flops | bytes accessed | tf_op | source)
XLA Modules:
  0.0 97.1 jit_solution(17381624449041478687)
XLA Ops:
  0.0 3.4 %pre_0.1 = f32[16,21,8,128]{3,2,1,0:T(8,128)} custom-call(s32[8]{0:T(128)} %dest_hbm.1, s32[8]{0:T(128)} %level_hbm.3, f32[27,8,4096]{2,1,0:T(8,128)} %bitcast.14), custom_call_target="tpu_custom_call" | custom-call | flops 10000000 | bytes 4000000 | tf_op jit(solution)/shard_map/pre_0/pallas_call | solution.py:204
  3.4 7.3 %all-to-all-start = ((f32[16,21,8,128]{3,2,1,0:T(8,128)}), f32[16,21,8,128]{3,2,1,0:T(8,128)S(1)}, u32[]{:S(2)}, u32[]{:S(2)}) async-start(f32[16,21,8,128]{3,2,1,0:T(8,128)} %pre_0.1), calls=%async_computation | async-start | bytes 2752512 | tf_op jit(solution)/shard_map/all_to_all | solution.py:641
  10.7 2.7 %pre_1.1 = f32[16,16,8,128]{3,2,1,0:T(8,128)} custom-call(s32[8]{0:T(128)} %dest_hbm.1, s32[8]{0:T(128)} %level_hbm.3, f32[27,8,4096]{2,1,0:T(8,128)} %bitcast.15), custom_call_target="tpu_custom_call" | custom-call | flops 10000000 | bytes 4000000 | tf_op jit(solution)/shard_map/pre_1/pallas_call | solution.py:204
  13.4 30.1 %all-to-all-done.refs_0_ = f32[16,21,8,128]{3,2,1,0:T(8,128)S(1)} async-done(((f32[16,21,8,128]{3,2,1,0:T(8,128)}), f32[16,21,8,128]{3,2,1,0:T(8,128)S(1)}, u32[]{:S(2)}, u32[]{:S(2)}) %all-to-all-start) | async-done | bytes 1376288 | tf_op jit(solution)/shard_map/all_to_all | solution.py:641
  43.5 3.6 %all-to-all-start.1 = ((f32[16,16,8,128]{3,2,1,0:T(8,128)}), f32[16,16,8,128]{3,2,1,0:T(8,128)S(1)}, u32[]{:S(2)}, u32[]{:S(2)}) async-start(f32[16,16,8,128]{3,2,1,0:T(8,128)} %pre_1.1), calls=%async_computation.1 | async-start | bytes 2097152 | tf_op jit(solution)/shard_map/all_to_all | solution.py:641
  47.1 1.7 %repack_0.1 = (f32[4,21,8,128]{3,2,1,0:T(8,128)S(1)}, f32[4,21,8,128]{3,2,1,0:T(8,128)S(1)}, f32[4,21,8,128]{3,2,1,0:T(8,128)S(1)}, f32[4,21,8,128]{3,2,1,0:T(8,128)S(1)}, s32[16]{0:T(128)S(1)}) custom-call(f32[16,21,8,128]{3,2,1,0:T(8,128)S(1)} %all-to-all-done.refs_0_), custom_call_target="tpu_custom_call" | custom-call | bytes 3000000 | tf_op jit(solution)/shard_map/repack_0/pallas_call | solution.py:287
  48.8 0.9 collective-permute-start
  49.7 0.7 collective-permute-start.1
  50.4 0.3 collective-permute-start.2
  50.7 8.4 %collective-permute-done.refs_0_ = f32[4,21,8,128]{3,2,1,0:T(8,128)S(1)} collective-permute-done((f32[4,21,8,128]{3,2,1,0:T(8,128)S(1)}, f32[4,21,8,128]{3,2,1,0:T(8,128)S(1)}, u32[]{:S(2)}, u32[]{:S(2)}) %collective-permute-start) | collective-permute-done | bytes 344096 | tf_op jit(solution)/shard_map/ppermute | solution.py:50
  59.1 7.4 %collective-permute-done.1.refs_1_ = f32[4,21,8,128]{3,2,1,0:T(8,128)S(1)} collective-permute-done((f32[4,21,8,128]{3,2,1,0:T(8,128)S(1)}, f32[4,21,8,128]{3,2,1,0:T(8,128)S(1)}, u32[]{:S(2)}, u32[]{:S(2)}) %collective-permute-start.1) | collective-permute-done | bytes 344096 | tf_op jit(solution)/shard_map/ppermute | solution.py:50
  66.6 1.7 %faces.1 = (f32[9,2,8,128]{3,2,1,0:T(8,128)S(1)}, f32[9,2,8,128]{3,2,1,0:T(8,128)S(1)}, f32[9,2,8,128]{3,2,1,0:T(8,128)S(1)}, f32[9,2,8,128]{3,2,1,0:T(8,128)S(1...) custom-call(f32[4,21,8,128]{3,2,1,0:T(8,128)S(1)} %collective-permute-done.refs_0_, ...), custom_call_target="tpu_custom_call" | custom-call | flops 10000000 | bytes 3000000 | tf_op jit(solution)/shard_map/faces/pallas_call | solution.py:507
  68.3 1.2 %collective-permute-start.4 = (f32[9,2,8,128]{3,2,0,1:T(8,128)S(1)}, f32[9,2,8,128]{3,2,0,1:T(8,128)S(1)}, u32[]{:S(2)}, u32[]{:S(2)}) collective-permute-start(f32[9,2,8,128]{3,2,0,1:T(8,128)S(1)} %copy.6), channel_id=1, source_target_pairs={{0,3},{1,0},{2,1},{3,2},{4,7},{5,4},{6,5},{7,6},{8,11},{9,8},{10,9... | collective-permute-start | bytes 221192 | tf_op jit(solution)/shard_map/ppermute | solution.py:621
  69.5 3.5 %all-to-all-done.1.refs_1_ = f32[16,16,8,128]{3,2,1,0:T(8,128)S(1)} async-done(((f32[16,16,8,128]{3,2,1,0:T(8,128)}), f32[16,16,8,128]{3,2,1,0:T(8,128)S(1)}, u32[]{:S(2)}, u32[]{:S(2)}) %all-to-all-start.1) | async-done | bytes 1048608 | tf_op jit(solution)/shard_map/all_to_all | solution.py:641
  73.1 0.0 collective-permute-done.4
  73.1 0.3 collective-permute-done.3
  73.3 0.8 repack_1.1
  74.1 0.1 collective-permute-start.5
  74.2 1.4 %collective-permute-start.9 = (f32[4,8,8,128]{3,2,1,0:T(8,128)S(1)}, f32[4,8,8,128]{3,2,1,0:T(8,128)S(1)}, u32[]{:S(2)}, u32[]{:S(2)}) collective-permute-start(f32[4,8,8,128]{3,2,1,0:T(8,128)S(1)} %get-tuple-element.56), channel_id=1, source_target_pairs={{0,3},{1,2},{2,1},{3,0},{4,7},{5,6},{6,5},{7,4},{8,11},{9,10},{10,... | collective-permute-start | bytes 393224 | tf_op jit(solution)/shard_map/ppermute | solution.py:50
  75.6 0.7 collective-permute-start.10
  76.4 0.0 collective-permute-done.5.refs_2_
  76.4 0.8 collective-permute-start.6
  77.1 0.7 collective-permute-start.7
  77.8 0.4 collective-permute-start.8
  78.3 1.2 %collective-permute-done.9.refs_0_ = f32[4,8,8,128]{3,2,1,0:T(8,128)S(1)} collective-permute-done((f32[4,8,8,128]{3,2,1,0:T(8,128)S(1)}, f32[4,8,8,128]{3,2,1,0:T(8,128)S(1)}, u32[]{:S(2)}, u32[]{:S(2)}) %collective-permute-start.9) | collective-permute-done | bytes 131104 | tf_op jit(solution)/shard_map/ppermute | solution.py:50
  79.5 3.9 %collective-permute-done.10.refs_1_ = f32[4,8,8,128]{3,2,1,0:T(8,128)S(1)} collective-permute-done((f32[4,8,8,128]{3,2,1,0:T(8,128)S(1)}, f32[4,8,8,128]{3,2,1,0:T(8,128)S(1)}, u32[]{:S(2)}, u32[]{:S(2)}) %collective-permute-start.10) | collective-permute-done | bytes 131104 | tf_op jit(solution)/shard_map/ppermute | solution.py:50
  83.4 2.9 %advance.1 = (f32[27,8,4096]{2,1,0:T(8,128)}, f32[27,32,8,128]{3,2,1,0:T(8,128)S(1)}, f32[9,16,8,128]{3,2,1,0:T(8,128)S(1)}, f32[9,16,8,128]{3,2,1,0:T(8,128)S(1)}) custom-call(s32[16]{0:T(128)S(1)} %get-tuple-element.40.plan_ref, f32[4,8,8,128]{3,2,1,0:T(8,128)S(1)} %collective-permute-done.9.refs_0_, f32[4,8,8,128]{3,2,1,0:T(8,128)S(1)} %collective-permute-done.10.refs_1_, ...), custom_call_target="tpu_custom_call" | custom-call | flops 10000000 | bytes 5000000 | tf_op jit(solution)/shard_map/advance/pallas_call | solution.py:585
  86.4 1.9 %collective-permute-start.11 = (f32[24,8,128]{2,1,0:T(8,128)S(1)}, f32[24,8,128]{2,1,0:T(8,128)S(1)}, u32[]{:S(2)}, u32[]{:S(2)}) collective-permute-start(f32[24,8,128]{2,1,0:T(8,128)S(1)} %get-tuple-element.63), channel_id=1, source_target_pairs={{0,4},{4,8},{8,12},{12,16},{16,20},{20,24},{24,28},{28,0},{1,5},{5... | collective-permute-start | bytes 294920 | tf_op jit(solution)/shard_map/ppermute | solution.py:621
  88.3 2.9 %collective-permute-start.12 = (f32[24,8,128]{2,1,0:T(8,128)S(1)}, f32[24,8,128]{2,1,0:T(8,128)S(1)}, u32[]{:S(2)}, u32[]{:S(2)}) collective-permute-start(f32[24,8,128]{2,1,0:T(8,128)S(1)} %get-tuple-element.65), channel_id=1, source_target_pairs={{0,28},{4,0},{8,4},{12,8},{16,12},{20,16},{24,20},{28,24},{1,29},{... | collective-permute-start | bytes 294920 | tf_op jit(solution)/shard_map/ppermute | solution.py:621
  91.2 2.7 %collective-permute-done.11.refs_8_ = f32[24,8,128]{2,1,0:T(8,128)S(1)} collective-permute-done((f32[24,8,128]{2,1,0:T(8,128)S(1)}, f32[24,8,128]{2,1,0:T(8,128)S(1)}, u32[]{:S(2)}, u32[]{:S(2)}) %collective-permute-start.11) | collective-permute-done | bytes 98336 | tf_op jit(solution)/shard_map/ppermute | solution.py:621
  93.9 0.1 collective-permute-done.12.refs_9_
  94.0 3.1 %finish.1 = f32[27,8,4096]{2,1,0:T(8,128)} custom-call(s32[16]{0:T(128)S(1)} %get-tuple-element.40.plan_ref, f32[4,8,8,128]{3,2,1,0:T(8,128)S(1)} %collective-permute-done.6.refs_0_, f32[4,8,8,128]{3,2,1,0:T(8,128)S(1)} %collective-permute-done.7.refs_1_, f32[4,8,8,128]{3,2,1,0:T(8,128)S(1)} %collective-permute-done.8.refs_2_, ...), custom_call_target="tpu_custom_call", output_to_operand_aliasing={{}: (11, {})} | custom-call | flops 10000000 | bytes 5000000 | tf_op jit(solution)/shard_map/finish/pallas_call | solution.py:606
  (12 shorter events, 0.1 us)
Async XLA Ops:
  3.4 40.1 %all-to-all-start = ((f32[16,21,8,128]{3,2,1,0:T(8,128)}), f32[16,21,8,128]{3,2,1,0:T(8,128)S(1)}, u32[]{:S(2)}, u32[]{:S(2)}) async-start(f32[16,21,8,128]{3,2,1,0:T(8,128)} %pre_0.1), calls=%async_computation | async-start | bytes 2752512 | tf_op jit(solution)/shard_map/all_to_all | solution.py:641
  43.5 29.6 %all-to-all-start.1 = ((f32[16,16,8,128]{3,2,1,0:T(8,128)}), f32[16,16,8,128]{3,2,1,0:T(8,128)S(1)}, u32[]{:S(2)}, u32[]{:S(2)}) async-start(f32[16,16,8,128]{3,2,1,0:T(8,128)} %pre_1.1), calls=%async_computation.1 | async-start | bytes 2097152 | tf_op jit(solution)/shard_map/all_to_all | solution.py:641
  48.8 10.4 %collective-permute-start = (f32[4,21,8,128]{3,2,1,0:T(8,128)S(1)}, f32[4,21,8,128]{3,2,1,0:T(8,128)S(1)}, u32[]{:S(2)}, u32[]{:S(2)}) collective-permute-start(f32[4,21,8,128]{3,2,1,0:T(8,128)S(1)} %get-tuple-element.36), channel_id=1, source_target_pairs={{0,3},{1,2},{2,1},{3,0},{4,7},{5,6},{6,5},{7,4},{8,11},{9,10},{10,... | collective-permute-start | bytes 1032200 | tf_op jit(solution)/shard_map/ppermute | solution.py:50
  49.7 16.9 %collective-permute-start.1 = (f32[4,21,8,128]{3,2,1,0:T(8,128)S(1)}, f32[4,21,8,128]{3,2,1,0:T(8,128)S(1)}, u32[]{:S(2)}, u32[]{:S(2)}) collective-permute-start(f32[4,21,8,128]{3,2,1,0:T(8,128)S(1)} %get-tuple-element.37), channel_id=1, source_target_pairs={{0,2},{1,3},{2,0},{3,1},{4,6},{5,7},{6,4},{7,5},{8,10},{9,11},{10,... | collective-permute-start | bytes 1032200 | tf_op jit(solution)/shard_map/ppermute | solution.py:50
  50.4 16.1 %collective-permute-start.2 = (f32[4,21,8,128]{3,2,1,0:T(8,128)S(1)}, f32[4,21,8,128]{3,2,1,0:T(8,128)S(1)}, u32[]{:S(2)}, u32[]{:S(2)}) collective-permute-start(f32[4,21,8,128]{3,2,1,0:T(8,128)S(1)} %get-tuple-element.38), channel_id=1, source_target_pairs={{0,1},{1,0},{2,3},{3,2},{4,5},{5,4},{6,7},{7,6},{8,9},{9,8},{10,11... | collective-permute-start | bytes 1032200 | tf_op jit(solution)/shard_map/ppermute | solution.py:50
  68.3 4.7 %collective-permute-start.4 = (f32[9,2,8,128]{3,2,0,1:T(8,128)S(1)}, f32[9,2,8,128]{3,2,0,1:T(8,128)S(1)}, u32[]{:S(2)}, u32[]{:S(2)}) collective-permute-start(f32[9,2,8,128]{3,2,0,1:T(8,128)S(1)} %copy.6), channel_id=1, source_target_pairs={{0,3},{1,0},{2,1},{3,2},{4,7},{5,4},{6,5},{7,6},{8,11},{9,8},{10,9... | collective-permute-start | bytes 221192 | tf_op jit(solution)/shard_map/ppermute | solution.py:621
  69.5 3.8 %collective-permute-start.3 = (f32[9,2,8,128]{3,2,0,1:T(8,128)S(1)}, f32[9,2,8,128]{3,2,0,1:T(8,128)S(1)}, u32[]{:S(2)}, u32[]{:S(2)}) collective-permute-start(f32[9,2,8,128]{3,2,0,1:T(8,128)S(1)} %copy.5), channel_id=1, source_target_pairs={{0,1},{1,2},{2,3},{3,0},{4,5},{5,6},{6,7},{7,4},{8,9},{9,10},{10,1... | collective-permute-start | bytes 221192 | tf_op jit(solution)/shard_map/ppermute | solution.py:621
  74.1 2.2 %collective-permute-start.5 = (f32[4,8,8,128]{3,2,1,0:T(8,128)S(1)}, f32[4,8,8,128]{3,2,1,0:T(8,128)S(1)}, u32[]{:S(2)}, u32[]{:S(2)}) collective-permute-start(f32[4,8,8,128]{3,2,1,0:T(8,128)S(1)} %get-tuple-element.47), channel_id=1, source_target_pairs={{0,1},{1,0},{2,3},{3,2},{4,5},{5,4},{6,7},{7,6},{8,9},{9,8},{10,11... | collective-permute-start | bytes 393224 | tf_op jit(solution)/shard_map/ppermute | solution.py:50
  74.2 5.3 %collective-permute-start.9 = (f32[4,8,8,128]{3,2,1,0:T(8,128)S(1)}, f32[4,8,8,128]{3,2,1,0:T(8,128)S(1)}, u32[]{:S(2)}, u32[]{:S(2)}) collective-permute-start(f32[4,8,8,128]{3,2,1,0:T(8,128)S(1)} %get-tuple-element.56), channel_id=1, source_target_pairs={{0,3},{1,2},{2,1},{3,0},{4,7},{5,6},{6,5},{7,4},{8,11},{9,10},{10,... | collective-permute-start | bytes 393224 | tf_op jit(solution)/shard_map/ppermute | solution.py:50
  75.6 7.8 %collective-permute-start.10 = (f32[4,8,8,128]{3,2,1,0:T(8,128)S(1)}, f32[4,8,8,128]{3,2,1,0:T(8,128)S(1)}, u32[]{:S(2)}, u32[]{:S(2)}) collective-permute-start(f32[4,8,8,128]{3,2,1,0:T(8,128)S(1)} %get-tuple-element.57), channel_id=1, source_target_pairs={{0,2},{1,3},{2,0},{3,1},{4,6},{5,7},{6,4},{7,5},{8,10},{9,11},{10,... | collective-permute-start | bytes 393224 | tf_op jit(solution)/shard_map/ppermute | solution.py:50
  76.4 17.6 %collective-permute-start.6 = (f32[4,8,8,128]{3,2,1,0:T(8,128)S(1)}, f32[4,8,8,128]{3,2,1,0:T(8,128)S(1)}, u32[]{:S(2)}, u32[]{:S(2)}) collective-permute-start(f32[4,8,8,128]{3,2,1,0:T(8,128)S(1)} %get-tuple-element.48), channel_id=1, source_target_pairs={{0,3},{1,2},{2,1},{3,0},{4,7},{5,6},{6,5},{7,4},{8,11},{9,10},{10,... | collective-permute-start | bytes 393224 | tf_op jit(solution)/shard_map/ppermute | solution.py:50
  77.1 16.9 %collective-permute-start.7 = (f32[4,8,8,128]{3,2,1,0:T(8,128)S(1)}, f32[4,8,8,128]{3,2,1,0:T(8,128)S(1)}, u32[]{:S(2)}, u32[]{:S(2)}) collective-permute-start(f32[4,8,8,128]{3,2,1,0:T(8,128)S(1)} %get-tuple-element.50), channel_id=1, source_target_pairs={{0,2},{1,3},{2,0},{3,1},{4,6},{5,7},{6,4},{7,5},{8,10},{9,11},{10,... | collective-permute-start | bytes 393224 | tf_op jit(solution)/shard_map/ppermute | solution.py:50
  77.8 16.2 %collective-permute-start.8 = (f32[4,8,8,128]{3,2,1,0:T(8,128)S(1)}, f32[4,8,8,128]{3,2,1,0:T(8,128)S(1)}, u32[]{:S(2)}, u32[]{:S(2)}) collective-permute-start(f32[4,8,8,128]{3,2,1,0:T(8,128)S(1)} %get-tuple-element.52), channel_id=1, source_target_pairs={{0,1},{1,0},{2,3},{3,2},{4,5},{5,4},{6,7},{7,6},{8,9},{9,8},{10,11... | collective-permute-start | bytes 393224 | tf_op jit(solution)/shard_map/ppermute | solution.py:50
  86.4 7.5 %collective-permute-start.11 = (f32[24,8,128]{2,1,0:T(8,128)S(1)}, f32[24,8,128]{2,1,0:T(8,128)S(1)}, u32[]{:S(2)}, u32[]{:S(2)}) collective-permute-start(f32[24,8,128]{2,1,0:T(8,128)S(1)} %get-tuple-element.63), channel_id=1, source_target_pairs={{0,4},{4,8},{8,12},{12,16},{16,20},{20,24},{24,28},{28,0},{1,5},{5... | collective-permute-start | bytes 294920 | tf_op jit(solution)/shard_map/ppermute | solution.py:621
  88.3 5.7 %collective-permute-start.12 = (f32[24,8,128]{2,1,0:T(8,128)S(1)}, f32[24,8,128]{2,1,0:T(8,128)S(1)}, u32[]{:S(2)}, u32[]{:S(2)}) collective-permute-start(f32[24,8,128]{2,1,0:T(8,128)S(1)} %get-tuple-element.65), channel_id=1, source_target_pairs={{0,28},{4,0},{8,4},{12,8},{16,12},{20,16},{24,20},{28,24},{1,29},{... | collective-permute-start | bytes 294920 | tf_op jit(solution)/shard_map/ppermute | solution.py:621

commit v14 on v11

--- a/solution.py
+++ b/solution.py
@@ -259,9 +259,11 @@
                 count_ref[d] = k + 1
                 plan_ref[d * cap + k] = e
 
-    tiles = outs[0].shape[1]
     for place, out in enumerate(outs):
-        quarter, d = divmod(place, col_count)
+        tiles = out.shape[1]
+        quarter, d = divmod(place - 1, col_count - 1) if part else (0, place)
+        if part and place == 0:
+            quarter, d = 0, col_count - 1
         for k in range(cap):
             e = plan_ref[d * cap + k]
 
@@ -282,14 +284,16 @@
     scratch = []
     if part == 0:
         scratch = tag_scratch(1, landed.shape[0]) + [pltpu.SMEM((col_count,), jnp.int32)]
-    quarters = len(INNER) if part else 1
-    shape = (cap, landed.shape[1] // quarters) + landed.shape[2:]
+    tiles = landed.shape[1]
+    sizes = [tiles] * col_count
+    if part:
+        sizes = [tiles] + [tiles // len(INNER)] * (len(INNER) * (col_count - 1))
     packed = pl.pallas_call(
         functools.partial(repack_kernel, cap, col_count, blocks, part),
         in_specs=([scalars] if part else []) + [whole],
-        out_specs=[whole] * (quarters * col_count) + ([] if part else [scalars]),
+        out_specs=[whole] * len(sizes) + ([] if part else [scalars]),
         scratch_shapes=scratch,
-        out_shape=[jax.ShapeDtypeStruct(shape, jnp.float32)] * (quarters * col_count)
+        out_shape=[jax.ShapeDtypeStruct((cap, size) + landed.shape[2:], jnp.float32) for size in sizes]
         + ([] if part else [jax.ShapeDtypeStruct((col_count * cap,), jnp.int32)]),
         compiler_params=pltpu.CompilerParams(vmem_limit_bytes=VMEM_LIMIT),
         cost_estimate=pl.CostEstimate(flops=0, bytes_accessed=3 * 10**6, transcendentals=0),
@@ -353,15 +357,18 @@
     return result
 
 
-def unload(plan_ref, ins, fields_ref):
-    cap, tiles = ins[0].shape[:2]
+def unload(plan_ref, ins, fields_ref, index=0):
+    cap = ins[0].shape[0]
+    tiles = ins[-1].shape[1]
     for e in range(len(ins) * cap):
         t = plan_ref[e]
+        in_ref = ins[e // cap]
+        first = index * tiles if in_ref.shape[1] > tiles else 0
 
         @pl.when(t >= 0)
         def _():
             for tile in range(tiles):
-                fields_ref[pl.ds(tile * SUB * SUB + t, SUB, stride=SUB), :] = ins[e // cap][e % cap, tile]
+                fields_ref[pl.ds(tile * SUB * SUB + t, SUB, stride=SUB), :] = in_ref[e % cap, first + tile]
 
 
 def row_of(ref, row):
@@ -571,7 +578,7 @@
         to += rows
     for copy in copies:
         copy.start()
-    unload(plan_ref, ins, late_ref)
+    unload(plan_ref, ins, late_ref, 1)
     fill_inner(fields_ref, late_ref, INNER[1], main_ref)
     fill_sides(below_in, above_in, below_ref, above_ref, 5, 15)
     for copy in copies:
@@ -651,7 +658,7 @@
         return lax.all_to_all(sent, "row", split_axis=0, concat_axis=0, tiled=True)
 
     def to_columns(packed):
-        return [exchanged(packed[d], "col", d) for d in range(col_count - 1, 0, -1)] + [packed[0]]
+        return [exchanged(packed[d], "col", d) for d in range(len(packed) - 1, 0, -1)] + [packed[0]]
 
     sent = prepared(0)
     early_row = to_rows(sent)
@@ -663,7 +670,10 @@
     down = jnp.concatenate([xlo.reshape(18, SUB, LANES), below[:3, 0], above[:3, 0]])
     xlo, xhi = shifted(up, "row", 1), shifted(down, "row", -1)
     packed = repack(after(late_row, up, down), plan, 1, col_count, cap_col, blocks)
-    middle, last = to_columns(packed[:col_count]), to_columns(packed[col_count:])
+    far, *packed = packed
+    far = exchanged(far, "col", col_count - 1)
+    middle = [far] + to_columns(packed[: col_count - 1])
+    last = [far] + to_columns(packed[col_count - 1 :])
     out, kept = advance(picked, middle, fields, xlo, xhi, below, above)
     return jnp.transpose(finish(picked, last, fields, kept, below, above, out), (1, 0, 2))
 

time: 94.3 us -> 91.7 us (0.972)
  waiting for transfers between devices: 54.6 us -> 52.9 us
    ppermute x9 -> x8, waiting for transfers between devices: 19 us -> 17.7 us  [exchanged(): return lax.ppermute(value, axis, pairs)]
    ppermute x9 -> x8, starting transfers between devices: 5.59 us -> 4.72 us  [exchanged(): return lax.ppermute(value, axis, pairs)]
  transfers between devices with their start and end apart: 15 -> 14, of which waited for: 10 -> 7; matrix products, arithmetic and copies ran while one was open for 0% -> 0% of each run, Pallas kernels for 10% -> 10%
where the time goes in v14:
time: 91.7 us; the launch traced here: 91.4 us
  waiting for transfers between devices  52.9 us (58%)
  starting transfers between devices  22.1 us (24%)
  Pallas kernels  16.3 us (18%)
    all_to_all x2, waiting for transfers between devices, to_rows(): return lax.all_to_all(sent, 'row', split_axis=0, concat_axis=0, tiled=True)  30.9 us
    ppermute x8, waiting for transfers between devices, exchanged(): return lax.ppermute(value, axis, pairs)  17.7 us
    all_to_all x2, starting transfers between devices, to_rows(): return lax.all_to_all(sent, 'row', split_axis=0, concat_axis=0, tiled=True)  10.9 us
    ppermute x4, starting transfers between devices, shifted(): lax.ppermute(value, axis, [(i, (i + step) % count) for i in range(count)])  6.52 us
    pallas_call x2, Pallas kernels, pre(): pl.pallas_call(functools.partial(pre_kernel, cap, row_count, per_row, par...  6.11 us
    ppermute x8, starting transfers between devices, exchanged(): return lax.ppermute(value, axis, pairs)  4.72 us
    ppermute x4, waiting for transfers between devices, shifted(): lax.ppermute(value, axis, [(i, (i + step) % count) for i in range(count)])  4.23 us
    pallas_call x1, Pallas kernels, advance(): pl.pallas_call(functools.partial(advance_kernel, len(homes)), in_specs=[p...  3.15 us
  transfers between devices with their start and end apart: 14, of which 7 were waited for; matrix products, arithmetic and copies ran while one was open for 0% of the time, Pallas kernels for 10%

profile of v14, /device:TPU:0, one launch (start us, length us, event | category | flops | bytes accessed | tf_op | source)
XLA Modules:
  0.0 91.4 jit_solution(16105453097456338097)
XLA Ops:
  0.0 3.4 %pre_0.1 = f32[16,21,8,128]{3,2,1,0:T(8,128)} custom-call(s32[8]{0:T(128)} %dest_hbm.1, s32[8]{0:T(128)} %level_hbm.3, f32[27,8,4096]{2,1,0:T(8,128)} %bitcast.14), custom_call_target="tpu_custom_call" | custom-call | flops 10000000 | bytes 4000000 | tf_op jit(solution)/shard_map/pre_0/pallas_call | solution.py:204
  3.4 7.3 %all-to-all-start = ((f32[16,21,8,128]{3,2,1,0:T(8,128)}), f32[16,21,8,128]{3,2,1,0:T(8,128)S(1)}, u32[]{:S(2)}, u32[]{:S(2)}) async-start(f32[16,21,8,128]{3,2,1,0:T(8,128)} %pre_0.1), calls=%async_computation | async-start | bytes 2752512 | tf_op jit(solution)/shard_map/all_to_all | solution.py:658
  10.7 2.7 %pre_1.1 = f32[16,16,8,128]{3,2,1,0:T(8,128)} custom-call(s32[8]{0:T(128)} %dest_hbm.1, s32[8]{0:T(128)} %level_hbm.3, f32[27,8,4096]{2,1,0:T(8,128)} %bitcast.15), custom_call_target="tpu_custom_call" | custom-call | flops 10000000 | bytes 4000000 | tf_op jit(solution)/shard_map/pre_1/pallas_call | solution.py:204
  13.4 30.1 %all-to-all-done.refs_0_ = f32[16,21,8,128]{3,2,1,0:T(8,128)S(1)} async-done(((f32[16,21,8,128]{3,2,1,0:T(8,128)}), f32[16,21,8,128]{3,2,1,0:T(8,128)S(1)}, u32[]{:S(2)}, u32[]{:S(2)}) %all-to-all-start) | async-done | bytes 1376288 | tf_op jit(solution)/shard_map/all_to_all | solution.py:658
  43.5 3.6 %all-to-all-start.1 = ((f32[16,16,8,128]{3,2,1,0:T(8,128)}), f32[16,16,8,128]{3,2,1,0:T(8,128)S(1)}, u32[]{:S(2)}, u32[]{:S(2)}) async-start(f32[16,16,8,128]{3,2,1,0:T(8,128)} %pre_1.1), calls=%async_computation.1 | async-start | bytes 2097152 | tf_op jit(solution)/shard_map/all_to_all | solution.py:658
  47.1 1.7 %repack_0.1 = (f32[4,21,8,128]{3,2,1,0:T(8,128)S(1)}, f32[4,21,8,128]{3,2,1,0:T(8,128)S(1)}, f32[4,21,8,128]{3,2,1,0:T(8,128)S(1)}, f32[4,21,8,128]{3,2,1,0:T(8,128)S(1)}, s32[16]{0:T(128)S(1)}) custom-call(f32[16,21,8,128]{3,2,1,0:T(8,128)S(1)} %all-to-all-done.refs_0_), custom_call_target="tpu_custom_call" | custom-call | bytes 3000000 | tf_op jit(solution)/shard_map/repack_0/pallas_call | solution.py:291
  48.8 0.9 %collective-permute-start = (f32[4,21,8,128]{3,2,1,0:T(8,128)S(1)}, f32[4,21,8,128]{3,2,1,0:T(8,128)S(1)}, u32[]{:S(2)}, u32[]{:S(2)}) collective-permute-start(f32[4,21,8,128]{3,2,1,0:T(8,128)S(1)} %get-tuple-element.27), channel_id=1, source_target_pairs={{0,3},{1,2},{2,1},{3,0},{4,7},{5,6},{6,5},{7,4},{8,11},{9,10},{10,... | collective-permute-start | bytes 1032200 | tf_op jit(solution)/shard_map/ppermute | solution.py:50
  49.7 0.7 collective-permute-start.1
  50.4 0.3 collective-permute-start.2
  50.7 8.4 %collective-permute-done.refs_0_ = f32[4,21,8,128]{3,2,1,0:T(8,128)S(1)} collective-permute-done((f32[4,21,8,128]{3,2,1,0:T(8,128)S(1)}, f32[4,21,8,128]{3,2,1,0:T(8,128)S(1)}, u32[]{:S(2)}, u32[]{:S(2)}) %collective-permute-start) | collective-permute-done | bytes 344096 | tf_op jit(solution)/shard_map/ppermute | solution.py:50
  59.1 7.4 %collective-permute-done.1.refs_1_ = f32[4,21,8,128]{3,2,1,0:T(8,128)S(1)} collective-permute-done((f32[4,21,8,128]{3,2,1,0:T(8,128)S(1)}, f32[4,21,8,128]{3,2,1,0:T(8,128)S(1)}, u32[]{:S(2)}, u32[]{:S(2)}) %collective-permute-start.1) | collective-permute-done | bytes 344096 | tf_op jit(solution)/shard_map/ppermute | solution.py:50
  66.6 0.0 collective-permute-done.2.refs_2_
  66.6 1.7 %faces.1 = (f32[9,2,8,128]{3,2,1,0:T(8,128)S(1)}, f32[9,2,8,128]{3,2,1,0:T(8,128)S(1)}, f32[9,2,8,128]{3,2,1,0:T(8,128)S(1)}, f32[9,2,8,128]{3,2,1,0:T(8,128)S(1...) custom-call(f32[4,21,8,128]{3,2,1,0:T(8,128)S(1)} %collective-permute-done.refs_0_, ...), custom_call_target="tpu_custom_call" | custom-call | flops 10000000 | bytes 3000000 | tf_op jit(solution)/shard_map/faces/pallas_call | solution.py:514
  68.3 0.1 collective-permute-start.3
  68.4 1.7 %collective-permute-start.4 = (f32[9,2,8,128]{3,2,1,0:T(8,128)S(1)}, f32[9,2,8,128]{3,2,1,0:T(8,128)S(1)}, u32[]{:S(2)}, u32[]{:S(2)}) collective-permute-start(f32[9,2,8,128]{3,2,1,0:T(8,128)S(1)} %get-tuple-element.36), channel_id=1, source_target_pairs={{0,3},{1,0},{2,1},{3,2},{4,7},{5,4},{6,5},{7,6},{8,11},{9,8},{10,9... | collective-permute-start | bytes 221192 | tf_op jit(solution)/shard_map/ppermute | solution.py:638
  70.1 2.0 %collective-permute-done.3.refs_7_.refs_6_ = f32[9,2,8,128]{3,2,1,0:T(8,128)S(1)} collective-permute-done((f32[9,2,8,128]{3,2,1,0:T(8,128)S(1)}, f32[9,2,8,128]{3,2,1,0:T(8,128)S(1)}, u32[]{:S(2)}, u32[]{:S(2)}) %collective-permute-start.3) | collective-permute-done | bytes 73760 | tf_op jit(solution)/shard_map/ppermute | solution.py:638
  72.1 0.0 collective-permute-done.4.refs_8_.refs_7_
  72.2 0.9 all-to-all-done.1.refs_1_
  73.1 0.8 repack_1.1
  73.8 1.2 %collective-permute-start.5 = (f32[4,16,8,128]{3,2,1,0:T(8,128)S(1)}, f32[4,16,8,128]{3,2,1,0:T(8,128)S(1)}, u32[]{:S(2)}, u32[]{:S(2)}) collective-permute-start(f32[4,16,8,128]{3,2,1,0:T(8,128)S(1)} %get-tuple-element.39), channel_id=1, source_target_pairs={{0,3},{1,2},{2,1},{3,0},{4,7},{5,6},{6,5},{7,4},{8,11},{9,10},{10,... | collective-permute-start | bytes 786440 | tf_op jit(solution)/shard_map/ppermute | solution.py:50
  75.1 1.7 %collective-permute-start.10 = (f32[24,8,128]{2,1,0:T(8,128)S(1)}, f32[24,8,128]{2,1,0:T(8,128)S(1)}, u32[]{:S(2)}, u32[]{:S(2)}) collective-permute-start(f32[24,8,128]{2,1,0:T(8,128)S(1)} %pad_maximum_fusion), channel_id=1, source_target_pairs={{0,4},{4,8},{8,12},{12,16},{16,20},{20,24},{24,28},{28,0},{1,5},{5... | collective-permute-start | bytes 294920 | tf_op jit(solution)/shard_map/ppermute | solution.py:638
  76.8 3.0 %collective-permute-start.11 = (f32[24,8,128]{2,1,0:T(8,128)S(1)}, f32[24,8,128]{2,1,0:T(8,128)S(1)}, u32[]{:S(2)}, u32[]{:S(2)}) collective-permute-start(f32[24,8,128]{2,1,0:T(8,128)S(1)} %pad_maximum_fusion.1), channel_id=1, source_target_pairs={{0,28},{4,0},{8,4},{12,8},{16,12},{20,16},{24,20},{28,24},{1,29},{... | collective-permute-start | bytes 294920 | tf_op jit(solution)/shard_map/ppermute | solution.py:638
  79.8 1.1 %collective-permute-start.8 = (f32[4,8,8,128]{3,2,1,0:T(8,128)S(1)}, f32[4,8,8,128]{3,2,1,0:T(8,128)S(1)}, u32[]{:S(2)}, u32[]{:S(2)}) collective-permute-start(f32[4,8,8,128]{3,2,1,0:T(8,128)S(1)} %get-tuple-element.44), channel_id=1, source_target_pairs={{0,2},{1,3},{2,0},{3,1},{4,6},{5,7},{6,4},{7,5},{8,10},{9,11},{10,... | collective-permute-start | bytes 393224 | tf_op jit(solution)/shard_map/ppermute | solution.py:50
  80.8 2.2 %collective-permute-done.10.refs_5_ = f32[24,8,128]{2,1,0:T(8,128)S(1)} collective-permute-done((f32[24,8,128]{2,1,0:T(8,128)S(1)}, f32[24,8,128]{2,1,0:T(8,128)S(1)}, u32[]{:S(2)}, u32[]{:S(2)}) %collective-permute-start.10) | collective-permute-done | bytes 98336 | tf_op jit(solution)/shard_map/ppermute | solution.py:638
  83.0 0.5 collective-permute-start.6
  83.6 0.0 collective-permute-done.11.refs_6_
  83.6 1.8 %collective-permute-done.8.refs_1_ = f32[4,8,8,128]{3,2,1,0:T(8,128)S(1)} collective-permute-done((f32[4,8,8,128]{3,2,1,0:T(8,128)S(1)}, f32[4,8,8,128]{3,2,1,0:T(8,128)S(1)}, u32[]{:S(2)}, u32[]{:S(2)}) %collective-permute-start.8) | collective-permute-done | bytes 131104 | tf_op jit(solution)/shard_map/ppermute | solution.py:50
  85.4 0.0 collective-permute-done.9.refs_2_
  85.4 3.2 %advance.1 = (f32[27,8,4096]{2,1,0:T(8,128)}, f32[27,12,8,128]{3,2,1,0:T(8,128)S(1)}) custom-call(s32[16]{0:T(128)S(1)} %get-tuple-element.31.plan_ref, f32[4,16,8,128]{3,2,1,0:T(8,128)S(1)} %collective-permute-done.5.refs_0_, f32[4,8,8,128]{3,2,1,0:T(8,128)S(1)} %collective-permute-done.8.refs_1_, f32[4,8,8,128]{3,2,1,0:T(8,128)S(1)} %collective-permute-done.9.refs_2_, ...), custom_call_target="tpu_custom_call" | custom-call | flops 10000000 | bytes 5000000 | tf_op jit(solution)/shard_map/advance/pallas_call | solution.py:604
  88.5 0.0 collective-permute-done.6.refs_1_
  88.5 0.0 collective-permute-done.7.refs_2_
  88.6 2.9 %finish.1 = f32[27,8,4096]{2,1,0:T(8,128)} custom-call(s32[16]{0:T(128)S(1)} %get-tuple-element.31.plan_ref, f32[4,16,8,128]{3,2,1,0:T(8,128)S(1)} %collective-permute-done.5.refs_0_, f32[4,8,8,128]{3,2,1,0:T(8,128)S(1)} %collective-permute-done.6.refs_1_, f32[4,8,8,128]{3,2,1,0:T(8,128)S(1)} %collective-permute-done.7.refs_2_, ...), custom_call_target="tpu_custom_call", output_to_operand_aliasing={{}: (9, {})} | custom-call | flops 10000000 | bytes 5000000 | tf_op jit(solution)/shard_map/finish/pallas_call | solution.py:623
  (7 shorter events, 0.0 us)
Async XLA Ops:
  3.4 40.1 %all-to-all-start = ((f32[16,21,8,128]{3,2,1,0:T(8,128)}), f32[16,21,8,128]{3,2,1,0:T(8,128)S(1)}, u32[]{:S(2)}, u32[]{:S(2)}) async-start(f32[16,21,8,128]{3,2,1,0:T(8,128)} %pre_0.1), calls=%async_computation | async-start | bytes 2752512 | tf_op jit(solution)/shard_map/all_to_all | solution.py:658
  43.5 29.6 %all-to-all-start.1 = ((f32[16,16,8,128]{3,2,1,0:T(8,128)}), f32[16,16,8,128]{3,2,1,0:T(8,128)S(1)}, u32[]{:S(2)}, u32[]{:S(2)}) async-start(f32[16,16,8,128]{3,2,1,0:T(8,128)} %pre_1.1), calls=%async_computation.1 | async-start | bytes 2097152 | tf_op jit(solution)/shard_map/all_to_all | solution.py:658
  48.8 10.4 %collective-permute-start = (f32[4,21,8,128]{3,2,1,0:T(8,128)S(1)}, f32[4,21,8,128]{3,2,1,0:T(8,128)S(1)}, u32[]{:S(2)}, u32[]{:S(2)}) collective-permute-start(f32[4,21,8,128]{3,2,1,0:T(8,128)S(1)} %get-tuple-element.27), channel_id=1, source_target_pairs={{0,3},{1,2},{2,1},{3,0},{4,7},{5,6},{6,5},{7,4},{8,11},{9,10},{10,... | collective-permute-start | bytes 1032200 | tf_op jit(solution)/shard_map/ppermute | solution.py:50
  49.7 16.9 %collective-permute-start.1 = (f32[4,21,8,128]{3,2,1,0:T(8,128)S(1)}, f32[4,21,8,128]{3,2,1,0:T(8,128)S(1)}, u32[]{:S(2)}, u32[]{:S(2)}) collective-permute-start(f32[4,21,8,128]{3,2,1,0:T(8,128)S(1)} %get-tuple-element.28), channel_id=1, source_target_pairs={{0,2},{1,3},{2,0},{3,1},{4,6},{5,7},{6,4},{7,5},{8,10},{9,11},{10,... | collective-permute-start | bytes 1032200 | tf_op jit(solution)/shard_map/ppermute | solution.py:50
  50.4 16.1 %collective-permute-start.2 = (f32[4,21,8,128]{3,2,1,0:T(8,128)S(1)}, f32[4,21,8,128]{3,2,1,0:T(8,128)S(1)}, u32[]{:S(2)}, u32[]{:S(2)}) collective-permute-start(f32[4,21,8,128]{3,2,1,0:T(8,128)S(1)} %get-tuple-element.29), channel_id=1, source_target_pairs={{0,1},{1,0},{2,3},{3,2},{4,5},{5,4},{6,7},{7,6},{8,9},{9,8},{10,11... | collective-permute-start | bytes 1032200 | tf_op jit(solution)/shard_map/ppermute | solution.py:50
  68.3 3.8 %collective-permute-start.3 = (f32[9,2,8,128]{3,2,1,0:T(8,128)S(1)}, f32[9,2,8,128]{3,2,1,0:T(8,128)S(1)}, u32[]{:S(2)}, u32[]{:S(2)}) collective-permute-start(f32[9,2,8,128]{3,2,1,0:T(8,128)S(1)} %get-tuple-element.35), channel_id=1, source_target_pairs={{0,1},{1,2},{2,3},{3,0},{4,5},{5,6},{6,7},{7,4},{8,9},{9,10},{10,1... | collective-permute-start | bytes 221192 | tf_op jit(solution)/shard_map/ppermute | solution.py:638
  68.4 3.7 %collective-permute-start.4 = (f32[9,2,8,128]{3,2,1,0:T(8,128)S(1)}, f32[9,2,8,128]{3,2,1,0:T(8,128)S(1)}, u32[]{:S(2)}, u32[]{:S(2)}) collective-permute-start(f32[9,2,8,128]{3,2,1,0:T(8,128)S(1)} %get-tuple-element.36), channel_id=1, source_target_pairs={{0,3},{1,0},{2,1},{3,2},{4,7},{5,4},{6,5},{7,6},{8,11},{9,8},{10,9... | collective-permute-start | bytes 221192 | tf_op jit(solution)/shard_map/ppermute | solution.py:638
  73.8 11.5 %collective-permute-start.5 = (f32[4,16,8,128]{3,2,1,0:T(8,128)S(1)}, f32[4,16,8,128]{3,2,1,0:T(8,128)S(1)}, u32[]{:S(2)}, u32[]{:S(2)}) collective-permute-start(f32[4,16,8,128]{3,2,1,0:T(8,128)S(1)} %get-tuple-element.39), channel_id=1, source_target_pairs={{0,3},{1,2},{2,1},{3,0},{4,7},{5,6},{6,5},{7,4},{8,11},{9,10},{10,... | collective-permute-start | bytes 786440 | tf_op jit(solution)/shard_map/ppermute | solution.py:50
  75.1 8.0 %collective-permute-start.10 = (f32[24,8,128]{2,1,0:T(8,128)S(1)}, f32[24,8,128]{2,1,0:T(8,128)S(1)}, u32[]{:S(2)}, u32[]{:S(2)}) collective-permute-start(f32[24,8,128]{2,1,0:T(8,128)S(1)} %pad_maximum_fusion), channel_id=1, source_target_pairs={{0,4},{4,8},{8,12},{12,16},{16,20},{20,24},{24,28},{28,0},{1,5},{5... | collective-permute-start | bytes 294920 | tf_op jit(solution)/shard_map/ppermute | solution.py:638
  76.8 6.8 %collective-permute-start.11 = (f32[24,8,128]{2,1,0:T(8,128)S(1)}, f32[24,8,128]{2,1,0:T(8,128)S(1)}, u32[]{:S(2)}, u32[]{:S(2)}) collective-permute-start(f32[24,8,128]{2,1,0:T(8,128)S(1)} %pad_maximum_fusion.1), channel_id=1, source_target_pairs={{0,28},{4,0},{8,4},{12,8},{16,12},{20,16},{24,20},{28,24},{1,29},{... | collective-permute-start | bytes 294920 | tf_op jit(solution)/shard_map/ppermute | solution.py:638
  79.8 5.6 %collective-permute-start.8 = (f32[4,8,8,128]{3,2,1,0:T(8,128)S(1)}, f32[4,8,8,128]{3,2,1,0:T(8,128)S(1)}, u32[]{:S(2)}, u32[]{:S(2)}) collective-permute-start(f32[4,8,8,128]{3,2,1,0:T(8,128)S(1)} %get-tuple-element.44), channel_id=1, source_target_pairs={{0,2},{1,3},{2,0},{3,1},{4,6},{5,7},{6,4},{7,5},{8,10},{9,11},{10,... | collective-permute-start | bytes 393224 | tf_op jit(solution)/shard_map/ppermute | solution.py:50
  80.8 4.5 %collective-permute-start.9 = (f32[4,8,8,128]{3,2,1,0:T(8,128)S(1)}, f32[4,8,8,128]{3,2,1,0:T(8,128)S(1)}, u32[]{:S(2)}, u32[]{:S(2)}) collective-permute-start(f32[4,8,8,128]{3,2,1,0:T(8,128)S(1)} %get-tuple-element.45), channel_id=1, source_target_pairs={{0,1},{1,0},{2,3},{3,2},{4,5},{5,4},{6,7},{7,6},{8,9},{9,8},{10,11... | collective-permute-start | bytes 393224 | tf_op jit(solution)/shard_map/ppermute | solution.py:50
  83.0 5.5 %collective-permute-start.6 = (f32[4,8,8,128]{3,2,1,0:T(8,128)S(1)}, f32[4,8,8,128]{3,2,1,0:T(8,128)S(1)}, u32[]{:S(2)}, u32[]{:S(2)}) collective-permute-start(f32[4,8,8,128]{3,2,1,0:T(8,128)S(1)} %get-tuple-element.40), channel_id=1, source_target_pairs={{0,2},{1,3},{2,0},{3,1},{4,6},{5,7},{6,4},{7,5},{8,10},{9,11},{10,... | collective-permute-start | bytes 393224 | tf_op jit(solution)/shard_map/ppermute | solution.py:50
  83.6 5.0 %collective-permute-start.7 = (f32[4,8,8,128]{3,2,1,0:T(8,128)S(1)}, f32[4,8,8,128]{3,2,1,0:T(8,128)S(1)}, u32[]{:S(2)}, u32[]{:S(2)}) collective-permute-start(f32[4,8,8,128]{3,2,1,0:T(8,128)S(1)} %get-tuple-element.41), channel_id=1, source_target_pairs={{0,1},{1,0},{2,3},{3,2},{4,5},{5,4},{6,7},{7,6},{8,9},{9,8},{10,11... | collective-permute-start | bytes 393224 | tf_op jit(solution)/shard_map/ppermute | solution.py:50

commit v15 on v14

--- a/solution.py
+++ b/solution.py
@@ -459,7 +459,7 @@
                 out_ref[q, :, c * LANES : (c + 1) * LANES] = value
 
 
-def stream_pairs(pairs, out_hbm, pair_ref, sems, *lattice):
+def stream_pairs(pairs, out_hbm, pair_ref, sems, *lattice, meanwhile=lambda: None):
     span = pair_ref.shape[3]
 
     def copy(i):
@@ -470,6 +470,7 @@
     for i, pair in enumerate(pairs):
         stream_pair(2 * pair, pair_ref.at[i], *lattice)
         copy(i).start()
+    meanwhile()
     for i in range(len(pairs)):
         copy(i).wait()
 
@@ -548,14 +549,15 @@
         for half in range(2):
             main_ref[18 + q, half] = xlo_ref[q * 2 + half]
             main_ref[q, 2 * EDGE + 2 + half] = xhi_ref[q * 2 + half]
-    to = 0
-    for first, last in KEPT:
-        for row in range(2 * first + 2, 2 * last + 2):
-            for q in range(NQ):
-                kept_ref[q, to] = main_ref[q, row]
-            to += 1
-
-    stream_pairs(PAIRS[0], out_ref, pair_ref, sems, main_ref, below_ref, above_ref)
+    def keep_rows():
+        to = 0
+        for first, last in KEPT:
+            for row in range(2 * first + 2, 2 * last + 2):
+                for q in range(NQ):
+                    kept_ref[q, to] = main_ref[q, row]
+                to += 1
+
+    stream_pairs(PAIRS[0], out_ref, pair_ref, sems, main_ref, below_ref, above_ref, meanwhile=keep_rows)
 
 
 def finish_kernel(count, plan_ref, *refs):

time: 91.7 us -> 91.7 us (level)
  no operation moved by 1% of the time
where the time goes in v15:
time: 91.7 us; the launch traced here: 91.4 us
  waiting for transfers between devices  52.9 us (58%)
  starting transfers between devices  22.1 us (24%)
  Pallas kernels  16.3 us (18%)
    all_to_all x2, waiting for transfers between devices, to_rows(): return lax.all_to_all(sent, 'row', split_axis=0, concat_axis=0, tiled=True)  30.9 us
    ppermute x8, waiting for transfers between devices, exchanged(): return lax.ppermute(value, axis, pairs)  17.7 us
    all_to_all x2, starting transfers between devices, to_rows(): return lax.all_to_all(sent, 'row', split_axis=0, concat_axis=0, tiled=True)  10.9 us
    ppermute x4, starting transfers between devices, shifted(): lax.ppermute(value, axis, [(i, (i + step) % count) for i in range(count)])  6.52 us
    pallas_call x2, Pallas kernels, pre(): pl.pallas_call(functools.partial(pre_kernel, cap, row_count, per_row, par...  6.11 us
    ppermute x8, starting transfers between devices, exchanged(): return lax.ppermute(value, axis, pairs)  4.72 us
    ppermute x4, waiting for transfers between devices, shifted(): lax.ppermute(value, axis, [(i, (i + step) % count) for i in range(count)])  4.23 us
    pallas_call x1, Pallas kernels, advance(): pl.pallas_call(functools.partial(advance_kernel, len(homes)), in_specs=[p...  3.15 us
  transfers between devices with their start and end apart: 14, of which 7 were waited for; matrix products, arithmetic and copies ran while one was open for 0% of the time, Pallas kernels for 10%

profile of v15, /device:TPU:0, one launch (start us, length us, event | category | flops | bytes accessed | tf_op | source)
XLA Modules:
  0.0 91.4 jit_solution(16105453097456338097)
XLA Ops:
  0.0 3.4 %pre_0.1 = f32[16,21,8,128]{3,2,1,0:T(8,128)} custom-call(s32[8]{0:T(128)} %dest_hbm.1, s32[8]{0:T(128)} %level_hbm.3, f32[27,8,4096]{2,1,0:T(8,128)} %bitcast.14), custom_call_target="tpu_custom_call" | custom-call | flops 10000000 | bytes 4000000 | tf_op jit(solution)/shard_map/pre_0/pallas_call | solution.py:204
  3.4 7.3 %all-to-all-start = ((f32[16,21,8,128]{3,2,1,0:T(8,128)}), f32[16,21,8,128]{3,2,1,0:T(8,128)S(1)}, u32[]{:S(2)}, u32[]{:S(2)}) async-start(f32[16,21,8,128]{3,2,1,0:T(8,128)} %pre_0.1), calls=%async_computation | async-start | bytes 2752512 | tf_op jit(solution)/shard_map/all_to_all | solution.py:660
  10.7 2.7 %pre_1.1 = f32[16,16,8,128]{3,2,1,0:T(8,128)} custom-call(s32[8]{0:T(128)} %dest_hbm.1, s32[8]{0:T(128)} %level_hbm.3, f32[27,8,4096]{2,1,0:T(8,128)} %bitcast.15), custom_call_target="tpu_custom_call" | custom-call | flops 10000000 | bytes 4000000 | tf_op jit(solution)/shard_map/pre_1/pallas_call | solution.py:204
  13.4 30.1 %all-to-all-done.refs_0_ = f32[16,21,8,128]{3,2,1,0:T(8,128)S(1)} async-done(((f32[16,21,8,128]{3,2,1,0:T(8,128)}), f32[16,21,8,128]{3,2,1,0:T(8,128)S(1)}, u32[]{:S(2)}, u32[]{:S(2)}) %all-to-all-start) | async-done | bytes 1376288 | tf_op jit(solution)/shard_map/all_to_all | solution.py:660
  43.5 3.6 %all-to-all-start.1 = ((f32[16,16,8,128]{3,2,1,0:T(8,128)}), f32[16,16,8,128]{3,2,1,0:T(8,128)S(1)}, u32[]{:S(2)}, u32[]{:S(2)}) async-start(f32[16,16,8,128]{3,2,1,0:T(8,128)} %pre_1.1), calls=%async_computation.1 | async-start | bytes 2097152 | tf_op jit(solution)/shard_map/all_to_all | solution.py:660
  47.1 1.7 %repack_0.1 = (f32[4,21,8,128]{3,2,1,0:T(8,128)S(1)}, f32[4,21,8,128]{3,2,1,0:T(8,128)S(1)}, f32[4,21,8,128]{3,2,1,0:T(8,128)S(1)}, f32[4,21,8,128]{3,2,1,0:T(8,128)S(1)}, s32[16]{0:T(128)S(1)}) custom-call(f32[16,21,8,128]{3,2,1,0:T(8,128)S(1)} %all-to-all-done.refs_0_), custom_call_target="tpu_custom_call" | custom-call | bytes 3000000 | tf_op jit(solution)/shard_map/repack_0/pallas_call | solution.py:291
  48.8 0.9 %collective-permute-start = (f32[4,21,8,128]{3,2,1,0:T(8,128)S(1)}, f32[4,21,8,128]{3,2,1,0:T(8,128)S(1)}, u32[]{:S(2)}, u32[]{:S(2)}) collective-permute-start(f32[4,21,8,128]{3,2,1,0:T(8,128)S(1)} %get-tuple-element.27), channel_id=1, source_target_pairs={{0,3},{1,2},{2,1},{3,0},{4,7},{5,6},{6,5},{7,4},{8,11},{9,10},{10,... | collective-permute-start | bytes 1032200 | tf_op jit(solution)/shard_map/ppermute | solution.py:50
  49.7 0.7 collective-permute-start.1
  50.4 0.3 collective-permute-start.2
  50.7 8.4 %collective-permute-done.refs_0_ = f32[4,21,8,128]{3,2,1,0:T(8,128)S(1)} collective-permute-done((f32[4,21,8,128]{3,2,1,0:T(8,128)S(1)}, f32[4,21,8,128]{3,2,1,0:T(8,128)S(1)}, u32[]{:S(2)}, u32[]{:S(2)}) %collective-permute-start) | collective-permute-done | bytes 344096 | tf_op jit(solution)/shard_map/ppermute | solution.py:50
  59.1 7.4 %collective-permute-done.1.refs_1_ = f32[4,21,8,128]{3,2,1,0:T(8,128)S(1)} collective-permute-done((f32[4,21,8,128]{3,2,1,0:T(8,128)S(1)}, f32[4,21,8,128]{3,2,1,0:T(8,128)S(1)}, u32[]{:S(2)}, u32[]{:S(2)}) %collective-permute-start.1) | collective-permute-done | bytes 344096 | tf_op jit(solution)/shard_map/ppermute | solution.py:50
  66.6 0.0 collective-permute-done.2.refs_2_
  66.6 1.7 %faces.1 = (f32[9,2,8,128]{3,2,1,0:T(8,128)S(1)}, f32[9,2,8,128]{3,2,1,0:T(8,128)S(1)}, f32[9,2,8,128]{3,2,1,0:T(8,128)S(1)}, f32[9,2,8,128]{3,2,1,0:T(8,128)S(1...) custom-call(f32[4,21,8,128]{3,2,1,0:T(8,128)S(1)} %collective-permute-done.refs_0_, ...), custom_call_target="tpu_custom_call" | custom-call | flops 10000000 | bytes 3000000 | tf_op jit(solution)/shard_map/faces/pallas_call | solution.py:515
  68.3 0.1 collective-permute-start.3
  68.4 1.7 %collective-permute-start.4 = (f32[9,2,8,128]{3,2,1,0:T(8,128)S(1)}, f32[9,2,8,128]{3,2,1,0:T(8,128)S(1)}, u32[]{:S(2)}, u32[]{:S(2)}) collective-permute-start(f32[9,2,8,128]{3,2,1,0:T(8,128)S(1)} %get-tuple-element.36), channel_id=1, source_target_pairs={{0,3},{1,0},{2,1},{3,2},{4,7},{5,4},{6,5},{7,6},{8,11},{9,8},{10,9... | collective-permute-start | bytes 221192 | tf_op jit(solution)/shard_map/ppermute | solution.py:640
  70.1 2.0 %collective-permute-done.3.refs_7_.refs_6_ = f32[9,2,8,128]{3,2,1,0:T(8,128)S(1)} collective-permute-done((f32[9,2,8,128]{3,2,1,0:T(8,128)S(1)}, f32[9,2,8,128]{3,2,1,0:T(8,128)S(1)}, u32[]{:S(2)}, u32[]{:S(2)}) %collective-permute-start.3) | collective-permute-done | bytes 73760 | tf_op jit(solution)/shard_map/ppermute | solution.py:640
  72.1 0.0 collective-permute-done.4.refs_8_.refs_7_
  72.2 0.9 all-to-all-done.1.refs_1_
  73.1 0.8 repack_1.1
  73.8 1.2 %collective-permute-start.5 = (f32[4,16,8,128]{3,2,1,0:T(8,128)S(1)}, f32[4,16,8,128]{3,2,1,0:T(8,128)S(1)}, u32[]{:S(2)}, u32[]{:S(2)}) collective-permute-start(f32[4,16,8,128]{3,2,1,0:T(8,128)S(1)} %get-tuple-element.39), channel_id=1, source_target_pairs={{0,3},{1,2},{2,1},{3,0},{4,7},{5,6},{6,5},{7,4},{8,11},{9,10},{10,... | collective-permute-start | bytes 786440 | tf_op jit(solution)/shard_map/ppermute | solution.py:50
  75.1 1.7 %collective-permute-start.10 = (f32[24,8,128]{2,1,0:T(8,128)S(1)}, f32[24,8,128]{2,1,0:T(8,128)S(1)}, u32[]{:S(2)}, u32[]{:S(2)}) collective-permute-start(f32[24,8,128]{2,1,0:T(8,128)S(1)} %pad_maximum_fusion), channel_id=1, source_target_pairs={{0,4},{4,8},{8,12},{12,16},{16,20},{20,24},{24,28},{28,0},{1,5},{5... | collective-permute-start | bytes 294920 | tf_op jit(solution)/shard_map/ppermute | solution.py:640
  76.8 3.0 %collective-permute-start.11 = (f32[24,8,128]{2,1,0:T(8,128)S(1)}, f32[24,8,128]{2,1,0:T(8,128)S(1)}, u32[]{:S(2)}, u32[]{:S(2)}) collective-permute-start(f32[24,8,128]{2,1,0:T(8,128)S(1)} %pad_maximum_fusion.1), channel_id=1, source_target_pairs={{0,28},{4,0},{8,4},{12,8},{16,12},{20,16},{24,20},{28,24},{1,29},{... | collective-permute-start | bytes 294920 | tf_op jit(solution)/shard_map/ppermute | solution.py:640
  79.8 1.1 %collective-permute-start.8 = (f32[4,8,8,128]{3,2,1,0:T(8,128)S(1)}, f32[4,8,8,128]{3,2,1,0:T(8,128)S(1)}, u32[]{:S(2)}, u32[]{:S(2)}) collective-permute-start(f32[4,8,8,128]{3,2,1,0:T(8,128)S(1)} %get-tuple-element.44), channel_id=1, source_target_pairs={{0,2},{1,3},{2,0},{3,1},{4,6},{5,7},{6,4},{7,5},{8,10},{9,11},{10,... | collective-permute-start | bytes 393224 | tf_op jit(solution)/shard_map/ppermute | solution.py:50
  80.8 0.0 collective-permute-start.9
  80.8 2.2 %collective-permute-done.10.refs_5_ = f32[24,8,128]{2,1,0:T(8,128)S(1)} collective-permute-done((f32[24,8,128]{2,1,0:T(8,128)S(1)}, f32[24,8,128]{2,1,0:T(8,128)S(1)}, u32[]{:S(2)}, u32[]{:S(2)}) %collective-permute-start.10) | collective-permute-done | bytes 98336 | tf_op jit(solution)/shard_map/ppermute | solution.py:640
  83.0 0.5 collective-permute-start.6
  83.5 0.0 collective-permute-start.7
  83.6 1.8 %collective-permute-done.8.refs_1_ = f32[4,8,8,128]{3,2,1,0:T(8,128)S(1)} collective-permute-done((f32[4,8,8,128]{3,2,1,0:T(8,128)S(1)}, f32[4,8,8,128]{3,2,1,0:T(8,128)S(1)}, u32[]{:S(2)}, u32[]{:S(2)}) %collective-permute-start.8) | collective-permute-done | bytes 131104 | tf_op jit(solution)/shard_map/ppermute | solution.py:50
  85.4 0.0 collective-permute-done.5.refs_0_
  85.4 3.2 %advance.1 = (f32[27,8,4096]{2,1,0:T(8,128)}, f32[27,12,8,128]{3,2,1,0:T(8,128)S(1)}) custom-call(s32[16]{0:T(128)S(1)} %get-tuple-element.31.plan_ref, f32[4,16,8,128]{3,2,1,0:T(8,128)S(1)} %collective-permute-done.5.refs_0_, f32[4,8,8,128]{3,2,1,0:T(8,128)S(1)} %collective-permute-done.8.refs_1_, f32[4,8,8,128]{3,2,1,0:T(8,128)S(1)} %collective-permute-done.9.refs_2_, ...), custom_call_target="tpu_custom_call" | custom-call | flops 10000000 | bytes 5000000 | tf_op jit(solution)/shard_map/advance/pallas_call | solution.py:606
  88.5 0.0 collective-permute-done.7.refs_2_
  88.5 2.9 %finish.1 = f32[27,8,4096]{2,1,0:T(8,128)} custom-call(s32[16]{0:T(128)S(1)} %get-tuple-element.31.plan_ref, f32[4,16,8,128]{3,2,1,0:T(8,128)S(1)} %collective-permute-done.5.refs_0_, f32[4,8,8,128]{3,2,1,0:T(8,128)S(1)} %collective-permute-done.6.refs_1_, f32[4,8,8,128]{3,2,1,0:T(8,128)S(1)} %collective-permute-done.7.refs_2_, ...), custom_call_target="tpu_custom_call", output_to_operand_aliasing={{}: (9, {})} | custom-call | flops 10000000 | bytes 5000000 | tf_op jit(solution)/shard_map/finish/pallas_call | solution.py:625
  (7 shorter events, 0.0 us)
Async XLA Ops:
  3.4 40.1 %all-to-all-start = ((f32[16,21,8,128]{3,2,1,0:T(8,128)}), f32[16,21,8,128]{3,2,1,0:T(8,128)S(1)}, u32[]{:S(2)}, u32[]{:S(2)}) async-start(f32[16,21,8,128]{3,2,1,0:T(8,128)} %pre_0.1), calls=%async_computation | async-start | bytes 2752512 | tf_op jit(solution)/shard_map/all_to_all | solution.py:660
  43.5 29.6 %all-to-all-start.1 = ((f32[16,16,8,128]{3,2,1,0:T(8,128)}), f32[16,16,8,128]{3,2,1,0:T(8,128)S(1)}, u32[]{:S(2)}, u32[]{:S(2)}) async-start(f32[16,16,8,128]{3,2,1,0:T(8,128)} %pre_1.1), calls=%async_computation.1 | async-start | bytes 2097152 | tf_op jit(solution)/shard_map/all_to_all | solution.py:660
  48.8 10.4 %collective-permute-start = (f32[4,21,8,128]{3,2,1,0:T(8,128)S(1)}, f32[4,21,8,128]{3,2,1,0:T(8,128)S(1)}, u32[]{:S(2)}, u32[]{:S(2)}) collective-permute-start(f32[4,21,8,128]{3,2,1,0:T(8,128)S(1)} %get-tuple-element.27), channel_id=1, source_target_pairs={{0,3},{1,2},{2,1},{3,0},{4,7},{5,6},{6,5},{7,4},{8,11},{9,10},{10,... | collective-permute-start | bytes 1032200 | tf_op jit(solution)/shard_map/ppermute | solution.py:50
  49.7 16.9 %collective-permute-start.1 = (f32[4,21,8,128]{3,2,1,0:T(8,128)S(1)}, f32[4,21,8,128]{3,2,1,0:T(8,128)S(1)}, u32[]{:S(2)}, u32[]{:S(2)}) collective-permute-start(f32[4,21,8,128]{3,2,1,0:T(8,128)S(1)} %get-tuple-element.28), channel_id=1, source_target_pairs={{0,2},{1,3},{2,0},{3,1},{4,6},{5,7},{6,4},{7,5},{8,10},{9,11},{10,... | collective-permute-start | bytes 1032200 | tf_op jit(solution)/shard_map/ppermute | solution.py:50
  50.4 16.1 %collective-permute-start.2 = (f32[4,21,8,128]{3,2,1,0:T(8,128)S(1)}, f32[4,21,8,128]{3,2,1,0:T(8,128)S(1)}, u32[]{:S(2)}, u32[]{:S(2)}) collective-permute-start(f32[4,21,8,128]{3,2,1,0:T(8,128)S(1)} %get-tuple-element.29), channel_id=1, source_target_pairs={{0,1},{1,0},{2,3},{3,2},{4,5},{5,4},{6,7},{7,6},{8,9},{9,8},{10,11... | collective-permute-start | bytes 1032200 | tf_op jit(solution)/shard_map/ppermute | solution.py:50
  68.3 3.8 %collective-permute-start.3 = (f32[9,2,8,128]{3,2,1,0:T(8,128)S(1)}, f32[9,2,8,128]{3,2,1,0:T(8,128)S(1)}, u32[]{:S(2)}, u32[]{:S(2)}) collective-permute-start(f32[9,2,8,128]{3,2,1,0:T(8,128)S(1)} %get-tuple-element.35), channel_id=1, source_target_pairs={{0,1},{1,2},{2,3},{3,0},{4,5},{5,6},{6,7},{7,4},{8,9},{9,10},{10,1... | collective-permute-start | bytes 221192 | tf_op jit(solution)/shard_map/ppermute | solution.py:640
  68.4 3.7 %collective-permute-start.4 = (f32[9,2,8,128]{3,2,1,0:T(8,128)S(1)}, f32[9,2,8,128]{3,2,1,0:T(8,128)S(1)}, u32[]{:S(2)}, u32[]{:S(2)}) collective-permute-start(f32[9,2,8,128]{3,2,1,0:T(8,128)S(1)} %get-tuple-element.36), channel_id=1, source_target_pairs={{0,3},{1,0},{2,1},{3,2},{4,7},{5,4},{6,5},{7,6},{8,11},{9,8},{10,9... | collective-permute-start | bytes 221192 | tf_op jit(solution)/shard_map/ppermute | solution.py:640
  73.8 11.5 %collective-permute-start.5 = (f32[4,16,8,128]{3,2,1,0:T(8,128)S(1)}, f32[4,16,8,128]{3,2,1,0:T(8,128)S(1)}, u32[]{:S(2)}, u32[]{:S(2)}) collective-permute-start(f32[4,16,8,128]{3,2,1,0:T(8,128)S(1)} %get-tuple-element.39), channel_id=1, source_target_pairs={{0,3},{1,2},{2,1},{3,0},{4,7},{5,6},{6,5},{7,4},{8,11},{9,10},{10,... | collective-permute-start | bytes 786440 | tf_op jit(solution)/shard_map/ppermute | solution.py:50
  75.1 8.0 %collective-permute-start.10 = (f32[24,8,128]{2,1,0:T(8,128)S(1)}, f32[24,8,128]{2,1,0:T(8,128)S(1)}, u32[]{:S(2)}, u32[]{:S(2)}) collective-permute-start(f32[24,8,128]{2,1,0:T(8,128)S(1)} %pad_maximum_fusion), channel_id=1, source_target_pairs={{0,4},{4,8},{8,12},{12,16},{16,20},{20,24},{24,28},{28,0},{1,5},{5... | collective-permute-start | bytes 294920 | tf_op jit(solution)/shard_map/ppermute | solution.py:640
  76.8 6.8 %collective-permute-start.11 = (f32[24,8,128]{2,1,0:T(8,128)S(1)}, f32[24,8,128]{2,1,0:T(8,128)S(1)}, u32[]{:S(2)}, u32[]{:S(2)}) collective-permute-start(f32[24,8,128]{2,1,0:T(8,128)S(1)} %pad_maximum_fusion.1), channel_id=1, source_target_pairs={{0,28},{4,0},{8,4},{12,8},{16,12},{20,16},{24,20},{28,24},{1,29},{... | collective-permute-start | bytes 294920 | tf_op jit(solution)/shard_map/ppermute | solution.py:640
  79.8 5.6 %collective-permute-start.8 = (f32[4,8,8,128]{3,2,1,0:T(8,128)S(1)}, f32[4,8,8,128]{3,2,1,0:T(8,128)S(1)}, u32[]{:S(2)}, u32[]{:S(2)}) collective-permute-start(f32[4,8,8,128]{3,2,1,0:T(8,128)S(1)} %get-tuple-element.44), channel_id=1, source_target_pairs={{0,2},{1,3},{2,0},{3,1},{4,6},{5,7},{6,4},{7,5},{8,10},{9,11},{10,... | collective-permute-start | bytes 393224 | tf_op jit(solution)/shard_map/ppermute | solution.py:50
  80.8 4.5 %collective-permute-start.9 = (f32[4,8,8,128]{3,2,1,0:T(8,128)S(1)}, f32[4,8,8,128]{3,2,1,0:T(8,128)S(1)}, u32[]{:S(2)}, u32[]{:S(2)}) collective-permute-start(f32[4,8,8,128]{3,2,1,0:T(8,128)S(1)} %get-tuple-element.45), channel_id=1, source_target_pairs={{0,1},{1,0},{2,3},{3,2},{4,5},{5,4},{6,7},{7,6},{8,9},{9,8},{10,11... | collective-permute-start | bytes 393224 | tf_op jit(solution)/shard_map/ppermute | solution.py:50
  83.0 5.5 %collective-permute-start.6 = (f32[4,8,8,128]{3,2,1,0:T(8,128)S(1)}, f32[4,8,8,128]{3,2,1,0:T(8,128)S(1)}, u32[]{:S(2)}, u32[]{:S(2)}) collective-permute-start(f32[4,8,8,128]{3,2,1,0:T(8,128)S(1)} %get-tuple-element.40), channel_id=1, source_target_pairs={{0,2},{1,3},{2,0},{3,1},{4,6},{5,7},{6,4},{7,5},{8,10},{9,11},{10,... | collective-permute-start | bytes 393224 | tf_op jit(solution)/shard_map/ppermute | solution.py:50
  83.5 5.0 %collective-permute-start.7 = (f32[4,8,8,128]{3,2,1,0:T(8,128)S(1)}, f32[4,8,8,128]{3,2,1,0:T(8,128)S(1)}, u32[]{:S(2)}, u32[]{:S(2)}) collective-permute-start(f32[4,8,8,128]{3,2,1,0:T(8,128)S(1)} %get-tuple-element.41), channel_id=1, source_target_pairs={{0,1},{1,0},{2,3},{3,2},{4,5},{5,4},{6,7},{7,6},{8,9},{9,8},{10,11... | collective-permute-start | bytes 393224 | tf_op jit(solution)/shard_map/ppermute | solution.py:50
